TPU v7x, 256 devices: a whole 4x4x8 slice. The times are simulated.
256 devices in a mesh: dp: 16 (over y, x_hi, core), tensor: 16 (over x_lo, z).
Axes of the slice: x: 4 (x_hi: 2, x_lo: 2; x = x_hi * 2 + x_lo), y: 4, z: 8, core: 2. Of those that a mesh axis runs over, the one named last changes fastest.
Arguments:
- acts: bfloat16 [32, 256, 36864], P('dp', None, 'tensor'), may hold values from -18 to 18
- out_grads: bfloat16 [32, 256, 4608], P('dp', None, 'tensor'), may hold values from -0.000115088994 to 0.000115088994
- other_sq: float32 [32, 128], P('dp', 'tensor'), may hold values from 0.00390625 to 0.2109375
- noise: float32 [4608, 36864], P('dp', 'tensor'), may hold values from -6 to 6
Outputs:
- noisy_grad: float32 [4608, 36864], P('dp', 'tensor')
All inputs are finite; a program needn't handle non-finite values.
Results may differ from a plain program's by a relative error of at most 0.019.
Values may be sent and summed in bfloat16 or wider, within the bound.
No kernel may reach another device: no remote copies, remote signals or barrier semaphores. Data moves between devices by JAX's collectives and lax.ppermute only.
A program may use at most 192 MiB of HBM per device.

v0:
```python
import math

import jax
import jax.numpy as jnp
from jax import lax
from jax.sharding import PartitionSpec as P

clip_norm = 2.5


def shards(acts, out_grads, other_sq, noise):
    full_grads = lax.all_gather(out_grads, "tensor", axis=2, tiled=True)
    width = full_grads.shape[2]
    hidden_all = acts.shape[2] * lax.axis_size("tensor")
    batch_all = acts.shape[0] * lax.axis_size("dp")
    act_gram = jnp.einsum("btf,bsf->bts", acts, acts, preferred_element_type=jnp.float32)
    grad_gram = jnp.einsum(
        "btd,bsd->bts", full_grads, full_grads, preferred_element_type=jnp.float32
    )
    other_local = jnp.sum(other_sq, axis=1)
    gram_total, other_total = (
        lax.psum(act_gram.astype(jnp.bfloat16), "tensor").astype(jnp.float32),
        lax.psum(other_local.astype(jnp.bfloat16), "tensor").astype(jnp.float32),
    )
    squares = jnp.sum(gram_total * grad_gram, axis=(1, 2))
    total = squares + other_total
    clip = jnp.minimum(1.0, clip_norm / jnp.sqrt(total))

    def add_example(inner, item):
        grad_b, act_b = item
        term = jnp.einsum("td,tf->df", grad_b, act_b, preferred_element_type=jnp.float32)
        term = lax.optimization_barrier(term.astype(jnp.bfloat16))
        return (inner + term.astype(jnp.float32), None)

    scaled = (clip[:, None, None] * full_grads.astype(jnp.float32)).astype(jnp.bfloat16)
    empty = jnp.zeros(
        (width // lax.axis_size("dp") * lax.axis_size("dp"), acts.shape[2]), jnp.float32
    )
    result, _ = lax.scan(add_example, empty, (scaled, acts))
    summed = lax.psum_scatter(
        result.astype(jnp.bfloat16), "dp", scatter_dimension=0, tiled=True
    ).astype(jnp.float32)
    factor = math.sqrt(hidden_all * width) / clip_norm
    return (factor * summed + noise) / math.sqrt(batch_all)


def solution(mesh):
    placed = (
        P("dp", None, "tensor"),
        P("dp", None, "tensor"),
        P("dp", "tensor"),
        P("dp", "tensor"),
    )
    return jax.shard_map(
        shards, mesh=mesh, in_specs=placed, out_specs=P("dp", "tensor"), check_vma=False
    )
```

profile of v0, /device:TPU:32, one launch (start us, length us, event | category | flops | bytes accessed | tf_op | source)
XLA Modules:
  0.0 517.4 jit_solution(15497265456044680491)
XLA Ops:
  6.5 0.0 copy-start.3
  6.5 0.0 all-reduce.2.cloned.1.call-start
  6.5 3.9 convolution_convert_fusion.1
  10.4 0.0 all-reduce.2.cloned.1.call-update
  10.5 0.0 all-gather.2.cloned.1.call-start
  10.5 0.7 all-gather.2.cloned.1.call-update
  11.2 0.0 reduce-scatter.2.cloned.1.call-start
  11.3 0.0 copy-done.3
  11.3 0.1 reduce_sum.19
  11.4 34.4 %psum.15 = bf16[2]{0:T(256)(128)(2,1)S(1)} all-reduce(bf16[2]{0:T(256)(128)(2,1)S(1)} %reduce_sum.19), channel_id=1, replica_groups=mesh['dp'=16,'tensor'=16] {'tensor'}, use_global_device_ids=true, to_apply=%region_3.0 | all-reduce | flops 2 | bytes 8 | tf_op jit(solution)/shard_map/psum | solution.py:23
  45.8 100.7 %all-reduce.2.cloned.1.call-done = bf16[2,256,256]{2,1,0:T(8,128)(2,1)} async-done(((bf16[2,256,256]{2,1,0:T(8,128)(2,1)}), bf16[2,256,256]{2,1,0:T(8,128)(2,1)}) %all-reduce.2.cloned.1.call-update) | async-done | bytes 262160 | tf_op jit(solution)/shard_map/psum | solution.py:22
  146.5 77.2 %all-gather.2.cloned.1.call-done = bf16[2,256,4608]{1,2,0:T(8,128)(2,1)} async-done(((bf16[2,256,288]{1,2,0:T(8,128)(2,1)}), bf16[2,256,4608]{1,2,0:T(8,128)(2,1)}) %all-gather.2.cloned.1.call-update) | async-done | bytes 4718608 | tf_op jit(solution)/shard_map/all_gather | solution.py:12
  223.8 0.0 copy-start.1
  223.8 5.9 %fusion.5 = f32[2]{0:T(128)S(1)} fusion(bf16[2,256,4608]{1,2,0:T(8,128)(2,1)} %all-gather.2.cloned.1.call-done, bf16[2,256,256]{2,1,0:T(8,128)(2,1)} %all-reduce.2.cloned.1.call-done), kind=kOutput, calls=%fused_computation.11 | convolution fusion | flops 1208352768 | bytes 4980744 | tf_op jit(solution)/shard_map/btd,bsd->bts/dot_general | solution.py:17
  229.7 0.0 copy-done.1
  229.7 0.0 copy-start
  229.7 3.6 multiply_convert_fusion
  233.3 0.0 copy-done
  233.3 77.9 %while.11 = (s32[]{:T(128)}, f32[4608,2304]{1,0:T(8,128)}, bf16[2,256,4608]{1,2,0:T(8,128)(2,1)}, bf16[2,256,2304]{2,1,0:T(8,128)(2,1)S(1)}, s32[]{:T(128)}, /*index=5*/s32[]{:T(128)}) while((s32[]{:T(128)}, f32[4608,2304]{1,0:T(8,128)}, bf16[2,256,4608]{1,2,0:T(8,128)(2,1)}, bf16[2,256,2304]{2,1,0:T(8,128)(2,1)S(1)}, s32[]{:T(128)}, ...), condition=%wide.region_5.6_spmd.clone, body=%wide.region_4.5_spmd.clone.sunk | while | flops 5478285312 | bytes 130942040 | solution.py:39
  233.3 11.7 %convolution_convert_fusion.3 = bf16[4608,2304]{1,0:T(8,128)(2,1)} fusion(bf16[2,256,4608]{1,2,0:T(8,128)(2,1)} %get-tuple-element.94, s32[]{:T(128)S(6)} %copy.10, bf16[2,256,2304]{2,1,0:T(8,128)(2,1)S(1)} %get-tuple-element.95), kind=kOutput, calls=%fused_computation.1.clone.1 | convolution fusion | flops 5446434816 | bytes 24773632 | tf_op jit(solution)/shard_map/while/body/eval_jaxpr/td,tf->df/dot_general | solution.py:31
  245.0 20.2 %select_add_fusion.2 = f32[4608,2304]{1,0:T(8,128)} fusion(f32[4608,2304]{1,0:T(8,128)} %get-tuple-element.87, bf16[4608,2304]{1,0:T(8,128)(2,1)} %convolution_convert_fusion.3, pred[]{:T(512)S(6)} %compare.3), kind=kLoop, calls=%fused_computation.clone.1 | loop fusion | flops 31850496 | bytes 106168320 | tf_op jit(solution)/shard_map/while/body/eval_jaxpr/add | solution.py:33
  265.2 11.7 %convolution_convert_fusion.3 = bf16[4608,2304]{1,0:T(8,128)(2,1)} fusion(bf16[2,256,4608]{1,2,0:T(8,128)(2,1)} %get-tuple-element.94, s32[]{:T(128)S(6)} %copy.10, bf16[2,256,2304]{2,1,0:T(8,128)(2,1)S(1)} %get-tuple-element.95), kind=kOutput, calls=%fused_computation.1.clone.1 | convolution fusion | flops 5446434816 | bytes 24773632 | tf_op jit(solution)/shard_map/while/body/eval_jaxpr/td,tf->df/dot_general | solution.py:31
  276.9 34.3 %select_add_fusion.2 = f32[4608,2304]{1,0:T(8,128)} fusion(f32[4608,2304]{1,0:T(8,128)} %get-tuple-element.87, bf16[4608,2304]{1,0:T(8,128)(2,1)} %convolution_convert_fusion.3, pred[]{:T(512)S(6)} %compare.3), kind=kLoop, calls=%fused_computation.clone.1 | loop fusion | flops 31850496 | bytes 106168320 | tf_op jit(solution)/shard_map/while/body/eval_jaxpr/add | solution.py:33
  311.2 21.5 %convert_element_type.36 = bf16[4608,2304]{1,0:T(8,128)(2,1)} convert(f32[4608,2304]{1,0:T(8,128)} %get-tuple-element.27) | non-fusion elementwise | flops 10616832 | bytes 63700992 | tf_op jit(solution)/shard_map/convert_element_type | solution.py:41
  332.7 0.0 copy-start.2
  332.7 0.0 reduce-scatter.2.cloned.1.call-update
  332.7 175.0 %reduce-scatter.2.cloned.1.call-done = bf16[288,2304]{1,0:T(8,128)(2,1)} async-done(((bf16[4608,2304]{1,0:T(8,128)(2,1)}), bf16[288,2304]{1,0:T(8,128)(2,1)}) %reduce-scatter.2.cloned.1.call-update) | async-done | bytes 1327120 | tf_op jit(solution)/shard_map/reduce_scatter | solution.py:40
  507.7 0.0 copy-done.2
  507.7 3.2 add_multiply_fusion
  (2 shorter events, 0.0 us)
Async XLA Ops:
  6.5 4.7 copy-start.3
  6.5 140.0 %all-reduce.2.cloned.1.call-start = ((), (), s32[]{:S(2)}) async-start(), calls=%async_computation.1 | async-start | bytes 524288 | tf_op jit(solution)/shard_map/psum | solution.py:22
  10.5 213.3 %all-gather.2.cloned.1.call-start = ((), (), s32[]{:S(2)}) async-start(), calls=%async_computation.2 | async-start | bytes 5013504 | tf_op jit(solution)/shard_map/all_gather | solution.py:12
  11.2 496.5 %reduce-scatter.2.cloned.1.call-start = ((), (), s32[]{:S(2)}) async-start(), calls=%async_computation.3 | async-start | bytes 22560768 | tf_op jit(solution)/shard_map/reduce_scatter | solution.py:40
  223.8 5.9 %copy-start.1 = (bf16[2,256,4608]{1,2,0:T(8,128)(2,1)S(1)}, bf16[2,256,4608]{1,2,0:T(8,128)(2,1)}, u32[]{:S(2)}) copy-start(bf16[2,256,4608]{1,2,0:T(8,128)(2,1)} %all-gather.2.cloned.1.call-done) | copy-start | bytes 14155780
  229.7 3.6 copy-start
  332.7 175.0 %copy-start.2 = (f32[288,2304]{1,0:T(8,128)S(1)}, f32[288,2304]{1,0:T(8,128)}, u32[]{:S(2)}) copy-start(f32[288,2304]{1,0:T(8,128)} %param.9) | copy-start | bytes 7962628
Sparse Core Ops, SparseCore 0:
  10.6 135.8 all-reduce.1
  148.4 75.2 all-gather.1
  332.8 174.8 reduce-scatter.1
where the time goes:
time: 518 us; the launch traced here: 517 us
  waiting for transfers between devices  354 us (68%)
  other arithmetic  82.9 us (16%)
  blocking collectives  34.4 us (7%)
  matrix products  33.2 us (6%)
  between operations  13.1 us (3%)
    reduce_scatter x1, waiting for transfers between devices, shards(): lax.psum_scatter(result.astype(jnp.bfloat16), 'dp', scatter_dimension=0,...  175 us
    psum x1, waiting for transfers between devices, shards(): lax.psum(act_gram.astype(jnp.bfloat16), 'tensor').astype(jnp.float32)  101 us
    all_gather x1, waiting for transfers between devices, shards(): full_grads = lax.all_gather(out_grads, 'tensor', axis=2, tiled=True)  77.2 us
    add x2, other arithmetic, add_example(): return (inner + term.astype(jnp.float32), None)  54.5 us
    psum x1, blocking collectives, shards(): lax.psum(other_local.astype(jnp.bfloat16), 'tensor').astype(jnp.float32)  34.4 us
    dot_general x2, matrix products, add_example(): jnp.einsum('td,tf->df', grad_b, act_b, preferred_element_type=jnp.float32)  23.4 us
    convert_element_type x1, other arithmetic, shards(): result.astype(jnp.bfloat16)  21.5 us
  transfers between devices with their start and end apart: 3, of which 3 were waited for; matrix products, arithmetic and copies ran while one was open for 0% of the time, Pallas kernels for 0%

commit v1 on v0

v1 whole, which is shorter than its diff:
```python
import functools
import math

import jax
import jax.numpy as jnp
from jax import lax
from jax.experimental import pallas as pl
from jax.experimental.pallas import tpu as pltpu
from jax.sharding import PartitionSpec as P

clip_norm = 2.5
AXES = ("dp", "tensor")
NY, NX, NZ = 4, 4, 8
OFF = (0, 1, 2, -1)
BF = jnp.bfloat16
F32 = jnp.float32


def coords(i):
    dp, te = divmod(i, 2 * NZ)
    return dp // 4, (dp // 2) % 2, dp % 2, te // NZ, te % NZ


def index(y, xh, c, xl, z):
    return ((y % NY * 2 + xh) * 2 + c) * 2 * NZ + xl * NZ + z % NZ


def perm_of(move):
    return [(i, index(*move(*coords(i)))) for i in range(NY * NX * NZ * 2)]


def along_x(step):
    def move(y, xh, c, xl, z):
        x = (xh * 2 + xl + step) % NX
        return y, x // 2, c, x % 2, z

    return perm_of(move)


def along_y(step):
    return perm_of(lambda y, xh, c, xl, z: (y + step, xh, c, xl, z))


def along_z(step):
    return perm_of(lambda y, xh, c, xl, z: (y, xh, c, xl, z + step))


def flip_z(bit):
    return perm_of(lambda y, xh, c, xl, z: (y, xh, c, xl, z ^ bit))


def spread(flip):
    def move(y, xh, c, xl, z):
        t, u = (z // 2) % 2, z % 2
        m = 2 * (xh ^ t) + (c ^ u)
        return y, t, u, xl ^ flip, z + OFF[m]

    return perm_of(move)


CORE = perm_of(lambda y, xh, c, xl, z: (y, xh, 1 - c, xl, z))
XHI = perm_of(lambda y, xh, c, xl, z: (y, 1 - xh, c, xl, z))
XLO = perm_of(lambda y, xh, c, xl, z: (y, xh, c, 1 - xl, z))


def send(value, perm):
    return lax.ppermute(value, AXES, perm)


SLOTS = (2, 1, 3, 0)


def scale_kernel(place_ref, clip_ref, *refs):
    pieces, out_ref = refs[:-1], refs[-1]
    blocks = []
    for ref in pieces:
        blocks += [ref.at[0], ref.at[1]]
    half = out_ref.shape[3] // 2
    for i, block in enumerate(blocks):
        slot, m = place_ref[2 * i], place_ref[2 * i + 1]
        for e in range(2):
            cols = slice(e * half, (e + 1) * half)
            out_ref[slot, m, :, cols] = (
                clip_ref[2 * m + e] * block[:, cols].astype(F32)
            ).astype(BF)


def scale_grads(places, clips, pieces):
    _, rows, tokens = pieces[0].shape
    smem = pl.BlockSpec(memory_space=pltpu.SMEM)
    vmem = pl.BlockSpec(memory_space=pltpu.VMEM)
    return pl.pallas_call(
        scale_kernel,
        out_shape=jax.ShapeDtypeStruct((4, 4, rows, tokens), BF),
        in_specs=[smem, smem] + [vmem] * len(pieces),
        out_specs=vmem,
        cost_estimate=pl.CostEstimate(
            flops=16 * rows * tokens, bytes_accessed=64 * rows * tokens, transcendentals=0
        ),
        compiler_params=pltpu.CompilerParams(vmem_limit_bytes=40 * 1024 * 1024),
        name="scale_grads",
    )(places, clips, *pieces)


def product_kernel(s_ref, *refs):
    acts, outs = refs[:6], refs[6:]
    slots, _, rows, tokens = s_ref.shape
    j, steps = pl.program_id(0), pl.num_programs(0)
    total = None
    first = 0
    for a_ref in acts:
        count = a_ref.shape[0]
        m, start = first // tokens, first % tokens
        left = s_ref[:, m, :, start : start + count].reshape(slots * rows, count)
        part = jnp.dot(left, a_ref[...], preferred_element_type=F32)
        total = part if total is None else total + part
        first += count
    total = total.astype(outs[0].dtype)
    if len(outs) == 1:
        outs[0][...] = total
        return

    @pl.when(j < steps // 2)
    def _():
        for slot in range(slots):
            outs[2 * slot][...] = total[slot * rows : (slot + 1) * rows]

    @pl.when(j >= steps // 2)
    def _():
        for slot in range(slots):
            outs[2 * slot + 1][...] = total[slot * rows : (slot + 1) * rows]


def product(scaled, first, slots, acts, tile, split):
    _, quarters, rows, tokens = scaled.shape
    width = acts[0].shape[1]
    steps = width // tile
    if split:
        out_shape = [jax.ShapeDtypeStruct((rows, width // 2), BF)] * (2 * slots)
        low = pl.BlockSpec((rows, tile), lambda j: (0, jnp.minimum(j, steps // 2 - 1)))
        high = pl.BlockSpec((rows, tile), lambda j: (0, jnp.maximum(j - steps // 2, 0)))
        out_specs = [low, high] * slots
    else:
        out_shape = [jax.ShapeDtypeStruct((rows, width), F32)]
        out_specs = [pl.BlockSpec((rows, tile), lambda j: (0, j))]
    depth = quarters * tokens
    return pl.pallas_call(
        product_kernel,
        out_shape=out_shape,
        grid=(steps,),
        in_specs=[
            pl.BlockSpec((slots, quarters, rows, tokens), lambda j: (first // slots, 0, 0, 0))
        ]
        + [pl.BlockSpec((a.shape[0], tile), lambda j: (0, j)) for a in acts],
        out_specs=out_specs,
        cost_estimate=pl.CostEstimate(
            flops=2 * slots * rows * depth * width,
            bytes_accessed=2 * (slots * rows * depth + depth * width + slots * rows * width),
            transcendentals=0,
        ),
        compiler_params=pltpu.CompilerParams(vmem_limit_bytes=40 * 1024 * 1024),
        name=f"product_{first}",
    )(scaled, *acts)


def halved(grams, bit, perm):
    low, high = jnp.split(grams, 2, axis=1)
    keep, give = jnp.where(bit == 0, low, high), jnp.where(bit == 0, high, low)
    return (keep.astype(F32) + send(give, perm).astype(F32)).astype(BF)


def shards(acts, out_grads, other_sq, noise):
    dp, te = lax.axis_index("dp"), lax.axis_index("tensor")
    y, xh, c, xl, z = dp // 4, (dp // 2) % 2, dp % 2, te // NZ, te % NZ
    examples, seq, columns = acts.shape
    tokens = examples * seq
    features = out_grads.shape[2]
    half = columns // 2
    stage = lax.optimization_barrier

    flat = acts.reshape(tokens, columns)
    up = send(flat[:seq], along_x(1))
    down = send(flat[seq:], along_x(-1))
    grads_t = out_grads.reshape(tokens, features).T
    own = jnp.stack([send(grads_t, spread(0)), send(grads_t, spread(1))])
    fwd, bwd = [own], [own]
    fwd.append(send(own, along_z(1)))
    bwd.append(send(own, along_z(-1)))
    act_gram = jnp.einsum("btf,bsf->bts", acts, acts, preferred_element_type=F32)
    grad_gram = jnp.einsum("btf,bsf->bts", out_grads, out_grads, preferred_element_type=F32)
    grams = jnp.concatenate([act_gram, grad_gram]).astype(BF)
    grams = halved(grams, xl, XLO)
    grams = halved(grams, z // 4, flip_z(4))
    grams = halved(grams, (z // 2) % 2, flip_z(2))
    up, down, fwd[1], bwd[1], grams = stage((up, down, fwd[1], bwd[1], grams))

    up, down = send(up, along_x(1)), send(down, along_x(-1))
    sibling = send(flat, CORE)
    for _ in range(2):
        fwd.append(send(fwd[-1], along_z(1)))
        bwd.append(send(bwd[-1], along_z(-1)))
    grams = halved(grams, z % 2, flip_z(1)).astype(F32)
    total = jnp.sum(grams[:examples] * grams[examples:], axis=(1, 2)) + jnp.sum(other_sq, axis=1)
    total = total + send(total, flip_z(1))
    total = total + send(total, flip_z(2))
    up, down, fwd[3], bwd[3], total = stage((up, down, fwd[3], bwd[3], total))

    far = [send(fwd[3][0], along_z(1)), send(bwd[3][1], along_z(-1))]
    up_sibling, down_sibling = send(up, CORE), send(down, CORE)
    total = total + send(total, flip_z(4))
    total = total + send(total, XLO)
    far[0], far[1], total = stage((far[0], far[1], total))
    far = jnp.stack(far)
    clip = jnp.minimum(1.0, clip_norm / jnp.sqrt(total))
    clips = jnp.concatenate([clip, send(clip, CORE)])
    clips = jnp.concatenate([clips, send(clips, XHI)])

    pieces = [own, fwd[1], fwd[2], fwd[3], far, bwd[3], bwd[2], bwd[1]]
    places = []
    for r in range(NZ):
        q = (z - r - 2 * xh - c) % NZ
        m = jnp.where(q % 4 == 3, 3, q % 4)
        k = jnp.where(q % 4 == 3, (q // 4 + 1) % 2, q // 4)
        for f in range(2):
            step = (2 * (f ^ xl) + k - y) % 4
            slot = jnp.where(step == 2, 0, jnp.where(step == 0, 3, jnp.where(step == 1, 1, 2)))
            places += [slot, m]
    places = jnp.stack(places).astype(jnp.int32)
    scaled = scale_grads(places, clips, pieces)

    held = [flat, sibling, up, down, up_sibling, down_sibling]
    tile = columns // 6
    far_a, far_b = product(scaled, 0, 1, held, tile, True)
    from_down, from_up = send(far_a, along_y(1)), send(far_b, along_y(-1))
    (next_a, next_b), (prev_a, prev_b) = [
        product(scaled, slot, 1, held, tile, True) for slot in (1, 2)
    ]
    next_b, prev_a = send(next_b, along_y(1)), send(prev_a, along_y(-1))
    next_a = send((next_a.astype(F32) + from_down.astype(F32)).astype(BF), along_y(1))
    prev_b = send((prev_b.astype(F32) + from_up.astype(F32)).astype(BF), along_y(-1))
    (mine,) = product(scaled, 3, 1, held, tile, False)

    width = features * 2 * NZ
    factor = math.sqrt(columns * 2 * NZ * width) / clip_norm
    base = factor * mine + noise
    summed = jnp.concatenate(
        [next_a.astype(F32) + prev_a.astype(F32), next_b.astype(F32) + prev_b.astype(F32)], axis=1
    )
    return (base + factor * summed) / math.sqrt(examples * 4 * NY)


def solution(mesh):
    placed = (
        P("dp", None, "tensor"),
        P("dp", None, "tensor"),
        P("dp", "tensor"),
        P("dp", "tensor"),
    )
    return jax.shard_map(
        shards, mesh=mesh, in_specs=placed, out_specs=P("dp", "tensor"), check_vma=False
    )
```

time: 518 us -> 202 us (0.39)
  waiting for transfers between devices: 354 us -> 86.8 us
  other arithmetic: 82.9 us -> 11.2 us
  starting transfers between devices: 0.08 us -> 51 us
  blocking collectives: 34.4 us -> 0 us
  Pallas kernels: 0 us -> 32.6 us
  matrix products: 33.2 us -> 4.73 us
  local copies, waits for them, and re-layouts: 0.02 us -> 14.2 us
  between operations: 13.1 us -> 0.4 us
    reduce_scatter x1 -> x0, waiting for transfers between devices: 175 us -> none  [shards(): lax.psum_scatter(result.astype(jnp.bfloat16), 'dp', scatter_dimension=0,...]
    psum x1 -> x0, waiting for transfers between devices: 101 us -> none  [shards(): lax.psum(act_gram.astype(jnp.bfloat16), 'tensor').astype(jnp.float32)]
    ppermute x0 -> x33, waiting for transfers between devices: none -> 86.8 us  [send(): return lax.ppermute(value, AXES, perm)]
    all_gather x1 -> x0, waiting for transfers between devices: 77.2 us -> none  [shards(): full_grads = lax.all_gather(out_grads, 'tensor', axis=2, tiled=True)]
    add x2 -> x7, other arithmetic: 54.5 us -> 0.3 us  [the longest x1 0.14 us: shards(): next_a.astype(F32) + prev_a.astype(F32)]
    ppermute x0 -> x33, starting transfers between devices: none -> 51 us  [send(): return lax.ppermute(value, AXES, perm)]
    psum x1 -> x0, blocking collectives: 34.4 us -> none  [shards(): lax.psum(other_local.astype(jnp.bfloat16), 'tensor').astype(jnp.float32)]
    pallas_call x0 -> x5, Pallas kernels: none -> 32.6 us  [the longest x4 30.8 us: product(): pl.pallas_call(product_kernel, out_shape=out_shape, grid=(steps,), in_spe...]
  transfers between devices with their start and end apart: 3 -> 33, of which waited for: 3 -> 15; matrix products, arithmetic and copies ran while one was open for 0% -> 8% of each run, Pallas kernels for 0% -> 12%
where the time goes in v1:
time: 202 us; the launch traced here: 201 us
  waiting for transfers between devices  86.8 us (43%)
  starting transfers between devices  51 us (25%)
  Pallas kernels  32.6 us (16%)
  local copies, waits for them, and re-layouts  14.2 us (7%)
  other arithmetic  11.2 us (6%)
  matrix products  4.73 us (2%)
    ppermute x33, waiting for transfers between devices, send(): return lax.ppermute(value, AXES, perm)  86.8 us
    ppermute x33, starting transfers between devices, send(): return lax.ppermute(value, AXES, perm)  51 us
    pallas_call x4, Pallas kernels, product(): pl.pallas_call(product_kernel, out_shape=out_shape, grid=(steps,), in_spe...  30.8 us
    unnamed x40, local copies, waits for them, and re-layouts  10.1 us
  transfers between devices with their start and end apart: 33, of which 15 were waited for; matrix products, arithmetic and copies ran while one was open for 8% of the time, Pallas kernels for 12%

profile of v1, /device:TPU:32, one launch (start us, length us, event | category | flops | bytes accessed | tf_op | source)
XLA Modules:
  0.0 200.9 jit_solution(8505465508438345201)
XLA Ops:
  0.0 1.0 copy.6
  1.0 2.4 %collective-permute-start.3 = (bf16[288,512]{1,0:T(8,128)(2,1)S(1)}, bf16[288,512]{1,0:T(8,128)(2,1)}, u32[]{:S(2)}, u32[]{:S(2)}) collective-permute-start(bf16[288,512]{1,0:T(8,128)(2,1)S(1)} %bitcast.51), channel_id=1, source_target_pairs={{0,8},{1,26},{2,44},{3,58},{4,12},{5,30},{6,40},{7,62},{8,0},{9,18... | collective-permute-start | bytes 884744 | tf_op jit(solution)/shard_map/ppermute | solution.py:67
  3.3 3.6 %collective-permute-start.2 = (bf16[288,512]{1,0:T(8,128)(2,1)S(1)}, bf16[288,512]{1,0:T(8,128)(2,1)}, u32[]{:S(2)}, u32[]{:S(2)}) collective-permute-start(bf16[288,512]{1,0:T(8,128)(2,1)S(1)} %bitcast.52), channel_id=1, source_target_pairs={{0,0},{1,18},{2,36},{3,50},{4,4},{5,22},{6,32},{7,54},{8,8},{9,26}... | collective-permute-start | bytes 884744 | tf_op jit(solution)/shard_map/ppermute | solution.py:67
  6.9 1.4 convolution_convert_fusion
  8.4 3.3 %convolution_convert_fusion.1 = bf16[2,256,256]{2,1,0:T(8,128)(2,1)S(1)} fusion(bf16[2,256,2304]{2,1,0:T(8,128)(2,1)} %param.4), kind=kOutput, calls=%fused_computation.8 | convolution fusion | flops 604110848 | bytes 2621440 | tf_op jit(solution)/shard_map/btf,bsf->bts/dot_general | solution.py:189
  12.1 1.6 slice_bitcast_fusion
  13.7 1.8 collective-permute-start
  15.5 1.4 collective-permute-start.1
  16.9 5.1 %collective-permute-done.6 = bf16[4,128,256]{2,1,0:T(8,128)(2,1)} collective-permute-done((bf16[4,128,256]{2,1,0:T(8,128)(2,1)S(1)}, bf16[4,128,256]{2,1,0:T(8,128)(2,1)}, u32[]{:S(2)}, u32[]{:S(2)}) %collective-permute-start.6) | collective-permute-done | bytes 262176 | tf_op jit(solution)/shard_map/ppermute | solution.py:67
  22.0 1.0 add_convert_fusion.2
  23.1 0.7 broadcast_select_fusion.1
  23.7 8.7 %collective-permute-start.7 = (bf16[4,64,256]{2,1,0:T(8,128)(2,1)}, bf16[4,64,256]{2,1,0:T(8,128)(2,1)}, u32[]{:S(2)}, u32[]{:S(2)}) collective-permute-start(bf16[4,64,256]{2,1,0:T(8,128)(2,1)} %broadcast_select_fusion.1), channel_id=1, source_target_pairs={{0,4},{1,5},{2,6},{3,7},{4,0},{5,1},{6,2},{7,3},{8,12},{9,13},{10,... | collective-permute-start | bytes 393224 | tf_op jit(solution)/shard_map/ppermute | solution.py:67
  32.4 1.1 pad_maximum_fusion.refs_0_
  33.7 2.0 %collective-permute-start.5 = (bf16[2,288,512]{2,1,0:T(8,128)(2,1)S(1)}, bf16[2,288,512]{2,1,0:T(8,128)(2,1)}, u32[]{:S(2)}, u32[]{:S(2)}) collective-permute-start(bf16[2,288,512]{2,1,0:T(8,128)(2,1)S(1)} %pad_maximum_fusion.refs_0_), channel_id=1, source_target_pairs={{0,7},{1,0},{2,1},{3,2},{4,3},{5,4},{6,5},{7,6},{8,15},{9,8},{10,9... | collective-permute-start | bytes 1769480 | tf_op jit(solution)/shard_map/ppermute | solution.py:67
  35.7 3.4 %collective-permute-done.7 = bf16[4,64,256]{2,1,0:T(8,128)(2,1)} collective-permute-done((bf16[4,64,256]{2,1,0:T(8,128)(2,1)}, bf16[4,64,256]{2,1,0:T(8,128)(2,1)}, u32[]{:S(2)}, u32[]{:S(2)}) %collective-permute-start.7) | collective-permute-done | bytes 131104 | tf_op jit(solution)/shard_map/ppermute | solution.py:67
  39.1 1.0 add_convert_fusion.3
  40.1 0.6 copy-done.17
  40.7 0.6 broadcast_select_fusion.2
  41.4 8.4 %collective-permute-done.8 = bf16[4,32,256]{2,1,0:T(8,128)(2,1)} collective-permute-done((bf16[4,32,256]{2,1,0:T(8,128)(2,1)}, bf16[4,32,256]{2,1,0:T(8,128)(2,1)}, u32[]{:S(2)}, u32[]{:S(2)}) %collective-permute-start.8) | collective-permute-done | bytes 65568 | tf_op jit(solution)/shard_map/ppermute | solution.py:67
  49.8 0.9 add_convert_fusion.4
  51.4 0.6 broadcast_select_fusion.3
  52.0 2.3 %collective-permute-start.15 = (bf16[4,16,256]{2,1,0:T(8,128)(2,1)}, bf16[4,16,256]{2,1,0:T(8,128)(2,1)}, u32[]{:S(2)}, u32[]{:S(2)}) collective-permute-start(bf16[4,16,256]{2,1,0:T(8,128)(2,1)} %broadcast_select_fusion.3), channel_id=1, source_target_pairs={{0,1},{1,0},{2,3},{3,2},{4,5},{5,4},{6,7},{7,6},{8,9},{9,8},{10,11... | collective-permute-start | bytes 98312 | tf_op jit(solution)/shard_map/ppermute | solution.py:67
  54.4 1.7 collective-permute-start.9
  56.0 1.6 collective-permute-start.10
  57.7 1.7 collective-permute-start.11
  59.7 0.8 fusion.3
  60.6 1.3 collective-permute-start.16
  61.9 8.4 %collective-permute-done.16 = f32[2]{0:T(128)S(1)} collective-permute-done((f32[2]{0:T(128)S(1)}, f32[2]{0:T(128)S(1)}, u32[]{:S(2)}, u32[]{:S(2)}) %collective-permute-start.16) | collective-permute-done | bytes 40 | tf_op jit(solution)/shard_map/ppermute | solution.py:67
  70.3 2.1 %collective-permute-start.17 = (f32[2]{0:T(128)S(1)}, f32[2]{0:T(128)S(1)}, u32[]{:S(2)}, u32[]{:S(2)}) collective-permute-start(f32[2]{0:T(128)S(1)} %add.363), channel_id=1, source_target_pairs={{0,2},{1,3},{2,0},{3,1},{4,6},{5,7},{6,4},{7,5},{8,10},{9,11},{10,... | collective-permute-start | bytes 32 | tf_op jit(solution)/shard_map/ppermute | solution.py:67
  72.4 2.3 %collective-permute-done.17 = f32[2]{0:T(128)S(1)} collective-permute-done((f32[2]{0:T(128)S(1)}, f32[2]{0:T(128)S(1)}, u32[]{:S(2)}, u32[]{:S(2)}) %collective-permute-start.17) | collective-permute-done | bytes 40 | tf_op jit(solution)/shard_map/ppermute | solution.py:67
  74.8 3.1 %collective-permute-start.12 = (bf16[2,288,512]{2,1,0:T(8,128)(2,1)S(1)}, bf16[2,288,512]{2,1,0:T(8,128)(2,1)S(1)}, u32[]{:S(2)}, u32[]{:S(2)}) collective-permute-start(bf16[2,288,512]{2,1,0:T(8,128)(2,1)S(1)} %collective-permute-done.11.refs_2_), channel_id=1, source_target_pairs={{0,1},{1,2},{2,3},{3,4},{4,5},{5,6},{6,7},{7,0},{8,9},{9,10},{10,1... | collective-permute-start | bytes 1769480 | tf_op jit(solution)/shard_map/ppermute | solution.py:67
  77.8 0.8 copy-done.10
  78.7 0.8 copy-done.12
  79.5 1.9 collective-permute-done.9.refs_2_
  81.9 9.2 %collective-permute-done.12.refs_3_ = bf16[2,288,512]{2,1,0:T(8,128)(2,1)S(1)} collective-permute-done((bf16[2,288,512]{2,1,0:T(8,128)(2,1)S(1)}, bf16[2,288,512]{2,1,0:T(8,128)(2,1)S(1)}, u32[]{:S(2)}, u32[]{:S(2)}) %collective-permute-start.12) | collective-permute-done | bytes 589856 | tf_op jit(solution)/shard_map/ppermute | solution.py:67
  91.1 3.0 %collective-permute-done.14.refs_5_ = bf16[2,288,512]{2,1,0:T(8,128)(2,1)S(1)} collective-permute-done((bf16[2,288,512]{2,1,0:T(8,128)(2,1)S(1)}, bf16[2,288,512]{2,1,0:T(8,128)(2,1)S(1)}, u32[]{:S(2)}, u32[]{:S(2)}) %collective-permute-start.14) | collective-permute-done | bytes 589856 | tf_op jit(solution)/shard_map/ppermute | solution.py:67
  94.6 0.7 slice_bitcast_fusion.3
  95.4 0.8 copy-done.4
  96.2 1.7 collective-permute-start.18
  97.9 0.9 collective-permute-start.20
  98.8 0.7 slice_bitcast_fusion.2
  99.5 5.8 %collective-permute-done.20 = f32[2]{0:T(128)S(1)} collective-permute-done((f32[2]{0:T(128)S(1)}, f32[2]{0:T(128)S(1)}, u32[]{:S(2)}, u32[]{:S(2)}) %collective-permute-start.20) | collective-permute-done | bytes 40 | tf_op jit(solution)/shard_map/ppermute | solution.py:67
  105.4 3.5 %collective-permute-done.21 = f32[2]{0:T(128)S(1)} collective-permute-done((f32[2]{0:T(128)S(1)}, f32[2]{0:T(128)S(1)}, u32[]{:S(2)}, u32[]{:S(2)}) %collective-permute-start.21) | collective-permute-done | bytes 40 | tf_op jit(solution)/shard_map/ppermute | solution.py:67
  108.9 2.8 %collective-permute-start.19 = (bf16[288,512]{1,0:T(8,128)(2,1)}, bf16[288,512]{1,0:T(8,128)(2,1)}, u32[]{:S(2)}, u32[]{:S(2)}) collective-permute-start(bf16[288,512]{1,0:T(8,128)(2,1)} %slice_bitcast_fusion.2), channel_id=1, source_target_pairs={{0,7},{1,0},{2,1},{3,2},{4,3},{5,4},{6,5},{7,6},{8,15},{9,8},{10,9... | collective-permute-start | bytes 884744 | tf_op jit(solution)/shard_map/ppermute | solution.py:67
  111.8 5.6 %collective-permute-done.19 = bf16[288,512]{1,0:T(8,128)(2,1)} collective-permute-done((bf16[288,512]{1,0:T(8,128)(2,1)}, bf16[288,512]{1,0:T(8,128)(2,1)}, u32[]{:S(2)}, u32[]{:S(2)}) %collective-permute-start.19) | collective-permute-done | bytes 294944 | tf_op jit(solution)/shard_map/ppermute | solution.py:67
  117.5 1.1 pad_maximum_fusion.1.refs_4_
  118.7 2.1 %collective-permute-start.23 = (f32[4]{0:T(128)S(1)}, f32[4]{0:T(128)S(1)}, u32[]{:S(2)}, u32[]{:S(2)}) collective-permute-start(f32[4]{0:T(128)S(1)} %pad_maximum_fusion.3), channel_id=1, source_target_pairs={{0,32},{1,33},{2,34},{3,35},{4,36},{5,37},{6,38},{7,39},{8,40},{9,... | collective-permute-start | bytes 56 | tf_op jit(solution)/shard_map/ppermute | solution.py:67
  120.8 3.0 %collective-permute-done.23 = f32[4]{0:T(128)S(1)} collective-permute-done((f32[4]{0:T(128)S(1)}, f32[4]{0:T(128)S(1)}, u32[]{:S(2)}, u32[]{:S(2)}) %collective-permute-start.23) | collective-permute-done | bytes 48 | tf_op jit(solution)/shard_map/ppermute | solution.py:67
  123.9 1.1 copy-done.7
  124.9 1.1 copy-done.9
  126.0 1.1 copy-done.11
  127.0 1.1 copy-done.13
  128.1 1.8 scale_grads.1.s_ref
  130.0 2.1 %copy-done = bf16[4,4,288,512]{3,2,1,0:T(8,128)(2,1)} copy-done((bf16[4,4,288,512]{3,2,1,0:T(8,128)(2,1)}, bf16[4,4,288,512]{3,2,1,0:T(8,128)(2,1)S(1)}, u32[]{:S(2)}) %copy-start) | copy-done | bytes 4718616
  132.1 7.8 %product_0.1 = (bf16[288,1152]{1,0:T(8,128)(2,1)S(1)}, bf16[288,1152]{1,0:T(8,128)(2,1)S(1)}) custom-call(bf16[4,4,288,512]{3,2,1,0:T(8,128)(2,1)} %copy-done, bf16[512,2304]{1,0:T(8,128)(2,1)S(1)} %bitcast.46, bf16[512,2304]{1,0:T(8,128)(2,1)} %collective-permute-done.24.refs_1_, bf16[256,2304]{1,0:T(8,128)(2,1)S(1)} %collective-permute-done.9.refs_2_, ...), custom_call_target="tpu_custom_call" | custom-call | flops 2717908992 | bytes 11943936 | tf_op jit(solution)/shard_map/product_0/pallas_call | solution.py:147
  139.9 3.1 %collective-permute-start.31 = (bf16[288,1152]{1,0:T(8,128)(2,1)S(1)}, bf16[288,1152]{1,0:T(8,128)(2,1)S(1)}, u32[]{:S(2)}, u32[]{:S(2)}) collective-permute-start(bf16[288,1152]{1,0:T(8,128)(2,1)S(1)} %get-tuple-element.42), channel_id=1, source_target_pairs={{0,192},{1,193},{2,194},{3,195},{4,196},{5,197},{6,198},{7,199},{8... | collective-permute-start | bytes 1990664 | tf_op jit(solution)/shard_map/ppermute | solution.py:67
  143.0 7.7 %product_1.1 = (bf16[288,1152]{1,0:T(8,128)(2,1)S(1)}, bf16[288,1152]{1,0:T(8,128)(2,1)S(1)}) custom-call(bf16[4,4,288,512]{3,2,1,0:T(8,128)(2,1)} %copy-done, bf16[512,2304]{1,0:T(8,128)(2,1)S(1)} %bitcast.47, bf16[512,2304]{1,0:T(8,128)(2,1)} %collective-permute-done.24.refs_1_, bf16[256,2304]{1,0:T(8,128)(2,1)S(1)} %collective-permute-done.9.refs_2_, ...), custom_call_target="tpu_custom_call" | custom-call | flops 2717908992 | bytes 11943936 | tf_op jit(solution)/shard_map/product_1/pallas_call | solution.py:147
  151.4 7.7 %product_2.1 = (bf16[288,1152]{1,0:T(8,128)(2,1)S(1)}, bf16[288,1152]{1,0:T(8,128)(2,1)S(1)}) custom-call(bf16[4,4,288,512]{3,2,1,0:T(8,128)(2,1)} %copy-done, bf16[512,2304]{1,0:T(8,128)(2,1)S(1)} %bitcast.48, bf16[512,2304]{1,0:T(8,128)(2,1)} %collective-permute-done.24.refs_1_, bf16[256,2304]{1,0:T(8,128)(2,1)S(1)} %collective-permute-done.9.refs_2_, ...), custom_call_target="tpu_custom_call" | custom-call | flops 2717908992 | bytes 11943936 | tf_op jit(solution)/shard_map/product_2/pallas_call | solution.py:147
  159.1 3.0 %collective-permute-start.29 = (bf16[288,1152]{1,0:T(8,128)(2,1)S(1)}, bf16[288,1152]{1,0:T(8,128)(2,1)S(1)}, u32[]{:S(2)}, u32[]{:S(2)}) collective-permute-start(bf16[288,1152]{1,0:T(8,128)(2,1)S(1)} %get-tuple-element.39), channel_id=1, source_target_pairs={{0,192},{1,193},{2,194},{3,195},{4,196},{5,197},{6,198},{7,199},{8... | collective-permute-start | bytes 1990664 | tf_op jit(solution)/shard_map/ppermute | solution.py:67
  162.3 1.8 collective-permute-start.32
  164.1 18.0 %collective-permute-done.27 = bf16[288,1152]{1,0:T(8,128)(2,1)S(1)} collective-permute-done((bf16[288,1152]{1,0:T(8,128)(2,1)S(1)}, bf16[288,1152]{1,0:T(8,128)(2,1)S(1)}, u32[]{:S(2)}, u32[]{:S(2)}) %collective-permute-start.27) | collective-permute-done | bytes 663584 | tf_op jit(solution)/shard_map/ppermute | solution.py:67
  182.4 7.6 %product_3.1 = f32[288,2304]{1,0:T(8,128)S(1)} custom-call(bf16[4,4,288,512]{3,2,1,0:T(8,128)(2,1)} %copy-done, bf16[512,2304]{1,0:T(8,128)(2,1)S(1)} %bitcast.49, bf16[512,2304]{1,0:T(8,128)(2,1)} %collective-permute-done.24.refs_1_, bf16[256,2304]{1,0:T(8,128)(2,1)S(1)} %collective-permute-done.9.refs_2_, ...), custom_call_target="tpu_custom_call" | custom-call | flops 2717908992 | bytes 11943936 | tf_op jit(solution)/shard_map/product_3/pallas_call | solution.py:147
  190.1 8.4 %collective-permute-done.28 = bf16[288,1152]{1,0:T(8,128)(2,1)S(1)} collective-permute-done((bf16[288,1152]{1,0:T(8,128)(2,1)S(1)}, bf16[288,1152]{1,0:T(8,128)(2,1)S(1)}, u32[]{:S(2)}, u32[]{:S(2)}) %collective-permute-start.28) | collective-permute-done | bytes 663584 | tf_op jit(solution)/shard_map/ppermute | solution.py:67
  198.7 2.2 %fusion.1 = f32[288,2304]{1,0:T(8,128)} fusion(f32[288,1152]{1,0:T(8,128)S(1)} %convert_add_fusion, f32[288,1152]{1,0:T(8,128)S(1)} %convert_add_fusion.1, f32[288,2304]{1,0:T(8,128)S(1)} %copy-done.14, f32[288,2304]{1,0:T(8,128)S(1)} %product_3.1), kind=kLoop, calls=%fused_computation.2 | loop fusion | flops 3981312 | bytes 10616832 | tf_op jit(solution)/shard_map/div | solution.py:249
  (79 shorter events, 4.5 us)
Async XLA Ops:
  1.0 31.4 %collective-permute-start.3 = (bf16[288,512]{1,0:T(8,128)(2,1)S(1)}, bf16[288,512]{1,0:T(8,128)(2,1)}, u32[]{:S(2)}, u32[]{:S(2)}) collective-permute-start(bf16[288,512]{1,0:T(8,128)(2,1)S(1)} %bitcast.51), channel_id=1, source_target_pairs={{0,8},{1,26},{2,44},{3,58},{4,12},{5,30},{6,40},{7,62},{8,0},{9,18... | collective-permute-start | bytes 884744 | tf_op jit(solution)/shard_map/ppermute | solution.py:67
  3.3 29.1 %collective-permute-start.2 = (bf16[288,512]{1,0:T(8,128)(2,1)S(1)}, bf16[288,512]{1,0:T(8,128)(2,1)}, u32[]{:S(2)}, u32[]{:S(2)}) collective-permute-start(bf16[288,512]{1,0:T(8,128)(2,1)S(1)} %bitcast.52), channel_id=1, source_target_pairs={{0,0},{1,18},{2,36},{3,50},{4,4},{5,22},{6,32},{7,54},{8,8},{9,26}... | collective-permute-start | bytes 884744 | tf_op jit(solution)/shard_map/ppermute | solution.py:67
  8.3 3.7 %copy-start.1 = (bf16[2,256,2304]{2,1,0:T(8,128)(2,1)S(1)}, bf16[2,256,2304]{2,1,0:T(8,128)(2,1)}, u32[]{:S(2)}) copy-start(bf16[2,256,2304]{2,1,0:T(8,128)(2,1)} %param.4) | copy-start | bytes 7077892
  11.8 10.2 %collective-permute-start.6 = (bf16[4,128,256]{2,1,0:T(8,128)(2,1)S(1)}, bf16[4,128,256]{2,1,0:T(8,128)(2,1)}, u32[]{:S(2)}, u32[]{:S(2)}) collective-permute-start(bf16[4,128,256]{2,1,0:T(8,128)(2,1)S(1)} %broadcast_select_fusion), channel_id=1, source_target_pairs={{0,8},{1,9},{2,10},{3,11},{4,12},{5,13},{6,14},{7,15},{8,0},{9,1},... | collective-permute-start | bytes 786440 | tf_op jit(solution)/shard_map/ppermute | solution.py:67
  13.7 37.1 %collective-permute-start = (bf16[256,2304]{1,0:T(8,128)(2,1)}, bf16[256,2304]{1,0:T(8,128)(2,1)}, u32[]{:S(2)}, u32[]{:S(2)}) collective-permute-start(bf16[256,2304]{1,0:T(8,128)(2,1)} %get-tuple-element.44), channel_id=1, source_target_pairs={{0,8},{1,9},{2,10},{3,11},{4,12},{5,13},{6,14},{7,15},{8,32},{9,33... | collective-permute-start | bytes 3538952 | tf_op jit(solution)/shard_map/ppermute | solution.py:67
  15.5 35.4 %collective-permute-start.1 = (bf16[256,2304]{1,0:T(8,128)(2,1)}, bf16[256,2304]{1,0:T(8,128)(2,1)}, u32[]{:S(2)}, u32[]{:S(2)}) collective-permute-start(bf16[256,2304]{1,0:T(8,128)(2,1)} %get-tuple-element.43), channel_id=1, source_target_pairs={{0,40},{1,41},{2,42},{3,43},{4,44},{5,45},{6,46},{7,47},{8,0},{9,1... | collective-permute-start | bytes 3538952 | tf_op jit(solution)/shard_map/ppermute | solution.py:67
  23.0 9.4 %copy-start.15 = (bf16[4,128,256]{2,1,0:T(8,128)(2,1)}, bf16[4,128,256]{2,1,0:T(8,128)(2,1)S(1)}, u32[]{:S(2)}) copy-start(bf16[4,128,256]{2,1,0:T(8,128)(2,1)S(1)} %add_convert_fusion.2) | copy-start | bytes 786436
  23.1 31.2 %copy-start.19 = (f32[2,8]{1,0:T(2,128)S(1)}, f32[2,8]{1,0:T(2,128)}, u32[]{:S(2)}) copy-start(f32[2,8]{1,0:T(2,128)} %param.6) | copy-start | bytes 196
  23.7 15.4 %collective-permute-start.7 = (bf16[4,64,256]{2,1,0:T(8,128)(2,1)}, bf16[4,64,256]{2,1,0:T(8,128)(2,1)}, u32[]{:S(2)}, u32[]{:S(2)}) collective-permute-start(bf16[4,64,256]{2,1,0:T(8,128)(2,1)} %broadcast_select_fusion.1), channel_id=1, source_target_pairs={{0,4},{1,5},{2,6},{3,7},{4,0},{5,1},{6,2},{7,3},{8,12},{9,13},{10,... | collective-permute-start | bytes 393224 | tf_op jit(solution)/shard_map/ppermute | solution.py:67
  32.4 6.7 %copy-start.16 = (bf16[4,128,256]{2,1,0:T(8,128)(2,1)S(1)}, bf16[4,128,256]{2,1,0:T(8,128)(2,1)}, u32[]{:S(2)}) copy-start(bf16[4,128,256]{2,1,0:T(8,128)(2,1)} %copy-done.15) | copy-start | bytes 786436
  33.6 20.7 %copy-start.2 = (bf16[2,288,512]{2,1,0:T(8,128)(2,1)}, bf16[2,288,512]{2,1,0:T(8,128)(2,1)S(1)}, u32[]{:S(2)}) copy-start(bf16[2,288,512]{2,1,0:T(8,128)(2,1)S(1)} %pad_maximum_fusion.refs_0_) | copy-start | bytes 1769476
  33.6 17.2 %collective-permute-start.4 = (bf16[2,288,512]{2,1,0:T(8,128)(2,1)S(1)}, bf16[2,288,512]{2,1,0:T(8,128)(2,1)S(1)}, u32[]{:S(2)}, u32[]{:S(2)}) collective-permute-start(bf16[2,288,512]{2,1,0:T(8,128)(2,1)S(1)} %pad_maximum_fusion.refs_0_), channel_id=1, source_target_pairs={{0,1},{1,2},{2,3},{3,4},{4,5},{5,6},{6,7},{7,0},{8,9},{9,10},{10,1... | collective-permute-start | bytes 1769480 | tf_op jit(solution)/shard_map/ppermute | solution.py:67
  33.7 17.1 %collective-permute-start.5 = (bf16[2,288,512]{2,1,0:T(8,128)(2,1)S(1)}, bf16[2,288,512]{2,1,0:T(8,128)(2,1)}, u32[]{:S(2)}, u32[]{:S(2)}) collective-permute-start(bf16[2,288,512]{2,1,0:T(8,128)(2,1)S(1)} %pad_maximum_fusion.refs_0_), channel_id=1, source_target_pairs={{0,7},{1,0},{2,1},{3,2},{4,3},{5,4},{6,5},{7,6},{8,15},{9,8},{10,9... | collective-permute-start | bytes 1769480 | tf_op jit(solution)/shard_map/ppermute | solution.py:67
  40.1 0.7 copy-start.17
  41.4 8.4 %collective-permute-start.8 = (bf16[4,32,256]{2,1,0:T(8,128)(2,1)}, bf16[4,32,256]{2,1,0:T(8,128)(2,1)}, u32[]{:S(2)}, u32[]{:S(2)}) collective-permute-start(bf16[4,32,256]{2,1,0:T(8,128)(2,1)} %broadcast_select_fusion.2), channel_id=1, source_target_pairs={{0,2},{1,3},{2,0},{3,1},{4,6},{5,7},{6,4},{7,5},{8,10},{9,11},{10,... | collective-permute-start | bytes 196616 | tf_op jit(solution)/shard_map/ppermute | solution.py:67
  50.8 0.6 copy-start.18
  50.8 3.5 %copy-start.8 = (bf16[2,288,512]{2,1,0:T(8,128)(2,1)}, bf16[2,288,512]{2,1,0:T(8,128)(2,1)S(1)}, u32[]{:S(2)}) copy-start(bf16[2,288,512]{2,1,0:T(8,128)(2,1)S(1)} %collective-permute-done.4.refs_1_) | copy-start | bytes 1769476
  52.0 7.7 %collective-permute-start.15 = (bf16[4,16,256]{2,1,0:T(8,128)(2,1)}, bf16[4,16,256]{2,1,0:T(8,128)(2,1)}, u32[]{:S(2)}, u32[]{:S(2)}) collective-permute-start(bf16[4,16,256]{2,1,0:T(8,128)(2,1)} %broadcast_select_fusion.3), channel_id=1, source_target_pairs={{0,1},{1,0},{2,3},{3,2},{4,5},{5,4},{6,7},{7,6},{8,9},{9,8},{10,11... | collective-permute-start | bytes 98312 | tf_op jit(solution)/shard_map/ppermute | solution.py:67
  54.4 27.0 %collective-permute-start.9 = (bf16[256,2304]{1,0:T(8,128)(2,1)}, bf16[256,2304]{1,0:T(8,128)(2,1)S(1)}, u32[]{:S(2)}, u32[]{:S(2)}) collective-permute-start(bf16[256,2304]{1,0:T(8,128)(2,1)} %collective-permute-done), channel_id=1, source_target_pairs={{0,8},{1,9},{2,10},{3,11},{4,12},{5,13},{6,14},{7,15},{8,32},{9,33... | collective-permute-start | bytes 3538952 | tf_op jit(solution)/shard_map/ppermute | solution.py:67
  56.0 25.9 %collective-permute-start.10 = (bf16[256,2304]{1,0:T(8,128)(2,1)}, bf16[256,2304]{1,0:T(8,128)(2,1)}, u32[]{:S(2)}, u32[]{:S(2)}) collective-permute-start(bf16[256,2304]{1,0:T(8,128)(2,1)} %collective-permute-done.1), channel_id=1, source_target_pairs={{0,40},{1,41},{2,42},{3,43},{4,44},{5,45},{6,46},{7,47},{8,0},{9,1... | collective-permute-start | bytes 3538952 | tf_op jit(solution)/shard_map/ppermute | solution.py:67
  57.7 17.1 %collective-permute-start.11 = (bf16[2,288,512]{2,1,0:T(8,128)(2,1)}, bf16[2,288,512]{2,1,0:T(8,128)(2,1)S(1)}, u32[]{:S(2)}, u32[]{:S(2)}) collective-permute-start(bf16[2,288,512]{2,1,0:T(8,128)(2,1)} %copy-done.8), channel_id=1, source_target_pairs={{0,1},{1,2},{2,3},{3,4},{4,5},{5,6},{6,7},{7,0},{8,9},{9,10},{10,1... | collective-permute-start | bytes 1769480 | tf_op jit(solution)/shard_map/ppermute | solution.py:67
  59.4 19.3 %collective-permute-start.13 = (bf16[2,288,512]{2,1,0:T(8,128)(2,1)}, bf16[2,288,512]{2,1,0:T(8,128)(2,1)S(1)}, u32[]{:S(2)}, u32[]{:S(2)}) collective-permute-start(bf16[2,288,512]{2,1,0:T(8,128)(2,1)} %collective-permute-done.5.refs_7_), channel_id=1, source_target_pairs={{0,7},{1,0},{2,1},{3,2},{4,3},{5,4},{6,5},{7,6},{8,15},{9,8},{10,9... | collective-permute-start | bytes 1769480 | tf_op jit(solution)/shard_map/ppermute | solution.py:67
  60.6 9.7 %collective-permute-start.16 = (f32[2]{0:T(128)S(1)}, f32[2]{0:T(128)S(1)}, u32[]{:S(2)}, u32[]{:S(2)}) collective-permute-start(f32[2]{0:T(128)S(1)} %add.362), channel_id=1, source_target_pairs={{0,1},{1,0},{2,3},{3,2},{4,5},{5,4},{6,7},{7,6},{8,9},{9,8},{10,11... | collective-permute-start | bytes 32 | tf_op jit(solution)/shard_map/ppermute | solution.py:67
  70.3 4.4 %collective-permute-start.17 = (f32[2]{0:T(128)S(1)}, f32[2]{0:T(128)S(1)}, u32[]{:S(2)}, u32[]{:S(2)}) collective-permute-start(f32[2]{0:T(128)S(1)} %add.363), channel_id=1, source_target_pairs={{0,2},{1,3},{2,0},{3,1},{4,6},{5,7},{6,4},{7,5},{8,10},{9,11},{10,... | collective-permute-start | bytes 32 | tf_op jit(solution)/shard_map/ppermute | solution.py:67
  74.8 57.3 %collective-permute-start.24 = (bf16[512,2304]{1,0:T(8,128)(2,1)S(1)}, bf16[512,2304]{1,0:T(8,128)(2,1)}, u32[]{:S(2)}, u32[]{:S(2)}) collective-permute-start(bf16[512,2304]{1,0:T(8,128)(2,1)S(1)} %bitcast.45), channel_id=1, source_target_pairs={{0,16},{1,17},{2,18},{3,19},{4,20},{5,21},{6,22},{7,23},{8,24},{9,... | collective-permute-start | bytes 7077896 | tf_op jit(solution)/shard_map/ppermute | solution.py:67
  74.8 16.3 %collective-permute-start.12 = (bf16[2,288,512]{2,1,0:T(8,128)(2,1)S(1)}, bf16[2,288,512]{2,1,0:T(8,128)(2,1)S(1)}, u32[]{:S(2)}, u32[]{:S(2)}) collective-permute-start(bf16[2,288,512]{2,1,0:T(8,128)(2,1)S(1)} %collective-permute-done.11.refs_2_), channel_id=1, source_target_pairs={{0,1},{1,2},{2,3},{3,4},{4,5},{5,6},{6,7},{7,0},{8,9},{9,10},{10,1... | collective-permute-start | bytes 1769480 | tf_op jit(solution)/shard_map/ppermute | solution.py:67
  77.8 0.8 copy-start.10
  78.7 15.5 %collective-permute-start.14 = (bf16[2,288,512]{2,1,0:T(8,128)(2,1)S(1)}, bf16[2,288,512]{2,1,0:T(8,128)(2,1)S(1)}, u32[]{:S(2)}, u32[]{:S(2)}) collective-permute-start(bf16[2,288,512]{2,1,0:T(8,128)(2,1)S(1)} %collective-permute-done.13.refs_6_), channel_id=1, source_target_pairs={{0,7},{1,0},{2,1},{3,2},{4,3},{5,4},{6,5},{7,6},{8,15},{9,8},{10,9... | collective-permute-start | bytes 1769480 | tf_op jit(solution)/shard_map/ppermute | solution.py:67
  78.7 0.8 copy-start.12
  94.1 4.7 %copy-start.6 = (bf16[2,288,512]{2,1,0:T(8,128)(2,1)}, bf16[2,288,512]{2,1,0:T(8,128)(2,1)S(1)}, u32[]{:S(2)}) copy-start(bf16[2,288,512]{2,1,0:T(8,128)(2,1)S(1)} %collective-permute-done.14.refs_5_) | copy-start | bytes 1769476
  94.1 38.0 %collective-permute-start.25 = (bf16[256,2304]{1,0:T(8,128)(2,1)S(1)}, bf16[256,2304]{1,0:T(8,128)(2,1)}, u32[]{:S(2)}, u32[]{:S(2)}) collective-permute-start(bf16[256,2304]{1,0:T(8,128)(2,1)S(1)} %collective-permute-done.9.refs_2_), channel_id=1, source_target_pairs={{0,16},{1,17},{2,18},{3,19},{4,20},{5,21},{6,22},{7,23},{8,24},{9,... | collective-permute-start | bytes 3538952 | tf_op jit(solution)/shard_map/ppermute | solution.py:67
  94.1 38.0 %collective-permute-start.26 = (bf16[256,2304]{1,0:T(8,128)(2,1)}, bf16[256,2304]{1,0:T(8,128)(2,1)}, u32[]{:S(2)}, u32[]{:S(2)}) collective-permute-start(bf16[256,2304]{1,0:T(8,128)(2,1)} %collective-permute-done.10.refs_3_), channel_id=1, source_target_pairs={{0,16},{1,17},{2,18},{3,19},{4,20},{5,21},{6,22},{7,23},{8,24},{9,... | collective-permute-start | bytes 3538952 | tf_op jit(solution)/shard_map/ppermute | solution.py:67
  95.4 0.8 copy-start.4
  96.2 15.6 %collective-permute-start.18 = (bf16[288,512]{1,0:T(8,128)(2,1)}, bf16[288,512]{1,0:T(8,128)(2,1)}, u32[]{:S(2)}, u32[]{:S(2)}) collective-permute-start(bf16[288,512]{1,0:T(8,128)(2,1)} %slice_bitcast_fusion.3), channel_id=1, source_target_pairs={{0,1},{1,2},{2,3},{3,4},{4,5},{5,6},{6,7},{7,0},{8,9},{9,10},{10,1... | collective-permute-start | bytes 884744 | tf_op jit(solution)/shard_map/ppermute | solution.py:67
  97.9 7.4 %collective-permute-start.20 = (f32[2]{0:T(128)S(1)}, f32[2]{0:T(128)S(1)}, u32[]{:S(2)}, u32[]{:S(2)}) collective-permute-start(f32[2]{0:T(128)S(1)} %add.364), channel_id=1, source_target_pairs={{0,4},{1,5},{2,6},{3,7},{4,0},{5,1},{6,2},{7,3},{8,12},{9,13},{10,... | collective-permute-start | bytes 32 | tf_op jit(solution)/shard_map/ppermute | solution.py:67
  105.4 3.5 %collective-permute-start.21 = (f32[2]{0:T(128)S(1)}, f32[2]{0:T(128)S(1)}, u32[]{:S(2)}, u32[]{:S(2)}) collective-permute-start(f32[2]{0:T(128)S(1)} %add.365), channel_id=1, source_target_pairs={{0,8},{1,9},{2,10},{3,11},{4,12},{5,13},{6,14},{7,15},{8,0},{9,1},... | collective-permute-start | bytes 32 | tf_op jit(solution)/shard_map/ppermute | solution.py:67
  108.9 8.6 %collective-permute-start.19 = (bf16[288,512]{1,0:T(8,128)(2,1)}, bf16[288,512]{1,0:T(8,128)(2,1)}, u32[]{:S(2)}, u32[]{:S(2)}) collective-permute-start(bf16[288,512]{1,0:T(8,128)(2,1)} %slice_bitcast_fusion.2), channel_id=1, source_target_pairs={{0,7},{1,0},{2,1},{3,2},{4,3},{5,4},{6,5},{7,6},{8,15},{9,8},{10,9... | collective-permute-start | bytes 884744 | tf_op jit(solution)/shard_map/ppermute | solution.py:67
  111.8 12.0 %copy-start.3 = (bf16[2,288,512]{2,1,0:T(8,128)(2,1)S(1)}, bf16[2,288,512]{2,1,0:T(8,128)(2,1)}, u32[]{:S(2)}) copy-start(bf16[2,288,512]{2,1,0:T(8,128)(2,1)} %copy-done.2) | copy-start | bytes 1769476
  111.8 12.0 %copy-start.5 = (bf16[2,288,512]{2,1,0:T(8,128)(2,1)S(1)}, bf16[2,288,512]{2,1,0:T(8,128)(2,1)}, u32[]{:S(2)}) copy-start(bf16[2,288,512]{2,1,0:T(8,128)(2,1)} %copy-done.4) | copy-start | bytes 1769476
  117.5 1.1 collective-permute-start.22
  118.7 5.1 %collective-permute-start.23 = (f32[4]{0:T(128)S(1)}, f32[4]{0:T(128)S(1)}, u32[]{:S(2)}, u32[]{:S(2)}) collective-permute-start(f32[4]{0:T(128)S(1)} %pad_maximum_fusion.3), channel_id=1, source_target_pairs={{0,32},{1,33},{2,34},{3,35},{4,36},{5,37},{6,38},{7,39},{8,40},{9,... | collective-permute-start | bytes 56 | tf_op jit(solution)/shard_map/ppermute | solution.py:67
  123.8 1.1 copy-start.7
  124.9 1.1 copy-start.9
  126.0 1.1 copy-start.11
  127.0 1.1 copy-start.13
  130.0 2.1 %copy-start = (bf16[4,4,288,512]{3,2,1,0:T(8,128)(2,1)}, bf16[4,4,288,512]{3,2,1,0:T(8,128)(2,1)S(1)}, u32[]{:S(2)}) copy-start(bf16[4,4,288,512]{3,2,1,0:T(8,128)(2,1)S(1)} %scale_grads.1.s_ref) | copy-start | bytes 14155780
  139.9 22.3 %collective-permute-start.31 = (bf16[288,1152]{1,0:T(8,128)(2,1)S(1)}, bf16[288,1152]{1,0:T(8,128)(2,1)S(1)}, u32[]{:S(2)}, u32[]{:S(2)}) collective-permute-start(bf16[288,1152]{1,0:T(8,128)(2,1)S(1)} %get-tuple-element.42), channel_id=1, source_target_pairs={{0,192},{1,193},{2,194},{3,195},{4,196},{5,197},{6,198},{7,199},{8... | collective-permute-start | bytes 1990664 | tf_op jit(solution)/shard_map/ppermute | solution.py:67
  150.7 39.3 %collective-permute-start.30 = (bf16[288,1152]{1,0:T(8,128)(2,1)S(1)}, bf16[288,1152]{1,0:T(8,128)(2,1)S(1)}, u32[]{:S(2)}, u32[]{:S(2)}) collective-permute-start(bf16[288,1152]{1,0:T(8,128)(2,1)S(1)} %get-tuple-element.40), channel_id=1, source_target_pairs={{0,64},{1,65},{2,66},{3,67},{4,68},{5,69},{6,70},{7,71},{8,72},{9,... | collective-permute-start | bytes 1990664 | tf_op jit(solution)/shard_map/ppermute | solution.py:67
  150.8 31.3 %collective-permute-start.27 = (bf16[288,1152]{1,0:T(8,128)(2,1)S(1)}, bf16[288,1152]{1,0:T(8,128)(2,1)S(1)}, u32[]{:S(2)}, u32[]{:S(2)}) collective-permute-start(bf16[288,1152]{1,0:T(8,128)(2,1)S(1)} %get-tuple-element.38), channel_id=1, source_target_pairs={{0,64},{1,65},{2,66},{3,67},{4,68},{5,69},{6,70},{7,71},{8,72},{9,... | collective-permute-start | bytes 1990664 | tf_op jit(solution)/shard_map/ppermute | solution.py:67
  159.1 31.0 %collective-permute-start.29 = (bf16[288,1152]{1,0:T(8,128)(2,1)S(1)}, bf16[288,1152]{1,0:T(8,128)(2,1)S(1)}, u32[]{:S(2)}, u32[]{:S(2)}) collective-permute-start(bf16[288,1152]{1,0:T(8,128)(2,1)S(1)} %get-tuple-element.39), channel_id=1, source_target_pairs={{0,192},{1,193},{2,194},{3,195},{4,196},{5,197},{6,198},{7,199},{8... | collective-permute-start | bytes 1990664 | tf_op jit(solution)/shard_map/ppermute | solution.py:67
  162.3 27.7 %collective-permute-start.32 = (bf16[288,1152]{1,0:T(8,128)(2,1)S(1)}, bf16[288,1152]{1,0:T(8,128)(2,1)S(1)}, u32[]{:S(2)}, u32[]{:S(2)}) collective-permute-start(bf16[288,1152]{1,0:T(8,128)(2,1)S(1)} %add_convert_fusion), channel_id=1, source_target_pairs={{0,192},{1,193},{2,194},{3,195},{4,196},{5,197},{6,198},{7,199},{8... | collective-permute-start | bytes 1990664 | tf_op jit(solution)/shard_map/ppermute | solution.py:67
  182.3 16.3 %collective-permute-start.28 = (bf16[288,1152]{1,0:T(8,128)(2,1)S(1)}, bf16[288,1152]{1,0:T(8,128)(2,1)S(1)}, u32[]{:S(2)}, u32[]{:S(2)}) collective-permute-start(bf16[288,1152]{1,0:T(8,128)(2,1)S(1)} %add_convert_fusion.1), channel_id=1, source_target_pairs={{0,64},{1,65},{2,66},{3,67},{4,68},{5,69},{6,70},{7,71},{8,72},{9,... | collective-permute-start | bytes 1990664 | tf_op jit(solution)/shard_map/ppermute | solution.py:67
  190.1 8.6 %copy-start.14 = (f32[288,2304]{1,0:T(8,128)S(1)}, f32[288,2304]{1,0:T(8,128)}, u32[]{:S(2)}) copy-start(f32[288,2304]{1,0:T(8,128)} %param.7) | copy-start | bytes 7962628

commit v2 on v0

v2 whole, which is shorter than its diff:
```python
import functools
import math

import jax
import jax.numpy as jnp
from jax import lax
from jax.experimental import pallas as pl
from jax.experimental.pallas import tpu as pltpu
from jax.sharding import PartitionSpec as P

clip_norm = 2.5
AXES = ("dp", "tensor")
NY, NX, NZ = 4, 4, 8
STEP_Z = ((4, -3), (-1, 2), (0, 1), (-2, 3))
MEMBER = [0] * NZ
for away in range(NY):
    for other in range(2):
        MEMBER[STEP_Z[away][other] % NZ] = 2 * away + other
BF = jnp.bfloat16
F32 = jnp.float32


def coords(i):
    dp, te = divmod(i, 2 * NZ)
    return dp // 4, (dp // 2) % 2, dp % 2, te // NZ, te % NZ


def index(y, xh, c, xl, z):
    return ((y % NY * 2 + xh) * 2 + c) * 2 * NZ + xl * NZ + z % NZ


def perm_of(move):
    return [(i, index(*move(*coords(i)))) for i in range(NY * NX * NZ * 2)]


def along_x(step):
    def move(y, xh, c, xl, z):
        x = (xh * 2 + xl + step) % NX
        return y, x // 2, c, x % 2, z

    return perm_of(move)


def along_y(step):
    return perm_of(lambda y, xh, c, xl, z: (y + step, xh, c, xl, z))


def along_z(step):
    return perm_of(lambda y, xh, c, xl, z: (y, xh, c, xl, z + step))


def flip_z(bit):
    return perm_of(lambda y, xh, c, xl, z: (y, xh, c, xl, z ^ bit))


def spread(turn):
    def move(y, xh, c, xl, z):
        row_y, row_x, row_c = 2 * xl + z // 4, (z // 2) % 2, z % 2
        step = STEP_Z[(y - row_y) % NY][c ^ row_c]
        return row_y, xh, row_c, xl ^ row_x ^ turn, z + step

    return perm_of(move)


CORE = perm_of(lambda y, xh, c, xl, z: (y, xh, 1 - c, xl, z))
XHI = perm_of(lambda y, xh, c, xl, z: (y, 1 - xh, c, xl, z))
XLO = perm_of(lambda y, xh, c, xl, z: (y, xh, c, 1 - xl, z))


def send(value, perm):
    return lax.ppermute(value, AXES, perm)


def scale_kernel(theirs, id_ref, clip_ref, ring_ref, out_ref):
    dp = id_ref[0]
    y, xh, c = dp // 4, (dp // 2) % 2, dp % 2
    row_x = 1 - xh if theirs else xh
    source = 4 * (y % 2) + 2 * row_x + c
    half = out_ref.shape[2] // 2
    for z in range(NZ):
        m = id_ref[1 + (z - source + NZ) % NZ]
        member = 2 * ((y + m // 2) % NY) + (c + m) % 2
        for e in range(2):
            cols = slice(e * half, (e + 1) * half)
            out_ref[m, :, cols] = (
                clip_ref[2 * member + e] * ring_ref[z, :, cols].astype(F32)
            ).astype(BF)


def scale_grads(theirs, ids, clips, ring):
    _, rows, tokens = ring.shape
    smem = pl.BlockSpec(memory_space=pltpu.SMEM)
    vmem = pl.BlockSpec(memory_space=pltpu.VMEM)
    return pl.pallas_call(
        functools.partial(scale_kernel, theirs),
        out_shape=jax.ShapeDtypeStruct(ring.shape, BF),
        in_specs=[smem, smem, vmem],
        out_specs=vmem,
        cost_estimate=pl.CostEstimate(
            flops=8 * rows * tokens, bytes_accessed=32 * rows * tokens, transcendentals=0
        ),
        compiler_params=pltpu.CompilerParams(vmem_limit_bytes=24 * 1024 * 1024),
        name="scale_theirs" if theirs else "scale_mine",
    )(ids, clips, ring)


def product_kernel(s_ref, *refs):
    acts, out_ref = refs[:-1], refs[-1]
    tokens = s_ref.shape[2]
    total = None
    first = 0
    for a_ref in acts:
        count = a_ref.shape[0]
        m, start = first // tokens, first % tokens
        part = jnp.dot(s_ref[m, :, start : start + count], a_ref[...], preferred_element_type=F32)
        total = part if total is None else total + part
        first += count
    out_ref[...] = total.astype(out_ref.dtype)


def product(name, scaled, acts, width, tile, dtype):
    members, rows, tokens = scaled.shape
    depth = members * tokens

    def spec(height, first):
        return pl.BlockSpec((height, tile), lambda j: (0, j + first // tile))

    return pl.pallas_call(
        product_kernel,
        out_shape=jax.ShapeDtypeStruct((rows, width), dtype),
        grid=(width // tile,),
        in_specs=[pl.BlockSpec((members, rows, tokens), lambda j: (0, 0, 0))]
        + [spec(a.shape[0], first) for a, first in acts],
        out_specs=spec(rows, 0),
        cost_estimate=pl.CostEstimate(
            flops=2 * rows * depth * width,
            bytes_accessed=2 * (rows * depth + depth * width + rows * width),
            transcendentals=0,
        ),
        compiler_params=pltpu.CompilerParams(vmem_limit_bytes=40 * 1024 * 1024),
        name=name,
    )(scaled, *[a for a, _ in acts])


def shards(acts, out_grads, other_sq, noise):
    dp, te = lax.axis_index("dp"), lax.axis_index("tensor")
    y, xh, xl = dp // 4, (dp // 2) % 2, te // NZ
    examples, seq, columns = acts.shape
    tokens = examples * seq
    features = out_grads.shape[2]
    rows = features // 2
    tile = columns // 3
    stage = lax.optimization_barrier
    ids = jnp.stack([dp] + [jnp.int32(m) for m in MEMBER]).astype(jnp.int32)

    grads_t = out_grads.reshape(tokens, features).T
    sources = [send(grads_t, spread(0)), send(grads_t, spread(1))]

    def blocks(x):
        gram = jnp.einsum("btf,bsf->bts", x, x, preferred_element_type=F32).astype(BF)
        mid = seq // 2
        return jnp.stack([gram[:, :mid, :mid], gram[:, :mid, mid:], gram[:, mid:, mid:]])

    grams = jnp.stack([blocks(acts), blocks(out_grads)])
    flat = acts.reshape(tokens, columns)
    grams, flat = stage((grams, flat))

    def near(k):
        part = flat[:, k * tile : (k + 1) * tile]
        return send(part, along_y(1)), send(part, along_y(-1))

    below, above = near(0)
    below, above = [below], [above]
    sibling = send(flat, CORE)
    shape = grams.shape
    grams = jnp.moveaxis(grams.reshape(shape[:3] + (2 * NZ, -1, shape[4])), 3, 0)
    grams = lax.all_to_all(grams, "tensor", 0, 0, tiled=True).astype(F32).sum(axis=0)
    sources[0], sources[1], grams, flat = stage((sources[0], sources[1], grams, flat))

    turn = xl ^ (y // 2) ^ xh
    z_rings = [list(range(first, first + NZ)) for first in (0, NZ)]
    theirs, mine = [
        lax.all_gather(
            jnp.where(turn == t, sources[0], sources[1])[None],
            "tensor",
            axis=0,
            tiled=True,
            axis_index_groups=z_rings,
        )
        for t in (1, 0)
    ]
    for side, value in zip((below, above), near(1)):
        side.append(value)
    weight = jnp.array([1.0, 2.0, 1.0], F32)[:, None, None, None]
    total = jnp.sum(grams[0] * grams[1] * weight, axis=(0, 2, 3)) + jnp.sum(other_sq, axis=1)
    total = lax.all_to_all(
        jnp.broadcast_to(total, (2 * NZ, examples)), "tensor", 0, 0, tiled=True
    ).sum(axis=0)
    clip = jnp.minimum(1.0, clip_norm / jnp.sqrt(total))
    clip, below, above = stage((clip, below, above))

    far_below = send(jnp.concatenate([b[:seq] for b in below], axis=1), along_y(1))
    far_above = send(jnp.concatenate([a[seq:] for a in above], axis=1), along_y(-1))
    clip, far_below, far_above, flat = stage((clip, far_below, far_above, flat))
    columns_y = [[4 * k + 2 * x + core for k in range(NY) for core in range(2)] for x in range(2)]
    clips = lax.all_to_all(
        jnp.broadcast_to(clip, (2 * NY, examples)),
        "dp",
        0,
        0,
        tiled=True,
        axis_index_groups=columns_y,
    ).reshape(-1)
    clips, flat, far_below, far_above = stage((clips, flat, far_below, far_above))
    for side, value in zip((below, above), near(2)):
        side.append(value)

    def swap(array):
        return send(array, CORE)

    far_sibling = [swap(far_below), swap(far_above)]
    near_sibling = [(swap(above[k]), swap(below[k])) for k in range(2)]

    def held(k, far, far_other, first):
        parts = [(flat, k * tile), (sibling, k * tile), (above[k], 0), (near_sibling[k][0], 0)]
        parts += [(a, first) for a in far + far_other]
        return parts + [(below[k], 0), (near_sibling[k][1], 0)]

    scaled = scale_grads(True, ids, clips, theirs)
    early = [held(k, [far_below, far_above], far_sibling, k * tile) for k in range(2)]
    part = jnp.concatenate(
        [product(f"theirs_{k}", scaled, early[k], tile, tile, BF) for k in range(2)], axis=1
    )
    low, high = send(part[:rows], along_x(1)), send(part[rows:], along_x(-1))
    low, high, below[2], above[2] = stage((low, high, below[2], above[2]))
    low, high = send(low, along_x(1)), send(high, along_x(-1))
    far = [send(below[2][:seq], along_y(1)), send(above[2][seq:], along_y(-1))]
    near_sibling.append((swap(above[2]), swap(below[2])))
    low, high, far = stage((low, high, far))

    late = held(2, far, [swap(a) for a in far], 0)
    part = product("theirs_2", scaled, late, tile, tile, BF)
    part, mine = stage((part, mine))
    low2, high2 = send(part[:rows], along_x(1)), send(part[rows:], along_x(-1))
    scaled = scale_grads(False, ids, clips, mine)
    own = [product(f"mine_{k}", scaled, early[k], tile, tile, F32) for k in range(2)]
    low2, high2 = send(low2, along_x(1)), send(high2, along_x(-1))
    own.append(product("mine_2", scaled, late, tile, tile, F32))

    width = features * 2 * NZ
    factor = math.sqrt(columns * 2 * NZ * width) / clip_norm
    root = math.sqrt(examples * 4 * NY)
    parts = []
    for k in range(3):
        up, down = (low2, high2) if k == 2 else (low, high)
        first = 0 if k == 2 else k * tile
        got = jnp.concatenate([a[:, first : first + tile] for a in (up, down)]).astype(F32)
        parts.append((factor * (own[k] + got) + noise[:, k * tile : (k + 1) * tile]) / root)
    return jnp.concatenate(parts, axis=1)


def solution(mesh):
    placed = (
        P("dp", None, "tensor"),
        P("dp", None, "tensor"),
        P("dp", "tensor"),
        P("dp", "tensor"),
    )
    return jax.shard_map(
        shards, mesh=mesh, in_specs=placed, out_specs=P("dp", "tensor"), check_vma=False
    )
```

time: 518 us -> 224 us (0.43)
  waiting for transfers between devices: 354 us -> 93.8 us
  other arithmetic: 82.9 us -> 5.39 us
  starting transfers between devices: 0.08 us -> 51.8 us
  matrix products: 33.2 us -> 3.57 us
  blocking collectives: 34.4 us -> 7.77 us
  Pallas kernels: 0 us -> 25.9 us
  local copies, waits for them, and re-layouts: 0.02 us -> 19.7 us
    reduce_scatter x1 -> x0, waiting for transfers between devices: 175 us -> none  [shards(): lax.psum_scatter(result.astype(jnp.bfloat16), 'dp', scatter_dimension=0,...]
    psum x1 -> x0, waiting for transfers between devices: 101 us -> none  [shards(): lax.psum(act_gram.astype(jnp.bfloat16), 'tensor').astype(jnp.float32)]
    all_gather x1 -> x2, waiting for transfers between devices: 77.2 us -> 0.01 us  [shards(): lax.all_gather(jnp.where(turn == t, sources[0], sources[1])[None], 'tenso...]
    ppermute x0 -> x31, waiting for transfers between devices: none -> 73.7 us  [send(): return lax.ppermute(value, AXES, perm)]
    add x2 -> x1, other arithmetic: 54.5 us -> 0.01 us  [shards(): jnp.sum(grams[0] * grams[1] * weight, axis=(0, 2, 3))]
    ppermute x0 -> x31, starting transfers between devices: none -> 34.5 us  [send(): return lax.ppermute(value, AXES, perm)]
    psum x1 -> x0, blocking collectives: 34.4 us -> none  [shards(): lax.psum(other_local.astype(jnp.bfloat16), 'tensor').astype(jnp.float32)]
    dot_general x4 -> x2, matrix products: 33.2 us -> 3.57 us  [blocks(): jnp.einsum('btf,bsf->bts', x, x, preferred_element_type=F32).astype(BF)]
  transfers between devices with their start and end apart: 3 -> 35, of which waited for: 3 -> 16; matrix products, arithmetic and copies ran while one was open for 0% -> 5% of each run, Pallas kernels for 0% -> 12%
where the time goes in v2:
time: 224 us; the launch traced here: 222 us
  waiting for transfers between devices  93.8 us (42%)
  starting transfers between devices  51.8 us (23%)
  Pallas kernels  25.9 us (12%)
  local copies, waits for them, and re-layouts  19.7 us (9%)
  between operations  13.9 us (6%)
  blocking collectives  7.77 us (3%)
  other arithmetic  5.39 us (2%)
  matrix products  3.57 us (2%)
    ppermute x31, waiting for transfers between devices, send(): return lax.ppermute(value, AXES, perm)  73.7 us
    ppermute x31, starting transfers between devices, send(): return lax.ppermute(value, AXES, perm)  34.5 us
    pallas_call x6, Pallas kernels, product(): pl.pallas_call(product_kernel, out_shape=jax.ShapeDtypeStruct((rows, widt...  23.8 us
    all_to_all x1, waiting for transfers between devices, shards(): lax.all_to_all(grams, 'tensor', 0, 0, tiled=True).astype(F32).sum(axis=0)  12.9 us
    all_to_all x1, starting transfers between devices, shards(): lax.all_to_all(grams, 'tensor', 0, 0, tiled=True).astype(F32).sum(axis=0)  9.52 us
    unnamed x56, local copies, waits for them, and re-layouts  8.67 us
    all_to_all x1, blocking collectives, shards(): lax.all_to_all(jnp.broadcast_to(clip, (2 * NY, examples)), 'dp', 0, 0, ti...  7.77 us
    all_to_all x1, starting transfers between devices, shards(): lax.all_to_all(jnp.broadcast_to(total, (2 * NZ, examples)), 'tensor', 0,...  7.73 us
  transfers between devices with their start and end apart: 35, of which 16 were waited for; matrix products, arithmetic and copies ran while one was open for 5% of the time, Pallas kernels for 12%

profile of v2, /device:TPU:32, one launch (start us, length us, event | category | flops | bytes accessed | tf_op | source)
XLA Modules:
  0.0 221.8 jit_solution(5918012113451403334)
XLA Ops:
  6.5 3.2 %convolution_convert_fusion.1 = bf16[2,256,256]{2,1,0:T(8,128)(2,1)S(1)} fusion(bf16[2,256,2304]{2,1,0:T(8,128)(2,1)} %param.5), kind=kOutput, calls=%fused_computation.2 | convolution fusion | flops 604110848 | bytes 2621440 | tf_op jit(solution)/shard_map/btf,bsf->bts/dot_general | solution.py:160
  10.3 0.8 copy_bitcast_fusion
  11.1 9.5 %all-to-all-start = ((bf16[16,2,3,2,8,128]{5,4,3,2,1,0:T(8,128)(2,1)}), bf16[16,2,3,2,8,128]{5,4,3,2,1,0:T(8,128)(2,1)S(1)}, u32[]{:S(2)}, u32[]{:S(2)}) async-start(bf16[16,2,3,2,8,128]{5,4,3,2,1,0:T(8,128)(2,1)} %copy_bitcast_fusion), calls=%async_computation | async-start | bytes 786432 | tf_op jit(solution)/shard_map/all_to_all | solution.py:177
  20.7 3.4 %collective-permute-start.1 = (bf16[288,512]{1,0:T(8,128)(2,1)S(1)}, bf16[288,512]{1,0:T(8,128)(2,1)S(1)}, u32[]{:S(2)}, u32[]{:S(2)}) collective-permute-start(bf16[288,512]{1,0:T(8,128)(2,1)S(1)} %bitcast.50), channel_id=1, source_target_pairs={{0,12},{1,30},{2,6},{3,16},{4,74},{5,88},{6,68},{7,82},{8,128},{9,... | collective-permute-start | bytes 884744 | tf_op jit(solution)/shard_map/ppermute | solution.py:71
  24.2 2.4 %collective-permute-start = (bf16[288,512]{1,0:T(8,128)(2,1)S(1)}, bf16[288,512]{1,0:T(8,128)(2,1)}, u32[]{:S(2)}, u32[]{:S(2)}) collective-permute-start(bf16[288,512]{1,0:T(8,128)(2,1)S(1)} %bitcast.51), channel_id=1, source_target_pairs={{0,4},{1,22},{2,14},{3,24},{4,66},{5,80},{6,76},{7,90},{8,136},{9,... | collective-permute-start | bytes 884744 | tf_op jit(solution)/shard_map/ppermute | solution.py:71
  26.6 12.9 %all-to-all-done = bf16[16,2,3,2,8,128]{5,4,3,2,1,0:T(8,128)(2,1)S(1)} async-done(((bf16[16,2,3,2,8,128]{5,4,3,2,1,0:T(8,128)(2,1)}), bf16[16,2,3,2,8,128]{5,4,3,2,1,0:T(8,128)(2,1)S(1)}, u32[]{:S(2)}, u32[]{:S(2)}) %all-to-all-start) | async-done | bytes 393248 | tf_op jit(solution)/shard_map/all_to_all | solution.py:177
  39.6 15.7 %collective-permute-done.1 = bf16[288,512]{1,0:T(8,128)(2,1)S(1)} collective-permute-done((bf16[288,512]{1,0:T(8,128)(2,1)S(1)}, bf16[288,512]{1,0:T(8,128)(2,1)S(1)}, u32[]{:S(2)}, u32[]{:S(2)}) %collective-permute-start.1) | collective-permute-done | bytes 294944 | tf_op jit(solution)/shard_map/ppermute | solution.py:71
  55.3 5.3 %collective-permute-done = bf16[288,512]{1,0:T(8,128)(2,1)} collective-permute-done((bf16[288,512]{1,0:T(8,128)(2,1)S(1)}, bf16[288,512]{1,0:T(8,128)(2,1)}, u32[]{:S(2)}, u32[]{:S(2)}) %collective-permute-start) | collective-permute-done | bytes 294944 | tf_op jit(solution)/shard_map/ppermute | solution.py:71
  60.6 1.8 broadcast_select_fusion
  62.4 0.9 slice.92
  63.4 2.0 collective-permute-start.2
  65.4 0.9 slice.93
  66.3 1.2 collective-permute-start.5
  67.5 0.8 collective-permute-start.3
  68.4 2.7 %collective-permute-start.8 = (bf16[512,2304]{1,0:T(8,128)(2,1)S(1)}, bf16[512,2304]{1,0:T(8,128)(2,1)}, u32[]{:S(2)}, u32[]{:S(2)}) collective-permute-start(bf16[512,2304]{1,0:T(8,128)(2,1)S(1)} %bitcast.39), channel_id=1, source_target_pairs={{0,16},{1,17},{2,18},{3,19},{4,20},{5,21},{6,22},{7,23},{8,24},{9,... | collective-permute-start | bytes 7077896 | tf_op jit(solution)/shard_map/ppermute | solution.py:71
  71.4 0.6 broadcast_in_dim.13
  72.0 7.7 %all-to-all-start.1 = ((f32[16,1,2]{2,1,0:T(1,128)}), f32[16,1,2]{2,1,0:T(1,128)S(1)}, u32[]{:S(2)}, u32[]{:S(2)}) async-start(f32[16,1,2]{2,1,0:T(1,128)} %broadcast_in_dim.13), calls=%async_computation.1 | async-start | bytes 16384 | tf_op jit(solution)/shard_map/all_to_all | solution.py:196
  79.7 0.7 all-gather.7.cloned.1.call-update
  80.4 6.5 %all-to-all-done.1 = f32[16,1,2]{2,1,0:T(1,128)S(1)} async-done(((f32[16,1,2]{2,1,0:T(1,128)}), f32[16,1,2]{2,1,0:T(1,128)S(1)}, u32[]{:S(2)}, u32[]{:S(2)}) %all-to-all-start.1) | async-done | bytes 160 | tf_op jit(solution)/shard_map/all_to_all | solution.py:196
  87.0 11.0 %collective-permute-done.5.refs_2_ = bf16[512,768]{1,0:T(8,128)(2,1)} collective-permute-done((bf16[512,768]{1,0:T(8,128)(2,1)}, bf16[512,768]{1,0:T(8,128)(2,1)}, u32[]{:S(2)}, u32[]{:S(2)}) %collective-permute-start.5) | collective-permute-done | bytes 786464 | tf_op jit(solution)/shard_map/ppermute | solution.py:71
  98.0 3.7 %collective-permute-done.3.refs_8_ = bf16[512,768]{1,0:T(8,128)(2,1)} collective-permute-done((bf16[512,768]{1,0:T(8,128)(2,1)}, bf16[512,768]{1,0:T(8,128)(2,1)}, u32[]{:S(2)}, u32[]{:S(2)}) %collective-permute-start.3) | collective-permute-done | bytes 786464 | tf_op jit(solution)/shard_map/ppermute | solution.py:71
  101.7 1.0 slice.94
  102.8 1.0 slice.95
  103.8 1.0 slice.97
  105.1 2.1 collective-permute-start.6
  107.7 17.0 %collective-permute-done.7.refs_5_ = bf16[256,1536]{1,0:T(8,128)(2,1)S(1)} collective-permute-done((bf16[256,1536]{1,0:T(8,128)(2,1)S(1)}, bf16[256,1536]{1,0:T(8,128)(2,1)S(1)}, u32[]{:S(2)}, u32[]{:S(2)}) %collective-permute-start.7) | collective-permute-done | bytes 786464 | tf_op jit(solution)/shard_map/ppermute | solution.py:71
  124.7 1.5 collective-permute-done.6.refs_4_
  126.2 7.8 %all_to_all.17 = f32[8,1,2]{2,1,0:T(1,128)S(1)} all-to-all(f32[8,1,2]{2,1,0:T(1,128)S(1)} %broadcast_in_dim.14), channel_id=1, replica_groups={{0,16,64,80,128,144,192,208},{32,48,96,112,160,176,224,240},{1,17,65,81..., dimensions={0} | all-to-all | bytes 128 | tf_op jit(solution)/shard_map/all_to_all | solution.py:206
  134.4 0.7 reduce.4
  136.3 0.9 slice.100
  137.3 1.7 copy-done.13
  138.9 1.0 scale_theirs.1.s_ref
  140.1 1.2 collective-permute-start.18
  141.3 0.9 collective-permute-start.17
  142.1 4.5 %theirs_1.1 = bf16[288,768]{1,0:T(8,128)(2,1)S(1)} custom-call(bf16[8,288,512]{2,1,0:T(8,128)(2,1)S(1)} %scale_theirs.1.s_ref, bf16[512,2304]{1,0:T(8,128)(2,1)S(1)} %bitcast.41, bf16[512,2304]{1,0:T(8,128)(2,1)} %collective-permute-done.8.refs_1_, bf16[512,768]{1,0:T(8,128)(2,1)} %collective-permute-done.5.refs_2_, ...), custom_call_target="tpu_custom_call" | custom-call | flops 1811939328 | bytes 9093120 | tf_op jit(solution)/shard_map/theirs_1/pallas_call | solution.py:128
  146.6 4.2 %theirs_0.1 = bf16[288,768]{1,0:T(8,128)(2,1)S(1)} custom-call(bf16[8,288,512]{2,1,0:T(8,128)(2,1)S(1)} %scale_theirs.1.s_ref, bf16[512,2304]{1,0:T(8,128)(2,1)S(1)} %bitcast.42, bf16[512,2304]{1,0:T(8,128)(2,1)} %collective-permute-done.8.refs_1_, bf16[512,768]{1,0:T(8,128)(2,1)S(1)} %copy-done.6, bf16[512,768]{1,0:T(8,128)(2,1)} %collective-permute-done.9.refs_3_, ...), custom_call_target="tpu_custom_call" | custom-call | flops 1811939328 | bytes 9093120 | tf_op jit(solution)/shard_map/theirs_0/pallas_call | solution.py:128
  150.9 2.3 %collective-permute-start.16 = (bf16[144,1536]{1,0:T(8,128)(2,1)S(1)}, bf16[144,1536]{1,0:T(8,128)(2,1)S(1)}, u32[]{:S(2)}, u32[]{:S(2)}) collective-permute-start(bf16[144,1536]{1,0:T(8,128)(2,1)S(1)} %get-tuple-element.66), channel_id=1, source_target_pairs={{0,40},{1,41},{2,42},{3,43},{4,44},{5,45},{6,46},{7,47},{8,0},{9,1... | collective-permute-start | bytes 1327112 | tf_op jit(solution)/shard_map/ppermute | solution.py:71
  153.2 6.4 %collective-permute-done.18.refs_2_ = bf16[512,768]{1,0:T(8,128)(2,1)S(1)} collective-permute-done((bf16[512,768]{1,0:T(8,128)(2,1)S(1)}, bf16[512,768]{1,0:T(8,128)(2,1)S(1)}, u32[]{:S(2)}, u32[]{:S(2)}) %collective-permute-start.18) | collective-permute-done | bytes 786464 | tf_op jit(solution)/shard_map/ppermute | solution.py:71
  159.6 2.1 collective-permute-done.17.refs_8_
  161.8 0.8 collective-permute-done.16
  162.6 3.1 %collective-permute-done.15 = bf16[144,1536]{1,0:T(8,128)(2,1)S(1)} collective-permute-done((bf16[144,1536]{1,0:T(8,128)(2,1)S(1)}, bf16[144,1536]{1,0:T(8,128)(2,1)S(1)}, u32[]{:S(2)}, u32[]{:S(2)}) %collective-permute-start.15) | collective-permute-done | bytes 442400 | tf_op jit(solution)/shard_map/ppermute | solution.py:71
  165.8 0.7 collective-permute-start.22
  166.4 3.2 %collective-permute-start.21 = (bf16[144,1536]{1,0:T(8,128)(2,1)S(1)}, bf16[144,1536]{1,0:T(8,128)(2,1)}, u32[]{:S(2)}, u32[]{:S(2)}) collective-permute-start(bf16[144,1536]{1,0:T(8,128)(2,1)S(1)} %collective-permute-done.16), channel_id=1, source_target_pairs={{0,40},{1,41},{2,42},{3,43},{4,44},{5,45},{6,46},{7,47},{8,0},{9,1... | collective-permute-start | bytes 1327112 | tf_op jit(solution)/shard_map/ppermute | solution.py:71
  169.7 2.7 %collective-permute-start.23 = (bf16[256,768]{1,0:T(8,128)(2,1)S(1)}, bf16[256,768]{1,0:T(8,128)(2,1)S(1)}, u32[]{:S(2)}, u32[]{:S(2)}) collective-permute-start(bf16[256,768]{1,0:T(8,128)(2,1)S(1)} %slice.102), channel_id=1, source_target_pairs={{0,192},{1,193},{2,194},{3,195},{4,196},{5,197},{6,198},{7,199},{8... | collective-permute-start | bytes 1179656 | tf_op jit(solution)/shard_map/ppermute | solution.py:71
  172.4 3.9 %collective-permute-done.22.refs_4_ = bf16[256,768]{1,0:T(8,128)(2,1)S(1)} collective-permute-done((bf16[256,768]{1,0:T(8,128)(2,1)S(1)}, bf16[256,768]{1,0:T(8,128)(2,1)S(1)}, u32[]{:S(2)}, u32[]{:S(2)}) %collective-permute-start.22) | collective-permute-done | bytes 393248 | tf_op jit(solution)/shard_map/ppermute | solution.py:71
  176.4 2.0 collective-permute-done.23.refs_5_
  179.0 0.8 fusion.2
  180.2 0.6 collective-permute-done.25.refs_7_
  180.8 3.2 %theirs_2.1 = bf16[288,768]{1,0:T(8,128)(2,1)S(1)} custom-call(bf16[8,288,512]{2,1,0:T(8,128)(2,1)S(1)} %scale_theirs.1.s_ref, bf16[512,2304]{1,0:T(8,128)(2,1)S(1)} %bitcast.43, bf16[512,2304]{1,0:T(8,128)(2,1)} %collective-permute-done.8.refs_1_, bf16[512,768]{1,0:T(8,128)(2,1)S(1)} %collective-permute-done.18.refs_2_, ...), custom_call_target="tpu_custom_call" | custom-call | flops 1811939328 | bytes 9093120 | tf_op jit(solution)/shard_map/theirs_2/pallas_call | solution.py:128
  184.0 0.9 copy-done.8
  184.9 0.9 copy-done.10
  185.8 0.8 copy-done.14
  186.5 0.8 copy-done.17
  187.3 0.7 copy-done.19
  188.0 1.1 fusion.4
  189.2 3.2 %collective-permute-start.29 = (bf16[144,768]{1,0:T(8,128)(2,1)S(1)}, bf16[144,768]{1,0:T(8,128)(2,1)S(1)}, u32[]{:S(2)}, u32[]{:S(2)}) collective-permute-start(bf16[144,768]{1,0:T(8,128)(2,1)S(1)} %get-tuple-element.75), channel_id=1, source_target_pairs={{0,40},{1,41},{2,42},{3,43},{4,44},{5,45},{6,46},{7,47},{8,0},{9,1... | collective-permute-start | bytes 663560 | tf_op jit(solution)/shard_map/ppermute | solution.py:71
  192.4 1.1 fusion.3
  193.5 1.7 copy-done.12
  195.2 1.0 scale_mine.1.s_ref
  197.4 3.2 %mine_2.1 = f32[288,768]{1,0:T(8,128)S(1)} custom-call(bf16[8,288,512]{2,1,0:T(8,128)(2,1)S(1)} %scale_mine.1.s_ref, bf16[512,2304]{1,0:T(8,128)(2,1)S(1)} %bitcast.44, bf16[512,2304]{1,0:T(8,128)(2,1)} %collective-permute-done.8.refs_1_, bf16[512,768]{1,0:T(8,128)(2,1)S(1)} %copy-done.2, bf16[512,768]{1,0:T(8,128)(2,1)S(1)} %copy-done.9, ...), custom_call_target="tpu_custom_call" | custom-call | flops 1811939328 | bytes 9093120 | tf_op jit(solution)/shard_map/mine_2/pallas_call | solution.py:128
  200.6 3.2 %collective-permute-start.30 = (bf16[144,768]{1,0:T(8,128)(2,1)S(1)}, bf16[144,768]{1,0:T(8,128)(2,1)S(1)}, u32[]{:S(2)}, u32[]{:S(2)}) collective-permute-start(bf16[144,768]{1,0:T(8,128)(2,1)S(1)} %collective-permute-done.29), channel_id=1, source_target_pairs={{0,40},{1,41},{2,42},{3,43},{4,44},{5,45},{6,46},{7,47},{8,0},{9,1... | collective-permute-start | bytes 663560 | tf_op jit(solution)/shard_map/ppermute | solution.py:71
  203.9 4.4 %mine_1.1 = f32[288,768]{1,0:T(8,128)S(1)} custom-call(bf16[8,288,512]{2,1,0:T(8,128)(2,1)S(1)} %scale_mine.1.s_ref, bf16[512,2304]{1,0:T(8,128)(2,1)S(1)} %bitcast.45, bf16[512,2304]{1,0:T(8,128)(2,1)} %collective-permute-done.8.refs_1_, bf16[512,768]{1,0:T(8,128)(2,1)} %collective-permute-done.5.refs_2_, bf16[512,768]{1,0:T(8,128)(2,1)} %collective-permute-done.13.refs_3_, ...), custom_call_target="tpu_custom_call" | custom-call | flops 1811939328 | bytes 9093120 | tf_op jit(solution)/shard_map/mine_1/pallas_call | solution.py:128
  208.4 4.3 %mine_0.1 = f32[288,768]{1,0:T(8,128)S(1)} custom-call(bf16[8,288,512]{2,1,0:T(8,128)(2,1)S(1)} %scale_mine.1.s_ref, bf16[512,2304]{1,0:T(8,128)(2,1)S(1)} %bitcast.46, bf16[512,2304]{1,0:T(8,128)(2,1)} %collective-permute-done.8.refs_1_, bf16[512,768]{1,0:T(8,128)(2,1)S(1)} %copy-done.7, bf16[512,768]{1,0:T(8,128)(2,1)} %collective-permute-done.9.refs_3_, ...), custom_call_target="tpu_custom_call" | custom-call | flops 1811939328 | bytes 9093120 | tf_op jit(solution)/shard_map/mine_0/pallas_call | solution.py:128
  213.3 1.7 pad_maximum_fusion
  (111 shorter events, 6.7 us)
Async XLA Ops:
  6.5 3.3 %copy-start.21 = (bf16[2,256,288]{1,2,0:T(8,128)(2,1)S(1)}, bf16[2,256,288]{1,2,0:T(8,128)(2,1)}, u32[]{:S(2)}) copy-start(bf16[2,256,288]{1,2,0:T(8,128)(2,1)} %param.6) | copy-start | bytes 884740
  10.3 52.2 %copy-start = (bf16[2,256,2304]{2,1,0:T(8,128)(2,1)S(1)}, bf16[2,256,2304]{2,1,0:T(8,128)(2,1)}, u32[]{:S(2)}) copy-start(bf16[2,256,2304]{2,1,0:T(8,128)(2,1)} %param.5) | copy-start | bytes 7077892
  11.1 28.4 %all-to-all-start = ((bf16[16,2,3,2,8,128]{5,4,3,2,1,0:T(8,128)(2,1)}), bf16[16,2,3,2,8,128]{5,4,3,2,1,0:T(8,128)(2,1)S(1)}, u32[]{:S(2)}, u32[]{:S(2)}) async-start(bf16[16,2,3,2,8,128]{5,4,3,2,1,0:T(8,128)(2,1)} %copy_bitcast_fusion), calls=%async_computation | async-start | bytes 786432 | tf_op jit(solution)/shard_map/all_to_all | solution.py:177
  20.7 116.6 %all-gather.5.cloned.1.call-start = ((), (), s32[]{:S(2)}) async-start(), calls=%async_computation.3 | async-start | bytes 2654208 | tf_op jit(solution)/shard_map/all_gather | solution.py:183
  20.7 34.5 %collective-permute-start.1 = (bf16[288,512]{1,0:T(8,128)(2,1)S(1)}, bf16[288,512]{1,0:T(8,128)(2,1)S(1)}, u32[]{:S(2)}, u32[]{:S(2)}) collective-permute-start(bf16[288,512]{1,0:T(8,128)(2,1)S(1)} %bitcast.50), channel_id=1, source_target_pairs={{0,12},{1,30},{2,6},{3,16},{4,74},{5,88},{6,68},{7,82},{8,128},{9,... | collective-permute-start | bytes 884744 | tf_op jit(solution)/shard_map/ppermute | solution.py:71
  24.2 36.4 %collective-permute-start = (bf16[288,512]{1,0:T(8,128)(2,1)S(1)}, bf16[288,512]{1,0:T(8,128)(2,1)}, u32[]{:S(2)}, u32[]{:S(2)}) collective-permute-start(bf16[288,512]{1,0:T(8,128)(2,1)S(1)} %bitcast.51), channel_id=1, source_target_pairs={{0,4},{1,22},{2,14},{3,24},{4,66},{5,80},{6,76},{7,90},{8,136},{9,... | collective-permute-start | bytes 884744 | tf_op jit(solution)/shard_map/ppermute | solution.py:71
  39.6 31.5 %copy-start.26 = (f32[2,8]{1,0:T(2,128)S(1)}, f32[2,8]{1,0:T(2,128)}, u32[]{:S(2)}) copy-start(f32[2,8]{1,0:T(2,128)} %param.7) | copy-start | bytes 196
  39.6 31.6 %copy-start.27 = (f32[3]{0:T(128)S(1)}, f32[3]{0:T(128)}, u32[]{:S(2)}) copy-start(f32[3]{0:T(128)} %constant.91.clone) | copy-start | bytes 40
  63.4 23.6 %collective-permute-start.4 = (bf16[512,768]{1,0:T(8,128)(2,1)}, bf16[512,768]{1,0:T(8,128)(2,1)S(1)}, u32[]{:S(2)}, u32[]{:S(2)}) collective-permute-start(bf16[512,768]{1,0:T(8,128)(2,1)} %slice.92), channel_id=1, source_target_pairs={{0,192},{1,193},{2,194},{3,195},{4,196},{5,197},{6,198},{7,199},{8... | collective-permute-start | bytes 2359304 | tf_op jit(solution)/shard_map/ppermute | solution.py:71
  63.4 23.6 %collective-permute-start.2 = (bf16[512,768]{1,0:T(8,128)(2,1)}, bf16[512,768]{1,0:T(8,128)(2,1)}, u32[]{:S(2)}, u32[]{:S(2)}) collective-permute-start(bf16[512,768]{1,0:T(8,128)(2,1)} %slice.92), channel_id=1, source_target_pairs={{0,64},{1,65},{2,66},{3,67},{4,68},{5,69},{6,70},{7,71},{8,72},{9,... | collective-permute-start | bytes 2359304 | tf_op jit(solution)/shard_map/ppermute | solution.py:71
  66.3 31.7 %collective-permute-start.5 = (bf16[512,768]{1,0:T(8,128)(2,1)}, bf16[512,768]{1,0:T(8,128)(2,1)}, u32[]{:S(2)}, u32[]{:S(2)}) collective-permute-start(bf16[512,768]{1,0:T(8,128)(2,1)} %slice.93), channel_id=1, source_target_pairs={{0,192},{1,193},{2,194},{3,195},{4,196},{5,197},{6,198},{7,199},{8... | collective-permute-start | bytes 2359304 | tf_op jit(solution)/shard_map/ppermute | solution.py:71
  67.5 34.2 %collective-permute-start.3 = (bf16[512,768]{1,0:T(8,128)(2,1)}, bf16[512,768]{1,0:T(8,128)(2,1)}, u32[]{:S(2)}, u32[]{:S(2)}) collective-permute-start(bf16[512,768]{1,0:T(8,128)(2,1)} %slice.93), channel_id=1, source_target_pairs={{0,64},{1,65},{2,66},{3,67},{4,68},{5,69},{6,70},{7,71},{8,72},{9,... | collective-permute-start | bytes 2359304 | tf_op jit(solution)/shard_map/ppermute | solution.py:71
  68.4 71.6 %collective-permute-start.8 = (bf16[512,2304]{1,0:T(8,128)(2,1)S(1)}, bf16[512,2304]{1,0:T(8,128)(2,1)}, u32[]{:S(2)}, u32[]{:S(2)}) collective-permute-start(bf16[512,2304]{1,0:T(8,128)(2,1)S(1)} %bitcast.39), channel_id=1, source_target_pairs={{0,16},{1,17},{2,18},{3,19},{4,20},{5,21},{6,22},{7,23},{8,24},{9,... | collective-permute-start | bytes 7077896 | tf_op jit(solution)/shard_map/ppermute | solution.py:71
  72.0 14.9 %all-to-all-start.1 = ((f32[16,1,2]{2,1,0:T(1,128)}), f32[16,1,2]{2,1,0:T(1,128)S(1)}, u32[]{:S(2)}, u32[]{:S(2)}) async-start(f32[16,1,2]{2,1,0:T(1,128)} %broadcast_in_dim.13), calls=%async_computation.1 | async-start | bytes 16384 | tf_op jit(solution)/shard_map/all_to_all | solution.py:196
  79.7 108.3 %all-gather.7.cloned.1.call-start = ((), (), s32[]{:S(2)}) async-start(), calls=%async_computation.4 | async-start | bytes 2654208 | tf_op jit(solution)/shard_map/all_gather | solution.py:183
  87.0 17.9 %copy-start.5 = (bf16[512,768]{1,0:T(8,128)(2,1)}, bf16[512,768]{1,0:T(8,128)(2,1)S(1)}, u32[]{:S(2)}) copy-start(bf16[512,768]{1,0:T(8,128)(2,1)S(1)} %collective-permute-done.4.refs_2_) | copy-start | bytes 2359300
  104.9 19.8 %collective-permute-start.7 = (bf16[256,1536]{1,0:T(8,128)(2,1)S(1)}, bf16[256,1536]{1,0:T(8,128)(2,1)S(1)}, u32[]{:S(2)}, u32[]{:S(2)}) collective-permute-start(bf16[256,1536]{1,0:T(8,128)(2,1)S(1)} %pad_maximum_fusion.2), channel_id=1, source_target_pairs={{0,192},{1,193},{2,194},{3,195},{4,196},{5,197},{6,198},{7,199},{8... | collective-permute-start | bytes 2359304 | tf_op jit(solution)/shard_map/ppermute | solution.py:71
  105.1 21.1 %collective-permute-start.6 = (bf16[256,1536]{1,0:T(8,128)(2,1)S(1)}, bf16[256,1536]{1,0:T(8,128)(2,1)}, u32[]{:S(2)}, u32[]{:S(2)}) collective-permute-start(bf16[256,1536]{1,0:T(8,128)(2,1)S(1)} %pad_maximum_fusion.1), channel_id=1, source_target_pairs={{0,64},{1,65},{2,66},{3,67},{4,68},{5,69},{6,70},{7,71},{8,72},{9,... | collective-permute-start | bytes 2359304 | tf_op jit(solution)/shard_map/ppermute | solution.py:71
  107.1 28.6 %collective-permute-start.14 = (bf16[512,768]{1,0:T(8,128)(2,1)}, bf16[512,768]{1,0:T(8,128)(2,1)}, u32[]{:S(2)}, u32[]{:S(2)}) collective-permute-start(bf16[512,768]{1,0:T(8,128)(2,1)} %collective-permute-done.3.refs_8_), channel_id=1, source_target_pairs={{0,16},{1,17},{2,18},{3,19},{4,20},{5,21},{6,22},{7,23},{8,24},{9,... | collective-permute-start | bytes 2359304 | tf_op jit(solution)/shard_map/ppermute | solution.py:71
  107.2 28.7 %collective-permute-start.13 = (bf16[512,768]{1,0:T(8,128)(2,1)}, bf16[512,768]{1,0:T(8,128)(2,1)}, u32[]{:S(2)}, u32[]{:S(2)}) collective-permute-start(bf16[512,768]{1,0:T(8,128)(2,1)} %collective-permute-done.5.refs_2_), channel_id=1, source_target_pairs={{0,16},{1,17},{2,18},{3,19},{4,20},{5,21},{6,22},{7,23},{8,24},{9,... | collective-permute-start | bytes 2359304 | tf_op jit(solution)/shard_map/ppermute | solution.py:71
  135.2 6.1 %collective-permute-start.10 = (bf16[256,1536]{1,0:T(8,128)(2,1)}, bf16[256,1536]{1,0:T(8,128)(2,1)}, u32[]{:S(2)}, u32[]{:S(2)}) collective-permute-start(bf16[256,1536]{1,0:T(8,128)(2,1)} %collective-permute-done.6.refs_4_), channel_id=1, source_target_pairs={{0,16},{1,17},{2,18},{3,19},{4,20},{5,21},{6,22},{7,23},{8,24},{9,... | collective-permute-start | bytes 2359304 | tf_op jit(solution)/shard_map/ppermute | solution.py:71
  135.2 6.9 %collective-permute-start.11 = (bf16[256,1536]{1,0:T(8,128)(2,1)S(1)}, bf16[256,1536]{1,0:T(8,128)(2,1)}, u32[]{:S(2)}, u32[]{:S(2)}) collective-permute-start(bf16[256,1536]{1,0:T(8,128)(2,1)S(1)} %collective-permute-done.7.refs_5_), channel_id=1, source_target_pairs={{0,16},{1,17},{2,18},{3,19},{4,20},{5,21},{6,22},{7,23},{8,24},{9,... | collective-permute-start | bytes 2359304 | tf_op jit(solution)/shard_map/ppermute | solution.py:71
  135.7 10.9 %collective-permute-start.12 = (bf16[512,768]{1,0:T(8,128)(2,1)}, bf16[512,768]{1,0:T(8,128)(2,1)}, u32[]{:S(2)}, u32[]{:S(2)}) collective-permute-start(bf16[512,768]{1,0:T(8,128)(2,1)} %collective-permute-done.2.refs_8_), channel_id=1, source_target_pairs={{0,16},{1,17},{2,18},{3,19},{4,20},{5,21},{6,22},{7,23},{8,24},{9,... | collective-permute-start | bytes 2359304 | tf_op jit(solution)/shard_map/ppermute | solution.py:71
  135.8 10.8 %collective-permute-start.9 = (bf16[512,768]{1,0:T(8,128)(2,1)}, bf16[512,768]{1,0:T(8,128)(2,1)}, u32[]{:S(2)}, u32[]{:S(2)}) collective-permute-start(bf16[512,768]{1,0:T(8,128)(2,1)} %copy-done.5), channel_id=1, source_target_pairs={{0,16},{1,17},{2,18},{3,19},{4,20},{5,21},{6,22},{7,23},{8,24},{9,... | collective-permute-start | bytes 2359304 | tf_op jit(solution)/shard_map/ppermute | solution.py:71
  137.3 1.7 copy-start.13
  138.9 1.1 copy-start.25
  140.0 6.7 %copy-start.6 = (bf16[512,768]{1,0:T(8,128)(2,1)S(1)}, bf16[512,768]{1,0:T(8,128)(2,1)}, u32[]{:S(2)}) copy-start(bf16[512,768]{1,0:T(8,128)(2,1)} %copy-done.5) | copy-start | bytes 2359300
  140.1 19.6 %collective-permute-start.18 = (bf16[512,768]{1,0:T(8,128)(2,1)S(1)}, bf16[512,768]{1,0:T(8,128)(2,1)S(1)}, u32[]{:S(2)}, u32[]{:S(2)}) collective-permute-start(bf16[512,768]{1,0:T(8,128)(2,1)S(1)} %copy-done.25), channel_id=1, source_target_pairs={{0,192},{1,193},{2,194},{3,195},{4,196},{5,197},{6,198},{7,199},{8... | collective-permute-start | bytes 2359304 | tf_op jit(solution)/shard_map/ppermute | solution.py:71
  141.3 20.5 %collective-permute-start.17 = (bf16[512,768]{1,0:T(8,128)(2,1)S(1)}, bf16[512,768]{1,0:T(8,128)(2,1)S(1)}, u32[]{:S(2)}, u32[]{:S(2)}) collective-permute-start(bf16[512,768]{1,0:T(8,128)(2,1)S(1)} %copy-done.25), channel_id=1, source_target_pairs={{0,64},{1,65},{2,66},{3,67},{4,68},{5,69},{6,70},{7,71},{8,72},{9,... | collective-permute-start | bytes 2359304 | tf_op jit(solution)/shard_map/ppermute | solution.py:71
  150.9 11.7 %collective-permute-start.16 = (bf16[144,1536]{1,0:T(8,128)(2,1)S(1)}, bf16[144,1536]{1,0:T(8,128)(2,1)S(1)}, u32[]{:S(2)}, u32[]{:S(2)}) collective-permute-start(bf16[144,1536]{1,0:T(8,128)(2,1)S(1)} %get-tuple-element.66), channel_id=1, source_target_pairs={{0,40},{1,41},{2,42},{3,43},{4,44},{5,45},{6,46},{7,47},{8,0},{9,1... | collective-permute-start | bytes 1327112 | tf_op jit(solution)/shard_map/ppermute | solution.py:71
  153.2 12.5 %collective-permute-start.15 = (bf16[144,1536]{1,0:T(8,128)(2,1)S(1)}, bf16[144,1536]{1,0:T(8,128)(2,1)S(1)}, u32[]{:S(2)}, u32[]{:S(2)}) collective-permute-start(bf16[144,1536]{1,0:T(8,128)(2,1)S(1)} %get-tuple-element.67), channel_id=1, source_target_pairs={{0,8},{1,9},{2,10},{3,11},{4,12},{5,13},{6,14},{7,15},{8,32},{9,33... | collective-permute-start | bytes 1327112 | tf_op jit(solution)/shard_map/ppermute | solution.py:71
  159.6 21.2 %copy-start.1 = (bf16[512,768]{1,0:T(8,128)(2,1)}, bf16[512,768]{1,0:T(8,128)(2,1)S(1)}, u32[]{:S(2)}) copy-start(bf16[512,768]{1,0:T(8,128)(2,1)S(1)} %collective-permute-done.18.refs_2_) | copy-start | bytes 2359300
  161.8 19.0 %copy-start.3 = (bf16[512,768]{1,0:T(8,128)(2,1)}, bf16[512,768]{1,0:T(8,128)(2,1)S(1)}, u32[]{:S(2)}) copy-start(bf16[512,768]{1,0:T(8,128)(2,1)S(1)} %collective-permute-done.17.refs_8_) | copy-start | bytes 2359300
  165.8 10.6 %collective-permute-start.22 = (bf16[256,768]{1,0:T(8,128)(2,1)S(1)}, bf16[256,768]{1,0:T(8,128)(2,1)S(1)}, u32[]{:S(2)}, u32[]{:S(2)}) collective-permute-start(bf16[256,768]{1,0:T(8,128)(2,1)S(1)} %slice.101), channel_id=1, source_target_pairs={{0,64},{1,65},{2,66},{3,67},{4,68},{5,69},{6,70},{7,71},{8,72},{9,... | collective-permute-start | bytes 1179656 | tf_op jit(solution)/shard_map/ppermute | solution.py:71
  166.4 12.0 %collective-permute-start.20 = (bf16[144,1536]{1,0:T(8,128)(2,1)S(1)}, bf16[144,1536]{1,0:T(8,128)(2,1)S(1)}, u32[]{:S(2)}, u32[]{:S(2)}) collective-permute-start(bf16[144,1536]{1,0:T(8,128)(2,1)S(1)} %collective-permute-done.15), channel_id=1, source_target_pairs={{0,8},{1,9},{2,10},{3,11},{4,12},{5,13},{6,14},{7,15},{8,32},{9,33... | collective-permute-start | bytes 1327112 | tf_op jit(solution)/shard_map/ppermute | solution.py:71
  166.4 12.0 %collective-permute-start.21 = (bf16[144,1536]{1,0:T(8,128)(2,1)S(1)}, bf16[144,1536]{1,0:T(8,128)(2,1)}, u32[]{:S(2)}, u32[]{:S(2)}) collective-permute-start(bf16[144,1536]{1,0:T(8,128)(2,1)S(1)} %collective-permute-done.16), channel_id=1, source_target_pairs={{0,40},{1,41},{2,42},{3,43},{4,44},{5,45},{6,46},{7,47},{8,0},{9,1... | collective-permute-start | bytes 1327112 | tf_op jit(solution)/shard_map/ppermute | solution.py:71
  169.7 8.7 %collective-permute-start.23 = (bf16[256,768]{1,0:T(8,128)(2,1)S(1)}, bf16[256,768]{1,0:T(8,128)(2,1)S(1)}, u32[]{:S(2)}, u32[]{:S(2)}) collective-permute-start(bf16[256,768]{1,0:T(8,128)(2,1)S(1)} %slice.102), channel_id=1, source_target_pairs={{0,192},{1,193},{2,194},{3,195},{4,196},{5,197},{6,198},{7,199},{8... | collective-permute-start | bytes 1179656 | tf_op jit(solution)/shard_map/ppermute | solution.py:71
  172.4 7.4 %collective-permute-start.19 = (bf16[512,768]{1,0:T(8,128)(2,1)S(1)}, bf16[512,768]{1,0:T(8,128)(2,1)S(1)}, u32[]{:S(2)}, u32[]{:S(2)}) collective-permute-start(bf16[512,768]{1,0:T(8,128)(2,1)S(1)} %collective-permute-done.18.refs_2_), channel_id=1, source_target_pairs={{0,16},{1,17},{2,18},{3,19},{4,20},{5,21},{6,22},{7,23},{8,24},{9,... | collective-permute-start | bytes 2359304 | tf_op jit(solution)/shard_map/ppermute | solution.py:71
  176.4 3.4 %collective-permute-start.26 = (bf16[512,768]{1,0:T(8,128)(2,1)S(1)}, bf16[512,768]{1,0:T(8,128)(2,1)S(1)}, u32[]{:S(2)}, u32[]{:S(2)}) collective-permute-start(bf16[512,768]{1,0:T(8,128)(2,1)S(1)} %collective-permute-done.17.refs_8_), channel_id=1, source_target_pairs={{0,16},{1,17},{2,18},{3,19},{4,20},{5,21},{6,22},{7,23},{8,24},{9,... | collective-permute-start | bytes 2359304 | tf_op jit(solution)/shard_map/ppermute | solution.py:71
  178.4 2.4 %copy-start.15 = (bf16[256,768]{1,0:T(8,128)(2,1)}, bf16[256,768]{1,0:T(8,128)(2,1)S(1)}, u32[]{:S(2)}) copy-start(bf16[256,768]{1,0:T(8,128)(2,1)S(1)} %collective-permute-done.23.refs_5_) | copy-start | bytes 1179652
  178.4 1.8 collective-permute-start.24
  178.5 2.3 %collective-permute-start.25 = (bf16[256,768]{1,0:T(8,128)(2,1)S(1)}, bf16[256,768]{1,0:T(8,128)(2,1)S(1)}, u32[]{:S(2)}, u32[]{:S(2)}) collective-permute-start(bf16[256,768]{1,0:T(8,128)(2,1)S(1)} %collective-permute-done.23.refs_5_), channel_id=1, source_target_pairs={{0,16},{1,17},{2,18},{3,19},{4,20},{5,21},{6,22},{7,23},{8,24},{9,... | collective-permute-start | bytes 1179656 | tf_op jit(solution)/shard_map/ppermute | solution.py:71
  184.0 0.9 copy-start.8
  184.9 0.9 copy-start.10
  185.8 0.8 copy-start.14
  186.5 0.8 copy-start.17
  187.3 0.8 copy-start.19
  189.1 11.4 %collective-permute-start.27 = (bf16[144,768]{1,0:T(8,128)(2,1)S(1)}, bf16[144,768]{1,0:T(8,128)(2,1)S(1)}, u32[]{:S(2)}, u32[]{:S(2)}) collective-permute-start(bf16[144,768]{1,0:T(8,128)(2,1)S(1)} %get-tuple-element.74), channel_id=1, source_target_pairs={{0,8},{1,9},{2,10},{3,11},{4,12},{5,13},{6,14},{7,15},{8,32},{9,33... | collective-permute-start | bytes 663560 | tf_op jit(solution)/shard_map/ppermute | solution.py:71
  189.2 11.4 %collective-permute-start.29 = (bf16[144,768]{1,0:T(8,128)(2,1)S(1)}, bf16[144,768]{1,0:T(8,128)(2,1)S(1)}, u32[]{:S(2)}, u32[]{:S(2)}) collective-permute-start(bf16[144,768]{1,0:T(8,128)(2,1)S(1)} %get-tuple-element.75), channel_id=1, source_target_pairs={{0,40},{1,41},{2,42},{3,43},{4,44},{5,45},{6,46},{7,47},{8,0},{9,1... | collective-permute-start | bytes 663560 | tf_op jit(solution)/shard_map/ppermute | solution.py:71
  193.5 1.7 copy-start.12
  195.2 1.1 copy-start.2
  195.2 1.4 copy-start.4
  195.2 1.6 copy-start.9
  195.2 1.8 copy-start.11
  195.2 1.9 copy-start.16
  195.2 2.0 copy-start.18
  195.2 2.1 copy-start.20
  200.5 7.8 %copy-start.7 = (bf16[512,768]{1,0:T(8,128)(2,1)S(1)}, bf16[512,768]{1,0:T(8,128)(2,1)}, u32[]{:S(2)}) copy-start(bf16[512,768]{1,0:T(8,128)(2,1)} %copy-done.5) | copy-start | bytes 2359300
  200.5 12.2 %collective-permute-start.28 = (bf16[144,768]{1,0:T(8,128)(2,1)S(1)}, bf16[144,768]{1,0:T(8,128)(2,1)S(1)}, u32[]{:S(2)}, u32[]{:S(2)}) collective-permute-start(bf16[144,768]{1,0:T(8,128)(2,1)S(1)} %collective-permute-done.27), channel_id=1, source_target_pairs={{0,8},{1,9},{2,10},{3,11},{4,12},{5,13},{6,14},{7,15},{8,32},{9,33... | collective-permute-start | bytes 663560 | tf_op jit(solution)/shard_map/ppermute | solution.py:71
  200.6 12.1 %collective-permute-start.30 = (bf16[144,768]{1,0:T(8,128)(2,1)S(1)}, bf16[144,768]{1,0:T(8,128)(2,1)S(1)}, u32[]{:S(2)}, u32[]{:S(2)}) collective-permute-start(bf16[144,768]{1,0:T(8,128)(2,1)S(1)} %collective-permute-done.29), channel_id=1, source_target_pairs={{0,40},{1,41},{2,42},{3,43},{4,44},{5,45},{6,46},{7,47},{8,0},{9,1... | collective-permute-start | bytes 663560 | tf_op jit(solution)/shard_map/ppermute | solution.py:71
  208.3 4.4 %copy-start.22 = (f32[288,2304]{1,0:T(8,128)S(1)}, f32[288,2304]{1,0:T(8,128)}, u32[]{:S(2)}) copy-start(f32[288,2304]{1,0:T(8,128)} %param.8) | copy-start | bytes 7962628
  208.3 4.4 %copy-start.23 = (bf16[144,768]{1,0:T(8,128)(2,1)S(1)}, bf16[144,768]{1,0:T(8,128)(2,1)}, u32[]{:S(2)}) copy-start(bf16[144,768]{1,0:T(8,128)(2,1)} %get-tuple-element.70) | copy-start | bytes 663556
  208.4 4.4 %copy-start.24 = (bf16[144,768]{1,0:T(8,128)(2,1)S(1)}, bf16[144,768]{1,0:T(8,128)(2,1)}, u32[]{:S(2)}) copy-start(bf16[144,768]{1,0:T(8,128)(2,1)} %get-tuple-element.71) | copy-start | bytes 663556
Sparse Core Ops, SparseCore 0:
  62.5 42.8 all-gather.4
  107.2 40.0 all-gather.6

commit v3 on v2

--- a/solution.py
+++ b/solution.py
@@ -1,4 +1,3 @@
-import functools
 import math
 
 import jax
@@ -11,11 +10,6 @@
 clip_norm = 2.5
 AXES = ("dp", "tensor")
 NY, NX, NZ = 4, 4, 8
-STEP_Z = ((4, -3), (-1, 2), (0, 1), (-2, 3))
-MEMBER = [0] * NZ
-for away in range(NY):
-    for other in range(2):
-        MEMBER[STEP_Z[away][other] % NZ] = 2 * away + other
 BF = jnp.bfloat16
 F32 = jnp.float32
 
@@ -56,10 +50,11 @@
 def spread(turn):
     def move(y, xh, c, xl, z):
         row_y, row_x, row_c = 2 * xl + z // 4, (z // 2) % 2, z % 2
-        step = STEP_Z[(y - row_y) % NY][c ^ row_c]
+        step = 2 * ((y - row_y) % NY) + (c ^ row_c) - 2 * row_x
         return row_y, xh, row_c, xl ^ row_x ^ turn, z + step
 
-    return perm_of(move)
+    inside = perm_of(lambda *at: at[:1] + move(*at)[1:])
+    return inside, [(mid, end) for (_, mid), (_, end) in zip(inside, perm_of(move))]
 
 
 CORE = perm_of(lambda y, xh, c, xl, z: (y, xh, 1 - c, xl, z))
@@ -71,14 +66,12 @@
     return lax.ppermute(value, AXES, perm)
 
 
-def scale_kernel(theirs, id_ref, clip_ref, ring_ref, out_ref):
+def scale_kernel(id_ref, clip_ref, ring_ref, out_ref):
     dp = id_ref[0]
-    y, xh, c = dp // 4, (dp // 2) % 2, dp % 2
-    row_x = 1 - xh if theirs else xh
-    source = 4 * (y % 2) + 2 * row_x + c
+    y, c = dp // 4, dp % 2
     half = out_ref.shape[2] // 2
     for z in range(NZ):
-        m = id_ref[1 + (z - source + NZ) % NZ]
+        m = (z - 4 * (y % 2) - c + NZ) % NZ
         member = 2 * ((y + m // 2) % NY) + (c + m) % 2
         for e in range(2):
             cols = slice(e * half, (e + 1) * half)
@@ -87,12 +80,12 @@
             ).astype(BF)
 
 
-def scale_grads(theirs, ids, clips, ring):
+def scale_grads(name, ids, clips, ring):
     _, rows, tokens = ring.shape
     smem = pl.BlockSpec(memory_space=pltpu.SMEM)
     vmem = pl.BlockSpec(memory_space=pltpu.VMEM)
     return pl.pallas_call(
-        functools.partial(scale_kernel, theirs),
+        scale_kernel,
         out_shape=jax.ShapeDtypeStruct(ring.shape, BF),
         in_specs=[smem, smem, vmem],
         out_specs=vmem,
@@ -100,7 +93,7 @@
             flops=8 * rows * tokens, bytes_accessed=32 * rows * tokens, transcendentals=0
         ),
         compiler_params=pltpu.CompilerParams(vmem_limit_bytes=24 * 1024 * 1024),
-        name="scale_theirs" if theirs else "scale_mine",
+        name=name,
     )(ids, clips, ring)
 
 
@@ -144,17 +137,18 @@
 
 def shards(acts, out_grads, other_sq, noise):
     dp, te = lax.axis_index("dp"), lax.axis_index("tensor")
-    y, xh, xl = dp // 4, (dp // 2) % 2, te // NZ
+    y, xh, xl, z = dp // 4, (dp // 2) % 2, te // NZ, te % NZ
     examples, seq, columns = acts.shape
     tokens = examples * seq
     features = out_grads.shape[2]
     rows = features // 2
     tile = columns // 3
     stage = lax.optimization_barrier
-    ids = jnp.stack([dp] + [jnp.int32(m) for m in MEMBER]).astype(jnp.int32)
+    ids = dp.reshape(1).astype(jnp.int32)
 
     grads_t = out_grads.reshape(tokens, features).T
-    sources = [send(grads_t, spread(0)), send(grads_t, spread(1))]
+    routes = [spread(0), spread(1)]
+    sources = [send(grads_t, inside) for inside, _ in routes]
 
     def blocks(x):
         gram = jnp.einsum("btf,bsf->bts", x, x, preferred_element_type=F32).astype(BF)
@@ -165,17 +159,22 @@
     flat = acts.reshape(tokens, columns)
     grams, flat = stage((grams, flat))
 
-    def near(k):
-        part = flat[:, k * tile : (k + 1) * tile]
+    def near(part):
         return send(part, along_y(1)), send(part, along_y(-1))
 
-    below, above = near(0)
-    below, above = [below], [above]
+    def halved(grams, bit, perm):
+        low, high = jnp.split(grams, 2, axis=3)
+        keep, give = jnp.where(bit == 0, low, high), jnp.where(bit == 0, high, low)
+        return (keep.astype(F32) + send(give, perm).astype(F32)).astype(BF)
+
+    below0, above0 = near(flat[:, :tile])
     sibling = send(flat, CORE)
-    shape = grams.shape
-    grams = jnp.moveaxis(grams.reshape(shape[:3] + (2 * NZ, -1, shape[4])), 3, 0)
-    grams = lax.all_to_all(grams, "tensor", 0, 0, tiled=True).astype(F32).sum(axis=0)
-    sources[0], sources[1], grams, flat = stage((sources[0], sources[1], grams, flat))
+    grams = halved(grams, xl, XLO)
+    sources, grams, below0, above0 = stage((sources, grams, below0, above0))
+    sources = [send(block, steps) for block, (_, steps) in zip(sources, routes)]
+    grams = halved(grams, z % 2, flip_z(1))
+    sources, grams, flat = stage((sources, grams, flat))
+    below1, above1 = near(flat[:, tile:])
 
     turn = xl ^ (y // 2) ^ xh
     z_rings = [list(range(first, first + NZ)) for first in (0, NZ)]
@@ -189,19 +188,16 @@
         )
         for t in (1, 0)
     ]
-    for side, value in zip((below, above), near(1)):
-        side.append(value)
+    for bit, perm in (((z // 2) % 2, flip_z(2)), (z // 4, flip_z(4))):
+        grams = halved(grams, bit, perm)
+    grams = grams.astype(F32)
     weight = jnp.array([1.0, 2.0, 1.0], F32)[:, None, None, None]
     total = jnp.sum(grams[0] * grams[1] * weight, axis=(0, 2, 3)) + jnp.sum(other_sq, axis=1)
-    total = lax.all_to_all(
-        jnp.broadcast_to(total, (2 * NZ, examples)), "tensor", 0, 0, tiled=True
-    ).sum(axis=0)
+    for perm in (XLO, flip_z(1), flip_z(2), flip_z(4)):
+        total = total + send(total, perm)
     clip = jnp.minimum(1.0, clip_norm / jnp.sqrt(total))
-    clip, below, above = stage((clip, below, above))
-
-    far_below = send(jnp.concatenate([b[:seq] for b in below], axis=1), along_y(1))
-    far_above = send(jnp.concatenate([a[seq:] for a in above], axis=1), along_y(-1))
-    clip, far_below, far_above, flat = stage((clip, far_below, far_above, flat))
+
+    clip, below1, above1 = stage((clip, below1, above1))
     columns_y = [[4 * k + 2 * x + core for k in range(NY) for core in range(2)] for x in range(2)]
     clips = lax.all_to_all(
         jnp.broadcast_to(clip, (2 * NY, examples)),
@@ -211,38 +207,42 @@
         tiled=True,
         axis_index_groups=columns_y,
     ).reshape(-1)
-    clips, flat, far_below, far_above = stage((clips, flat, far_below, far_above))
-    for side, value in zip((below, above), near(2)):
-        side.append(value)
+    clips, below0, above0, below1, above1 = stage((clips, below0, above0, below1, above1))
+
+    def ahead(first, second):
+        return jnp.concatenate([first, second[:, :tile]], axis=1)
+
+    far = [
+        send(ahead(below0[:seq], below1[:seq]), along_y(1)),
+        send(ahead(above0[seq:], above1[seq:]), along_y(-1)),
+    ]
+    far2 = [send(below1[:seq, tile:], along_y(1)), send(above1[seq:, tile:], along_y(-1))]
 
     def swap(array):
         return send(array, CORE)
 
-    far_sibling = [swap(far_below), swap(far_above)]
-    near_sibling = [(swap(above[k]), swap(below[k])) for k in range(2)]
-
-    def held(k, far, far_other, first):
-        parts = [(flat, k * tile), (sibling, k * tile), (above[k], 0), (near_sibling[k][0], 0)]
-        parts += [(a, first) for a in far + far_other]
-        return parts + [(below[k], 0), (near_sibling[k][1], 0)]
-
-    scaled = scale_grads(True, ids, clips, theirs)
-    early = [held(k, [far_below, far_above], far_sibling, k * tile) for k in range(2)]
-    part = jnp.concatenate(
-        [product(f"theirs_{k}", scaled, early[k], tile, tile, BF) for k in range(2)], axis=1
-    )
+    near0 = [above0, swap(above0)], [below0, swap(below0)]
+    near1 = [above1, swap(above1)], [below1, swap(below1)]
+
+    def held(k, near, first, far, first_far):
+        parts = [(flat, k * tile), (sibling, k * tile)] + [(a, first) for a in near[0]]
+        parts += [(a, first_far) for a in far + [swap(a) for a in far]]
+        return parts + [(a, first) for a in near[1]]
+
+    scaled = scale_grads("scale_theirs", ids, clips, theirs)
+    early = [held(0, near0, 0, far, 0), held(1, near1, 0, far, tile)]
+    part = product("theirs_0", scaled, early[0], tile, tile, BF)
+    part, far2, scaled = stage((part, far2, scaled))
+    part = jnp.concatenate([part, product("theirs_1", scaled, early[1], tile, tile, BF)], axis=1)
     low, high = send(part[:rows], along_x(1)), send(part[rows:], along_x(-1))
-    low, high, below[2], above[2] = stage((low, high, below[2], above[2]))
+    low, high = stage((low, high))
     low, high = send(low, along_x(1)), send(high, along_x(-1))
-    far = [send(below[2][:seq], along_y(1)), send(above[2][seq:], along_y(-1))]
-    near_sibling.append((swap(above[2]), swap(below[2])))
-    low, high, far = stage((low, high, far))
-
-    late = held(2, far, [swap(a) for a in far], 0)
+
+    late = held(2, near1, tile, far2, 0)
     part = product("theirs_2", scaled, late, tile, tile, BF)
     part, mine = stage((part, mine))
     low2, high2 = send(part[:rows], along_x(1)), send(part[rows:], along_x(-1))
-    scaled = scale_grads(False, ids, clips, mine)
+    scaled = scale_grads("scale_mine", ids, clips, mine)
     own = [product(f"mine_{k}", scaled, early[k], tile, tile, F32) for k in range(2)]
     low2, high2 = send(low2, along_x(1)), send(high2, along_x(-1))
     own.append(product("mine_2", scaled, late, tile, tile, F32))

time: 224 us -> 228 us (1.018)
  waiting for transfers between devices: 93.8 us -> 56.9 us
  starting transfers between devices: 51.8 us -> 86.3 us
  other arithmetic: 5.39 us -> 9.04 us
    ppermute x31 -> x37, starting transfers between devices: 34.5 us -> 86.2 us  [send(): return lax.ppermute(value, AXES, perm)]
    all_to_all x2 -> x0, waiting for transfers between devices: 19.4 us -> none  [the longest x1 12.9 us: shards(): lax.all_to_all(grams, 'tensor', 0, 0, tiled=True).astype(F32).sum(axis=0)]
    all_to_all x2 -> x0, starting transfers between devices: 17.2 us -> none  [the longest x1 9.52 us: shards(): lax.all_to_all(grams, 'tensor', 0, 0, tiled=True).astype(F32).sum(axis=0)]
    ppermute x31 -> x37, waiting for transfers between devices: 73.7 us -> 56.9 us  [send(): return lax.ppermute(value, AXES, perm)]
    unnamed x56 -> x54, local copies, waits for them, and re-layouts: 8.67 us -> 10.2 us
    slice x9 -> x7, local copies, waits for them, and re-layouts: 5.95 us -> 7.11 us  [the longest x1 1.93 us: shards(): above1[seq:, tile:]]
  transfers between devices with their start and end apart: 35 -> 39, of which waited for: 16 -> 16; matrix products, arithmetic and copies ran while one was open for 5% -> 7% of each run, Pallas kernels for 12% -> 12%
where the time goes in v3:
time: 228 us; the launch traced here: 226 us
  starting transfers between devices  86.3 us (38%)
  waiting for transfers between devices  56.9 us (25%)
  Pallas kernels  26.7 us (12%)
  local copies, waits for them, and re-layouts  21.5 us (9%)
  between operations  13.9 us (6%)
  other arithmetic  9.04 us (4%)
  blocking collectives  8.01 us (4%)
  matrix products  3.58 us (2%)
    ppermute x37, starting transfers between devices, send(): return lax.ppermute(value, AXES, perm)  86.2 us
    ppermute x37, waiting for transfers between devices, send(): return lax.ppermute(value, AXES, perm)  56.9 us
    pallas_call x6, Pallas kernels, product(): pl.pallas_call(product_kernel, out_shape=jax.ShapeDtypeStruct((rows, widt...  24.7 us
    unnamed x54, local copies, waits for them, and re-layouts  10.2 us
    all_to_all x1, blocking collectives, shards(): lax.all_to_all(jnp.broadcast_to(clip, (2 * NY, examples)), 'dp', 0, 0, ti...  8.01 us
  transfers between devices with their start and end apart: 39, of which 16 were waited for; matrix products, arithmetic and copies ran while one was open for 7% of the time, Pallas kernels for 12%

profile of v3, /device:TPU:32, one launch (start us, length us, event | category | flops | bytes accessed | tf_op | source)
XLA Modules:
  0.0 226.0 jit_solution(18198510293817843139)
XLA Ops:
  6.5 3.2 %convolution_convert_fusion.1 = bf16[2,256,256]{2,1,0:T(8,128)(2,1)S(1)} fusion(bf16[2,256,2304]{2,1,0:T(8,128)(2,1)} %param.5), kind=kOutput, calls=%fused_computation.2 | convolution fusion | flops 604110848 | bytes 2621440 | tf_op jit(solution)/shard_map/btf,bsf->bts/dot_general | solution.py:154
  10.3 1.1 copy-done
  11.4 0.9 slice.91
  12.4 3.0 %collective-permute-start.4 = (bf16[512,768]{1,0:T(8,128)(2,1)}, bf16[512,768]{1,0:T(8,128)(2,1)S(1)}, u32[]{:S(2)}, u32[]{:S(2)}) collective-permute-start(bf16[512,768]{1,0:T(8,128)(2,1)} %slice.91), channel_id=1, source_target_pairs={{0,192},{1,193},{2,194},{3,195},{4,196},{5,197},{6,198},{7,199},{8... | collective-permute-start | bytes 2359304 | tf_op jit(solution)/shard_map/ppermute | solution.py:66
  15.4 0.7 broadcast_select_fusion.2
  16.1 1.5 collective-permute-start.2
  17.6 1.7 copy.8
  19.3 2.7 %collective-permute-start.1 = (bf16[288,512]{1,0:T(8,128)(2,1)}, bf16[288,512]{1,0:T(8,128)(2,1)}, u32[]{:S(2)}, u32[]{:S(2)}) collective-permute-start(bf16[288,512]{1,0:T(8,128)(2,1)} %bitcast.1), channel_id=1, source_target_pairs={{0,8},{1,26},{2,0},{3,18},{4,10},{5,28},{6,2},{7,20},{8,4},{9,22},... | collective-permute-start | bytes 884744 | tf_op jit(solution)/shard_map/ppermute | solution.py:66
  22.0 2.9 %collective-permute-start = (bf16[288,512]{1,0:T(8,128)(2,1)}, bf16[288,512]{1,0:T(8,128)(2,1)}, u32[]{:S(2)}, u32[]{:S(2)}) collective-permute-start(bf16[288,512]{1,0:T(8,128)(2,1)} %bitcast.1), channel_id=1, source_target_pairs={{0,0},{1,18},{2,8},{3,26},{4,2},{5,20},{6,10},{7,28},{8,12},{9,30}... | collective-permute-start | bytes 884744 | tf_op jit(solution)/shard_map/ppermute | solution.py:66
  24.9 1.0 add_convert_fusion
  25.9 7.9 %collective-permute-done.1 = bf16[288,512]{1,0:T(8,128)(2,1)} collective-permute-done((bf16[288,512]{1,0:T(8,128)(2,1)}, bf16[288,512]{1,0:T(8,128)(2,1)}, u32[]{:S(2)}, u32[]{:S(2)}) %collective-permute-start.1) | collective-permute-done | bytes 294944 | tf_op jit(solution)/shard_map/ppermute | solution.py:66
  34.0 1.9 collective-permute-done.3.refs_8_
  35.9 0.8 collective-permute-start.7
  36.7 1.6 collective-permute-start.5
  38.3 3.8 %collective-permute-start.6 = (bf16[288,512]{1,0:T(8,128)(2,1)}, bf16[288,512]{1,0:T(8,128)(2,1)}, u32[]{:S(2)}, u32[]{:S(2)}) collective-permute-start(bf16[288,512]{1,0:T(8,128)(2,1)} %collective-permute-done.1), channel_id=1, source_target_pairs={{8,8},{26,26},{0,0},{18,18},{10,74},{28,92},{2,66},{20,84},{4,132}... | collective-permute-start | bytes 884744 | tf_op jit(solution)/shard_map/ppermute | solution.py:66
  42.1 1.0 add_convert_fusion.1
  43.1 1.8 broadcast_select_fusion
  45.0 1.3 slice.94
  46.3 36.4 %collective-permute-start.15 = (bf16[512,1536]{1,0:T(8,128)(2,1)}, bf16[512,1536]{1,0:T(8,128)(2,1)}, u32[]{:S(2)}, u32[]{:S(2)}) collective-permute-start(bf16[512,1536]{1,0:T(8,128)(2,1)} %slice.94), channel_id=1, source_target_pairs={{0,192},{1,193},{2,194},{3,195},{4,196},{5,197},{6,198},{7,199},{8... | collective-permute-start | bytes 4718600 | tf_op jit(solution)/shard_map/ppermute | solution.py:66
  83.0 4.8 %collective-permute-done.8 = bf16[2,3,2,16,128]{4,3,2,1,0:T(8,128)(2,1)S(1)} collective-permute-done((bf16[2,3,2,16,128]{4,3,2,1,0:T(8,128)(2,1)S(1)}, bf16[2,3,2,16,128]{4,3,2,1,0:T(8,128)(2,1)S(1)}, u32[]{:S(2)}, u32[]{:S(2)}) %collective-permute-start.8) | collective-permute-done | bytes 49184 | tf_op jit(solution)/shard_map/ppermute | solution.py:66
  87.9 4.4 %collective-permute-start.9 = (bf16[2,3,2,8,128]{4,3,2,1,0:T(8,128)(2,1)S(1)}, bf16[2,3,2,8,128]{4,3,2,1,0:T(8,128)(2,1)S(1)}, u32[]{:S(2)}, u32[]{:S(2)}) collective-permute-start(bf16[2,3,2,8,128]{4,3,2,1,0:T(8,128)(2,1)S(1)} %broadcast_select_fusion.5), channel_id=1, source_target_pairs={{0,4},{1,5},{2,6},{3,7},{4,0},{5,1},{6,2},{7,3},{8,12},{9,13},{10,... | collective-permute-start | bytes 73736 | tf_op jit(solution)/shard_map/ppermute | solution.py:66
  92.4 3.6 %collective-permute-done.9 = bf16[2,3,2,8,128]{4,3,2,1,0:T(8,128)(2,1)S(1)} collective-permute-done((bf16[2,3,2,8,128]{4,3,2,1,0:T(8,128)(2,1)S(1)}, bf16[2,3,2,8,128]{4,3,2,1,0:T(8,128)(2,1)S(1)}, u32[]{:S(2)}, u32[]{:S(2)}) %collective-permute-start.9) | collective-permute-done | bytes 24608 | tf_op jit(solution)/shard_map/ppermute | solution.py:66
  96.5 3.4 %collective-permute-done.10 = f32[2]{0:T(128)S(1)} collective-permute-done((f32[2]{0:T(128)S(1)}, f32[2]{0:T(128)S(1)}, u32[]{:S(2)}, u32[]{:S(2)}) %collective-permute-start.10) | collective-permute-done | bytes 40 | tf_op jit(solution)/shard_map/ppermute | solution.py:66
  99.8 3.5 %collective-permute-done.11 = f32[2]{0:T(128)S(1)} collective-permute-done((f32[2]{0:T(128)S(1)}, f32[2]{0:T(128)S(1)}, u32[]{:S(2)}, u32[]{:S(2)}) %collective-permute-start.11) | collective-permute-done | bytes 40 | tf_op jit(solution)/shard_map/ppermute | solution.py:66
  103.4 2.0 collective-permute-start.12
  105.4 2.5 %collective-permute-done.12 = f32[2]{0:T(128)S(1)} collective-permute-done((f32[2]{0:T(128)S(1)}, f32[2]{0:T(128)S(1)}, u32[]{:S(2)}, u32[]{:S(2)}) %collective-permute-start.12) | collective-permute-done | bytes 40 | tf_op jit(solution)/shard_map/ppermute | solution.py:66
  107.8 4.7 %collective-permute-start.13 = (f32[2]{0:T(128)S(1)}, f32[2]{0:T(128)S(1)}, u32[]{:S(2)}, u32[]{:S(2)}) collective-permute-start(f32[2]{0:T(128)S(1)} %add.74), channel_id=1, source_target_pairs={{0,4},{1,5},{2,6},{3,7},{4,0},{5,1},{6,2},{7,3},{8,12},{9,13},{10,... | collective-permute-start | bytes 32 | tf_op jit(solution)/shard_map/ppermute | solution.py:66
  112.5 2.8 %collective-permute-done.13 = f32[2]{0:T(128)S(1)} collective-permute-done((f32[2]{0:T(128)S(1)}, f32[2]{0:T(128)S(1)}, u32[]{:S(2)}, u32[]{:S(2)}) %collective-permute-start.13) | collective-permute-done | bytes 40 | tf_op jit(solution)/shard_map/ppermute | solution.py:66
  115.3 1.7 collective-permute-done.14.refs_8_
  117.0 8.0 %all_to_all.6 = f32[8,1,2]{2,1,0:T(1,128)S(1)} all-to-all(f32[8,1,2]{2,1,0:T(1,128)S(1)} %broadcast_in_dim.10), channel_id=1, replica_groups={{0,16,64,80,128,144,192,208},{32,48,96,112,160,176,224,240},{1,17,65,81..., dimensions={0} | all-to-all | bytes 128 | tf_op jit(solution)/shard_map/all_to_all | solution.py:202
  126.3 1.1 slice.95
  127.3 1.9 fusion.5
  129.3 1.2 collective-permute-start.19
  130.6 1.9 fusion.6
  132.6 1.1 collective-permute-start.18
  134.2 14.5 %collective-permute-done.19.refs_5_ = bf16[256,1536]{1,0:T(8,128)(2,1)S(1)} collective-permute-done((bf16[256,1536]{1,0:T(8,128)(2,1)S(1)}, bf16[256,1536]{1,0:T(8,128)(2,1)S(1)}, u32[]{:S(2)}, u32[]{:S(2)}) %collective-permute-start.19) | collective-permute-done | bytes 786464 | tf_op jit(solution)/shard_map/ppermute | solution.py:66
  148.7 4.4 %collective-permute-done.18.refs_4_ = bf16[256,1536]{1,0:T(8,128)(2,1)} collective-permute-done((bf16[256,1536]{1,0:T(8,128)(2,1)S(1)}, bf16[256,1536]{1,0:T(8,128)(2,1)}, u32[]{:S(2)}, u32[]{:S(2)}) %collective-permute-start.18) | collective-permute-done | bytes 786464 | tf_op jit(solution)/shard_map/ppermute | solution.py:66
  153.1 0.9 copy-done.9
  154.5 0.9 copy-done.12
  155.4 0.9 copy-done.2
  156.3 3.2 %collective-permute-start.24 = (bf16[256,768]{1,0:T(8,128)(2,1)}, bf16[256,768]{1,0:T(8,128)(2,1)}, u32[]{:S(2)}, u32[]{:S(2)}) collective-permute-start(bf16[256,768]{1,0:T(8,128)(2,1)} %get-tuple-element.62), channel_id=1, source_target_pairs={{0,192},{1,193},{2,194},{3,195},{4,196},{5,197},{6,198},{7,199},{8... | collective-permute-start | bytes 1179656 | tf_op jit(solution)/shard_map/ppermute | solution.py:66
  159.5 1.7 copy-done.15
  161.2 1.0 scale_theirs.1.s_ref
  163.1 3.6 %theirs_0.1 = bf16[288,768]{1,0:T(8,128)(2,1)S(1)} custom-call(bf16[8,288,512]{2,1,0:T(8,128)(2,1)S(1)} %scale_theirs.1.s_ref, bf16[512,2304]{1,0:T(8,128)(2,1)S(1)} %bitcast.38, bf16[512,2304]{1,0:T(8,128)(2,1)} %collective-permute-done.16.refs_1_, bf16[512,768]{1,0:T(8,128)(2,1)S(1)} %copy-done.7, bf16[512,768]{1,0:T(8,128)(2,1)S(1)} %copy-done.10, ...), custom_call_target="tpu_custom_call" | custom-call | flops 1811939328 | bytes 9093120 | tf_op jit(solution)/shard_map/theirs_0/pallas_call | solution.py:121
  166.7 1.2 collective-permute-done.23.refs_4_
  168.6 4.3 %theirs_1.1 = bf16[288,768]{1,0:T(8,128)(2,1)S(1)} custom-call(bf16[8,288,512]{2,1,0:T(8,128)(2,1)S(1)} %scale_theirs.1.s_ref, bf16[512,2304]{1,0:T(8,128)(2,1)S(1)} %bitcast.39, bf16[512,2304]{1,0:T(8,128)(2,1)} %collective-permute-done.16.refs_1_, bf16[512,1536]{1,0:T(8,128)(2,1)} %collective-permute-done.15.refs_2_, ...), custom_call_target="tpu_custom_call" | custom-call | flops 1811939328 | bytes 9093120 | tf_op jit(solution)/shard_map/theirs_1/pallas_call | solution.py:121
  173.0 1.0 pad_maximum_fusion.3
  174.0 5.1 %collective-permute-start.30 = (bf16[144,1536]{1,0:T(8,128)(2,1)}, bf16[144,1536]{1,0:T(8,128)(2,1)}, u32[]{:S(2)}, u32[]{:S(2)}) collective-permute-start(bf16[144,1536]{1,0:T(8,128)(2,1)} %get-tuple-element.66), channel_id=1, source_target_pairs={{0,40},{1,41},{2,42},{3,43},{4,44},{5,45},{6,46},{7,47},{8,0},{9,1... | collective-permute-start | bytes 1327112 | tf_op jit(solution)/shard_map/ppermute | solution.py:66
  179.1 4.2 %theirs_2.1 = bf16[288,768]{1,0:T(8,128)(2,1)S(1)} custom-call(bf16[8,288,512]{2,1,0:T(8,128)(2,1)S(1)} %scale_theirs.1.s_ref, bf16[512,2304]{1,0:T(8,128)(2,1)S(1)} %bitcast.40, bf16[512,2304]{1,0:T(8,128)(2,1)} %collective-permute-done.16.refs_1_, bf16[512,1536]{1,0:T(8,128)(2,1)} %collective-permute-done.15.refs_2_, ...), custom_call_target="tpu_custom_call" | custom-call | flops 1811939328 | bytes 9093120 | tf_op jit(solution)/shard_map/theirs_2/pallas_call | solution.py:121
  183.3 0.8 copy-done.17
  184.0 0.8 copy-done.18
  184.8 0.8 copy-done.20
  185.5 1.8 fusion.9
  187.3 0.8 collective-permute-start.33
  188.1 2.6 %collective-permute-start.35 = (bf16[144,768]{1,0:T(8,128)(2,1)S(1)}, bf16[144,768]{1,0:T(8,128)(2,1)}, u32[]{:S(2)}, u32[]{:S(2)}) collective-permute-start(bf16[144,768]{1,0:T(8,128)(2,1)S(1)} %get-tuple-element.75), channel_id=1, source_target_pairs={{0,40},{1,41},{2,42},{3,43},{4,44},{5,45},{6,46},{7,47},{8,0},{9,1... | collective-permute-start | bytes 663560 | tf_op jit(solution)/shard_map/ppermute | solution.py:66
  190.6 1.7 copy-done.16
  192.3 1.0 scale_mine.1.s_ref
  193.5 3.6 %mine_0.1 = f32[288,768]{1,0:T(8,128)S(1)} custom-call(bf16[8,288,512]{2,1,0:T(8,128)(2,1)S(1)} %scale_mine.1.s_ref, bf16[512,2304]{1,0:T(8,128)(2,1)S(1)} %bitcast.41, bf16[512,2304]{1,0:T(8,128)(2,1)} %collective-permute-done.16.refs_1_, bf16[512,768]{1,0:T(8,128)(2,1)S(1)} %copy-done.8, bf16[512,768]{1,0:T(8,128)(2,1)S(1)} %copy-done.11, ...), custom_call_target="tpu_custom_call" | custom-call | flops 1811939328 | bytes 9093120 | tf_op jit(solution)/shard_map/mine_0/pallas_call | solution.py:121
  197.2 3.3 %collective-permute-start.32 = (bf16[144,1536]{1,0:T(8,128)(2,1)}, bf16[144,1536]{1,0:T(8,128)(2,1)S(1)}, u32[]{:S(2)}, u32[]{:S(2)}) collective-permute-start(bf16[144,1536]{1,0:T(8,128)(2,1)} %collective-permute-done.30), channel_id=1, source_target_pairs={{0,40},{1,41},{2,42},{3,43},{4,44},{5,45},{6,46},{7,47},{8,0},{9,1... | collective-permute-start | bytes 1327112 | tf_op jit(solution)/shard_map/ppermute | solution.py:66
  200.5 4.6 %mine_1.1 = f32[288,768]{1,0:T(8,128)S(1)} custom-call(bf16[8,288,512]{2,1,0:T(8,128)(2,1)S(1)} %scale_mine.1.s_ref, bf16[512,2304]{1,0:T(8,128)(2,1)} %bitcast.34, bf16[512,2304]{1,0:T(8,128)(2,1)} %collective-permute-done.16.refs_1_, bf16[512,1536]{1,0:T(8,128)(2,1)} %collective-permute-done.15.refs_2_, bf16[512,1536]{1,0:T(8,128)(2,1)} %collective-permute-done.25.refs_3_, ...), custom_call_target="tpu_custom_call" | custom-call | flops 1811939328 | bytes 9093120 | tf_op jit(solution)/shard_map/mine_1/pallas_call | solution.py:121
  205.1 4.3 %mine_2.1 = f32[288,768]{1,0:T(8,128)S(1)} custom-call(bf16[8,288,512]{2,1,0:T(8,128)(2,1)S(1)} %scale_mine.1.s_ref, bf16[512,2304]{1,0:T(8,128)(2,1)S(1)} %bitcast.42, bf16[512,2304]{1,0:T(8,128)(2,1)} %collective-permute-done.16.refs_1_, bf16[512,1536]{1,0:T(8,128)(2,1)} %collective-permute-done.15.refs_2_, ...), custom_call_target="tpu_custom_call" | custom-call | flops 1811939328 | bytes 9093120 | tf_op jit(solution)/shard_map/mine_2/pallas_call | solution.py:121
  209.6 3.2 %collective-permute-start.36 = (bf16[144,768]{1,0:T(8,128)(2,1)}, bf16[144,768]{1,0:T(8,128)(2,1)S(1)}, u32[]{:S(2)}, u32[]{:S(2)}) collective-permute-start(bf16[144,768]{1,0:T(8,128)(2,1)} %collective-permute-done.35), channel_id=1, source_target_pairs={{0,40},{1,41},{2,42},{3,43},{4,44},{5,45},{6,46},{7,47},{8,0},{9,1... | collective-permute-start | bytes 663560 | tf_op jit(solution)/shard_map/ppermute | solution.py:66
  212.9 4.0 %collective-permute-done.34 = bf16[144,768]{1,0:T(8,128)(2,1)S(1)} collective-permute-done((bf16[144,768]{1,0:T(8,128)(2,1)}, bf16[144,768]{1,0:T(8,128)(2,1)S(1)}, u32[]{:S(2)}, u32[]{:S(2)}) %collective-permute-start.34) | collective-permute-done | bytes 221216 | tf_op jit(solution)/shard_map/ppermute | solution.py:66
  217.5 1.7 pad_maximum_fusion
  (121 shorter events, 6.5 us)
Async XLA Ops:
  6.5 3.3 %copy-start.22 = (bf16[2,256,288]{1,2,0:T(8,128)(2,1)S(1)}, bf16[2,256,288]{1,2,0:T(8,128)(2,1)}, u32[]{:S(2)}) copy-start(bf16[2,256,288]{1,2,0:T(8,128)(2,1)} %param.6) | copy-start | bytes 884740
  6.5 153.0 %all-gather.5.cloned.1.call-start = ((), (), s32[]{:S(2)}) async-start(), calls=%async_computation.1 | async-start | bytes 2654208 | tf_op jit(solution)/shard_map/all_gather | solution.py:182
  9.8 1.7 copy-start
  12.4 21.6 %collective-permute-start.4 = (bf16[512,768]{1,0:T(8,128)(2,1)}, bf16[512,768]{1,0:T(8,128)(2,1)S(1)}, u32[]{:S(2)}, u32[]{:S(2)}) collective-permute-start(bf16[512,768]{1,0:T(8,128)(2,1)} %slice.91), channel_id=1, source_target_pairs={{0,192},{1,193},{2,194},{3,195},{4,196},{5,197},{6,198},{7,199},{8... | collective-permute-start | bytes 2359304 | tf_op jit(solution)/shard_map/ppermute | solution.py:66
  15.4 20.5 %collective-permute-start.3 = (bf16[512,768]{1,0:T(8,128)(2,1)}, bf16[512,768]{1,0:T(8,128)(2,1)}, u32[]{:S(2)}, u32[]{:S(2)}) collective-permute-start(bf16[512,768]{1,0:T(8,128)(2,1)} %slice.91), channel_id=1, source_target_pairs={{0,64},{1,65},{2,66},{3,67},{4,68},{5,69},{6,70},{7,71},{8,72},{9,... | collective-permute-start | bytes 2359304 | tf_op jit(solution)/shard_map/ppermute | solution.py:66
  16.1 8.8 %collective-permute-start.2 = (bf16[2,3,2,64,128]{4,3,2,1,0:T(8,128)(2,1)}, bf16[2,3,2,64,128]{4,3,2,1,0:T(8,128)(2,1)}, u32[]{:S(2)}, u32[]{:S(2)}) collective-permute-start(bf16[2,3,2,64,128]{4,3,2,1,0:T(8,128)(2,1)} %broadcast_select_fusion.2), channel_id=1, source_target_pairs={{0,8},{1,9},{2,10},{3,11},{4,12},{5,13},{6,14},{7,15},{8,0},{9,1},... | collective-permute-start | bytes 589832 | tf_op jit(solution)/shard_map/ppermute | solution.py:66
  19.3 14.6 %collective-permute-start.1 = (bf16[288,512]{1,0:T(8,128)(2,1)}, bf16[288,512]{1,0:T(8,128)(2,1)}, u32[]{:S(2)}, u32[]{:S(2)}) collective-permute-start(bf16[288,512]{1,0:T(8,128)(2,1)} %bitcast.1), channel_id=1, source_target_pairs={{0,8},{1,26},{2,0},{3,18},{4,10},{5,28},{6,2},{7,20},{8,4},{9,22},... | collective-permute-start | bytes 884744 | tf_op jit(solution)/shard_map/ppermute | solution.py:66
  22.0 12.0 %collective-permute-start = (bf16[288,512]{1,0:T(8,128)(2,1)}, bf16[288,512]{1,0:T(8,128)(2,1)}, u32[]{:S(2)}, u32[]{:S(2)}) collective-permute-start(bf16[288,512]{1,0:T(8,128)(2,1)} %bitcast.1), channel_id=1, source_target_pairs={{0,0},{1,18},{2,8},{3,26},{4,2},{5,20},{6,10},{7,28},{8,12},{9,30}... | collective-permute-start | bytes 884744 | tf_op jit(solution)/shard_map/ppermute | solution.py:66
  25.9 10.0 %copy-start.24 = (bf16[2,3,2,64,128]{4,3,2,1,0:T(8,128)(2,1)}, bf16[2,3,2,64,128]{4,3,2,1,0:T(8,128)(2,1)S(1)}, u32[]{:S(2)}) copy-start(bf16[2,3,2,64,128]{4,3,2,1,0:T(8,128)(2,1)S(1)} %add_convert_fusion) | copy-start | bytes 589828
  34.0 92.3 %copy-start.5 = (bf16[512,768]{1,0:T(8,128)(2,1)}, bf16[512,768]{1,0:T(8,128)(2,1)S(1)}, u32[]{:S(2)}) copy-start(bf16[512,768]{1,0:T(8,128)(2,1)S(1)} %collective-permute-done.4.refs_2_) | copy-start | bytes 2359300
  35.9 6.1 %collective-permute-start.7 = (bf16[2,3,2,32,128]{4,3,2,1,0:T(8,128)(2,1)S(1)}, bf16[2,3,2,32,128]{4,3,2,1,0:T(8,128)(2,1)}, u32[]{:S(2)}, u32[]{:S(2)}) collective-permute-start(bf16[2,3,2,32,128]{4,3,2,1,0:T(8,128)(2,1)S(1)} %broadcast_select_fusion.3), channel_id=1, source_target_pairs={{0,1},{1,0},{2,3},{3,2},{4,5},{5,4},{6,7},{7,6},{8,9},{9,8},{10,11... | collective-permute-start | bytes 294920 | tf_op jit(solution)/shard_map/ppermute | solution.py:66
  36.7 6.4 %collective-permute-start.5 = (bf16[288,512]{1,0:T(8,128)(2,1)}, bf16[288,512]{1,0:T(8,128)(2,1)S(1)}, u32[]{:S(2)}, u32[]{:S(2)}) collective-permute-start(bf16[288,512]{1,0:T(8,128)(2,1)} %collective-permute-done), channel_id=1, source_target_pairs={{0,0},{18,18},{8,8},{26,26},{2,66},{20,84},{10,74},{28,92},{12,140... | collective-permute-start | bytes 884744 | tf_op jit(solution)/shard_map/ppermute | solution.py:66
  38.3 4.8 %collective-permute-start.6 = (bf16[288,512]{1,0:T(8,128)(2,1)}, bf16[288,512]{1,0:T(8,128)(2,1)}, u32[]{:S(2)}, u32[]{:S(2)}) collective-permute-start(bf16[288,512]{1,0:T(8,128)(2,1)} %collective-permute-done.1), channel_id=1, source_target_pairs={{8,8},{26,26},{0,0},{18,18},{10,74},{28,92},{2,66},{20,84},{4,132}... | collective-permute-start | bytes 884744 | tf_op jit(solution)/shard_map/ppermute | solution.py:66
  43.1 49.2 %copy-start.25 = (f32[2,8]{1,0:T(2,128)S(1)}, f32[2,8]{1,0:T(2,128)}, u32[]{:S(2)}) copy-start(f32[2,8]{1,0:T(2,128)} %param.7) | copy-start | bytes 196
  45.0 51.1 %copy-start.26 = (f32[3]{0:T(128)S(1)}, f32[3]{0:T(128)}, u32[]{:S(2)}) copy-start(f32[3]{0:T(128)} %constant.105.clone) | copy-start | bytes 40
  45.0 140.6 %all-gather.7.cloned.1.call-start = ((), (), s32[]{:S(2)}) async-start(), calls=%async_computation.2 | async-start | bytes 2654208 | tf_op jit(solution)/shard_map/all_gather | solution.py:182
  46.3 69.0 %collective-permute-start.15 = (bf16[512,1536]{1,0:T(8,128)(2,1)}, bf16[512,1536]{1,0:T(8,128)(2,1)}, u32[]{:S(2)}, u32[]{:S(2)}) collective-permute-start(bf16[512,1536]{1,0:T(8,128)(2,1)} %slice.94), channel_id=1, source_target_pairs={{0,192},{1,193},{2,194},{3,195},{4,196},{5,197},{6,198},{7,199},{8... | collective-permute-start | bytes 4718600 | tf_op jit(solution)/shard_map/ppermute | solution.py:66
  82.7 34.2 %collective-permute-start.14 = (bf16[512,1536]{1,0:T(8,128)(2,1)}, bf16[512,1536]{1,0:T(8,128)(2,1)}, u32[]{:S(2)}, u32[]{:S(2)}) collective-permute-start(bf16[512,1536]{1,0:T(8,128)(2,1)} %slice.94), channel_id=1, source_target_pairs={{0,64},{1,65},{2,66},{3,67},{4,68},{5,69},{6,70},{7,71},{8,72},{9,... | collective-permute-start | bytes 4718600 | tf_op jit(solution)/shard_map/ppermute | solution.py:66
  82.8 5.1 %collective-permute-start.8 = (bf16[2,3,2,16,128]{4,3,2,1,0:T(8,128)(2,1)S(1)}, bf16[2,3,2,16,128]{4,3,2,1,0:T(8,128)(2,1)S(1)}, u32[]{:S(2)}, u32[]{:S(2)}) collective-permute-start(bf16[2,3,2,16,128]{4,3,2,1,0:T(8,128)(2,1)S(1)} %broadcast_select_fusion.4), channel_id=1, source_target_pairs={{0,2},{1,3},{2,0},{3,1},{4,6},{5,7},{6,4},{7,5},{8,10},{9,11},{10,... | collective-permute-start | bytes 147464 | tf_op jit(solution)/shard_map/ppermute | solution.py:66
  82.9 51.3 %collective-permute-start.16 = (bf16[512,2304]{1,0:T(8,128)(2,1)S(1)}, bf16[512,2304]{1,0:T(8,128)(2,1)}, u32[]{:S(2)}, u32[]{:S(2)}) collective-permute-start(bf16[512,2304]{1,0:T(8,128)(2,1)S(1)} %bitcast.37), channel_id=1, source_target_pairs={{0,16},{1,17},{2,18},{3,19},{4,20},{5,21},{6,22},{7,23},{8,24},{9,... | collective-permute-start | bytes 7077896 | tf_op jit(solution)/shard_map/ppermute | solution.py:66
  87.9 8.2 %collective-permute-start.9 = (bf16[2,3,2,8,128]{4,3,2,1,0:T(8,128)(2,1)S(1)}, bf16[2,3,2,8,128]{4,3,2,1,0:T(8,128)(2,1)S(1)}, u32[]{:S(2)}, u32[]{:S(2)}) collective-permute-start(bf16[2,3,2,8,128]{4,3,2,1,0:T(8,128)(2,1)S(1)} %broadcast_select_fusion.5), channel_id=1, source_target_pairs={{0,4},{1,5},{2,6},{3,7},{4,0},{5,1},{6,2},{7,3},{8,12},{9,13},{10,... | collective-permute-start | bytes 73736 | tf_op jit(solution)/shard_map/ppermute | solution.py:66
  96.2 3.6 %collective-permute-start.10 = (f32[2]{0:T(128)S(1)}, f32[2]{0:T(128)S(1)}, u32[]{:S(2)}, u32[]{:S(2)}) collective-permute-start(f32[2]{0:T(128)S(1)} %add.71), channel_id=1, source_target_pairs={{0,8},{1,9},{2,10},{3,11},{4,12},{5,13},{6,14},{7,15},{8,0},{9,1},... | collective-permute-start | bytes 32 | tf_op jit(solution)/shard_map/ppermute | solution.py:66
  99.8 3.5 %collective-permute-start.11 = (f32[2]{0:T(128)S(1)}, f32[2]{0:T(128)S(1)}, u32[]{:S(2)}, u32[]{:S(2)}) collective-permute-start(f32[2]{0:T(128)S(1)} %add.72), channel_id=1, source_target_pairs={{0,1},{1,0},{2,3},{3,2},{4,5},{5,4},{6,7},{7,6},{8,9},{9,8},{10,11... | collective-permute-start | bytes 32 | tf_op jit(solution)/shard_map/ppermute | solution.py:66
  103.4 4.4 %collective-permute-start.12 = (f32[2]{0:T(128)S(1)}, f32[2]{0:T(128)S(1)}, u32[]{:S(2)}, u32[]{:S(2)}) collective-permute-start(f32[2]{0:T(128)S(1)} %add.73), channel_id=1, source_target_pairs={{0,2},{1,3},{2,0},{3,1},{4,6},{5,7},{6,4},{7,5},{8,10},{9,11},{10,... | collective-permute-start | bytes 32 | tf_op jit(solution)/shard_map/ppermute | solution.py:66
  107.8 7.5 %collective-permute-start.13 = (f32[2]{0:T(128)S(1)}, f32[2]{0:T(128)S(1)}, u32[]{:S(2)}, u32[]{:S(2)}) collective-permute-start(f32[2]{0:T(128)S(1)} %add.74), channel_id=1, source_target_pairs={{0,4},{1,5},{2,6},{3,7},{4,0},{5,1},{6,2},{7,3},{8,12},{9,13},{10,... | collective-permute-start | bytes 32 | tf_op jit(solution)/shard_map/ppermute | solution.py:66
  126.3 3.0 %slice-start = ((bf16[512,768]{1,0:T(8,128)(2,1)}), bf16[256,768]{1,0:T(8,128)(2,1)S(1)}, s32[]{:S(2)}) async-start(bf16[512,768]{1,0:T(8,128)(2,1)} %copy-done.5), calls=%async_computation.3 | async-start | bytes 786432 | tf_op jit(solution)/shard_map/slice | solution.py:217
  129.3 4.4 %copy-start.6 = (bf16[512,768]{1,0:T(8,128)(2,1)S(1)}, bf16[512,768]{1,0:T(8,128)(2,1)}, u32[]{:S(2)}) copy-start(bf16[512,768]{1,0:T(8,128)(2,1)} %copy-done.5) | copy-start | bytes 2359300
  129.3 19.3 %collective-permute-start.19 = (bf16[256,1536]{1,0:T(8,128)(2,1)S(1)}, bf16[256,1536]{1,0:T(8,128)(2,1)S(1)}, u32[]{:S(2)}, u32[]{:S(2)}) collective-permute-start(bf16[256,1536]{1,0:T(8,128)(2,1)S(1)} %pad_maximum_fusion.2), channel_id=1, source_target_pairs={{0,192},{1,193},{2,194},{3,195},{4,196},{5,197},{6,198},{7,199},{8... | collective-permute-start | bytes 2359304 | tf_op jit(solution)/shard_map/ppermute | solution.py:66
  132.6 20.6 %collective-permute-start.18 = (bf16[256,1536]{1,0:T(8,128)(2,1)S(1)}, bf16[256,1536]{1,0:T(8,128)(2,1)}, u32[]{:S(2)}, u32[]{:S(2)}) collective-permute-start(bf16[256,1536]{1,0:T(8,128)(2,1)S(1)} %pad_maximum_fusion.1), channel_id=1, source_target_pairs={{0,64},{1,65},{2,66},{3,67},{4,68},{5,69},{6,70},{7,71},{8,72},{9,... | collective-permute-start | bytes 2359304 | tf_op jit(solution)/shard_map/ppermute | solution.py:66
  133.7 19.4 %collective-permute-start.17 = (bf16[512,768]{1,0:T(8,128)(2,1)S(1)}, bf16[512,768]{1,0:T(8,128)(2,1)S(1)}, u32[]{:S(2)}, u32[]{:S(2)}) collective-permute-start(bf16[512,768]{1,0:T(8,128)(2,1)S(1)} %copy-done.6), channel_id=1, source_target_pairs={{0,16},{1,17},{2,18},{3,19},{4,20},{5,21},{6,22},{7,23},{8,24},{9,... | collective-permute-start | bytes 2359304 | tf_op jit(solution)/shard_map/ppermute | solution.py:66
  133.7 35.0 %collective-permute-start.28 = (bf16[512,1536]{1,0:T(8,128)(2,1)}, bf16[512,1536]{1,0:T(8,128)(2,1)}, u32[]{:S(2)}, u32[]{:S(2)}) collective-permute-start(bf16[512,1536]{1,0:T(8,128)(2,1)} %collective-permute-done.14.refs_8_), channel_id=1, source_target_pairs={{0,16},{1,17},{2,18},{3,19},{4,20},{5,21},{6,22},{7,23},{8,24},{9,... | collective-permute-start | bytes 4718600 | tf_op jit(solution)/shard_map/ppermute | solution.py:66
  134.2 34.4 %collective-permute-start.25 = (bf16[512,1536]{1,0:T(8,128)(2,1)}, bf16[512,1536]{1,0:T(8,128)(2,1)}, u32[]{:S(2)}, u32[]{:S(2)}) collective-permute-start(bf16[512,1536]{1,0:T(8,128)(2,1)} %collective-permute-done.15.refs_2_), channel_id=1, source_target_pairs={{0,16},{1,17},{2,18},{3,19},{4,20},{5,21},{6,22},{7,23},{8,24},{9,... | collective-permute-start | bytes 4718600 | tf_op jit(solution)/shard_map/ppermute | solution.py:66
  148.7 5.8 %collective-permute-start.22 = (bf16[512,768]{1,0:T(8,128)(2,1)}, bf16[512,768]{1,0:T(8,128)(2,1)S(1)}, u32[]{:S(2)}, u32[]{:S(2)}) collective-permute-start(bf16[512,768]{1,0:T(8,128)(2,1)} %collective-permute-done.3.refs_8_), channel_id=1, source_target_pairs={{0,16},{1,17},{2,18},{3,19},{4,20},{5,21},{6,22},{7,23},{8,24},{9,... | collective-permute-start | bytes 2359304 | tf_op jit(solution)/shard_map/ppermute | solution.py:66
  153.1 2.3 %collective-permute-start.21 = (bf16[256,1536]{1,0:T(8,128)(2,1)S(1)}, bf16[256,1536]{1,0:T(8,128)(2,1)S(1)}, u32[]{:S(2)}, u32[]{:S(2)}) collective-permute-start(bf16[256,1536]{1,0:T(8,128)(2,1)S(1)} %collective-permute-done.19.refs_5_), channel_id=1, source_target_pairs={{0,16},{1,17},{2,18},{3,19},{4,20},{5,21},{6,22},{7,23},{8,24},{9,... | collective-permute-start | bytes 2359304 | tf_op jit(solution)/shard_map/ppermute | solution.py:66
  153.1 0.9 copy-start.9
  154.0 8.2 %collective-permute-start.20 = (bf16[256,1536]{1,0:T(8,128)(2,1)}, bf16[256,1536]{1,0:T(8,128)(2,1)}, u32[]{:S(2)}, u32[]{:S(2)}) collective-permute-start(bf16[256,1536]{1,0:T(8,128)(2,1)} %collective-permute-done.18.refs_4_), channel_id=1, source_target_pairs={{0,16},{1,17},{2,18},{3,19},{4,20},{5,21},{6,22},{7,23},{8,24},{9,... | collective-permute-start | bytes 2359304 | tf_op jit(solution)/shard_map/ppermute | solution.py:66
  154.5 0.9 copy-start.12
  155.4 12.4 %collective-permute-start.23 = (bf16[256,768]{1,0:T(8,128)(2,1)}, bf16[256,768]{1,0:T(8,128)(2,1)S(1)}, u32[]{:S(2)}, u32[]{:S(2)}) collective-permute-start(bf16[256,768]{1,0:T(8,128)(2,1)} %get-tuple-element.64), channel_id=1, source_target_pairs={{0,64},{1,65},{2,66},{3,67},{4,68},{5,69},{6,70},{7,71},{8,72},{9,... | collective-permute-start | bytes 1179656 | tf_op jit(solution)/shard_map/ppermute | solution.py:66
  155.4 0.9 copy-start.2
  156.3 11.8 %collective-permute-start.24 = (bf16[256,768]{1,0:T(8,128)(2,1)}, bf16[256,768]{1,0:T(8,128)(2,1)}, u32[]{:S(2)}, u32[]{:S(2)}) collective-permute-start(bf16[256,768]{1,0:T(8,128)(2,1)} %get-tuple-element.62), channel_id=1, source_target_pairs={{0,192},{1,193},{2,194},{3,195},{4,196},{5,197},{6,198},{7,199},{8... | collective-permute-start | bytes 1179656 | tf_op jit(solution)/shard_map/ppermute | solution.py:66
  159.5 1.7 copy-start.15
  161.2 1.1 copy-start.3
  161.2 1.4 copy-start.7
  161.2 1.6 copy-start.10
  161.2 1.8 copy-start.13
  168.1 10.9 %collective-permute-start.26 = (bf16[256,768]{1,0:T(8,128)(2,1)S(1)}, bf16[256,768]{1,0:T(8,128)(2,1)S(1)}, u32[]{:S(2)}, u32[]{:S(2)}) collective-permute-start(bf16[256,768]{1,0:T(8,128)(2,1)S(1)} %collective-permute-done.23.refs_4_), channel_id=1, source_target_pairs={{0,16},{1,17},{2,18},{3,19},{4,20},{5,21},{6,22},{7,23},{8,24},{9,... | collective-permute-start | bytes 1179656 | tf_op jit(solution)/shard_map/ppermute | solution.py:66
  168.1 10.9 %collective-permute-start.27 = (bf16[256,768]{1,0:T(8,128)(2,1)}, bf16[256,768]{1,0:T(8,128)(2,1)S(1)}, u32[]{:S(2)}, u32[]{:S(2)}) collective-permute-start(bf16[256,768]{1,0:T(8,128)(2,1)} %collective-permute-done.24.refs_5_), channel_id=1, source_target_pairs={{0,16},{1,17},{2,18},{3,19},{4,20},{5,21},{6,22},{7,23},{8,24},{9,... | collective-permute-start | bytes 1179656 | tf_op jit(solution)/shard_map/ppermute | solution.py:66
  174.0 19.3 %collective-permute-start.30 = (bf16[144,1536]{1,0:T(8,128)(2,1)}, bf16[144,1536]{1,0:T(8,128)(2,1)}, u32[]{:S(2)}, u32[]{:S(2)}) collective-permute-start(bf16[144,1536]{1,0:T(8,128)(2,1)} %get-tuple-element.66), channel_id=1, source_target_pairs={{0,40},{1,41},{2,42},{3,43},{4,44},{5,45},{6,46},{7,47},{8,0},{9,1... | collective-permute-start | bytes 1327112 | tf_op jit(solution)/shard_map/ppermute | solution.py:66
  179.0 14.5 %collective-permute-start.29 = (bf16[144,1536]{1,0:T(8,128)(2,1)}, bf16[144,1536]{1,0:T(8,128)(2,1)}, u32[]{:S(2)}, u32[]{:S(2)}) collective-permute-start(bf16[144,1536]{1,0:T(8,128)(2,1)} %get-tuple-element.67), channel_id=1, source_target_pairs={{0,8},{1,9},{2,10},{3,11},{4,12},{5,13},{6,14},{7,15},{8,32},{9,33... | collective-permute-start | bytes 1327112 | tf_op jit(solution)/shard_map/ppermute | solution.py:66
  187.3 22.2 %collective-permute-start.33 = (bf16[144,768]{1,0:T(8,128)(2,1)}, bf16[144,768]{1,0:T(8,128)(2,1)}, u32[]{:S(2)}, u32[]{:S(2)}) collective-permute-start(bf16[144,768]{1,0:T(8,128)(2,1)} %get-tuple-element.74), channel_id=1, source_target_pairs={{0,8},{1,9},{2,10},{3,11},{4,12},{5,13},{6,14},{7,15},{8,32},{9,33... | collective-permute-start | bytes 663560 | tf_op jit(solution)/shard_map/ppermute | solution.py:66
  188.1 5.5 %copy-start.4 = (bf16[256,1536]{1,0:T(8,128)(2,1)S(1)}, bf16[256,1536]{1,0:T(8,128)(2,1)}, u32[]{:S(2)}) copy-start(bf16[256,1536]{1,0:T(8,128)(2,1)} %copy-done.2) | copy-start | bytes 2359300
  188.1 5.5 %copy-start.8 = (bf16[512,768]{1,0:T(8,128)(2,1)S(1)}, bf16[512,768]{1,0:T(8,128)(2,1)}, u32[]{:S(2)}) copy-start(bf16[512,768]{1,0:T(8,128)(2,1)} %copy-done.5) | copy-start | bytes 2359300
  188.1 5.5 %copy-start.11 = (bf16[512,768]{1,0:T(8,128)(2,1)S(1)}, bf16[512,768]{1,0:T(8,128)(2,1)}, u32[]{:S(2)}) copy-start(bf16[512,768]{1,0:T(8,128)(2,1)} %copy-done.9) | copy-start | bytes 2359300
  188.1 5.5 %copy-start.14 = (bf16[512,768]{1,0:T(8,128)(2,1)S(1)}, bf16[512,768]{1,0:T(8,128)(2,1)}, u32[]{:S(2)}) copy-start(bf16[512,768]{1,0:T(8,128)(2,1)} %copy-done.12) | copy-start | bytes 2359300
  188.1 21.5 %collective-permute-start.35 = (bf16[144,768]{1,0:T(8,128)(2,1)S(1)}, bf16[144,768]{1,0:T(8,128)(2,1)}, u32[]{:S(2)}, u32[]{:S(2)}) collective-permute-start(bf16[144,768]{1,0:T(8,128)(2,1)S(1)} %get-tuple-element.75), channel_id=1, source_target_pairs={{0,40},{1,41},{2,42},{3,43},{4,44},{5,45},{6,46},{7,47},{8,0},{9,1... | collective-permute-start | bytes 663560 | tf_op jit(solution)/shard_map/ppermute | solution.py:66
  190.6 1.7 copy-start.16
  193.5 19.3 %collective-permute-start.31 = (bf16[144,1536]{1,0:T(8,128)(2,1)}, bf16[144,1536]{1,0:T(8,128)(2,1)S(1)}, u32[]{:S(2)}, u32[]{:S(2)}) collective-permute-start(bf16[144,1536]{1,0:T(8,128)(2,1)} %collective-permute-done.29), channel_id=1, source_target_pairs={{0,8},{1,9},{2,10},{3,11},{4,12},{5,13},{6,14},{7,15},{8,32},{9,33... | collective-permute-start | bytes 1327112 | tf_op jit(solution)/shard_map/ppermute | solution.py:66
  197.2 7.9 %copy-start.1 = (bf16[2,256,2304]{2,1,0:T(8,128)(2,1)S(1)}, bf16[2,256,2304]{2,1,0:T(8,128)(2,1)}, u32[]{:S(2)}) copy-start(bf16[2,256,2304]{2,1,0:T(8,128)(2,1)} %param.5) | copy-start | bytes 7077892
  197.2 7.9 %copy-start.19 = (bf16[256,768]{1,0:T(8,128)(2,1)S(1)}, bf16[256,768]{1,0:T(8,128)(2,1)}, u32[]{:S(2)}) copy-start(bf16[256,768]{1,0:T(8,128)(2,1)} %copy-done.18) | copy-start | bytes 1179652
  197.2 7.9 %copy-start.21 = (bf16[256,768]{1,0:T(8,128)(2,1)S(1)}, bf16[256,768]{1,0:T(8,128)(2,1)}, u32[]{:S(2)}) copy-start(bf16[256,768]{1,0:T(8,128)(2,1)} %copy-done.20) | copy-start | bytes 1179652
  197.2 15.6 %collective-permute-start.32 = (bf16[144,1536]{1,0:T(8,128)(2,1)}, bf16[144,1536]{1,0:T(8,128)(2,1)S(1)}, u32[]{:S(2)}, u32[]{:S(2)}) collective-permute-start(bf16[144,1536]{1,0:T(8,128)(2,1)} %collective-permute-done.30), channel_id=1, source_target_pairs={{0,40},{1,41},{2,42},{3,43},{4,44},{5,45},{6,46},{7,47},{8,0},{9,1... | collective-permute-start | bytes 1327112 | tf_op jit(solution)/shard_map/ppermute | solution.py:66
  205.1 11.8 %copy-start.23 = (f32[288,2304]{1,0:T(8,128)S(1)}, f32[288,2304]{1,0:T(8,128)}, u32[]{:S(2)}) copy-start(f32[288,2304]{1,0:T(8,128)} %param.8) | copy-start | bytes 7962628
  209.5 7.4 %collective-permute-start.34 = (bf16[144,768]{1,0:T(8,128)(2,1)}, bf16[144,768]{1,0:T(8,128)(2,1)S(1)}, u32[]{:S(2)}, u32[]{:S(2)}) collective-permute-start(bf16[144,768]{1,0:T(8,128)(2,1)} %collective-permute-done.33), channel_id=1, source_target_pairs={{0,8},{1,9},{2,10},{3,11},{4,12},{5,13},{6,14},{7,15},{8,32},{9,33... | collective-permute-start | bytes 663560 | tf_op jit(solution)/shard_map/ppermute | solution.py:66
  209.6 7.3 %collective-permute-start.36 = (bf16[144,768]{1,0:T(8,128)(2,1)}, bf16[144,768]{1,0:T(8,128)(2,1)S(1)}, u32[]{:S(2)}, u32[]{:S(2)}) collective-permute-start(bf16[144,768]{1,0:T(8,128)(2,1)} %collective-permute-done.35), channel_id=1, source_target_pairs={{0,40},{1,41},{2,42},{3,43},{4,44},{5,45},{6,46},{7,47},{8,0},{9,1... | collective-permute-start | bytes 663560 | tf_op jit(solution)/shard_map/ppermute | solution.py:66
  (3 other events, 2.3 us)
Sparse Core Ops, SparseCore 0:
  45.1 75.2 all-gather.4
  122.2 40.2 all-gather.6

commit v4 on v1

v4 whole, which is shorter than its diff:
```python
import math

import jax
import jax.numpy as jnp
from jax import lax
from jax.experimental import pallas as pl
from jax.experimental.pallas import tpu as pltpu
from jax.sharding import PartitionSpec as P

clip_norm = 2.5
AXES = ("dp", "tensor")
NY, NX, NZ = 4, 4, 8
OFF = (0, 1, 2, -1)
BF = jnp.bfloat16
F32 = jnp.float32


def coords(i):
    dp, te = divmod(i, 2 * NZ)
    return dp // 4, (dp // 2) % 2, dp % 2, te // NZ, te % NZ


def index(y, xh, c, xl, z):
    return ((y % NY * 2 + xh) * 2 + c) * 2 * NZ + xl * NZ + z % NZ


def perm_of(move):
    return [(i, index(*move(*coords(i)))) for i in range(NY * NX * NZ * 2)]


def along_x(step):
    def move(y, xh, c, xl, z):
        x = (xh * 2 + xl + step) % NX
        return y, x // 2, c, x % 2, z

    return perm_of(move)


def along_y(step):
    return perm_of(lambda y, xh, c, xl, z: (y + step, xh, c, xl, z))


def along_z(step):
    return perm_of(lambda y, xh, c, xl, z: (y, xh, c, xl, z + step))


def flip_z(bit):
    return perm_of(lambda y, xh, c, xl, z: (y, xh, c, xl, z ^ bit))


def spread(flip):
    def move(y, xh, c, xl, z):
        t, u = (z // 2) % 2, z % 2
        m = 2 * (xh ^ t) + (c ^ u)
        return y, t, u, xl ^ flip, z + OFF[m]

    return perm_of(move)


CORE = perm_of(lambda y, xh, c, xl, z: (y, xh, 1 - c, xl, z))
XHI = perm_of(lambda y, xh, c, xl, z: (y, 1 - xh, c, xl, z))
XLO = perm_of(lambda y, xh, c, xl, z: (y, xh, c, 1 - xl, z))


def send(value, perm):
    return lax.ppermute(value, AXES, perm)


def scale_kernel(place_ref, clip_ref, *refs):
    pieces, out_ref = refs[:-1], refs[-1]
    dp, te = place_ref[0], place_ref[1]
    y, xh, c, xl, z = dp // 4, (dp // 2) % 2, dp % 2, te // NZ, te % NZ
    half = out_ref.shape[3] // 2
    for r in range(NZ):
        q = (z - r - 2 * xh - c + 2 * NZ) % NZ
        m = q % 4
        k = ((q + 1) // 4) % 2
        for f in range(2):
            step = (2 * ((f + xl) % 2) + k - y + 4) % 4
            slot = jnp.where(step == 0, 3, jnp.where(step == 1, 0, jnp.where(step == 2, 2, 1)))
            block = pieces[4 + f] if r == 4 else pieces[r + (r > 4)].at[f]
            member = (2 * (xh ^ (m // 2)) + (c ^ (m % 2)))
            for e in range(2):
                cols = slice(e * half, (e + 1) * half)
                out_ref[slot, m, :, cols] = (
                    clip_ref[2 * member + e] * block[:, cols].astype(F32)
                ).astype(BF)


def scale_grads(places, clips, pieces):
    _, rows, tokens = pieces[0].shape
    smem = pl.BlockSpec(memory_space=pltpu.SMEM)
    vmem = pl.BlockSpec(memory_space=pltpu.VMEM)
    return pl.pallas_call(
        scale_kernel,
        out_shape=jax.ShapeDtypeStruct((4, 4, rows, tokens), BF),
        in_specs=[smem, smem] + [vmem] * len(pieces),
        out_specs=vmem,
        cost_estimate=pl.CostEstimate(
            flops=16 * rows * tokens, bytes_accessed=rows * tokens, transcendentals=0
        ),
        compiler_params=pltpu.CompilerParams(vmem_limit_bytes=24 * 1024 * 1024),
        name="scale_grads",
    )(places, clips, *pieces)


def product_kernel(s_ref, *refs):
    acts, outs = refs[:6], refs[6:]
    slots, _, rows, tokens = s_ref.shape
    total = None
    first = 0
    for a_ref in acts:
        count = a_ref.shape[0]
        m, start = first // tokens, first % tokens
        left = s_ref[:, m, :, start : start + count].reshape(slots * rows, count)
        part = jnp.dot(left, a_ref[...], preferred_element_type=F32)
        total = part if total is None else total + part
        first += count
    first = 0
    for out_ref in outs:
        count = out_ref.shape[0]
        out_ref[...] = total[first : first + count].astype(out_ref.dtype)
        first += count


def product(name, scaled, first, slots, acts, tile, parts, dtype):
    _, quarters, rows, tokens = scaled.shape
    width = acts[0].shape[1]
    count = slots * rows // parts
    return pl.pallas_call(
        product_kernel,
        out_shape=[jax.ShapeDtypeStruct((count, width), dtype)] * parts,
        grid=(width // tile,),
        in_specs=[
            pl.BlockSpec((slots, quarters, rows, tokens), lambda j: (first // slots, 0, 0, 0))
        ]
        + [pl.BlockSpec((a.shape[0], tile), lambda j: (0, j)) for a in acts],
        out_specs=[pl.BlockSpec((count, tile), lambda j: (0, j))] * parts,
        cost_estimate=pl.CostEstimate(
            flops=2 * slots * rows * width, bytes_accessed=2 * rows * width, transcendentals=0
        ),
        compiler_params=pltpu.CompilerParams(vmem_limit_bytes=24 * 1024 * 1024),
        name=name,
    )(scaled, *acts)


def all_to_all(value, axis, groups):
    return lax.all_to_all(value, axis, 0, 0, tiled=True, axis_index_groups=groups)


def shards(acts, out_grads, other_sq, noise):
    dp, te = lax.axis_index("dp"), lax.axis_index("tensor")
    y, xh, c, xl, z = dp // 4, (dp // 2) % 2, dp % 2, te // NZ, te % NZ
    examples, seq, columns = acts.shape
    tokens = examples * seq
    features = out_grads.shape[2]
    rows = features // 2
    stage = lax.optimization_barrier
    z_rings = [list(range(first, first + NZ)) for first in (0, NZ)]
    chip_pairs = [list(range(first, first + 4)) for first in range(0, 4 * NY, 4)]

    flat = acts.reshape(tokens, columns)
    grads_t = out_grads.reshape(tokens, features).T
    sources = [send(grads_t, spread(0)), send(grads_t, spread(1))]

    def blocks(x):
        gram = jnp.einsum("btf,bsf->bts", x, x, preferred_element_type=F32).astype(BF)
        mid = seq // 2
        return jnp.stack([gram[:, :mid, :mid], gram[:, :mid, mid:], gram[:, mid:, mid:]])

    grams = jnp.stack([blocks(acts), blocks(out_grads)])
    low, high = jnp.split(grams, 2, axis=3)
    keep, give = jnp.where(xl == 0, low, high), jnp.where(xl == 0, high, low)
    grams = (keep.astype(F32) + send(give, XLO).astype(F32)).astype(BF)
    sources, grams, flat = stage((sources, grams, flat))

    up = send(flat[:seq], along_x(1))
    down = send(flat[seq:], along_x(-1))
    own = jnp.stack(sources)
    shape = grams.shape
    grams = jnp.moveaxis(grams.reshape(shape[:3] + (NZ, -1, shape[4])), 3, 0)
    grams = all_to_all(grams, "tensor", z_rings).astype(F32).sum(axis=0)
    weight = jnp.array([1.0, 2.0, 1.0], F32)[:, None, None, None]
    total = jnp.sum(grams[0] * grams[1] * weight, axis=(0, 2, 3)) + jnp.sum(other_sq, axis=1)
    total = all_to_all(jnp.broadcast_to(total, (NZ, examples)), "tensor", z_rings).sum(axis=0)
    own, total = stage((own, total))

    fwd, bwd = [own, send(own, along_z(1))], [own, send(own, along_z(-1))]
    up, down, total = stage((up, down, total))
    total = total + send(total, XLO)
    clip = jnp.minimum(1.0, clip_norm / jnp.sqrt(total))
    clips = all_to_all(jnp.broadcast_to(clip, (4, examples)), "dp", chip_pairs).reshape(-1)
    up, down, fwd[1], bwd[1], clips = stage((up, down, fwd[1], bwd[1], clips))

    up, down = send(up, along_x(1)), send(down, along_x(-1))
    sibling = send(flat, CORE)
    for _ in range(2):
        fwd.append(send(fwd[-1], along_z(1)))
        bwd.append(send(bwd[-1], along_z(-1)))
    up, down, fwd[3], bwd[3] = stage((up, down, fwd[3], bwd[3]))

    far = [send(fwd[3][0], along_z(1)), send(bwd[3][1], along_z(-1))]
    up_sibling, down_sibling = send(up, CORE), send(down, CORE)
    pieces = [own, fwd[1], fwd[2], fwd[3], far[0], far[1], bwd[3], bwd[2], bwd[1]]
    places = jnp.stack([dp, te]).astype(jnp.int32)
    scaled = scale_grads(places, clips, pieces)

    held = [flat, sibling, up, down, up_sibling, down_sibling]
    tile = columns // 3
    far_a, far_b = product("product_far", scaled, 2, 1, held, tile, 2, BF)
    from_down, from_up = send(far_a, along_y(1)), send(far_b, along_y(-1))
    next_a, next_b, prev_a, prev_b = product("product_near", scaled, 0, 2, held, tile, 4, BF)
    next_b, prev_a = send(next_b, along_y(1)), send(prev_a, along_y(-1))
    next_a = (next_a.astype(F32) + from_down.astype(F32)).astype(BF)
    prev_b = (prev_b.astype(F32) + from_up.astype(F32)).astype(BF)
    next_a, prev_b, scaled = stage((next_a, prev_b, scaled))
    next_a, prev_b = send(next_a, along_y(1)), send(prev_b, along_y(-1))
    (mine,) = product("product_own", scaled, 3, 1, held, tile, 1, F32)

    width = features * 2 * NZ
    factor = math.sqrt(columns * 2 * NZ * width) / clip_norm
    root = math.sqrt(examples * 4 * NY)
    summed = jnp.concatenate(
        [next_a.astype(F32) + prev_a.astype(F32), next_b.astype(F32) + prev_b.astype(F32)]
    )
    return (factor * (mine + summed) + noise) / root


def solution(mesh):
    placed = (
        P("dp", None, "tensor"),
        P("dp", None, "tensor"),
        P("dp", "tensor"),
        P("dp", "tensor"),
    )
    return jax.shard_map(
        shards, mesh=mesh, in_specs=placed, out_specs=P("dp", "tensor"), check_vma=False
    )
```

time: 202 us -> 186 us (0.921); the launches traced: 201 us -> 183 us
  Pallas kernels: 32.6 us -> 21 us
  blocking collectives: 0 us -> 9.28 us
  other arithmetic: 11.2 us -> 4.1 us
  waiting for transfers between devices: 86.8 us -> 81.6 us
    ppermute x33 -> x25, waiting for transfers between devices: 86.8 us -> 67.1 us  [send(): return lax.ppermute(value, AXES, perm)]
    ppermute x33 -> x25, starting transfers between devices: 51 us -> 35.2 us  [send(): return lax.ppermute(value, AXES, perm)]
    all_to_all x0 -> x2, waiting for transfers between devices: none -> 14.5 us  [all_to_all(): lax.all_to_all(value, axis, 0, 0, tiled=True, axis_index_groups=groups)]
    all_to_all x0 -> x2, starting transfers between devices: none -> 13.9 us  [all_to_all(): lax.all_to_all(value, axis, 0, 0, tiled=True, axis_index_groups=groups)]
    pallas_call x4 -> x3, Pallas kernels: 30.8 us -> 18.6 us  [product(): pl.pallas_call(product_kernel, out_shape=[jax.ShapeDtypeStruct((count, wi...]
    all_to_all x0 -> x1, blocking collectives: none -> 9.28 us  [all_to_all(): lax.all_to_all(value, axis, 0, 0, tiled=True, axis_index_groups=groups)]
    convert_element_type x6 -> x3, other arithmetic: 4.08 us -> 0.39 us  [the longest x1 0.15 us: shards(): prev_b = (prev_b.astype(F32) + from_up.astype(F32)).astype(BF)]
    another operation x2 -> x3, other arithmetic: 2.26 us -> 0.18 us  [the longest x1 0.07 us: shards(): places = jnp.stack([dp, te]).astype(jnp.int32)]
  transfers between devices with their start and end apart: 33 -> 27, of which waited for: 15 -> 15; matrix products, arithmetic and copies ran while one was open for 8% -> 3% of each run, Pallas kernels for 12% -> 9%
where the time goes in v4:
time: 186 us; the launch traced here: 183 us
  waiting for transfers between devices  81.6 us (44%)
  starting transfers between devices  49.2 us (26%)
  Pallas kernels  21 us (11%)
  local copies, waits for them, and re-layouts  13.7 us (7%)
  blocking collectives  9.28 us (5%)
  other arithmetic  4.1 us (2%)
  matrix products  3.57 us (2%)
    ppermute x25, waiting for transfers between devices, send(): return lax.ppermute(value, AXES, perm)  67.1 us
    ppermute x25, starting transfers between devices, send(): return lax.ppermute(value, AXES, perm)  35.2 us
    pallas_call x3, Pallas kernels, product(): pl.pallas_call(product_kernel, out_shape=[jax.ShapeDtypeStruct((count, wi...  18.6 us
    all_to_all x2, waiting for transfers between devices, all_to_all(): lax.all_to_all(value, axis, 0, 0, tiled=True, axis_index_groups=groups)  14.5 us
    all_to_all x2, starting transfers between devices, all_to_all(): lax.all_to_all(value, axis, 0, 0, tiled=True, axis_index_groups=groups)  13.9 us
    all_to_all x1, blocking collectives, all_to_all(): lax.all_to_all(value, axis, 0, 0, tiled=True, axis_index_groups=groups)  9.28 us
    unnamed x30, local copies, waits for them, and re-layouts  8.66 us
  transfers between devices with their start and end apart: 27, of which 15 were waited for; matrix products, arithmetic and copies ran while one was open for 3% of the time, Pallas kernels for 9%

profile of v4, /device:TPU:32, one launch (start us, length us, event | category | flops | bytes accessed | tf_op | source)
XLA Modules:
  0.0 182.7 jit_solution(16207725285850429455)
XLA Ops:
  0.0 3.2 %convolution_convert_fusion.1 = bf16[2,256,256]{2,1,0:T(8,128)(2,1)S(1)} fusion(bf16[2,256,2304]{2,1,0:T(8,128)(2,1)} %param.5), kind=kOutput, calls=%fused_computation.9 | convolution fusion | flops 604110848 | bytes 2621440 | tf_op jit(solution)/shard_map/btf,bsf->bts/dot_general | solution.py:167
  3.3 0.4 convolution_convert_fusion
  3.8 1.6 collective-permute-start.2
  5.4 1.1 collective-permute-start.1
  6.6 4.1 %collective-permute-start = (bf16[288,512]{1,0:T(8,128)(2,1)S(1)}, bf16[288,512]{1,0:T(8,128)(2,1)S(1)}, u32[]{:S(2)}, u32[]{:S(2)}) collective-permute-start(bf16[288,512]{1,0:T(8,128)(2,1)S(1)} %bitcast.51), channel_id=1, source_target_pairs={{0,0},{1,18},{2,36},{3,50},{4,4},{5,22},{6,32},{7,54},{8,8},{9,26}... | collective-permute-start | bytes 884744 | tf_op jit(solution)/shard_map/ppermute | solution.py:66
  10.7 6.8 %collective-permute-done.2 = bf16[2,3,2,64,128]{4,3,2,1,0:T(8,128)(2,1)S(1)} collective-permute-done((bf16[2,3,2,64,128]{4,3,2,1,0:T(8,128)(2,1)S(1)}, bf16[2,3,2,64,128]{4,3,2,1,0:T(8,128)(2,1)S(1)}, u32[]{:S(2)}, u32[]{:S(2)}) %collective-permute-start.2) | collective-permute-done | bytes 196640 | tf_op jit(solution)/shard_map/ppermute | solution.py:66
  17.6 1.6 fusion.7
  19.2 4.4 %collective-permute-start.4 = (bf16[256,2304]{1,0:T(8,128)(2,1)}, bf16[256,2304]{1,0:T(8,128)(2,1)}, u32[]{:S(2)}, u32[]{:S(2)}) collective-permute-start(bf16[256,2304]{1,0:T(8,128)(2,1)} %get-tuple-element.59), channel_id=1, source_target_pairs={{0,40},{1,41},{2,42},{3,43},{4,44},{5,45},{6,46},{7,47},{8,0},{9,1... | collective-permute-start | bytes 3538952 | tf_op jit(solution)/shard_map/ppermute | solution.py:66
  23.6 0.7 copy_bitcast_fusion
  24.3 9.4 %all-to-all-start = ((bf16[8,2,3,2,8,128]{5,4,3,2,1,0:T(8,128)(2,1)}), bf16[8,2,3,2,8,128]{5,4,3,2,1,0:T(8,128)(2,1)S(1)}, u32[]{:S(2)}, u32[]{:S(2)}) async-start(bf16[8,2,3,2,8,128]{5,4,3,2,1,0:T(8,128)(2,1)} %copy_bitcast_fusion), calls=%async_computation | async-start | bytes 393216 | tf_op jit(solution)/shard_map/all_to_all | solution.py:148
  33.8 8.3 %all-to-all-done = bf16[8,2,3,2,8,128]{5,4,3,2,1,0:T(8,128)(2,1)S(1)} async-done(((bf16[8,2,3,2,8,128]{5,4,3,2,1,0:T(8,128)(2,1)}), bf16[8,2,3,2,8,128]{5,4,3,2,1,0:T(8,128)(2,1)S(1)}, u32[]{:S(2)}, u32[]{:S(2)}) %all-to-all-start) | async-done | bytes 196640 | tf_op jit(solution)/shard_map/all_to_all | solution.py:148
  42.2 0.2 fusion.6
  42.4 0.6 broadcast_in_dim.7
  43.0 4.5 %all-to-all-start.1 = ((f32[8,1,2]{2,1,0:T(1,128)}), f32[8,1,2]{2,1,0:T(1,128)S(1)}, u32[]{:S(2)}, u32[]{:S(2)}) async-start(f32[8,1,2]{2,1,0:T(1,128)} %broadcast_in_dim.7), calls=%async_computation.1 | async-start | bytes 8192 | tf_op jit(solution)/shard_map/all_to_all | solution.py:148
  47.6 6.2 %all-to-all-done.1 = f32[8,1,2]{2,1,0:T(1,128)S(1)} async-done(((f32[8,1,2]{2,1,0:T(1,128)}), f32[8,1,2]{2,1,0:T(1,128)S(1)}, u32[]{:S(2)}, u32[]{:S(2)}) %all-to-all-start.1) | async-done | bytes 96 | tf_op jit(solution)/shard_map/all_to_all | solution.py:148
  53.8 1.5 collective-permute-start.6
  55.3 0.6 collective-permute-start.5
  55.9 0.8 copy-done.1
  56.7 3.5 %collective-permute-done.7 = f32[2]{0:T(128)S(1)} collective-permute-done((f32[2]{0:T(128)S(1)}, f32[2]{0:T(128)S(1)}, u32[]{:S(2)}, u32[]{:S(2)}) %collective-permute-start.7) | collective-permute-done | bytes 40 | tf_op jit(solution)/shard_map/ppermute | solution.py:66
  60.2 9.3 %all_to_all.17 = f32[4,1,2]{2,1,0:T(1,128)S(1)} all-to-all(f32[4,1,2]{2,1,0:T(1,128)S(1)} %broadcast_in_dim.8), channel_id=1, replica_groups={{0,16,32,48},{64,80,96,112},{128,144,160,176},{192,208,224,240},{1,17,3..., dimensions={0} | all-to-all | bytes 64 | tf_op jit(solution)/shard_map/all_to_all | solution.py:148
  69.5 0.5 broadcast.22
  70.0 0.7 reduce.4
  70.8 0.4 collective-permute-done.5.refs_1_
  71.1 0.6 collective-permute-start.8
  71.7 1.5 collective-permute-start.12
  73.2 1.1 collective-permute-start.9
  74.3 2.1 %collective-permute-start.10 = (bf16[256,2304]{1,0:T(8,128)(2,1)}, bf16[256,2304]{1,0:T(8,128)(2,1)}, u32[]{:S(2)}, u32[]{:S(2)}) collective-permute-start(bf16[256,2304]{1,0:T(8,128)(2,1)} %collective-permute-done.4), channel_id=1, source_target_pairs={{0,40},{1,41},{2,42},{3,43},{4,44},{5,45},{6,46},{7,47},{8,0},{9,1... | collective-permute-start | bytes 3538952 | tf_op jit(solution)/shard_map/ppermute | solution.py:66
  76.4 10.1 %collective-permute-done.8.refs_2_ = bf16[2,288,512]{2,1,0:T(8,128)(2,1)S(1)} collective-permute-done((bf16[2,288,512]{2,1,0:T(8,128)(2,1)}, bf16[2,288,512]{2,1,0:T(8,128)(2,1)S(1)}, u32[]{:S(2)}, u32[]{:S(2)}) %collective-permute-start.8) | collective-permute-done | bytes 589856 | tf_op jit(solution)/shard_map/ppermute | solution.py:66
  86.5 0.4 collective-permute-start.11
  86.9 0.8 copy-done.7
  87.7 2.6 %collective-permute-start.13 = (bf16[2,288,512]{2,1,0:T(8,128)(2,1)S(1)}, bf16[2,288,512]{2,1,0:T(8,128)(2,1)S(1)}, u32[]{:S(2)}, u32[]{:S(2)}) collective-permute-start(bf16[2,288,512]{2,1,0:T(8,128)(2,1)S(1)} %collective-permute-done.12.refs_7_), channel_id=1, source_target_pairs={{0,7},{1,0},{2,1},{3,2},{4,3},{5,4},{6,5},{7,6},{8,15},{9,8},{10,9... | collective-permute-start | bytes 1769480 | tf_op jit(solution)/shard_map/ppermute | solution.py:66
  90.3 0.9 copy-done.9
  91.2 10.7 %collective-permute-done.11.refs_3_ = bf16[2,288,512]{2,1,0:T(8,128)(2,1)S(1)} collective-permute-done((bf16[2,288,512]{2,1,0:T(8,128)(2,1)S(1)}, bf16[2,288,512]{2,1,0:T(8,128)(2,1)S(1)}, u32[]{:S(2)}, u32[]{:S(2)}) %collective-permute-start.11) | collective-permute-done | bytes 589856 | tf_op jit(solution)/shard_map/ppermute | solution.py:66
  102.1 0.5 collective-permute-start.18
  102.6 0.7 slice_bitcast_fusion.1
  103.3 0.8 copy-done.3
  104.1 0.7 slice_bitcast_fusion
  104.9 3.0 %collective-permute-start.15 = (bf16[288,512]{1,0:T(8,128)(2,1)}, bf16[288,512]{1,0:T(8,128)(2,1)}, u32[]{:S(2)}, u32[]{:S(2)}) collective-permute-start(bf16[288,512]{1,0:T(8,128)(2,1)} %slice_bitcast_fusion), channel_id=1, source_target_pairs={{0,7},{1,0},{2,1},{3,2},{4,3},{5,4},{6,5},{7,6},{8,15},{9,8},{10,9... | collective-permute-start | bytes 884744 | tf_op jit(solution)/shard_map/ppermute | solution.py:66
  108.0 7.5 %collective-permute-done.15.refs_5_ = bf16[288,512]{1,0:T(8,128)(2,1)} collective-permute-done((bf16[288,512]{1,0:T(8,128)(2,1)}, bf16[288,512]{1,0:T(8,128)(2,1)}, u32[]{:S(2)}, u32[]{:S(2)}) %collective-permute-start.15) | collective-permute-done | bytes 294944 | tf_op jit(solution)/shard_map/ppermute | solution.py:66
  115.5 3.3 %collective-permute-done.14.refs_4_ = bf16[288,512]{1,0:T(8,128)(2,1)} collective-permute-done((bf16[288,512]{1,0:T(8,128)(2,1)}, bf16[288,512]{1,0:T(8,128)(2,1)}, u32[]{:S(2)}, u32[]{:S(2)}) %collective-permute-start.14) | collective-permute-done | bytes 294944 | tf_op jit(solution)/shard_map/ppermute | solution.py:66
  118.8 1.1 copy-done.2
  119.9 1.1 copy-done.4
  120.9 1.1 copy-done.6
  122.0 1.1 copy-done.8
  123.1 1.1 copy-done.10
  124.1 2.4 %scale_grads.1.s_ref = bf16[4,4,288,512]{3,2,1,0:T(8,128)(2,1)S(1)} custom-call(s32[2]{0:T(128)S(1)} %pad_add_fusion.place_ref, f32[8]{0:T(128)S(1)} %reshape.26.clip_ref, bf16[2,288,512]{2,1,0:T(8,128)(2,1)S(1)} %copy-done.2, bf16[2,288,512]{2,1,0:T(8,128)(2,1)} %collective-permute-done.5.refs_1_, bf16[2,288,512]{2,1,0:T(8,128)(2,1)S(1)} %copy-done.8, ...), custom_call_target="tpu_custom_call" | custom-call | flops 2359296 | bytes 147456 | tf_op jit(solution)/shard_map/scale_grads/pallas_call | solution.py:94
  126.6 5.3 %product_far.1 = (bf16[144,2304]{1,0:T(8,128)(2,1)S(1)}, bf16[144,2304]{1,0:T(8,128)(2,1)S(1)}) custom-call(bf16[4,4,288,512]{3,2,1,0:T(8,128)(2,1)S(1)} %scale_grads.1.s_ref, bf16[512,2304]{1,0:T(8,128)(2,1)S(1)} %bitcast.46, bf16[512,2304]{1,0:T(8,128)(2,1)} %collective-permute-done.16.refs_1_, bf16[256,2304]{1,0:T(8,128)(2,1)S(1)} %collective-permute-done.9.refs_2_, ...), custom_call_target="tpu_custom_call" | custom-call | flops 1327104 | bytes 1327104 | tf_op jit(solution)/shard_map/product_far/pallas_call | solution.py:130
  131.9 1.7 collective-permute-start.19
  133.6 1.7 collective-permute-start.20
  135.2 7.9 %product_near.1 = (bf16[144,2304]{1,0:T(8,128)(2,1)S(1)}, bf16[144,2304]{1,0:T(8,128)(2,1)S(1)}, bf16[144,2304]{1,0:T(8,128)(2,1)S(1)}, bf16[144,2304]{1,0:T(8,128)(2,1)S(1)}) custom-call(bf16[4,4,288,512]{3,2,1,0:T(8,128)(2,1)S(1)} %scale_grads.1.s_ref, bf16[512,2304]{1,0:T(8,128)(2,1)S(1)} %bitcast.47, bf16[512,2304]{1,0:T(8,128)(2,1)} %collective-permute-done.16.refs_1_, ...), custom_call_target="tpu_custom_call" | custom-call | flops 2654208 | bytes 1327104 | tf_op jit(solution)/shard_map/product_near/pallas_call | solution.py:130
  143.1 1.9 %collective-permute-start.22 = (bf16[144,2304]{1,0:T(8,128)(2,1)S(1)}, bf16[144,2304]{1,0:T(8,128)(2,1)S(1)}, u32[]{:S(2)}, u32[]{:S(2)}) collective-permute-start(bf16[144,2304]{1,0:T(8,128)(2,1)S(1)} %get-tuple-element.56), channel_id=1, source_target_pairs={{0,192},{1,193},{2,194},{3,195},{4,196},{5,197},{6,198},{7,199},{8... | collective-permute-start | bytes 1990664 | tf_op jit(solution)/shard_map/ppermute | solution.py:66
  145.0 4.3 %collective-permute-done.19 = bf16[144,2304]{1,0:T(8,128)(2,1)S(1)} collective-permute-done((bf16[144,2304]{1,0:T(8,128)(2,1)S(1)}, bf16[144,2304]{1,0:T(8,128)(2,1)S(1)}, u32[]{:S(2)}, u32[]{:S(2)}) %collective-permute-start.19) | collective-permute-done | bytes 663584 | tf_op jit(solution)/shard_map/ppermute | solution.py:66
  149.3 0.2 add_convert_fusion.1
  149.5 1.9 %collective-permute-done.20 = bf16[144,2304]{1,0:T(8,128)(2,1)S(1)} collective-permute-done((bf16[144,2304]{1,0:T(8,128)(2,1)S(1)}, bf16[144,2304]{1,0:T(8,128)(2,1)S(1)}, u32[]{:S(2)}, u32[]{:S(2)}) %collective-permute-start.20) | collective-permute-done | bytes 663584 | tf_op jit(solution)/shard_map/ppermute | solution.py:66
  151.4 0.2 add_convert_fusion
  151.6 1.7 collective-permute-start.21
  153.2 1.3 collective-permute-start.23
  154.5 2.0 %collective-permute-start.24 = (bf16[144,2304]{1,0:T(8,128)(2,1)S(1)}, bf16[144,2304]{1,0:T(8,128)(2,1)S(1)}, u32[]{:S(2)}, u32[]{:S(2)}) collective-permute-start(bf16[144,2304]{1,0:T(8,128)(2,1)S(1)} %add_convert_fusion), channel_id=1, source_target_pairs={{0,192},{1,193},{2,194},{3,195},{4,196},{5,197},{6,198},{7,199},{8... | collective-permute-start | bytes 1990664 | tf_op jit(solution)/shard_map/ppermute | solution.py:66
  156.4 5.4 %product_own.1 = f32[288,2304]{1,0:T(8,128)S(1)} custom-call(bf16[4,4,288,512]{3,2,1,0:T(8,128)(2,1)S(1)} %scale_grads.1.s_ref, bf16[512,2304]{1,0:T(8,128)(2,1)S(1)} %bitcast.48, bf16[512,2304]{1,0:T(8,128)(2,1)} %collective-permute-done.16.refs_1_, bf16[256,2304]{1,0:T(8,128)(2,1)S(1)} %collective-permute-done.9.refs_2_, ...), custom_call_target="tpu_custom_call" | custom-call | flops 1327104 | bytes 1327104 | tf_op jit(solution)/shard_map/product_own/pallas_call | solution.py:130
  161.8 3.8 %collective-permute-done.22 = bf16[144,2304]{1,0:T(8,128)(2,1)S(1)} collective-permute-done((bf16[144,2304]{1,0:T(8,128)(2,1)S(1)}, bf16[144,2304]{1,0:T(8,128)(2,1)S(1)}, u32[]{:S(2)}, u32[]{:S(2)}) %collective-permute-start.22) | collective-permute-done | bytes 663584 | tf_op jit(solution)/shard_map/ppermute | solution.py:66
  165.6 5.1 %collective-permute-done.21 = bf16[144,2304]{1,0:T(8,128)(2,1)S(1)} collective-permute-done((bf16[144,2304]{1,0:T(8,128)(2,1)S(1)}, bf16[144,2304]{1,0:T(8,128)(2,1)S(1)}, u32[]{:S(2)}, u32[]{:S(2)}) %collective-permute-start.21) | collective-permute-done | bytes 663584 | tf_op jit(solution)/shard_map/ppermute | solution.py:66
  170.7 0.1 convert_add_fusion.1
  170.8 9.5 %collective-permute-done.23 = bf16[144,2304]{1,0:T(8,128)(2,1)S(1)} collective-permute-done((bf16[144,2304]{1,0:T(8,128)(2,1)S(1)}, bf16[144,2304]{1,0:T(8,128)(2,1)S(1)}, u32[]{:S(2)}, u32[]{:S(2)}) %collective-permute-start.23) | collective-permute-done | bytes 663584 | tf_op jit(solution)/shard_map/ppermute | solution.py:66
  180.5 2.2 %fusion.2 = f32[288,2304]{1,0:T(8,128)} fusion(f32[288,2304]{1,0:T(8,128)S(1)} %copy-done.12, f32[288,2304]{1,0:T(8,128)S(1)} %product_own.1, f32[144,2304]{1,0:T(8,128)S(1)} %convert_add_fusion, f32[144,2304]{1,0:T(8,128)S(1)} %convert_add_fusion.1), kind=kLoop, calls=%fused_computation.3 | loop fusion | flops 3317760 | bytes 10616832 | tf_op jit(solution)/shard_map/div | solution.py:226
  (55 shorter events, 1.2 us)
Async XLA Ops:
  0.0 3.3 %copy-start.11 = (bf16[2,256,288]{1,2,0:T(8,128)(2,1)S(1)}, bf16[2,256,288]{1,2,0:T(8,128)(2,1)}, u32[]{:S(2)}) copy-start(bf16[2,256,288]{1,2,0:T(8,128)(2,1)} %param.6) | copy-start | bytes 884740
  3.7 13.9 %copy-start = (bf16[2,256,2304]{2,1,0:T(8,128)(2,1)S(1)}, bf16[2,256,2304]{2,1,0:T(8,128)(2,1)}, u32[]{:S(2)}) copy-start(bf16[2,256,2304]{2,1,0:T(8,128)(2,1)} %param.5) | copy-start | bytes 7077892
  3.8 13.7 %collective-permute-start.2 = (bf16[2,3,2,64,128]{4,3,2,1,0:T(8,128)(2,1)S(1)}, bf16[2,3,2,64,128]{4,3,2,1,0:T(8,128)(2,1)S(1)}, u32[]{:S(2)}, u32[]{:S(2)}) collective-permute-start(bf16[2,3,2,64,128]{4,3,2,1,0:T(8,128)(2,1)S(1)} %broadcast_select_fusion), channel_id=1, source_target_pairs={{0,8},{1,9},{2,10},{3,11},{4,12},{5,13},{6,14},{7,15},{8,0},{9,1},... | collective-permute-start | bytes 589832 | tf_op jit(solution)/shard_map/ppermute | solution.py:66
  5.4 12.2 %collective-permute-start.1 = (bf16[288,512]{1,0:T(8,128)(2,1)S(1)}, bf16[288,512]{1,0:T(8,128)(2,1)S(1)}, u32[]{:S(2)}, u32[]{:S(2)}) collective-permute-start(bf16[288,512]{1,0:T(8,128)(2,1)S(1)} %bitcast.50), channel_id=1, source_target_pairs={{0,8},{1,26},{2,44},{3,58},{4,12},{5,30},{6,40},{7,62},{8,0},{9,18... | collective-permute-start | bytes 884744 | tf_op jit(solution)/shard_map/ppermute | solution.py:66
  6.6 11.0 %collective-permute-start = (bf16[288,512]{1,0:T(8,128)(2,1)S(1)}, bf16[288,512]{1,0:T(8,128)(2,1)S(1)}, u32[]{:S(2)}, u32[]{:S(2)}) collective-permute-start(bf16[288,512]{1,0:T(8,128)(2,1)S(1)} %bitcast.51), channel_id=1, source_target_pairs={{0,0},{1,18},{2,36},{3,50},{4,4},{5,22},{6,32},{7,54},{8,8},{9,26}... | collective-permute-start | bytes 884744 | tf_op jit(solution)/shard_map/ppermute | solution.py:66
  17.6 16.1 %copy-start.13 = (f32[2,8]{1,0:T(2,128)S(1)}, f32[2,8]{1,0:T(2,128)}, u32[]{:S(2)}) copy-start(f32[2,8]{1,0:T(2,128)} %param.7) | copy-start | bytes 196
  17.6 24.6 %copy-start.14 = (f32[3]{0:T(128)S(1)}, f32[3]{0:T(128)}, u32[]{:S(2)}) copy-start(f32[3]{0:T(128)} %constant.37.clone) | copy-start | bytes 40
  19.2 37.5 %collective-permute-start.4 = (bf16[256,2304]{1,0:T(8,128)(2,1)}, bf16[256,2304]{1,0:T(8,128)(2,1)}, u32[]{:S(2)}, u32[]{:S(2)}) collective-permute-start(bf16[256,2304]{1,0:T(8,128)(2,1)} %get-tuple-element.59), channel_id=1, source_target_pairs={{0,40},{1,41},{2,42},{3,43},{4,44},{5,45},{6,46},{7,47},{8,0},{9,1... | collective-permute-start | bytes 3538952 | tf_op jit(solution)/shard_map/ppermute | solution.py:66
  23.6 33.1 %collective-permute-start.3 = (bf16[256,2304]{1,0:T(8,128)(2,1)}, bf16[256,2304]{1,0:T(8,128)(2,1)}, u32[]{:S(2)}, u32[]{:S(2)}) collective-permute-start(bf16[256,2304]{1,0:T(8,128)(2,1)} %get-tuple-element.60), channel_id=1, source_target_pairs={{0,8},{1,9},{2,10},{3,11},{4,12},{5,13},{6,14},{7,15},{8,32},{9,33... | collective-permute-start | bytes 3538952 | tf_op jit(solution)/shard_map/ppermute | solution.py:66
  24.3 17.9 %all-to-all-start = ((bf16[8,2,3,2,8,128]{5,4,3,2,1,0:T(8,128)(2,1)}), bf16[8,2,3,2,8,128]{5,4,3,2,1,0:T(8,128)(2,1)S(1)}, u32[]{:S(2)}, u32[]{:S(2)}) async-start(bf16[8,2,3,2,8,128]{5,4,3,2,1,0:T(8,128)(2,1)} %copy_bitcast_fusion), calls=%async_computation | async-start | bytes 393216 | tf_op jit(solution)/shard_map/all_to_all | solution.py:148
  43.0 10.7 %all-to-all-start.1 = ((f32[8,1,2]{2,1,0:T(1,128)}), f32[8,1,2]{2,1,0:T(1,128)S(1)}, u32[]{:S(2)}, u32[]{:S(2)}) async-start(f32[8,1,2]{2,1,0:T(1,128)} %broadcast_in_dim.7), calls=%async_computation.1 | async-start | bytes 8192 | tf_op jit(solution)/shard_map/all_to_all | solution.py:148
  53.8 17.0 %collective-permute-start.6 = (bf16[2,288,512]{2,1,0:T(8,128)(2,1)S(1)}, bf16[2,288,512]{2,1,0:T(8,128)(2,1)}, u32[]{:S(2)}, u32[]{:S(2)}) collective-permute-start(bf16[2,288,512]{2,1,0:T(8,128)(2,1)S(1)} %pad_maximum_fusion.refs_0_), channel_id=1, source_target_pairs={{0,7},{1,0},{2,1},{3,2},{4,3},{5,4},{6,5},{7,6},{8,15},{9,8},{10,9... | collective-permute-start | bytes 1769480 | tf_op jit(solution)/shard_map/ppermute | solution.py:66
  55.3 15.8 %collective-permute-start.5 = (bf16[2,288,512]{2,1,0:T(8,128)(2,1)S(1)}, bf16[2,288,512]{2,1,0:T(8,128)(2,1)}, u32[]{:S(2)}, u32[]{:S(2)}) collective-permute-start(bf16[2,288,512]{2,1,0:T(8,128)(2,1)S(1)} %pad_maximum_fusion.refs_0_), channel_id=1, source_target_pairs={{0,1},{1,2},{2,3},{3,4},{4,5},{5,6},{6,7},{7,0},{8,9},{9,10},{10,1... | collective-permute-start | bytes 1769480 | tf_op jit(solution)/shard_map/ppermute | solution.py:66
  55.9 0.8 copy-start.1
  56.7 3.5 %collective-permute-start.7 = (f32[2]{0:T(128)S(1)}, f32[2]{0:T(128)S(1)}, u32[]{:S(2)}, u32[]{:S(2)}) collective-permute-start(f32[2]{0:T(128)S(1)} %reduce_sum.39), channel_id=1, source_target_pairs={{0,8},{1,9},{2,10},{3,11},{4,12},{5,13},{6,14},{7,15},{8,0},{9,1},... | collective-permute-start | bytes 32 | tf_op jit(solution)/shard_map/ppermute | solution.py:66
  71.1 15.4 %collective-permute-start.8 = (bf16[2,288,512]{2,1,0:T(8,128)(2,1)}, bf16[2,288,512]{2,1,0:T(8,128)(2,1)S(1)}, u32[]{:S(2)}, u32[]{:S(2)}) collective-permute-start(bf16[2,288,512]{2,1,0:T(8,128)(2,1)} %collective-permute-done.5.refs_1_), channel_id=1, source_target_pairs={{0,1},{1,2},{2,3},{3,4},{4,5},{5,6},{6,7},{7,0},{8,9},{9,10},{10,1... | collective-permute-start | bytes 1769480 | tf_op jit(solution)/shard_map/ppermute | solution.py:66
  71.7 16.0 %collective-permute-start.12 = (bf16[2,288,512]{2,1,0:T(8,128)(2,1)}, bf16[2,288,512]{2,1,0:T(8,128)(2,1)S(1)}, u32[]{:S(2)}, u32[]{:S(2)}) collective-permute-start(bf16[2,288,512]{2,1,0:T(8,128)(2,1)} %collective-permute-done.6.refs_8_), channel_id=1, source_target_pairs={{0,7},{1,0},{2,1},{3,2},{4,3},{5,4},{6,5},{7,6},{8,15},{9,8},{10,9... | collective-permute-start | bytes 1769480 | tf_op jit(solution)/shard_map/ppermute | solution.py:66
  73.2 28.8 %collective-permute-start.9 = (bf16[256,2304]{1,0:T(8,128)(2,1)}, bf16[256,2304]{1,0:T(8,128)(2,1)S(1)}, u32[]{:S(2)}, u32[]{:S(2)}) collective-permute-start(bf16[256,2304]{1,0:T(8,128)(2,1)} %collective-permute-done.3), channel_id=1, source_target_pairs={{0,8},{1,9},{2,10},{3,11},{4,12},{5,13},{6,14},{7,15},{8,32},{9,33... | collective-permute-start | bytes 3538952 | tf_op jit(solution)/shard_map/ppermute | solution.py:66
  74.3 27.6 %collective-permute-start.10 = (bf16[256,2304]{1,0:T(8,128)(2,1)}, bf16[256,2304]{1,0:T(8,128)(2,1)}, u32[]{:S(2)}, u32[]{:S(2)}) collective-permute-start(bf16[256,2304]{1,0:T(8,128)(2,1)} %collective-permute-done.4), channel_id=1, source_target_pairs={{0,40},{1,41},{2,42},{3,43},{4,44},{5,45},{6,46},{7,47},{8,0},{9,1... | collective-permute-start | bytes 3538952 | tf_op jit(solution)/shard_map/ppermute | solution.py:66
  76.4 50.1 %collective-permute-start.16 = (bf16[512,2304]{1,0:T(8,128)(2,1)S(1)}, bf16[512,2304]{1,0:T(8,128)(2,1)}, u32[]{:S(2)}, u32[]{:S(2)}) collective-permute-start(bf16[512,2304]{1,0:T(8,128)(2,1)S(1)} %bitcast.45), channel_id=1, source_target_pairs={{0,16},{1,17},{2,18},{3,19},{4,20},{5,21},{6,22},{7,23},{8,24},{9,... | collective-permute-start | bytes 7077896 | tf_op jit(solution)/shard_map/ppermute | solution.py:66
  86.5 15.4 %collective-permute-start.11 = (bf16[2,288,512]{2,1,0:T(8,128)(2,1)S(1)}, bf16[2,288,512]{2,1,0:T(8,128)(2,1)S(1)}, u32[]{:S(2)}, u32[]{:S(2)}) collective-permute-start(bf16[2,288,512]{2,1,0:T(8,128)(2,1)S(1)} %collective-permute-done.8.refs_2_), channel_id=1, source_target_pairs={{0,1},{1,2},{2,3},{3,4},{4,5},{5,6},{6,7},{7,0},{8,9},{9,10},{10,1... | collective-permute-start | bytes 1769480 | tf_op jit(solution)/shard_map/ppermute | solution.py:66
  86.9 0.8 copy-start.7
  87.7 14.2 %collective-permute-start.13 = (bf16[2,288,512]{2,1,0:T(8,128)(2,1)S(1)}, bf16[2,288,512]{2,1,0:T(8,128)(2,1)S(1)}, u32[]{:S(2)}, u32[]{:S(2)}) collective-permute-start(bf16[2,288,512]{2,1,0:T(8,128)(2,1)S(1)} %collective-permute-done.12.refs_7_), channel_id=1, source_target_pairs={{0,7},{1,0},{2,1},{3,2},{4,3},{5,4},{6,5},{7,6},{8,15},{9,8},{10,9... | collective-permute-start | bytes 1769480 | tf_op jit(solution)/shard_map/ppermute | solution.py:66
  90.3 0.9 copy-start.9
  102.0 1.3 copy-start.5
  102.0 24.6 %collective-permute-start.17 = (bf16[256,2304]{1,0:T(8,128)(2,1)S(1)}, bf16[256,2304]{1,0:T(8,128)(2,1)}, u32[]{:S(2)}, u32[]{:S(2)}) collective-permute-start(bf16[256,2304]{1,0:T(8,128)(2,1)S(1)} %collective-permute-done.9.refs_2_), channel_id=1, source_target_pairs={{0,16},{1,17},{2,18},{3,19},{4,20},{5,21},{6,22},{7,23},{8,24},{9,... | collective-permute-start | bytes 3538952 | tf_op jit(solution)/shard_map/ppermute | solution.py:66
  102.1 24.5 %collective-permute-start.18 = (bf16[256,2304]{1,0:T(8,128)(2,1)}, bf16[256,2304]{1,0:T(8,128)(2,1)}, u32[]{:S(2)}, u32[]{:S(2)}) collective-permute-start(bf16[256,2304]{1,0:T(8,128)(2,1)} %collective-permute-done.10.refs_3_), channel_id=1, source_target_pairs={{0,16},{1,17},{2,18},{3,19},{4,20},{5,21},{6,22},{7,23},{8,24},{9,... | collective-permute-start | bytes 3538952 | tf_op jit(solution)/shard_map/ppermute | solution.py:66
  103.3 0.8 copy-start.3
  104.9 10.7 %collective-permute-start.15 = (bf16[288,512]{1,0:T(8,128)(2,1)}, bf16[288,512]{1,0:T(8,128)(2,1)}, u32[]{:S(2)}, u32[]{:S(2)}) collective-permute-start(bf16[288,512]{1,0:T(8,128)(2,1)} %slice_bitcast_fusion), channel_id=1, source_target_pairs={{0,7},{1,0},{2,1},{3,2},{4,3},{5,4},{6,5},{7,6},{8,15},{9,8},{10,9... | collective-permute-start | bytes 884744 | tf_op jit(solution)/shard_map/ppermute | solution.py:66
  107.8 11.0 %collective-permute-start.14 = (bf16[288,512]{1,0:T(8,128)(2,1)}, bf16[288,512]{1,0:T(8,128)(2,1)}, u32[]{:S(2)}, u32[]{:S(2)}) collective-permute-start(bf16[288,512]{1,0:T(8,128)(2,1)} %slice_bitcast_fusion.1), channel_id=1, source_target_pairs={{0,1},{1,2},{2,3},{3,4},{4,5},{5,6},{6,7},{7,0},{8,9},{9,10},{10,1... | collective-permute-start | bytes 884744 | tf_op jit(solution)/shard_map/ppermute | solution.py:66
  118.8 1.1 copy-start.2
  119.9 1.1 copy-start.4
  120.9 1.1 copy-start.6
  122.0 1.1 copy-start.8
  123.1 1.1 copy-start.10
  131.9 17.4 %collective-permute-start.19 = (bf16[144,2304]{1,0:T(8,128)(2,1)S(1)}, bf16[144,2304]{1,0:T(8,128)(2,1)S(1)}, u32[]{:S(2)}, u32[]{:S(2)}) collective-permute-start(bf16[144,2304]{1,0:T(8,128)(2,1)S(1)} %get-tuple-element.51), channel_id=1, source_target_pairs={{0,64},{1,65},{2,66},{3,67},{4,68},{5,69},{6,70},{7,71},{8,72},{9,... | collective-permute-start | bytes 1990664 | tf_op jit(solution)/shard_map/ppermute | solution.py:66
  133.6 17.8 %collective-permute-start.20 = (bf16[144,2304]{1,0:T(8,128)(2,1)S(1)}, bf16[144,2304]{1,0:T(8,128)(2,1)S(1)}, u32[]{:S(2)}, u32[]{:S(2)}) collective-permute-start(bf16[144,2304]{1,0:T(8,128)(2,1)S(1)} %get-tuple-element.53), channel_id=1, source_target_pairs={{0,192},{1,193},{2,194},{3,195},{4,196},{5,197},{6,198},{7,199},{8... | collective-permute-start | bytes 1990664 | tf_op jit(solution)/shard_map/ppermute | solution.py:66
  143.1 22.5 %collective-permute-start.22 = (bf16[144,2304]{1,0:T(8,128)(2,1)S(1)}, bf16[144,2304]{1,0:T(8,128)(2,1)S(1)}, u32[]{:S(2)}, u32[]{:S(2)}) collective-permute-start(bf16[144,2304]{1,0:T(8,128)(2,1)S(1)} %get-tuple-element.56), channel_id=1, source_target_pairs={{0,192},{1,193},{2,194},{3,195},{4,196},{5,197},{6,198},{7,199},{8... | collective-permute-start | bytes 1990664 | tf_op jit(solution)/shard_map/ppermute | solution.py:66
  151.6 19.1 %collective-permute-start.21 = (bf16[144,2304]{1,0:T(8,128)(2,1)S(1)}, bf16[144,2304]{1,0:T(8,128)(2,1)S(1)}, u32[]{:S(2)}, u32[]{:S(2)}) collective-permute-start(bf16[144,2304]{1,0:T(8,128)(2,1)S(1)} %add_convert_fusion.1), channel_id=1, source_target_pairs={{0,64},{1,65},{2,66},{3,67},{4,68},{5,69},{6,70},{7,71},{8,72},{9,... | collective-permute-start | bytes 1990664 | tf_op jit(solution)/shard_map/ppermute | solution.py:66
  153.2 27.2 %collective-permute-start.23 = (bf16[144,2304]{1,0:T(8,128)(2,1)S(1)}, bf16[144,2304]{1,0:T(8,128)(2,1)S(1)}, u32[]{:S(2)}, u32[]{:S(2)}) collective-permute-start(bf16[144,2304]{1,0:T(8,128)(2,1)S(1)} %get-tuple-element.57), channel_id=1, source_target_pairs={{0,64},{1,65},{2,66},{3,67},{4,68},{5,69},{6,70},{7,71},{8,72},{9,... | collective-permute-start | bytes 1990664 | tf_op jit(solution)/shard_map/ppermute | solution.py:66
  154.5 25.9 %collective-permute-start.24 = (bf16[144,2304]{1,0:T(8,128)(2,1)S(1)}, bf16[144,2304]{1,0:T(8,128)(2,1)S(1)}, u32[]{:S(2)}, u32[]{:S(2)}) collective-permute-start(bf16[144,2304]{1,0:T(8,128)(2,1)S(1)} %add_convert_fusion), channel_id=1, source_target_pairs={{0,192},{1,193},{2,194},{3,195},{4,196},{5,197},{6,198},{7,199},{8... | collective-permute-start | bytes 1990664 | tf_op jit(solution)/shard_map/ppermute | solution.py:66
  170.8 9.7 %copy-start.12 = (f32[288,2304]{1,0:T(8,128)S(1)}, f32[288,2304]{1,0:T(8,128)}, u32[]{:S(2)}) copy-start(f32[288,2304]{1,0:T(8,128)} %param.8) | copy-start | bytes 7962628

commit v5 on v4

--- a/solution.py
+++ b/solution.py
@@ -67,35 +67,48 @@
 
 
 def scale_kernel(place_ref, clip_ref, *refs):
-    pieces, out_ref = refs[:-1], refs[-1]
+    pieces, out_ref, held_ref, arrived = refs[:-3], refs[-3], refs[-2], refs[-1]
     dp, te = place_ref[0], place_ref[1]
     y, xh, c, xl, z = dp // 4, (dp // 2) % 2, dp % 2, te // NZ, te % NZ
     half = out_ref.shape[3] // 2
+    copies = []
+    for i, piece in enumerate(pieces):
+        if i in (4, 5):
+            place = held_ref.at[4 + i]
+        else:
+            place = held_ref.at[pl.ds(2 * (i - (i > 5)), 2)]
+        copies.append(pltpu.make_async_copy(piece, place, arrived.at[i]))
+    for copy in copies:
+        copy.start()
     for r in range(NZ):
         q = (z - r - 2 * xh - c + 2 * NZ) % NZ
         m = q % 4
         k = ((q + 1) // 4) % 2
+        member = 2 * (xh ^ (m // 2)) + (c ^ (m % 2))
+        for copy in copies[4:6] if r == 4 else [copies[r + (r > 4)]]:
+            copy.wait()
         for f in range(2):
             step = (2 * ((f + xl) % 2) + k - y + 4) % 4
             slot = jnp.where(step == 0, 3, jnp.where(step == 1, 0, jnp.where(step == 2, 2, 1)))
-            block = pieces[4 + f] if r == 4 else pieces[r + (r > 4)].at[f]
-            member = (2 * (xh ^ (m // 2)) + (c ^ (m % 2)))
             for e in range(2):
                 cols = slice(e * half, (e + 1) * half)
                 out_ref[slot, m, :, cols] = (
-                    clip_ref[2 * member + e] * block[:, cols].astype(F32)
+                    clip_ref[2 * member + e] * held_ref[2 * r + f, :, cols].astype(F32)
                 ).astype(BF)
 
 
 def scale_grads(places, clips, pieces):
     _, rows, tokens = pieces[0].shape
     smem = pl.BlockSpec(memory_space=pltpu.SMEM)
-    vmem = pl.BlockSpec(memory_space=pltpu.VMEM)
     return pl.pallas_call(
         scale_kernel,
         out_shape=jax.ShapeDtypeStruct((4, 4, rows, tokens), BF),
-        in_specs=[smem, smem] + [vmem] * len(pieces),
-        out_specs=vmem,
+        in_specs=[smem, smem] + [pl.BlockSpec(memory_space=pl.ANY)] * len(pieces),
+        out_specs=pl.BlockSpec(memory_space=pltpu.VMEM),
+        scratch_shapes=[
+            pltpu.VMEM((2 * NZ, rows, tokens), BF),
+            pltpu.SemaphoreType.DMA((len(pieces),)),
+        ],
         cost_estimate=pl.CostEstimate(
             flops=16 * rows * tokens, bytes_accessed=rows * tokens, transcendentals=0
         ),
@@ -169,35 +182,34 @@
         return jnp.stack([gram[:, :mid, :mid], gram[:, :mid, mid:], gram[:, mid:, mid:]])
 
     grams = jnp.stack([blocks(acts), blocks(out_grads)])
-    low, high = jnp.split(grams, 2, axis=3)
-    keep, give = jnp.where(xl == 0, low, high), jnp.where(xl == 0, high, low)
-    grams = (keep.astype(F32) + send(give, XLO).astype(F32)).astype(BF)
-    sources, grams, flat = stage((sources, grams, flat))
+    grams = (grams.astype(F32) + send(grams, XLO).astype(F32)).astype(BF)
+    others = jnp.sum(other_sq, axis=1)
+    others = others + send(others, XLO)
+    sources, grams, flat, others = stage((sources, grams, flat, others))
 
     up = send(flat[:seq], along_x(1))
     down = send(flat[seq:], along_x(-1))
     own = jnp.stack(sources)
+    fwd, bwd = [own, send(own, along_z(1))], [own, send(own, along_z(-1))]
     shape = grams.shape
     grams = jnp.moveaxis(grams.reshape(shape[:3] + (NZ, -1, shape[4])), 3, 0)
     grams = all_to_all(grams, "tensor", z_rings).astype(F32).sum(axis=0)
     weight = jnp.array([1.0, 2.0, 1.0], F32)[:, None, None, None]
-    total = jnp.sum(grams[0] * grams[1] * weight, axis=(0, 2, 3)) + jnp.sum(other_sq, axis=1)
+    total = jnp.sum(grams[0] * grams[1] * weight, axis=(0, 2, 3)) + others
+    up, down, fwd[1], bwd[1], total = stage((up, down, fwd[1], bwd[1], total))
+
+    up, down = send(up, along_x(1)), send(down, along_x(-1))
+    fwd.append(send(fwd[1], along_z(1)))
+    bwd.append(send(bwd[1], along_z(-1)))
+    sibling = send(flat, CORE)
     total = all_to_all(jnp.broadcast_to(total, (NZ, examples)), "tensor", z_rings).sum(axis=0)
-    own, total = stage((own, total))
-
-    fwd, bwd = [own, send(own, along_z(1))], [own, send(own, along_z(-1))]
-    up, down, total = stage((up, down, total))
-    total = total + send(total, XLO)
+    fwd[2], bwd[2], total = stage((fwd[2], bwd[2], total))
+
+    fwd.append(send(fwd[2], along_z(1)))
+    bwd.append(send(bwd[2], along_z(-1)))
     clip = jnp.minimum(1.0, clip_norm / jnp.sqrt(total))
     clips = all_to_all(jnp.broadcast_to(clip, (4, examples)), "dp", chip_pairs).reshape(-1)
-    up, down, fwd[1], bwd[1], clips = stage((up, down, fwd[1], bwd[1], clips))
-
-    up, down = send(up, along_x(1)), send(down, along_x(-1))
-    sibling = send(flat, CORE)
-    for _ in range(2):
-        fwd.append(send(fwd[-1], along_z(1)))
-        bwd.append(send(bwd[-1], along_z(-1)))
-    up, down, fwd[3], bwd[3] = stage((up, down, fwd[3], bwd[3]))
+    fwd[3], bwd[3], clips, up, down = stage((fwd[3], bwd[3], clips, up, down))
 
     far = [send(fwd[3][0], along_z(1)), send(bwd[3][1], along_z(-1))]
     up_sibling, down_sibling = send(up, CORE), send(down, CORE)

time: 186 us -> 176 us (0.946)
  blocking collectives: 9.28 us -> 24.9 us
  waiting for transfers between devices: 81.6 us -> 69.6 us
  starting transfers between devices: 49.2 us -> 39.9 us
  local copies, waits for them, and re-layouts: 13.7 us -> 8.26 us
    all_to_all x1 -> x2, blocking collectives: 9.28 us -> 24.9 us  [all_to_all(): lax.all_to_all(value, axis, 0, 0, tiled=True, axis_index_groups=groups)]
    ppermute x25, waiting for transfers between devices: 67.1 us -> 58.3 us  [send(): return lax.ppermute(value, AXES, perm)]
    unnamed x30 -> x14, local copies, waits for them, and re-layouts: 8.66 us -> 1.09 us
    all_to_all x2 -> x1, starting transfers between devices: 13.9 us -> 8.26 us  [all_to_all(): lax.all_to_all(value, axis, 0, 0, tiled=True, axis_index_groups=groups)]
    ppermute x25, starting transfers between devices: 35.2 us -> 31.6 us  [send(): return lax.ppermute(value, AXES, perm)]
    all_to_all x2 -> x1, waiting for transfers between devices: 14.5 us -> 11.4 us  [all_to_all(): lax.all_to_all(value, axis, 0, 0, tiled=True, axis_index_groups=groups)]
    squeeze x2, local copies, waits for them, and re-layouts: 1.48 us -> 3.39 us  [shards(): far = [send(fwd[3][0], along_z(1)), send(bwd[3][1], along_z(-1))]]
  transfers between devices with their start and end apart: 27 -> 26, of which waited for: 15 -> 12; matrix products, arithmetic and copies ran while one was open for 3% -> 5% of each run, Pallas kernels for 9% -> 9%
where the time goes in v5:
time: 176 us; the launch traced here: 173 us
  waiting for transfers between devices  69.6 us (40%)
  starting transfers between devices  39.9 us (23%)
  blocking collectives  24.9 us (14%)
  Pallas kernels  21.6 us (12%)
  local copies, waits for them, and re-layouts  8.26 us (5%)
  other arithmetic  5.19 us (3%)
  matrix products  3.57 us (2%)
    ppermute x25, waiting for transfers between devices, send(): return lax.ppermute(value, AXES, perm)  58.3 us
    ppermute x25, starting transfers between devices, send(): return lax.ppermute(value, AXES, perm)  31.6 us
    all_to_all x2, blocking collectives, all_to_all(): lax.all_to_all(value, axis, 0, 0, tiled=True, axis_index_groups=groups)  24.9 us
    pallas_call x3, Pallas kernels, product(): pl.pallas_call(product_kernel, out_shape=[jax.ShapeDtypeStruct((count, wi...  18.6 us
    all_to_all x1, waiting for transfers between devices, all_to_all(): lax.all_to_all(value, axis, 0, 0, tiled=True, axis_index_groups=groups)  11.4 us
    all_to_all x1, starting transfers between devices, all_to_all(): lax.all_to_all(value, axis, 0, 0, tiled=True, axis_index_groups=groups)  8.26 us
    dot_general x2, matrix products, blocks(): jnp.einsum('btf,bsf->bts', x, x, preferred_element_type=F32).astype(BF)  3.57 us
  transfers between devices with their start and end apart: 26, of which 12 were waited for; matrix products, arithmetic and copies ran while one was open for 5% of the time, Pallas kernels for 9%

profile of v5, /device:TPU:32, one launch (start us, length us, event | category | flops | bytes accessed | tf_op | source)
XLA Modules:
  0.0 173.3 jit_solution(12295992693815435658)
XLA Ops:
  0.0 3.2 %convolution_convert_fusion.1 = bf16[2,256,256]{2,1,0:T(8,128)(2,1)S(1)} fusion(bf16[2,256,2304]{2,1,0:T(8,128)(2,1)} %param.5), kind=kOutput, calls=%fused_computation.9 | convolution fusion | flops 604110848 | bytes 2621440 | tf_op jit(solution)/shard_map/btf,bsf->bts/dot_general | solution.py:180
  3.3 0.4 convolution_convert_fusion
  3.6 0.0 copy-start.5
  3.8 1.6 collective-permute-start.2
  5.4 0.7 copy.16
  6.1 1.1 collective-permute-start.1
  7.2 4.1 %collective-permute-start = (bf16[288,512]{1,0:T(8,128)(2,1)}, bf16[288,512]{1,0:T(8,128)(2,1)}, u32[]{:S(2)}, u32[]{:S(2)}) collective-permute-start(bf16[288,512]{1,0:T(8,128)(2,1)} %bitcast.2), channel_id=1, source_target_pairs={{0,0},{1,18},{2,36},{3,50},{4,4},{5,22},{6,32},{7,54},{8,8},{9,26}... | collective-permute-start | bytes 884744 | tf_op jit(solution)/shard_map/ppermute | solution.py:66
  11.3 0.1 reduce_sum.36
  11.4 0.7 collective-permute-start.3
  12.1 13.3 %collective-permute-done.3 = f32[2]{0:T(128)S(1)} collective-permute-done((f32[2]{0:T(128)S(1)}, f32[2]{0:T(128)S(1)}, u32[]{:S(2)}, u32[]{:S(2)}) %collective-permute-start.3) | collective-permute-done | bytes 40 | tf_op jit(solution)/shard_map/ppermute | solution.py:66
  25.5 0.1 add_convert_fusion.2
  25.6 1.6 fusion.6
  27.2 2.0 %collective-permute-start.4 = (bf16[256,2304]{1,0:T(8,128)(2,1)}, bf16[256,2304]{1,0:T(8,128)(2,1)}, u32[]{:S(2)}, u32[]{:S(2)}) collective-permute-start(bf16[256,2304]{1,0:T(8,128)(2,1)} %get-tuple-element.60), channel_id=1, source_target_pairs={{0,8},{1,9},{2,10},{3,11},{4,12},{5,13},{6,14},{7,15},{8,32},{9,33... | collective-permute-start | bytes 3538952 | tf_op jit(solution)/shard_map/ppermute | solution.py:66
  29.2 0.8 copy.18
  30.0 8.3 %all-to-all-start = ((bf16[8,2,3,2,16,128]{5,4,3,2,1,0:T(8,128)(2,1)}), bf16[8,2,3,2,16,128]{5,4,3,2,1,0:T(8,128)(2,1)S(1)}, u32[]{:S(2)}, u32[]{:S(2)}) async-start(bf16[8,2,3,2,16,128]{5,4,3,2,1,0:T(8,128)(2,1)} %bitcast.42), calls=%async_computation | async-start | bytes 786432 | tf_op jit(solution)/shard_map/all_to_all | solution.py:161
  38.3 1.1 pad_maximum_fusion.refs_0_
  39.4 0.1 collective-permute-start.7
  39.5 2.0 %collective-permute-start.6 = (bf16[2,288,512]{2,1,0:T(8,128)(2,1)S(1)}, bf16[2,288,512]{2,1,0:T(8,128)(2,1)}, u32[]{:S(2)}, u32[]{:S(2)}) collective-permute-start(bf16[2,288,512]{2,1,0:T(8,128)(2,1)S(1)} %pad_maximum_fusion.refs_0_), channel_id=1, source_target_pairs={{0,1},{1,2},{2,3},{3,4},{4,5},{5,6},{6,7},{7,0},{8,9},{9,10},{10,1... | collective-permute-start | bytes 1769480 | tf_op jit(solution)/shard_map/ppermute | solution.py:66
  41.5 11.4 %all-to-all-done = bf16[8,2,3,2,16,128]{5,4,3,2,1,0:T(8,128)(2,1)S(1)} async-done(((bf16[8,2,3,2,16,128]{5,4,3,2,1,0:T(8,128)(2,1)}), bf16[8,2,3,2,16,128]{5,4,3,2,1,0:T(8,128)(2,1)S(1)}, u32[]{:S(2)}, u32[]{:S(2)}) %all-to-all-start) | async-done | bytes 393248 | tf_op jit(solution)/shard_map/all_to_all | solution.py:161
  52.9 0.1 convert_reduce_fusion
  52.9 0.2 fusion.5
  53.1 9.4 %collective-permute-done.7.refs_8_ = bf16[2,288,512]{2,1,0:T(8,128)(2,1)} collective-permute-done((bf16[2,288,512]{2,1,0:T(8,128)(2,1)S(1)}, bf16[2,288,512]{2,1,0:T(8,128)(2,1)}, u32[]{:S(2)}, u32[]{:S(2)}) %collective-permute-start.7) | collective-permute-done | bytes 589856 | tf_op jit(solution)/shard_map/ppermute | solution.py:66
  62.5 1.5 collective-permute-start.8
  64.0 0.6 collective-permute-start.9
  64.6 1.6 collective-permute-start.12
  66.2 1.6 collective-permute-start.13
  67.8 14.8 %all_to_all.17 = f32[8,1,2]{2,1,0:T(1,128)S(1)} all-to-all(f32[8,1,2]{2,1,0:T(1,128)S(1)} %broadcast_in_dim.7), channel_id=1, replica_groups={{0,1,2,3,4,5,6,7},{8,9,10,11,12,13,14,15},{16,17,18,19,20,21,22,23},{24..., dimensions={0} | all-to-all | bytes 128 | tf_op jit(solution)/shard_map/all_to_all | solution.py:161
  82.7 0.6 collective-permute-start.10
  83.4 1.5 collective-permute-start.11
  84.9 10.0 %all_to_all.18 = f32[4,1,2]{2,1,0:T(1,128)S(1)} all-to-all(f32[4,1,2]{2,1,0:T(1,128)S(1)} %broadcast_in_dim.8), channel_id=1, replica_groups={{0,16,32,48},{64,80,96,112},{128,144,160,176},{192,208,224,240},{1,17,3..., dimensions={0} | all-to-all | bytes 64 | tf_op jit(solution)/shard_map/all_to_all | solution.py:161
  94.9 0.5 broadcast.21
  95.4 0.7 reduce.4
  96.1 0.1 reshape.26.clip_ref
  96.1 0.9 collective-permute-done.10.refs_3_
  97.0 0.3 collective-permute-done.11.refs_6_
  97.3 0.5 collective-permute-start.18
  97.8 1.7 slice_bitcast_fusion.1
  99.5 1.7 slice_bitcast_fusion
  101.2 1.8 %collective-permute-start.15 = (bf16[288,512]{1,0:T(8,128)(2,1)}, bf16[288,512]{1,0:T(8,128)(2,1)}, u32[]{:S(2)}, u32[]{:S(2)}) collective-permute-start(bf16[288,512]{1,0:T(8,128)(2,1)} %slice_bitcast_fusion), channel_id=1, source_target_pairs={{0,7},{1,0},{2,1},{3,2},{4,3},{5,4},{6,5},{7,6},{8,15},{9,8},{10,9... | collective-permute-start | bytes 884744 | tf_op jit(solution)/shard_map/ppermute | solution.py:66
  103.0 0.2 collective-permute-start.14
  103.2 0.1 pad_add_fusion.place_ref
  103.3 7.2 %collective-permute-done.15.refs_5_ = bf16[288,512]{1,0:T(8,128)(2,1)} collective-permute-done((bf16[288,512]{1,0:T(8,128)(2,1)}, bf16[288,512]{1,0:T(8,128)(2,1)}, u32[]{:S(2)}, u32[]{:S(2)}) %collective-permute-start.15) | collective-permute-done | bytes 294944 | tf_op jit(solution)/shard_map/ppermute | solution.py:66
  110.5 2.5 %collective-permute-done.14.refs_4_ = bf16[288,512]{1,0:T(8,128)(2,1)} collective-permute-done((bf16[288,512]{1,0:T(8,128)(2,1)}, bf16[288,512]{1,0:T(8,128)(2,1)}, u32[]{:S(2)}, u32[]{:S(2)}) %collective-permute-start.14) | collective-permute-done | bytes 294944 | tf_op jit(solution)/shard_map/ppermute | solution.py:66
  113.0 1.1 copy-done.2
  114.1 3.0 %scale_grads.1.s_ref = bf16[4,4,288,512]{3,2,1,0:T(8,128)(2,1)S(1)} custom-call(s32[2]{0:T(128)S(1)} %pad_add_fusion.place_ref, f32[8]{0:T(128)S(1)} %reshape.26.clip_ref, bf16[2,288,512]{2,1,0:T(8,128)(2,1)S(1)} %copy-done.2, bf16[2,288,512]{2,1,0:T(8,128)(2,1)} %collective-permute-done.6.refs_1_, bf16[2,288,512]{2,1,0:T(8,128)(2,1)} %collective-permute-done.8.refs_2_, ...), custom_call_target="tpu_custom_call" | custom-call | flops 2359296 | bytes 147456 | tf_op jit(solution)/shard_map/scale_grads/pallas_call | solution.py:103
  117.1 5.3 %product_far.1 = (bf16[144,2304]{1,0:T(8,128)(2,1)S(1)}, bf16[144,2304]{1,0:T(8,128)(2,1)S(1)}) custom-call(bf16[4,4,288,512]{3,2,1,0:T(8,128)(2,1)S(1)} %scale_grads.1.s_ref, bf16[512,2304]{1,0:T(8,128)(2,1)S(1)} %bitcast.45, bf16[512,2304]{1,0:T(8,128)(2,1)} %collective-permute-done.16.refs_1_, bf16[256,2304]{1,0:T(8,128)(2,1)S(1)} %collective-permute-done.12.refs_2_, ...), custom_call_target="tpu_custom_call" | custom-call | flops 1327104 | bytes 1327104 | tf_op jit(solution)/shard_map/product_far/pallas_call | solution.py:143
  122.4 1.7 collective-permute-start.19
  124.1 1.7 collective-permute-start.20
  125.8 7.9 %product_near.1 = (bf16[144,2304]{1,0:T(8,128)(2,1)S(1)}, bf16[144,2304]{1,0:T(8,128)(2,1)S(1)}, bf16[144,2304]{1,0:T(8,128)(2,1)S(1)}, bf16[144,2304]{1,0:T(8,128)(2,1)S(1)}) custom-call(bf16[4,4,288,512]{3,2,1,0:T(8,128)(2,1)S(1)} %scale_grads.1.s_ref, bf16[512,2304]{1,0:T(8,128)(2,1)S(1)} %bitcast.46, bf16[512,2304]{1,0:T(8,128)(2,1)} %collective-permute-done.16.refs_1_, ...), custom_call_target="tpu_custom_call" | custom-call | flops 2654208 | bytes 1327104 | tf_op jit(solution)/shard_map/product_near/pallas_call | solution.py:143
  133.6 1.9 %collective-permute-start.22 = (bf16[144,2304]{1,0:T(8,128)(2,1)S(1)}, bf16[144,2304]{1,0:T(8,128)(2,1)S(1)}, u32[]{:S(2)}, u32[]{:S(2)}) collective-permute-start(bf16[144,2304]{1,0:T(8,128)(2,1)S(1)} %get-tuple-element.56), channel_id=1, source_target_pairs={{0,192},{1,193},{2,194},{3,195},{4,196},{5,197},{6,198},{7,199},{8... | collective-permute-start | bytes 1990664 | tf_op jit(solution)/shard_map/ppermute | solution.py:66
  135.5 4.3 %collective-permute-done.19 = bf16[144,2304]{1,0:T(8,128)(2,1)S(1)} collective-permute-done((bf16[144,2304]{1,0:T(8,128)(2,1)S(1)}, bf16[144,2304]{1,0:T(8,128)(2,1)S(1)}, u32[]{:S(2)}, u32[]{:S(2)}) %collective-permute-start.19) | collective-permute-done | bytes 663584 | tf_op jit(solution)/shard_map/ppermute | solution.py:66
  139.9 0.2 add_convert_fusion.1
  140.0 1.9 %collective-permute-done.20 = bf16[144,2304]{1,0:T(8,128)(2,1)S(1)} collective-permute-done((bf16[144,2304]{1,0:T(8,128)(2,1)S(1)}, bf16[144,2304]{1,0:T(8,128)(2,1)S(1)}, u32[]{:S(2)}, u32[]{:S(2)}) %collective-permute-start.20) | collective-permute-done | bytes 663584 | tf_op jit(solution)/shard_map/ppermute | solution.py:66
  141.9 0.2 add_convert_fusion
  142.1 1.7 collective-permute-start.21
  143.8 1.3 collective-permute-start.23
  145.0 2.0 %collective-permute-start.24 = (bf16[144,2304]{1,0:T(8,128)(2,1)S(1)}, bf16[144,2304]{1,0:T(8,128)(2,1)S(1)}, u32[]{:S(2)}, u32[]{:S(2)}) collective-permute-start(bf16[144,2304]{1,0:T(8,128)(2,1)S(1)} %add_convert_fusion), channel_id=1, source_target_pairs={{0,192},{1,193},{2,194},{3,195},{4,196},{5,197},{6,198},{7,199},{8... | collective-permute-start | bytes 1990664 | tf_op jit(solution)/shard_map/ppermute | solution.py:66
  147.0 5.4 %product_own.1 = f32[288,2304]{1,0:T(8,128)S(1)} custom-call(bf16[4,4,288,512]{3,2,1,0:T(8,128)(2,1)S(1)} %scale_grads.1.s_ref, bf16[512,2304]{1,0:T(8,128)(2,1)S(1)} %bitcast.47, bf16[512,2304]{1,0:T(8,128)(2,1)} %collective-permute-done.16.refs_1_, bf16[256,2304]{1,0:T(8,128)(2,1)S(1)} %collective-permute-done.12.refs_2_, ...), custom_call_target="tpu_custom_call" | custom-call | flops 1327104 | bytes 1327104 | tf_op jit(solution)/shard_map/product_own/pallas_call | solution.py:143
  152.4 3.8 %collective-permute-done.22 = bf16[144,2304]{1,0:T(8,128)(2,1)S(1)} collective-permute-done((bf16[144,2304]{1,0:T(8,128)(2,1)S(1)}, bf16[144,2304]{1,0:T(8,128)(2,1)S(1)}, u32[]{:S(2)}, u32[]{:S(2)}) %collective-permute-start.22) | collective-permute-done | bytes 663584 | tf_op jit(solution)/shard_map/ppermute | solution.py:66
  156.2 5.1 %collective-permute-done.21 = bf16[144,2304]{1,0:T(8,128)(2,1)S(1)} collective-permute-done((bf16[144,2304]{1,0:T(8,128)(2,1)S(1)}, bf16[144,2304]{1,0:T(8,128)(2,1)S(1)}, u32[]{:S(2)}, u32[]{:S(2)}) %collective-permute-start.21) | collective-permute-done | bytes 663584 | tf_op jit(solution)/shard_map/ppermute | solution.py:66
  161.2 0.1 convert_add_fusion.1
  161.4 9.5 %collective-permute-done.23 = bf16[144,2304]{1,0:T(8,128)(2,1)S(1)} collective-permute-done((bf16[144,2304]{1,0:T(8,128)(2,1)S(1)}, bf16[144,2304]{1,0:T(8,128)(2,1)S(1)}, u32[]{:S(2)}, u32[]{:S(2)}) %collective-permute-start.23) | collective-permute-done | bytes 663584 | tf_op jit(solution)/shard_map/ppermute | solution.py:66
  170.9 0.1 convert_add_fusion
  171.1 2.2 %fusion.2 = f32[288,2304]{1,0:T(8,128)} fusion(f32[288,2304]{1,0:T(8,128)S(1)} %copy-done.4, f32[288,2304]{1,0:T(8,128)S(1)} %product_own.1, f32[144,2304]{1,0:T(8,128)S(1)} %convert_add_fusion, f32[144,2304]{1,0:T(8,128)S(1)} %convert_add_fusion.1), kind=kLoop, calls=%fused_computation.3 | loop fusion | flops 3317760 | bytes 10616832 | tf_op jit(solution)/shard_map/div | solution.py:238
  (39 shorter events, 0.3 us)
Async XLA Ops:
  0.0 3.3 %copy-start.3 = (bf16[2,256,288]{1,2,0:T(8,128)(2,1)S(1)}, bf16[2,256,288]{1,2,0:T(8,128)(2,1)}, u32[]{:S(2)}) copy-start(bf16[2,256,288]{1,2,0:T(8,128)(2,1)} %param.6) | copy-start | bytes 884740
  3.6 7.7 %copy-start.5 = (f32[2,8]{1,0:T(2,128)S(1)}, f32[2,8]{1,0:T(2,128)}, u32[]{:S(2)}) copy-start(f32[2,8]{1,0:T(2,128)} %param.7) | copy-start | bytes 196
  3.8 21.8 %copy-start = (bf16[2,256,2304]{2,1,0:T(8,128)(2,1)S(1)}, bf16[2,256,2304]{2,1,0:T(8,128)(2,1)}, u32[]{:S(2)}) copy-start(bf16[2,256,2304]{2,1,0:T(8,128)(2,1)} %param.5) | copy-start | bytes 7077892
  3.8 21.6 %collective-permute-start.2 = (bf16[2,3,2,128,128]{4,3,2,1,0:T(8,128)(2,1)S(1)}, bf16[2,3,2,128,128]{4,3,2,1,0:T(8,128)(2,1)S(1)}, u32[]{:S(2)}, u32[]{:S(2)}) collective-permute-start(bf16[2,3,2,128,128]{4,3,2,1,0:T(8,128)(2,1)S(1)} %pad_maximum_fusion.1), channel_id=1, source_target_pairs={{0,8},{1,9},{2,10},{3,11},{4,12},{5,13},{6,14},{7,15},{8,0},{9,1},... | collective-permute-start | bytes 1179656 | tf_op jit(solution)/shard_map/ppermute | solution.py:66
  6.1 19.4 %collective-permute-start.1 = (bf16[288,512]{1,0:T(8,128)(2,1)}, bf16[288,512]{1,0:T(8,128)(2,1)}, u32[]{:S(2)}, u32[]{:S(2)}) collective-permute-start(bf16[288,512]{1,0:T(8,128)(2,1)} %bitcast.2), channel_id=1, source_target_pairs={{0,8},{1,26},{2,44},{3,58},{4,12},{5,30},{6,40},{7,62},{8,0},{9,18... | collective-permute-start | bytes 884744 | tf_op jit(solution)/shard_map/ppermute | solution.py:66
  7.2 18.4 %collective-permute-start = (bf16[288,512]{1,0:T(8,128)(2,1)}, bf16[288,512]{1,0:T(8,128)(2,1)}, u32[]{:S(2)}, u32[]{:S(2)}) collective-permute-start(bf16[288,512]{1,0:T(8,128)(2,1)} %bitcast.2), channel_id=1, source_target_pairs={{0,0},{1,18},{2,36},{3,50},{4,4},{5,22},{6,32},{7,54},{8,8},{9,26}... | collective-permute-start | bytes 884744 | tf_op jit(solution)/shard_map/ppermute | solution.py:66
  11.4 14.0 %collective-permute-start.3 = (f32[2]{0:T(128)S(1)}, f32[2]{0:T(128)S(1)}, u32[]{:S(2)}, u32[]{:S(2)}) collective-permute-start(f32[2]{0:T(128)S(1)} %reduce_sum.36), channel_id=1, source_target_pairs={{0,8},{1,9},{2,10},{3,11},{4,12},{5,13},{6,14},{7,15},{8,0},{9,1},... | collective-permute-start | bytes 32 | tf_op jit(solution)/shard_map/ppermute | solution.py:66
  27.2 35.3 %collective-permute-start.5 = (bf16[256,2304]{1,0:T(8,128)(2,1)}, bf16[256,2304]{1,0:T(8,128)(2,1)}, u32[]{:S(2)}, u32[]{:S(2)}) collective-permute-start(bf16[256,2304]{1,0:T(8,128)(2,1)} %get-tuple-element.59), channel_id=1, source_target_pairs={{0,40},{1,41},{2,42},{3,43},{4,44},{5,45},{6,46},{7,47},{8,0},{9,1... | collective-permute-start | bytes 3538952 | tf_op jit(solution)/shard_map/ppermute | solution.py:66
  27.2 35.3 %collective-permute-start.4 = (bf16[256,2304]{1,0:T(8,128)(2,1)}, bf16[256,2304]{1,0:T(8,128)(2,1)}, u32[]{:S(2)}, u32[]{:S(2)}) collective-permute-start(bf16[256,2304]{1,0:T(8,128)(2,1)} %get-tuple-element.60), channel_id=1, source_target_pairs={{0,8},{1,9},{2,10},{3,11},{4,12},{5,13},{6,14},{7,15},{8,32},{9,33... | collective-permute-start | bytes 3538952 | tf_op jit(solution)/shard_map/ppermute | solution.py:66
  30.0 22.9 %copy-start.6 = (f32[3]{0:T(128)S(1)}, f32[3]{0:T(128)}, u32[]{:S(2)}) copy-start(f32[3]{0:T(128)} %constant.20.clone) | copy-start | bytes 40
  30.0 22.9 %all-to-all-start = ((bf16[8,2,3,2,16,128]{5,4,3,2,1,0:T(8,128)(2,1)}), bf16[8,2,3,2,16,128]{5,4,3,2,1,0:T(8,128)(2,1)S(1)}, u32[]{:S(2)}, u32[]{:S(2)}) async-start(bf16[8,2,3,2,16,128]{5,4,3,2,1,0:T(8,128)(2,1)} %bitcast.42), calls=%async_computation | async-start | bytes 786432 | tf_op jit(solution)/shard_map/all_to_all | solution.py:161
  39.4 24.7 %copy-start.1 = (bf16[2,288,512]{2,1,0:T(8,128)(2,1)}, bf16[2,288,512]{2,1,0:T(8,128)(2,1)S(1)}, u32[]{:S(2)}) copy-start(bf16[2,288,512]{2,1,0:T(8,128)(2,1)S(1)} %pad_maximum_fusion.refs_0_) | copy-start | bytes 1769476
  39.4 23.1 %collective-permute-start.7 = (bf16[2,288,512]{2,1,0:T(8,128)(2,1)S(1)}, bf16[2,288,512]{2,1,0:T(8,128)(2,1)}, u32[]{:S(2)}, u32[]{:S(2)}) collective-permute-start(bf16[2,288,512]{2,1,0:T(8,128)(2,1)S(1)} %pad_maximum_fusion.refs_0_), channel_id=1, source_target_pairs={{0,7},{1,0},{2,1},{3,2},{4,3},{5,4},{6,5},{7,6},{8,15},{9,8},{10,9... | collective-permute-start | bytes 1769480 | tf_op jit(solution)/shard_map/ppermute | solution.py:66
  39.5 23.0 %collective-permute-start.6 = (bf16[2,288,512]{2,1,0:T(8,128)(2,1)S(1)}, bf16[2,288,512]{2,1,0:T(8,128)(2,1)}, u32[]{:S(2)}, u32[]{:S(2)}) collective-permute-start(bf16[2,288,512]{2,1,0:T(8,128)(2,1)S(1)} %pad_maximum_fusion.refs_0_), channel_id=1, source_target_pairs={{0,1},{1,2},{2,3},{3,4},{4,5},{5,6},{6,7},{7,0},{8,9},{9,10},{10,1... | collective-permute-start | bytes 1769480 | tf_op jit(solution)/shard_map/ppermute | solution.py:66
  62.5 20.2 %collective-permute-start.8 = (bf16[2,288,512]{2,1,0:T(8,128)(2,1)}, bf16[2,288,512]{2,1,0:T(8,128)(2,1)}, u32[]{:S(2)}, u32[]{:S(2)}) collective-permute-start(bf16[2,288,512]{2,1,0:T(8,128)(2,1)} %collective-permute-done.6.refs_1_), channel_id=1, source_target_pairs={{0,1},{1,2},{2,3},{3,4},{4,5},{5,6},{6,7},{7,0},{8,9},{9,10},{10,1... | collective-permute-start | bytes 1769480 | tf_op jit(solution)/shard_map/ppermute | solution.py:66
  64.0 18.7 %collective-permute-start.9 = (bf16[2,288,512]{2,1,0:T(8,128)(2,1)}, bf16[2,288,512]{2,1,0:T(8,128)(2,1)}, u32[]{:S(2)}, u32[]{:S(2)}) collective-permute-start(bf16[2,288,512]{2,1,0:T(8,128)(2,1)} %collective-permute-done.7.refs_8_), channel_id=1, source_target_pairs={{0,7},{1,0},{2,1},{3,2},{4,3},{5,4},{6,5},{7,6},{8,15},{9,8},{10,9... | collective-permute-start | bytes 1769480 | tf_op jit(solution)/shard_map/ppermute | solution.py:66
  64.6 32.7 %collective-permute-start.12 = (bf16[256,2304]{1,0:T(8,128)(2,1)}, bf16[256,2304]{1,0:T(8,128)(2,1)S(1)}, u32[]{:S(2)}, u32[]{:S(2)}) collective-permute-start(bf16[256,2304]{1,0:T(8,128)(2,1)} %collective-permute-done.4), channel_id=1, source_target_pairs={{0,8},{1,9},{2,10},{3,11},{4,12},{5,13},{6,14},{7,15},{8,32},{9,33... | collective-permute-start | bytes 3538952 | tf_op jit(solution)/shard_map/ppermute | solution.py:66
  66.2 31.1 %collective-permute-start.13 = (bf16[256,2304]{1,0:T(8,128)(2,1)}, bf16[256,2304]{1,0:T(8,128)(2,1)}, u32[]{:S(2)}, u32[]{:S(2)}) collective-permute-start(bf16[256,2304]{1,0:T(8,128)(2,1)} %collective-permute-done.5), channel_id=1, source_target_pairs={{0,40},{1,41},{2,42},{3,43},{4,44},{5,45},{6,46},{7,47},{8,0},{9,1... | collective-permute-start | bytes 3538952 | tf_op jit(solution)/shard_map/ppermute | solution.py:66
  67.8 49.2 %collective-permute-start.16 = (bf16[512,2304]{1,0:T(8,128)(2,1)S(1)}, bf16[512,2304]{1,0:T(8,128)(2,1)}, u32[]{:S(2)}, u32[]{:S(2)}) collective-permute-start(bf16[512,2304]{1,0:T(8,128)(2,1)S(1)} %bitcast.44), channel_id=1, source_target_pairs={{0,16},{1,17},{2,18},{3,19},{4,20},{5,21},{6,22},{7,23},{8,24},{9,... | collective-permute-start | bytes 7077896 | tf_op jit(solution)/shard_map/ppermute | solution.py:66
  82.7 14.3 %collective-permute-start.10 = (bf16[2,288,512]{2,1,0:T(8,128)(2,1)}, bf16[2,288,512]{2,1,0:T(8,128)(2,1)}, u32[]{:S(2)}, u32[]{:S(2)}) collective-permute-start(bf16[2,288,512]{2,1,0:T(8,128)(2,1)} %collective-permute-done.8.refs_2_), channel_id=1, source_target_pairs={{0,1},{1,2},{2,3},{3,4},{4,5},{5,6},{6,7},{7,0},{8,9},{9,10},{10,1... | collective-permute-start | bytes 1769480 | tf_op jit(solution)/shard_map/ppermute | solution.py:66
  83.4 13.9 %collective-permute-start.11 = (bf16[2,288,512]{2,1,0:T(8,128)(2,1)}, bf16[2,288,512]{2,1,0:T(8,128)(2,1)}, u32[]{:S(2)}, u32[]{:S(2)}) collective-permute-start(bf16[2,288,512]{2,1,0:T(8,128)(2,1)} %collective-permute-done.9.refs_7_), channel_id=1, source_target_pairs={{0,7},{1,0},{2,1},{3,2},{4,3},{5,4},{6,5},{7,6},{8,15},{9,8},{10,9... | collective-permute-start | bytes 1769480 | tf_op jit(solution)/shard_map/ppermute | solution.py:66
  97.3 19.8 %collective-permute-start.17 = (bf16[256,2304]{1,0:T(8,128)(2,1)S(1)}, bf16[256,2304]{1,0:T(8,128)(2,1)}, u32[]{:S(2)}, u32[]{:S(2)}) collective-permute-start(bf16[256,2304]{1,0:T(8,128)(2,1)S(1)} %collective-permute-done.12.refs_2_), channel_id=1, source_target_pairs={{0,16},{1,17},{2,18},{3,19},{4,20},{5,21},{6,22},{7,23},{8,24},{9,... | collective-permute-start | bytes 3538952 | tf_op jit(solution)/shard_map/ppermute | solution.py:66
  97.3 19.8 %collective-permute-start.18 = (bf16[256,2304]{1,0:T(8,128)(2,1)}, bf16[256,2304]{1,0:T(8,128)(2,1)}, u32[]{:S(2)}, u32[]{:S(2)}) collective-permute-start(bf16[256,2304]{1,0:T(8,128)(2,1)} %collective-permute-done.13.refs_3_), channel_id=1, source_target_pairs={{0,16},{1,17},{2,18},{3,19},{4,20},{5,21},{6,22},{7,23},{8,24},{9,... | collective-permute-start | bytes 3538952 | tf_op jit(solution)/shard_map/ppermute | solution.py:66
  101.2 9.3 %collective-permute-start.15 = (bf16[288,512]{1,0:T(8,128)(2,1)}, bf16[288,512]{1,0:T(8,128)(2,1)}, u32[]{:S(2)}, u32[]{:S(2)}) collective-permute-start(bf16[288,512]{1,0:T(8,128)(2,1)} %slice_bitcast_fusion), channel_id=1, source_target_pairs={{0,7},{1,0},{2,1},{3,2},{4,3},{5,4},{6,5},{7,6},{8,15},{9,8},{10,9... | collective-permute-start | bytes 884744 | tf_op jit(solution)/shard_map/ppermute | solution.py:66
  103.0 10.0 %collective-permute-start.14 = (bf16[288,512]{1,0:T(8,128)(2,1)}, bf16[288,512]{1,0:T(8,128)(2,1)}, u32[]{:S(2)}, u32[]{:S(2)}) collective-permute-start(bf16[288,512]{1,0:T(8,128)(2,1)} %slice_bitcast_fusion.1), channel_id=1, source_target_pairs={{0,1},{1,2},{2,3},{3,4},{4,5},{5,6},{6,7},{7,0},{8,9},{9,10},{10,1... | collective-permute-start | bytes 884744 | tf_op jit(solution)/shard_map/ppermute | solution.py:66
  113.0 1.1 copy-start.2
  122.4 17.4 %collective-permute-start.19 = (bf16[144,2304]{1,0:T(8,128)(2,1)S(1)}, bf16[144,2304]{1,0:T(8,128)(2,1)S(1)}, u32[]{:S(2)}, u32[]{:S(2)}) collective-permute-start(bf16[144,2304]{1,0:T(8,128)(2,1)S(1)} %get-tuple-element.51), channel_id=1, source_target_pairs={{0,64},{1,65},{2,66},{3,67},{4,68},{5,69},{6,70},{7,71},{8,72},{9,... | collective-permute-start | bytes 1990664 | tf_op jit(solution)/shard_map/ppermute | solution.py:66
  124.1 17.8 %collective-permute-start.20 = (bf16[144,2304]{1,0:T(8,128)(2,1)S(1)}, bf16[144,2304]{1,0:T(8,128)(2,1)S(1)}, u32[]{:S(2)}, u32[]{:S(2)}) collective-permute-start(bf16[144,2304]{1,0:T(8,128)(2,1)S(1)} %get-tuple-element.53), channel_id=1, source_target_pairs={{0,192},{1,193},{2,194},{3,195},{4,196},{5,197},{6,198},{7,199},{8... | collective-permute-start | bytes 1990664 | tf_op jit(solution)/shard_map/ppermute | solution.py:66
  133.6 22.5 %collective-permute-start.22 = (bf16[144,2304]{1,0:T(8,128)(2,1)S(1)}, bf16[144,2304]{1,0:T(8,128)(2,1)S(1)}, u32[]{:S(2)}, u32[]{:S(2)}) collective-permute-start(bf16[144,2304]{1,0:T(8,128)(2,1)S(1)} %get-tuple-element.56), channel_id=1, source_target_pairs={{0,192},{1,193},{2,194},{3,195},{4,196},{5,197},{6,198},{7,199},{8... | collective-permute-start | bytes 1990664 | tf_op jit(solution)/shard_map/ppermute | solution.py:66
  142.1 19.1 %collective-permute-start.21 = (bf16[144,2304]{1,0:T(8,128)(2,1)S(1)}, bf16[144,2304]{1,0:T(8,128)(2,1)S(1)}, u32[]{:S(2)}, u32[]{:S(2)}) collective-permute-start(bf16[144,2304]{1,0:T(8,128)(2,1)S(1)} %add_convert_fusion.1), channel_id=1, source_target_pairs={{0,64},{1,65},{2,66},{3,67},{4,68},{5,69},{6,70},{7,71},{8,72},{9,... | collective-permute-start | bytes 1990664 | tf_op jit(solution)/shard_map/ppermute | solution.py:66
  143.8 27.2 %collective-permute-start.23 = (bf16[144,2304]{1,0:T(8,128)(2,1)S(1)}, bf16[144,2304]{1,0:T(8,128)(2,1)S(1)}, u32[]{:S(2)}, u32[]{:S(2)}) collective-permute-start(bf16[144,2304]{1,0:T(8,128)(2,1)S(1)} %get-tuple-element.57), channel_id=1, source_target_pairs={{0,64},{1,65},{2,66},{3,67},{4,68},{5,69},{6,70},{7,71},{8,72},{9,... | collective-permute-start | bytes 1990664 | tf_op jit(solution)/shard_map/ppermute | solution.py:66
  145.0 25.9 %collective-permute-start.24 = (bf16[144,2304]{1,0:T(8,128)(2,1)S(1)}, bf16[144,2304]{1,0:T(8,128)(2,1)S(1)}, u32[]{:S(2)}, u32[]{:S(2)}) collective-permute-start(bf16[144,2304]{1,0:T(8,128)(2,1)S(1)} %add_convert_fusion), channel_id=1, source_target_pairs={{0,192},{1,193},{2,194},{3,195},{4,196},{5,197},{6,198},{7,199},{8... | collective-permute-start | bytes 1990664 | tf_op jit(solution)/shard_map/ppermute | solution.py:66
  161.4 9.7 %copy-start.4 = (f32[288,2304]{1,0:T(8,128)S(1)}, f32[288,2304]{1,0:T(8,128)}, u32[]{:S(2)}) copy-start(f32[288,2304]{1,0:T(8,128)} %param.8) | copy-start | bytes 7962628

commit v6 on v5

--- a/solution.py
+++ b/solution.py
@@ -190,28 +190,33 @@
     up = send(flat[:seq], along_x(1))
     down = send(flat[seq:], along_x(-1))
     own = jnp.stack(sources)
-    fwd, bwd = [own, send(own, along_z(1))], [own, send(own, along_z(-1))]
+    fwd, bwd = [own], [own]
+
+    def step_z():
+        fwd.append(send(fwd[-1], along_z(1)))
+        bwd.append(send(bwd[-1], along_z(-1)))
+
+    step_z()
+    fwd[1], bwd[1], grams = stage((fwd[1], bwd[1], grams))
+
+    step_z()
     shape = grams.shape
     grams = jnp.moveaxis(grams.reshape(shape[:3] + (NZ, -1, shape[4])), 3, 0)
     grams = all_to_all(grams, "tensor", z_rings).astype(F32).sum(axis=0)
     weight = jnp.array([1.0, 2.0, 1.0], F32)[:, None, None, None]
     total = jnp.sum(grams[0] * grams[1] * weight, axis=(0, 2, 3)) + others
-    up, down, fwd[1], bwd[1], total = stage((up, down, fwd[1], bwd[1], total))
-
+    up, down, fwd[2], bwd[2], total = stage((up, down, fwd[2], bwd[2], total))
+
+    step_z()
     up, down = send(up, along_x(1)), send(down, along_x(-1))
-    fwd.append(send(fwd[1], along_z(1)))
-    bwd.append(send(bwd[1], along_z(-1)))
     sibling = send(flat, CORE)
     total = all_to_all(jnp.broadcast_to(total, (NZ, examples)), "tensor", z_rings).sum(axis=0)
-    fwd[2], bwd[2], total = stage((fwd[2], bwd[2], total))
-
-    fwd.append(send(fwd[2], along_z(1)))
-    bwd.append(send(bwd[2], along_z(-1)))
+    fwd[3], bwd[3], total = stage((fwd[3], bwd[3], total))
+
+    far = [send(fwd[3][0], along_z(1)), send(bwd[3][1], along_z(-1))]
     clip = jnp.minimum(1.0, clip_norm / jnp.sqrt(total))
     clips = all_to_all(jnp.broadcast_to(clip, (4, examples)), "dp", chip_pairs).reshape(-1)
-    fwd[3], bwd[3], clips, up, down = stage((fwd[3], bwd[3], clips, up, down))
-
-    far = [send(fwd[3][0], along_z(1)), send(bwd[3][1], along_z(-1))]
+    far[0], far[1], clips, up, down = stage((far[0], far[1], clips, up, down))
     up_sibling, down_sibling = send(up, CORE), send(down, CORE)
     pieces = [own, fwd[1], fwd[2], fwd[3], far[0], far[1], bwd[3], bwd[2], bwd[1]]
     places = jnp.stack([dp, te]).astype(jnp.int32)
@@ -227,6 +232,7 @@
     prev_b = (prev_b.astype(F32) + from_up.astype(F32)).astype(BF)
     next_a, prev_b, scaled = stage((next_a, prev_b, scaled))
     next_a, prev_b = send(next_a, along_y(1)), send(prev_b, along_y(-1))
+    next_b, prev_a, scaled = stage((next_b, prev_a, scaled))
     (mine,) = product("product_own", scaled, 3, 1, held, tile, 1, F32)
 
     width = features * 2 * NZ

time: 176 us -> 181 us (1.028)
  local copies, waits for them, and re-layouts: 8.26 us -> 12.1 us
  starting transfers between devices: 39.9 us -> 42.5 us
    unnamed x14 -> x22, local copies, waits for them, and re-layouts: 1.09 us -> 4.81 us
    ppermute x25, starting transfers between devices: 31.6 us -> 33.5 us  [send(): return lax.ppermute(value, AXES, perm)]
  transfers between devices with their start and end apart: 26 -> 26, of which waited for: 12 -> 9; matrix products, arithmetic and copies ran while one was open for 5% -> 6% of each run, Pallas kernels for 9% -> 9%
where the time goes in v6:
time: 181 us; the launch traced here: 180 us
  waiting for transfers between devices  69.7 us (39%)
  starting transfers between devices  42.5 us (23%)
  blocking collectives  23.9 us (13%)
  Pallas kernels  21.4 us (12%)
  local copies, waits for them, and re-layouts  12.1 us (7%)
  other arithmetic  6.17 us (3%)
  matrix products  3.57 us (2%)
    ppermute x25, waiting for transfers between devices, send(): return lax.ppermute(value, AXES, perm)  57 us
    ppermute x25, starting transfers between devices, send(): return lax.ppermute(value, AXES, perm)  33.5 us
    all_to_all x2, blocking collectives, all_to_all(): lax.all_to_all(value, axis, 0, 0, tiled=True, axis_index_groups=groups)  23.9 us
    pallas_call x3, Pallas kernels, product(): pl.pallas_call(product_kernel, out_shape=[jax.ShapeDtypeStruct((count, wi...  18.6 us
    all_to_all x1, waiting for transfers between devices, all_to_all(): lax.all_to_all(value, axis, 0, 0, tiled=True, axis_index_groups=groups)  12.6 us
    all_to_all x1, starting transfers between devices, all_to_all(): lax.all_to_all(value, axis, 0, 0, tiled=True, axis_index_groups=groups)  9.02 us
    unnamed x22, local copies, waits for them, and re-layouts  4.81 us
  transfers between devices with their start and end apart: 26, of which 9 were waited for; matrix products, arithmetic and copies ran while one was open for 6% of the time, Pallas kernels for 9%

profile of v6, /device:TPU:32, one launch (start us, length us, event | category | flops | bytes accessed | tf_op | source)
XLA Modules:
  0.0 179.7 jit_solution(5920750792110677864)
XLA Ops:
  0.0 3.2 %convolution_convert_fusion.1 = bf16[2,256,256]{2,1,0:T(8,128)(2,1)S(1)} fusion(bf16[2,256,2304]{2,1,0:T(8,128)(2,1)} %param.5), kind=kOutput, calls=%fused_computation.9 | convolution fusion | flops 604110848 | bytes 2621440 | tf_op jit(solution)/shard_map/btf,bsf->bts/dot_general | solution.py:180
  3.3 0.3 convolution_convert_fusion
  3.6 0.0 copy-start.9
  3.8 1.6 collective-permute-start.2
  5.4 0.7 copy.16
  6.1 1.1 collective-permute-start.1
  7.2 4.1 %collective-permute-start = (bf16[288,512]{1,0:T(8,128)(2,1)}, bf16[288,512]{1,0:T(8,128)(2,1)}, u32[]{:S(2)}, u32[]{:S(2)}) collective-permute-start(bf16[288,512]{1,0:T(8,128)(2,1)} %bitcast.2), channel_id=1, source_target_pairs={{0,0},{1,18},{2,36},{3,50},{4,4},{5,22},{6,32},{7,54},{8,8},{9,26}... | collective-permute-start | bytes 884744 | tf_op jit(solution)/shard_map/ppermute | solution.py:66
  11.3 0.1 reduce_sum.36
  11.4 0.7 collective-permute-start.3
  12.1 13.3 %collective-permute-done.3 = f32[2]{0:T(128)S(1)} collective-permute-done((f32[2]{0:T(128)S(1)}, f32[2]{0:T(128)S(1)}, u32[]{:S(2)}, u32[]{:S(2)}) %collective-permute-start.3) | collective-permute-done | bytes 40 | tf_op jit(solution)/shard_map/ppermute | solution.py:66
  25.4 0.1 add_convert_fusion.2
  25.6 1.1 pad_maximum_fusion.refs_0_
  26.7 0.1 collective-permute-start.7
  26.8 2.0 %collective-permute-start.6 = (bf16[2,288,512]{2,1,0:T(8,128)(2,1)S(1)}, bf16[2,288,512]{2,1,0:T(8,128)(2,1)S(1)}, u32[]{:S(2)}, u32[]{:S(2)}) collective-permute-start(bf16[2,288,512]{2,1,0:T(8,128)(2,1)S(1)} %pad_maximum_fusion.refs_0_), channel_id=1, source_target_pairs={{0,1},{1,2},{2,3},{3,4},{4,5},{5,6},{6,7},{7,0},{8,9},{9,10},{10,1... | collective-permute-start | bytes 1769480 | tf_op jit(solution)/shard_map/ppermute | solution.py:66
  28.8 1.6 fusion.6
  30.4 2.0 %collective-permute-start.4 = (bf16[256,2304]{1,0:T(8,128)(2,1)}, bf16[256,2304]{1,0:T(8,128)(2,1)}, u32[]{:S(2)}, u32[]{:S(2)}) collective-permute-start(bf16[256,2304]{1,0:T(8,128)(2,1)} %get-tuple-element.72), channel_id=1, source_target_pairs={{0,8},{1,9},{2,10},{3,11},{4,12},{5,13},{6,14},{7,15},{8,32},{9,33... | collective-permute-start | bytes 3538952 | tf_op jit(solution)/shard_map/ppermute | solution.py:66
  32.4 9.7 %collective-permute-done.7.refs_8_ = bf16[2,288,512]{2,1,0:T(8,128)(2,1)S(1)} collective-permute-done((bf16[2,288,512]{2,1,0:T(8,128)(2,1)S(1)}, bf16[2,288,512]{2,1,0:T(8,128)(2,1)S(1)}, u32[]{:S(2)}, u32[]{:S(2)}) %collective-permute-start.7) | collective-permute-done | bytes 589856 | tf_op jit(solution)/shard_map/ppermute | solution.py:66
  42.1 0.9 copy.18
  43.0 9.0 %all-to-all-start = ((bf16[8,2,3,2,16,128]{5,4,3,2,1,0:T(8,128)(2,1)}), bf16[8,2,3,2,16,128]{5,4,3,2,1,0:T(8,128)(2,1)}, u32[]{:S(2)}, u32[]{:S(2)}) async-start(bf16[8,2,3,2,16,128]{5,4,3,2,1,0:T(8,128)(2,1)} %bitcast.49), calls=%async_computation | async-start | bytes 786432 | tf_op jit(solution)/shard_map/all_to_all | solution.py:161
  52.0 1.5 collective-permute-start.8
  53.5 0.6 collective-permute-start.9
  54.0 12.6 %all-to-all-done = bf16[8,2,3,2,16,128]{5,4,3,2,1,0:T(8,128)(2,1)} async-done(((bf16[8,2,3,2,16,128]{5,4,3,2,1,0:T(8,128)(2,1)}), bf16[8,2,3,2,16,128]{5,4,3,2,1,0:T(8,128)(2,1)}, u32[]{:S(2)}, u32[]{:S(2)}) %all-to-all-start) | async-done | bytes 393248 | tf_op jit(solution)/shard_map/all_to_all | solution.py:161
  66.7 1.1 convert_reduce_fusion
  67.7 0.2 fusion.5
  67.9 6.8 %collective-permute-done.8.refs_2_ = bf16[2,288,512]{2,1,0:T(8,128)(2,1)} collective-permute-done((bf16[2,288,512]{2,1,0:T(8,128)(2,1)S(1)}, bf16[2,288,512]{2,1,0:T(8,128)(2,1)}, u32[]{:S(2)}, u32[]{:S(2)}) %collective-permute-start.8) | collective-permute-done | bytes 589856 | tf_op jit(solution)/shard_map/ppermute | solution.py:66
  74.8 1.2 collective-permute-done.9.refs_7_
  75.9 1.5 collective-permute-start.10
  77.4 0.5 collective-permute-start.11
  77.9 1.5 collective-permute-start.14
  79.4 4.1 %collective-permute-start.15 = (bf16[256,2304]{1,0:T(8,128)(2,1)}, bf16[256,2304]{1,0:T(8,128)(2,1)}, u32[]{:S(2)}, u32[]{:S(2)}) collective-permute-start(bf16[256,2304]{1,0:T(8,128)(2,1)} %collective-permute-done.5), channel_id=1, source_target_pairs={{0,40},{1,41},{2,42},{3,43},{4,44},{5,45},{6,46},{7,47},{8,0},{9,1... | collective-permute-start | bytes 3538952 | tf_op jit(solution)/shard_map/ppermute | solution.py:66
  83.5 13.5 %all_to_all.17 = f32[8,1,2]{2,1,0:T(1,128)S(1)} all-to-all(f32[8,1,2]{2,1,0:T(1,128)S(1)} %broadcast_in_dim.7), channel_id=1, replica_groups={{0,1,2,3,4,5,6,7},{8,9,10,11,12,13,14,15},{16,17,18,19,20,21,22,23},{24..., dimensions={0} | all-to-all | bytes 128 | tf_op jit(solution)/shard_map/all_to_all | solution.py:161
  97.0 1.7 slice_bitcast_fusion.1
  98.7 1.7 slice_bitcast_fusion
  100.4 1.5 collective-permute-start.13
  101.9 0.6 collective-permute-start.12
  102.5 10.4 %all_to_all.18 = f32[4,1,2]{2,1,0:T(1,128)S(1)} all-to-all(f32[4,1,2]{2,1,0:T(1,128)S(1)} %broadcast_in_dim.8), channel_id=1, replica_groups={{0,16,32,48},{64,80,96,112},{128,144,160,176},{192,208,224,240},{1,17,3..., dimensions={0} | all-to-all | bytes 64 | tf_op jit(solution)/shard_map/all_to_all | solution.py:161
  112.9 0.6 broadcast.21
  113.5 0.7 reduce.4
  114.2 0.1 reshape.26.clip_ref
  114.3 0.1 collective-permute-start.17
  114.4 0.5 collective-permute-start.18
  114.9 0.1 pad_add_fusion.place_ref
  114.9 1.1 copy-done.2
  116.0 1.1 copy-done.4
  117.1 1.1 copy-done.6
  118.1 2.9 %scale_grads.1.s_ref = bf16[4,4,288,512]{3,2,1,0:T(8,128)(2,1)S(1)} custom-call(s32[2]{0:T(128)S(1)} %pad_add_fusion.place_ref, f32[8]{0:T(128)S(1)} %reshape.26.clip_ref, bf16[2,288,512]{2,1,0:T(8,128)(2,1)S(1)} %copy-done.2, bf16[2,288,512]{2,1,0:T(8,128)(2,1)S(1)} %copy-done.6, bf16[2,288,512]{2,1,0:T(8,128)(2,1)} %collective-permute-done.8.refs_2_, ...), custom_call_target="tpu_custom_call" | custom-call | flops 2359296 | bytes 147456 | tf_op jit(solution)/shard_map/scale_grads/pallas_call | solution.py:103
  121.0 5.3 %product_far.1 = (bf16[144,2304]{1,0:T(8,128)(2,1)S(1)}, bf16[144,2304]{1,0:T(8,128)(2,1)S(1)}) custom-call(bf16[4,4,288,512]{3,2,1,0:T(8,128)(2,1)S(1)} %scale_grads.1.s_ref, bf16[512,2304]{1,0:T(8,128)(2,1)S(1)} %bitcast.45, bf16[512,2304]{1,0:T(8,128)(2,1)} %collective-permute-done.16.refs_1_, bf16[256,2304]{1,0:T(8,128)(2,1)S(1)} %collective-permute-done.14.refs_2_, ...), custom_call_target="tpu_custom_call" | custom-call | flops 1327104 | bytes 1327104 | tf_op jit(solution)/shard_map/product_far/pallas_call | solution.py:143
  126.4 3.1 %collective-permute-start.22 = (bf16[144,2304]{1,0:T(8,128)(2,1)S(1)}, bf16[144,2304]{1,0:T(8,128)(2,1)S(1)}, u32[]{:S(2)}, u32[]{:S(2)}) collective-permute-start(bf16[144,2304]{1,0:T(8,128)(2,1)S(1)} %get-tuple-element.64), channel_id=1, source_target_pairs={{0,192},{1,193},{2,194},{3,195},{4,196},{5,197},{6,198},{7,199},{8... | collective-permute-start | bytes 1990664 | tf_op jit(solution)/shard_map/ppermute | solution.py:66
  129.4 7.9 %product_near.1 = (bf16[144,2304]{1,0:T(8,128)(2,1)S(1)}, bf16[144,2304]{1,0:T(8,128)(2,1)S(1)}, bf16[144,2304]{1,0:T(8,128)(2,1)S(1)}, bf16[144,2304]{1,0:T(8,128)(2,1)S(1)}) custom-call(bf16[4,4,288,512]{3,2,1,0:T(8,128)(2,1)S(1)} %scale_grads.1.s_ref, bf16[512,2304]{1,0:T(8,128)(2,1)S(1)} %bitcast.46, bf16[512,2304]{1,0:T(8,128)(2,1)} %collective-permute-done.16.refs_1_, ...), custom_call_target="tpu_custom_call" | custom-call | flops 2654208 | bytes 1327104 | tf_op jit(solution)/shard_map/product_near/pallas_call | solution.py:143
  137.3 0.7 collective-permute-start.19
  138.0 2.7 %collective-permute-start.20 = (bf16[144,2304]{1,0:T(8,128)(2,1)S(1)}, bf16[144,2304]{1,0:T(8,128)(2,1)S(1)}, u32[]{:S(2)}, u32[]{:S(2)}) collective-permute-start(bf16[144,2304]{1,0:T(8,128)(2,1)S(1)} %get-tuple-element.60), channel_id=1, source_target_pairs={{0,192},{1,193},{2,194},{3,195},{4,196},{5,197},{6,198},{7,199},{8... | collective-permute-start | bytes 1990664 | tf_op jit(solution)/shard_map/ppermute | solution.py:66
  140.7 4.0 %collective-permute-done.22 = bf16[144,2304]{1,0:T(8,128)(2,1)S(1)} collective-permute-done((bf16[144,2304]{1,0:T(8,128)(2,1)S(1)}, bf16[144,2304]{1,0:T(8,128)(2,1)S(1)}, u32[]{:S(2)}, u32[]{:S(2)}) %collective-permute-start.22) | collective-permute-done | bytes 663584 | tf_op jit(solution)/shard_map/ppermute | solution.py:66
  144.7 0.2 add_convert_fusion
  144.9 3.6 %collective-permute-done.21 = bf16[144,2304]{1,0:T(8,128)(2,1)S(1)} collective-permute-done((bf16[144,2304]{1,0:T(8,128)(2,1)S(1)}, bf16[144,2304]{1,0:T(8,128)(2,1)S(1)}, u32[]{:S(2)}, u32[]{:S(2)}) %collective-permute-start.21) | collective-permute-done | bytes 663584 | tf_op jit(solution)/shard_map/ppermute | solution.py:66
  148.4 0.2 add_convert_fusion.1
  148.6 0.1 collective-permute-start.23
  148.7 3.2 %collective-permute-start.24 = (bf16[144,2304]{1,0:T(8,128)(2,1)S(1)}, bf16[144,2304]{1,0:T(8,128)(2,1)S(1)}, u32[]{:S(2)}, u32[]{:S(2)}) collective-permute-start(bf16[144,2304]{1,0:T(8,128)(2,1)S(1)} %add_convert_fusion), channel_id=1, source_target_pairs={{0,192},{1,193},{2,194},{3,195},{4,196},{5,197},{6,198},{7,199},{8... | collective-permute-start | bytes 1990664 | tf_op jit(solution)/shard_map/ppermute | solution.py:66
  151.9 10.7 %collective-permute-done.19 = bf16[144,2304]{1,0:T(8,128)(2,1)S(1)} collective-permute-done((bf16[144,2304]{1,0:T(8,128)(2,1)S(1)}, bf16[144,2304]{1,0:T(8,128)(2,1)S(1)}, u32[]{:S(2)}, u32[]{:S(2)}) %collective-permute-start.19) | collective-permute-done | bytes 663584 | tf_op jit(solution)/shard_map/ppermute | solution.py:66
  162.7 5.4 %product_own.1 = f32[288,2304]{1,0:T(8,128)S(1)} custom-call(bf16[4,4,288,512]{3,2,1,0:T(8,128)(2,1)S(1)} %scale_grads.1.s_ref, bf16[512,2304]{1,0:T(8,128)(2,1)S(1)} %bitcast.47, bf16[512,2304]{1,0:T(8,128)(2,1)} %collective-permute-done.16.refs_1_, bf16[256,2304]{1,0:T(8,128)(2,1)S(1)} %collective-permute-done.14.refs_2_, ...), custom_call_target="tpu_custom_call" | custom-call | flops 1327104 | bytes 1327104 | tf_op jit(solution)/shard_map/product_own/pallas_call | solution.py:143
  168.0 7.7 %collective-permute-done.23 = bf16[144,2304]{1,0:T(8,128)(2,1)S(1)} collective-permute-done((bf16[144,2304]{1,0:T(8,128)(2,1)S(1)}, bf16[144,2304]{1,0:T(8,128)(2,1)S(1)}, u32[]{:S(2)}, u32[]{:S(2)}) %collective-permute-start.23) | collective-permute-done | bytes 663584 | tf_op jit(solution)/shard_map/ppermute | solution.py:66
  175.7 0.1 convert_add_fusion.1
  175.9 0.1 convert_add_fusion
  176.0 1.6 copy-done.8
  177.6 2.1 %fusion.2 = f32[288,2304]{1,0:T(8,128)} fusion(f32[288,2304]{1,0:T(8,128)S(1)} %copy-done.8, f32[288,2304]{1,0:T(8,128)S(1)} %product_own.1, f32[144,2304]{1,0:T(8,128)S(1)} %convert_add_fusion, f32[144,2304]{1,0:T(8,128)S(1)} %convert_add_fusion.1), kind=kLoop, calls=%fused_computation.3 | loop fusion | flops 3317760 | bytes 10616832 | tf_op jit(solution)/shard_map/div | solution.py:244
  (47 shorter events, 0.3 us)
Async XLA Ops:
  0.0 3.3 %copy-start.7 = (bf16[2,256,288]{1,2,0:T(8,128)(2,1)S(1)}, bf16[2,256,288]{1,2,0:T(8,128)(2,1)}, u32[]{:S(2)}) copy-start(bf16[2,256,288]{1,2,0:T(8,128)(2,1)} %param.6) | copy-start | bytes 884740
  3.6 7.7 %copy-start.9 = (f32[2,8]{1,0:T(2,128)S(1)}, f32[2,8]{1,0:T(2,128)}, u32[]{:S(2)}) copy-start(f32[2,8]{1,0:T(2,128)} %param.7) | copy-start | bytes 196
  3.8 21.6 %collective-permute-start.2 = (bf16[2,3,2,128,128]{4,3,2,1,0:T(8,128)(2,1)S(1)}, bf16[2,3,2,128,128]{4,3,2,1,0:T(8,128)(2,1)S(1)}, u32[]{:S(2)}, u32[]{:S(2)}) collective-permute-start(bf16[2,3,2,128,128]{4,3,2,1,0:T(8,128)(2,1)S(1)} %pad_maximum_fusion.1), channel_id=1, source_target_pairs={{0,8},{1,9},{2,10},{3,11},{4,12},{5,13},{6,14},{7,15},{8,0},{9,1},... | collective-permute-start | bytes 1179656 | tf_op jit(solution)/shard_map/ppermute | solution.py:66
  6.1 22.7 %copy-start = (bf16[2,256,2304]{2,1,0:T(8,128)(2,1)S(1)}, bf16[2,256,2304]{2,1,0:T(8,128)(2,1)}, u32[]{:S(2)}) copy-start(bf16[2,256,2304]{2,1,0:T(8,128)(2,1)} %param.5) | copy-start | bytes 7077892
  6.1 19.4 %collective-permute-start.1 = (bf16[288,512]{1,0:T(8,128)(2,1)}, bf16[288,512]{1,0:T(8,128)(2,1)}, u32[]{:S(2)}, u32[]{:S(2)}) collective-permute-start(bf16[288,512]{1,0:T(8,128)(2,1)} %bitcast.2), channel_id=1, source_target_pairs={{0,8},{1,26},{2,44},{3,58},{4,12},{5,30},{6,40},{7,62},{8,0},{9,18... | collective-permute-start | bytes 884744 | tf_op jit(solution)/shard_map/ppermute | solution.py:66
  7.2 18.4 %collective-permute-start = (bf16[288,512]{1,0:T(8,128)(2,1)}, bf16[288,512]{1,0:T(8,128)(2,1)}, u32[]{:S(2)}, u32[]{:S(2)}) collective-permute-start(bf16[288,512]{1,0:T(8,128)(2,1)} %bitcast.2), channel_id=1, source_target_pairs={{0,0},{1,18},{2,36},{3,50},{4,4},{5,22},{6,32},{7,54},{8,8},{9,26}... | collective-permute-start | bytes 884744 | tf_op jit(solution)/shard_map/ppermute | solution.py:66
  11.4 14.0 %collective-permute-start.3 = (f32[2]{0:T(128)S(1)}, f32[2]{0:T(128)S(1)}, u32[]{:S(2)}, u32[]{:S(2)}) collective-permute-start(f32[2]{0:T(128)S(1)} %reduce_sum.36), channel_id=1, source_target_pairs={{0,8},{1,9},{2,10},{3,11},{4,12},{5,13},{6,14},{7,15},{8,0},{9,1},... | collective-permute-start | bytes 32 | tf_op jit(solution)/shard_map/ppermute | solution.py:66
  26.7 3.7 %copy-start.1 = (bf16[2,288,512]{2,1,0:T(8,128)(2,1)}, bf16[2,288,512]{2,1,0:T(8,128)(2,1)S(1)}, u32[]{:S(2)}) copy-start(bf16[2,288,512]{2,1,0:T(8,128)(2,1)S(1)} %pad_maximum_fusion.refs_0_) | copy-start | bytes 1769476
  26.7 15.4 %collective-permute-start.7 = (bf16[2,288,512]{2,1,0:T(8,128)(2,1)S(1)}, bf16[2,288,512]{2,1,0:T(8,128)(2,1)S(1)}, u32[]{:S(2)}, u32[]{:S(2)}) collective-permute-start(bf16[2,288,512]{2,1,0:T(8,128)(2,1)S(1)} %pad_maximum_fusion.refs_0_), channel_id=1, source_target_pairs={{0,7},{1,0},{2,1},{3,2},{4,3},{5,4},{6,5},{7,6},{8,15},{9,8},{10,9... | collective-permute-start | bytes 1769480 | tf_op jit(solution)/shard_map/ppermute | solution.py:66
  26.8 15.3 %collective-permute-start.6 = (bf16[2,288,512]{2,1,0:T(8,128)(2,1)S(1)}, bf16[2,288,512]{2,1,0:T(8,128)(2,1)S(1)}, u32[]{:S(2)}, u32[]{:S(2)}) collective-permute-start(bf16[2,288,512]{2,1,0:T(8,128)(2,1)S(1)} %pad_maximum_fusion.refs_0_), channel_id=1, source_target_pairs={{0,1},{1,2},{2,3},{3,4},{4,5},{5,6},{6,7},{7,0},{8,9},{9,10},{10,1... | collective-permute-start | bytes 1769480 | tf_op jit(solution)/shard_map/ppermute | solution.py:66
  30.4 37.3 %copy-start.10 = (f32[3]{0:T(128)S(1)}, f32[3]{0:T(128)}, u32[]{:S(2)}) copy-start(f32[3]{0:T(128)} %constant.20.clone) | copy-start | bytes 40
  30.4 37.5 %collective-permute-start.5 = (bf16[256,2304]{1,0:T(8,128)(2,1)}, bf16[256,2304]{1,0:T(8,128)(2,1)}, u32[]{:S(2)}, u32[]{:S(2)}) collective-permute-start(bf16[256,2304]{1,0:T(8,128)(2,1)} %get-tuple-element.71), channel_id=1, source_target_pairs={{0,40},{1,41},{2,42},{3,43},{4,44},{5,45},{6,46},{7,47},{8,0},{9,1... | collective-permute-start | bytes 3538952 | tf_op jit(solution)/shard_map/ppermute | solution.py:66
  30.4 37.5 %collective-permute-start.4 = (bf16[256,2304]{1,0:T(8,128)(2,1)}, bf16[256,2304]{1,0:T(8,128)(2,1)}, u32[]{:S(2)}, u32[]{:S(2)}) collective-permute-start(bf16[256,2304]{1,0:T(8,128)(2,1)} %get-tuple-element.72), channel_id=1, source_target_pairs={{0,8},{1,9},{2,10},{3,11},{4,12},{5,13},{6,14},{7,15},{8,32},{9,33... | collective-permute-start | bytes 3538952 | tf_op jit(solution)/shard_map/ppermute | solution.py:66
  42.1 35.3 %copy-start.3 = (bf16[2,288,512]{2,1,0:T(8,128)(2,1)}, bf16[2,288,512]{2,1,0:T(8,128)(2,1)S(1)}, u32[]{:S(2)}) copy-start(bf16[2,288,512]{2,1,0:T(8,128)(2,1)S(1)} %collective-permute-done.7.refs_8_) | copy-start | bytes 1769476
  42.1 35.3 %copy-start.5 = (bf16[2,288,512]{2,1,0:T(8,128)(2,1)}, bf16[2,288,512]{2,1,0:T(8,128)(2,1)S(1)}, u32[]{:S(2)}) copy-start(bf16[2,288,512]{2,1,0:T(8,128)(2,1)S(1)} %collective-permute-done.6.refs_1_) | copy-start | bytes 1769476
  43.0 23.7 %all-to-all-start = ((bf16[8,2,3,2,16,128]{5,4,3,2,1,0:T(8,128)(2,1)}), bf16[8,2,3,2,16,128]{5,4,3,2,1,0:T(8,128)(2,1)}, u32[]{:S(2)}, u32[]{:S(2)}) async-start(bf16[8,2,3,2,16,128]{5,4,3,2,1,0:T(8,128)(2,1)} %bitcast.49), calls=%async_computation | async-start | bytes 786432 | tf_op jit(solution)/shard_map/all_to_all | solution.py:161
  52.0 22.8 %collective-permute-start.8 = (bf16[2,288,512]{2,1,0:T(8,128)(2,1)S(1)}, bf16[2,288,512]{2,1,0:T(8,128)(2,1)}, u32[]{:S(2)}, u32[]{:S(2)}) collective-permute-start(bf16[2,288,512]{2,1,0:T(8,128)(2,1)S(1)} %collective-permute-done.6.refs_1_), channel_id=1, source_target_pairs={{0,1},{1,2},{2,3},{3,4},{4,5},{5,6},{6,7},{7,0},{8,9},{9,10},{10,1... | collective-permute-start | bytes 1769480 | tf_op jit(solution)/shard_map/ppermute | solution.py:66
  53.5 22.5 %collective-permute-start.9 = (bf16[2,288,512]{2,1,0:T(8,128)(2,1)S(1)}, bf16[2,288,512]{2,1,0:T(8,128)(2,1)}, u32[]{:S(2)}, u32[]{:S(2)}) collective-permute-start(bf16[2,288,512]{2,1,0:T(8,128)(2,1)S(1)} %collective-permute-done.7.refs_8_), channel_id=1, source_target_pairs={{0,7},{1,0},{2,1},{3,2},{4,3},{5,4},{6,5},{7,6},{8,15},{9,8},{10,9... | collective-permute-start | bytes 1769480 | tf_op jit(solution)/shard_map/ppermute | solution.py:66
  75.9 21.1 %collective-permute-start.10 = (bf16[2,288,512]{2,1,0:T(8,128)(2,1)}, bf16[2,288,512]{2,1,0:T(8,128)(2,1)}, u32[]{:S(2)}, u32[]{:S(2)}) collective-permute-start(bf16[2,288,512]{2,1,0:T(8,128)(2,1)} %collective-permute-done.8.refs_2_), channel_id=1, source_target_pairs={{0,1},{1,2},{2,3},{3,4},{4,5},{5,6},{6,7},{7,0},{8,9},{9,10},{10,1... | collective-permute-start | bytes 1769480 | tf_op jit(solution)/shard_map/ppermute | solution.py:66
  77.4 19.6 %collective-permute-start.11 = (bf16[2,288,512]{2,1,0:T(8,128)(2,1)}, bf16[2,288,512]{2,1,0:T(8,128)(2,1)}, u32[]{:S(2)}, u32[]{:S(2)}) collective-permute-start(bf16[2,288,512]{2,1,0:T(8,128)(2,1)} %collective-permute-done.9.refs_7_), channel_id=1, source_target_pairs={{0,7},{1,0},{2,1},{3,2},{4,3},{5,4},{6,5},{7,6},{8,15},{9,8},{10,9... | collective-permute-start | bytes 1769480 | tf_op jit(solution)/shard_map/ppermute | solution.py:66
  77.9 36.3 %collective-permute-start.14 = (bf16[256,2304]{1,0:T(8,128)(2,1)}, bf16[256,2304]{1,0:T(8,128)(2,1)S(1)}, u32[]{:S(2)}, u32[]{:S(2)}) collective-permute-start(bf16[256,2304]{1,0:T(8,128)(2,1)} %collective-permute-done.4), channel_id=1, source_target_pairs={{0,8},{1,9},{2,10},{3,11},{4,12},{5,13},{6,14},{7,15},{8,32},{9,33... | collective-permute-start | bytes 3538952 | tf_op jit(solution)/shard_map/ppermute | solution.py:66
  79.4 34.8 %collective-permute-start.15 = (bf16[256,2304]{1,0:T(8,128)(2,1)}, bf16[256,2304]{1,0:T(8,128)(2,1)}, u32[]{:S(2)}, u32[]{:S(2)}) collective-permute-start(bf16[256,2304]{1,0:T(8,128)(2,1)} %collective-permute-done.5), channel_id=1, source_target_pairs={{0,40},{1,41},{2,42},{3,43},{4,44},{5,45},{6,46},{7,47},{8,0},{9,1... | collective-permute-start | bytes 3538952 | tf_op jit(solution)/shard_map/ppermute | solution.py:66
  83.5 37.5 %collective-permute-start.16 = (bf16[512,2304]{1,0:T(8,128)(2,1)S(1)}, bf16[512,2304]{1,0:T(8,128)(2,1)}, u32[]{:S(2)}, u32[]{:S(2)}) collective-permute-start(bf16[512,2304]{1,0:T(8,128)(2,1)S(1)} %bitcast.44), channel_id=1, source_target_pairs={{0,16},{1,17},{2,18},{3,19},{4,20},{5,21},{6,22},{7,23},{8,24},{9,... | collective-permute-start | bytes 7077896 | tf_op jit(solution)/shard_map/ppermute | solution.py:66
  100.4 13.8 %collective-permute-start.13 = (bf16[288,512]{1,0:T(8,128)(2,1)}, bf16[288,512]{1,0:T(8,128)(2,1)}, u32[]{:S(2)}, u32[]{:S(2)}) collective-permute-start(bf16[288,512]{1,0:T(8,128)(2,1)} %slice_bitcast_fusion), channel_id=1, source_target_pairs={{0,7},{1,0},{2,1},{3,2},{4,3},{5,4},{6,5},{7,6},{8,15},{9,8},{10,9... | collective-permute-start | bytes 884744 | tf_op jit(solution)/shard_map/ppermute | solution.py:66
  101.9 12.4 %collective-permute-start.12 = (bf16[288,512]{1,0:T(8,128)(2,1)}, bf16[288,512]{1,0:T(8,128)(2,1)}, u32[]{:S(2)}, u32[]{:S(2)}) collective-permute-start(bf16[288,512]{1,0:T(8,128)(2,1)} %slice_bitcast_fusion.1), channel_id=1, source_target_pairs={{0,1},{1,2},{2,3},{3,4},{4,5},{5,6},{6,7},{7,0},{8,9},{9,10},{10,1... | collective-permute-start | bytes 884744 | tf_op jit(solution)/shard_map/ppermute | solution.py:66
  114.3 6.7 %collective-permute-start.17 = (bf16[256,2304]{1,0:T(8,128)(2,1)S(1)}, bf16[256,2304]{1,0:T(8,128)(2,1)}, u32[]{:S(2)}, u32[]{:S(2)}) collective-permute-start(bf16[256,2304]{1,0:T(8,128)(2,1)S(1)} %collective-permute-done.14.refs_2_), channel_id=1, source_target_pairs={{0,16},{1,17},{2,18},{3,19},{4,20},{5,21},{6,22},{7,23},{8,24},{9,... | collective-permute-start | bytes 3538952 | tf_op jit(solution)/shard_map/ppermute | solution.py:66
  114.4 6.6 %collective-permute-start.18 = (bf16[256,2304]{1,0:T(8,128)(2,1)}, bf16[256,2304]{1,0:T(8,128)(2,1)}, u32[]{:S(2)}, u32[]{:S(2)}) collective-permute-start(bf16[256,2304]{1,0:T(8,128)(2,1)} %collective-permute-done.15.refs_3_), channel_id=1, source_target_pairs={{0,16},{1,17},{2,18},{3,19},{4,20},{5,21},{6,22},{7,23},{8,24},{9,... | collective-permute-start | bytes 3538952 | tf_op jit(solution)/shard_map/ppermute | solution.py:66
  114.9 1.1 copy-start.2
  116.0 1.1 copy-start.4
  117.1 1.1 copy-start.6
  126.4 18.3 %collective-permute-start.22 = (bf16[144,2304]{1,0:T(8,128)(2,1)S(1)}, bf16[144,2304]{1,0:T(8,128)(2,1)S(1)}, u32[]{:S(2)}, u32[]{:S(2)}) collective-permute-start(bf16[144,2304]{1,0:T(8,128)(2,1)S(1)} %get-tuple-element.64), channel_id=1, source_target_pairs={{0,192},{1,193},{2,194},{3,195},{4,196},{5,197},{6,198},{7,199},{8... | collective-permute-start | bytes 1990664 | tf_op jit(solution)/shard_map/ppermute | solution.py:66
  129.4 19.0 %collective-permute-start.21 = (bf16[144,2304]{1,0:T(8,128)(2,1)S(1)}, bf16[144,2304]{1,0:T(8,128)(2,1)S(1)}, u32[]{:S(2)}, u32[]{:S(2)}) collective-permute-start(bf16[144,2304]{1,0:T(8,128)(2,1)S(1)} %get-tuple-element.62), channel_id=1, source_target_pairs={{0,64},{1,65},{2,66},{3,67},{4,68},{5,69},{6,70},{7,71},{8,72},{9,... | collective-permute-start | bytes 1990664 | tf_op jit(solution)/shard_map/ppermute | solution.py:66
  137.3 25.3 %collective-permute-start.19 = (bf16[144,2304]{1,0:T(8,128)(2,1)S(1)}, bf16[144,2304]{1,0:T(8,128)(2,1)S(1)}, u32[]{:S(2)}, u32[]{:S(2)}) collective-permute-start(bf16[144,2304]{1,0:T(8,128)(2,1)S(1)} %get-tuple-element.59), channel_id=1, source_target_pairs={{0,64},{1,65},{2,66},{3,67},{4,68},{5,69},{6,70},{7,71},{8,72},{9,... | collective-permute-start | bytes 1990664 | tf_op jit(solution)/shard_map/ppermute | solution.py:66
  138.0 24.6 %collective-permute-start.20 = (bf16[144,2304]{1,0:T(8,128)(2,1)S(1)}, bf16[144,2304]{1,0:T(8,128)(2,1)S(1)}, u32[]{:S(2)}, u32[]{:S(2)}) collective-permute-start(bf16[144,2304]{1,0:T(8,128)(2,1)S(1)} %get-tuple-element.60), channel_id=1, source_target_pairs={{0,192},{1,193},{2,194},{3,195},{4,196},{5,197},{6,198},{7,199},{8... | collective-permute-start | bytes 1990664 | tf_op jit(solution)/shard_map/ppermute | solution.py:66
  148.6 27.1 %collective-permute-start.23 = (bf16[144,2304]{1,0:T(8,128)(2,1)S(1)}, bf16[144,2304]{1,0:T(8,128)(2,1)S(1)}, u32[]{:S(2)}, u32[]{:S(2)}) collective-permute-start(bf16[144,2304]{1,0:T(8,128)(2,1)S(1)} %add_convert_fusion.1), channel_id=1, source_target_pairs={{0,64},{1,65},{2,66},{3,67},{4,68},{5,69},{6,70},{7,71},{8,72},{9,... | collective-permute-start | bytes 1990664 | tf_op jit(solution)/shard_map/ppermute | solution.py:66
  148.7 27.2 %collective-permute-start.24 = (bf16[144,2304]{1,0:T(8,128)(2,1)S(1)}, bf16[144,2304]{1,0:T(8,128)(2,1)S(1)}, u32[]{:S(2)}, u32[]{:S(2)}) collective-permute-start(bf16[144,2304]{1,0:T(8,128)(2,1)S(1)} %add_convert_fusion), channel_id=1, source_target_pairs={{0,192},{1,193},{2,194},{3,195},{4,196},{5,197},{6,198},{7,199},{8... | collective-permute-start | bytes 1990664 | tf_op jit(solution)/shard_map/ppermute | solution.py:66
  175.9 1.8 copy-start.8

commit v7 on v5

--- a/solution.py
+++ b/solution.py
@@ -185,33 +185,31 @@
     grams = (grams.astype(F32) + send(grams, XLO).astype(F32)).astype(BF)
     others = jnp.sum(other_sq, axis=1)
     others = others + send(others, XLO)
-    sources, grams, flat, others = stage((sources, grams, flat, others))
+    own, grams, flat, others = stage((jnp.stack(sources), grams, flat, others))
 
     up = send(flat[:seq], along_x(1))
     down = send(flat[seq:], along_x(-1))
-    own = jnp.stack(sources)
+    sibling = send(flat, CORE)
     fwd, bwd = [own, send(own, along_z(1))], [own, send(own, along_z(-1))]
     shape = grams.shape
     grams = jnp.moveaxis(grams.reshape(shape[:3] + (NZ, -1, shape[4])), 3, 0)
     grams = all_to_all(grams, "tensor", z_rings).astype(F32).sum(axis=0)
     weight = jnp.array([1.0, 2.0, 1.0], F32)[:, None, None, None]
     total = jnp.sum(grams[0] * grams[1] * weight, axis=(0, 2, 3)) + others
-    up, down, fwd[1], bwd[1], total = stage((up, down, fwd[1], bwd[1], total))
+    up, down, sibling, fwd[1], bwd[1], total = stage((up, down, sibling, fwd[1], bwd[1], total))
 
     up, down = send(up, along_x(1)), send(down, along_x(-1))
     fwd.append(send(fwd[1], along_z(1)))
     bwd.append(send(bwd[1], along_z(-1)))
-    sibling = send(flat, CORE)
     total = all_to_all(jnp.broadcast_to(total, (NZ, examples)), "tensor", z_rings).sum(axis=0)
     fwd[2], bwd[2], total = stage((fwd[2], bwd[2], total))
 
     fwd.append(send(fwd[2], along_z(1)))
     bwd.append(send(bwd[2], along_z(-1)))
+    far = [send(fwd[2][0], along_z(2)), send(bwd[2][1], along_z(-2))]
     clip = jnp.minimum(1.0, clip_norm / jnp.sqrt(total))
     clips = all_to_all(jnp.broadcast_to(clip, (4, examples)), "dp", chip_pairs).reshape(-1)
-    fwd[3], bwd[3], clips, up, down = stage((fwd[3], bwd[3], clips, up, down))
-
-    far = [send(fwd[3][0], along_z(1)), send(bwd[3][1], along_z(-1))]
+    fwd[3], bwd[3], far, clips, up, down = stage((fwd[3], bwd[3], far, clips, up, down))
     up_sibling, down_sibling = send(up, CORE), send(down, CORE)
     pieces = [own, fwd[1], fwd[2], fwd[3], far[0], far[1], bwd[3], bwd[2], bwd[1]]
     places = jnp.stack([dp, te]).astype(jnp.int32)

time: 176 us -> 178 us (1.011); the launches traced: 173 us -> 177 us
  blocking collectives: 24.9 us -> 22.1 us
  local copies, waits for them, and re-layouts: 8.26 us -> 10.2 us
  other arithmetic: 5.19 us -> 7.04 us
    all_to_all x2, blocking collectives: 24.9 us -> 22.1 us  [all_to_all(): lax.all_to_all(value, axis, 0, 0, tiled=True, axis_index_groups=groups)]
    unnamed x14 -> x18, local copies, waits for them, and re-layouts: 1.09 us -> 3.46 us
  transfers between devices with their start and end apart: 26 -> 26, of which waited for: 12 -> 10; matrix products, arithmetic and copies ran while one was open for 5% -> 8% of each run, Pallas kernels for 9% -> 9%
where the time goes in v7:
time: 178 us; the launch traced here: 177 us
  waiting for transfers between devices  70.3 us (39%)
  starting transfers between devices  41.5 us (23%)
  blocking collectives  22.1 us (12%)
  Pallas kernels  21.5 us (12%)
  local copies, waits for them, and re-layouts  10.2 us (6%)
  other arithmetic  7.04 us (4%)
  matrix products  4.58 us (3%)
    ppermute x25, waiting for transfers between devices, send(): return lax.ppermute(value, AXES, perm)  57.9 us
    ppermute x25, starting transfers between devices, send(): return lax.ppermute(value, AXES, perm)  32.6 us
    all_to_all x2, blocking collectives, all_to_all(): lax.all_to_all(value, axis, 0, 0, tiled=True, axis_index_groups=groups)  22.1 us
    pallas_call x3, Pallas kernels, product(): pl.pallas_call(product_kernel, out_shape=[jax.ShapeDtypeStruct((count, wi...  18.6 us
    all_to_all x1, waiting for transfers between devices, all_to_all(): lax.all_to_all(value, axis, 0, 0, tiled=True, axis_index_groups=groups)  12.4 us
    all_to_all x1, starting transfers between devices, all_to_all(): lax.all_to_all(value, axis, 0, 0, tiled=True, axis_index_groups=groups)  8.85 us
    dot_general x2, matrix products, blocks(): jnp.einsum('btf,bsf->bts', x, x, preferred_element_type=F32).astype(BF)  4.58 us
  transfers between devices with their start and end apart: 26, of which 10 were waited for; matrix products, arithmetic and copies ran while one was open for 8% of the time, Pallas kernels for 9%

profile of v7, /device:TPU:32, one launch (start us, length us, event | category | flops | bytes accessed | tf_op | source)
XLA Modules:
  0.0 177.4 jit_solution(16319290972479052248)
XLA Ops:
  0.0 1.0 copy.16
  1.0 2.4 %collective-permute-start.1 = (bf16[288,512]{1,0:T(8,128)(2,1)S(1)}, bf16[288,512]{1,0:T(8,128)(2,1)S(1)}, u32[]{:S(2)}, u32[]{:S(2)}) collective-permute-start(bf16[288,512]{1,0:T(8,128)(2,1)S(1)} %bitcast.50), channel_id=1, source_target_pairs={{0,8},{1,26},{2,44},{3,58},{4,12},{5,30},{6,40},{7,62},{8,0},{9,18... | collective-permute-start | bytes 884744 | tf_op jit(solution)/shard_map/ppermute | solution.py:66
  3.3 3.6 %collective-permute-start = (bf16[288,512]{1,0:T(8,128)(2,1)S(1)}, bf16[288,512]{1,0:T(8,128)(2,1)}, u32[]{:S(2)}, u32[]{:S(2)}) collective-permute-start(bf16[288,512]{1,0:T(8,128)(2,1)S(1)} %bitcast.51), channel_id=1, source_target_pairs={{0,0},{1,18},{2,36},{3,50},{4,4},{5,22},{6,32},{7,54},{8,8},{9,26}... | collective-permute-start | bytes 884744 | tf_op jit(solution)/shard_map/ppermute | solution.py:66
  6.9 1.4 convolution_convert_fusion
  8.3 3.2 %convolution_convert_fusion.1 = bf16[2,256,256]{2,1,0:T(8,128)(2,1)S(1)} fusion(bf16[2,256,2304]{2,1,0:T(8,128)(2,1)} %param.5), kind=kOutput, calls=%fused_computation.9 | convolution fusion | flops 604110848 | bytes 2621440 | tf_op jit(solution)/shard_map/btf,bsf->bts/dot_general | solution.py:180
  11.7 0.8 pad_maximum_fusion.1
  12.4 0.2 collective-permute-start.2
  12.7 0.1 reduce_sum.36
  12.8 1.9 %collective-permute-start.3 = (f32[2]{0:T(128)S(1)}, f32[2]{0:T(128)S(1)}, u32[]{:S(2)}, u32[]{:S(2)}) collective-permute-start(f32[2]{0:T(128)S(1)} %reduce_sum.36), channel_id=1, source_target_pairs={{0,8},{1,9},{2,10},{3,11},{4,12},{5,13},{6,14},{7,15},{8,0},{9,1},... | collective-permute-start | bytes 32 | tf_op jit(solution)/shard_map/ppermute | solution.py:66
  14.7 10.3 %collective-permute-done.3 = f32[2]{0:T(128)S(1)} collective-permute-done((f32[2]{0:T(128)S(1)}, f32[2]{0:T(128)S(1)}, u32[]{:S(2)}, u32[]{:S(2)}) %collective-permute-start.3) | collective-permute-done | bytes 40 | tf_op jit(solution)/shard_map/ppermute | solution.py:66
  25.0 0.7 copy-done.6
  25.7 1.1 pad_maximum_fusion.refs_0_
  26.8 1.3 add_convert_fusion.2
  28.1 0.1 collective-permute-start.6
  28.2 1.6 fusion.6
  29.8 1.1 collective-permute-start.5
  30.9 0.9 collective-permute-start.4
  31.8 0.8 copy.18
  32.6 8.8 %all-to-all-start = ((bf16[8,2,3,2,16,128]{5,4,3,2,1,0:T(8,128)(2,1)}), bf16[8,2,3,2,16,128]{5,4,3,2,1,0:T(8,128)(2,1)S(1)}, u32[]{:S(2)}, u32[]{:S(2)}) async-start(bf16[8,2,3,2,16,128]{5,4,3,2,1,0:T(8,128)(2,1)} %bitcast.42), calls=%async_computation | async-start | bytes 786432 | tf_op jit(solution)/shard_map/all_to_all | solution.py:161
  41.5 2.0 %collective-permute-start.7 = (bf16[2,288,512]{2,1,0:T(8,128)(2,1)S(1)}, bf16[2,288,512]{2,1,0:T(8,128)(2,1)}, u32[]{:S(2)}, u32[]{:S(2)}) collective-permute-start(bf16[2,288,512]{2,1,0:T(8,128)(2,1)S(1)} %pad_maximum_fusion.refs_0_), channel_id=1, source_target_pairs={{0,1},{1,2},{2,3},{3,4},{4,5},{5,6},{6,7},{7,0},{8,9},{9,10},{10,1... | collective-permute-start | bytes 1769480 | tf_op jit(solution)/shard_map/ppermute | solution.py:66
  43.5 12.4 %all-to-all-done = bf16[8,2,3,2,16,128]{5,4,3,2,1,0:T(8,128)(2,1)S(1)} async-done(((bf16[8,2,3,2,16,128]{5,4,3,2,1,0:T(8,128)(2,1)}), bf16[8,2,3,2,16,128]{5,4,3,2,1,0:T(8,128)(2,1)S(1)}, u32[]{:S(2)}, u32[]{:S(2)}) %all-to-all-start) | async-done | bytes 393248 | tf_op jit(solution)/shard_map/all_to_all | solution.py:161
  56.0 0.2 fusion.5
  56.2 8.4 %collective-permute-done.8.refs_8_ = bf16[2,288,512]{2,1,0:T(8,128)(2,1)} collective-permute-done((bf16[2,288,512]{2,1,0:T(8,128)(2,1)S(1)}, bf16[2,288,512]{2,1,0:T(8,128)(2,1)}, u32[]{:S(2)}, u32[]{:S(2)}) %collective-permute-start.8) | collective-permute-done | bytes 589856 | tf_op jit(solution)/shard_map/ppermute | solution.py:66
  64.6 1.5 collective-permute-start.9
  66.1 0.6 collective-permute-start.10
  66.7 0.6 collective-permute-start.15
  67.3 2.6 %collective-permute-start.16 = (bf16[256,2304]{1,0:T(8,128)(2,1)}, bf16[256,2304]{1,0:T(8,128)(2,1)}, u32[]{:S(2)}, u32[]{:S(2)}) collective-permute-start(bf16[256,2304]{1,0:T(8,128)(2,1)} %collective-permute-done.5), channel_id=1, source_target_pairs={{0,40},{1,41},{2,42},{3,43},{4,44},{5,45},{6,46},{7,47},{8,0},{9,1... | collective-permute-start | bytes 3538952 | tf_op jit(solution)/shard_map/ppermute | solution.py:66
  69.9 14.3 %all_to_all.17 = f32[8,1,2]{2,1,0:T(1,128)S(1)} all-to-all(f32[8,1,2]{2,1,0:T(1,128)S(1)} %broadcast_in_dim.7), channel_id=1, replica_groups={{0,1,2,3,4,5,6,7},{8,9,10,11,12,13,14,15},{16,17,18,19,20,21,22,23},{24..., dimensions={0} | all-to-all | bytes 128 | tf_op jit(solution)/shard_map/all_to_all | solution.py:161
  84.2 1.0 slice_bitcast_fusion
  85.2 1.9 %collective-permute-start.14 = (bf16[288,512]{1,0:T(8,128)(2,1)S(1)}, bf16[288,512]{1,0:T(8,128)(2,1)S(1)}, u32[]{:S(2)}, u32[]{:S(2)}) collective-permute-start(bf16[288,512]{1,0:T(8,128)(2,1)S(1)} %slice_bitcast_fusion), channel_id=1, source_target_pairs={{0,6},{1,7},{2,0},{3,1},{4,2},{5,3},{6,4},{7,5},{8,14},{9,15},{10,... | collective-permute-start | bytes 884744 | tf_op jit(solution)/shard_map/ppermute | solution.py:66
  87.1 0.4 collective-permute-start.11
  87.5 1.7 collective-permute-start.12
  89.1 1.7 slice_bitcast_fusion.1
  90.8 11.5 %collective-permute-done.14.refs_5_ = bf16[288,512]{1,0:T(8,128)(2,1)S(1)} collective-permute-done((bf16[288,512]{1,0:T(8,128)(2,1)S(1)}, bf16[288,512]{1,0:T(8,128)(2,1)S(1)}, u32[]{:S(2)}, u32[]{:S(2)}) %collective-permute-start.14) | collective-permute-done | bytes 294944 | tf_op jit(solution)/shard_map/ppermute | solution.py:66
  102.3 0.7 copy-done.3
  103.1 0.5 collective-permute-start.13
  103.6 7.8 %all_to_all.18 = f32[4,1,2]{2,1,0:T(1,128)S(1)} all-to-all(f32[4,1,2]{2,1,0:T(1,128)S(1)} %broadcast_in_dim.8), channel_id=1, replica_groups={{0,16,32,48},{64,80,96,112},{128,144,160,176},{192,208,224,240},{1,17,3..., dimensions={0} | all-to-all | bytes 64 | tf_op jit(solution)/shard_map/all_to_all | solution.py:161
  111.4 0.5 broadcast.21
  111.9 0.6 reduce.4
  112.6 1.3 collective-permute-done.13.refs_4_
  113.9 0.1 collective-permute-start.17
  114.0 0.5 collective-permute-start.18
  114.6 1.1 copy-done.2
  115.7 1.0 copy-done.4
  116.6 2.9 %scale_grads.1.s_ref = bf16[4,4,288,512]{3,2,1,0:T(8,128)(2,1)S(1)} custom-call(s32[2]{0:T(128)S(1)} %pad_add_fusion.place_ref, f32[8]{0:T(128)S(1)} %reshape.26.clip_ref, bf16[2,288,512]{2,1,0:T(8,128)(2,1)S(1)} %copy-done.2, bf16[2,288,512]{2,1,0:T(8,128)(2,1)} %collective-permute-done.7.refs_1_, bf16[2,288,512]{2,1,0:T(8,128)(2,1)} %collective-permute-done.9.refs_2_, ...), custom_call_target="tpu_custom_call" | custom-call | flops 2359296 | bytes 147456 | tf_op jit(solution)/shard_map/scale_grads/pallas_call | solution.py:103
  119.6 5.3 %product_far.1 = (bf16[144,2304]{1,0:T(8,128)(2,1)S(1)}, bf16[144,2304]{1,0:T(8,128)(2,1)S(1)}) custom-call(bf16[4,4,288,512]{3,2,1,0:T(8,128)(2,1)S(1)} %scale_grads.1.s_ref, bf16[512,2304]{1,0:T(8,128)(2,1)S(1)} %bitcast.45, bf16[512,2304]{1,0:T(8,128)(2,1)} %collective-permute-done.6.refs_1_, bf16[256,2304]{1,0:T(8,128)(2,1)S(1)} %collective-permute-done.15.refs_2_, ...), custom_call_target="tpu_custom_call" | custom-call | flops 1327104 | bytes 1327104 | tf_op jit(solution)/shard_map/product_far/pallas_call | solution.py:143
  124.9 1.7 collective-permute-start.19
  126.5 1.7 collective-permute-start.20
  128.2 7.9 %product_near.1 = (bf16[144,2304]{1,0:T(8,128)(2,1)S(1)}, bf16[144,2304]{1,0:T(8,128)(2,1)S(1)}, bf16[144,2304]{1,0:T(8,128)(2,1)S(1)}, bf16[144,2304]{1,0:T(8,128)(2,1)S(1)}) custom-call(bf16[4,4,288,512]{3,2,1,0:T(8,128)(2,1)S(1)} %scale_grads.1.s_ref, bf16[512,2304]{1,0:T(8,128)(2,1)S(1)} %bitcast.46, bf16[512,2304]{1,0:T(8,128)(2,1)} %collective-permute-done.6.refs_1_, ...), custom_call_target="tpu_custom_call" | custom-call | flops 2654208 | bytes 1327104 | tf_op jit(solution)/shard_map/product_near/pallas_call | solution.py:143
  136.1 1.9 %collective-permute-start.22 = (bf16[144,2304]{1,0:T(8,128)(2,1)S(1)}, bf16[144,2304]{1,0:T(8,128)(2,1)S(1)}, u32[]{:S(2)}, u32[]{:S(2)}) collective-permute-start(bf16[144,2304]{1,0:T(8,128)(2,1)S(1)} %get-tuple-element.60), channel_id=1, source_target_pairs={{0,192},{1,193},{2,194},{3,195},{4,196},{5,197},{6,198},{7,199},{8... | collective-permute-start | bytes 1990664 | tf_op jit(solution)/shard_map/ppermute | solution.py:66
  138.0 5.2 %collective-permute-done.19 = bf16[144,2304]{1,0:T(8,128)(2,1)S(1)} collective-permute-done((bf16[144,2304]{1,0:T(8,128)(2,1)S(1)}, bf16[144,2304]{1,0:T(8,128)(2,1)S(1)}, u32[]{:S(2)}, u32[]{:S(2)}) %collective-permute-start.19) | collective-permute-done | bytes 663584 | tf_op jit(solution)/shard_map/ppermute | solution.py:66
  143.2 0.2 add_convert_fusion.1
  143.3 1.0 collective-permute-done.20
  144.3 0.2 add_convert_fusion
  144.5 1.7 collective-permute-start.21
  146.2 1.3 collective-permute-start.23
  147.4 2.0 %collective-permute-start.24 = (bf16[144,2304]{1,0:T(8,128)(2,1)S(1)}, bf16[144,2304]{1,0:T(8,128)(2,1)S(1)}, u32[]{:S(2)}, u32[]{:S(2)}) collective-permute-start(bf16[144,2304]{1,0:T(8,128)(2,1)S(1)} %add_convert_fusion), channel_id=1, source_target_pairs={{0,192},{1,193},{2,194},{3,195},{4,196},{5,197},{6,198},{7,199},{8... | collective-permute-start | bytes 1990664 | tf_op jit(solution)/shard_map/ppermute | solution.py:66
  149.4 5.4 %product_own.1 = f32[288,2304]{1,0:T(8,128)S(1)} custom-call(bf16[4,4,288,512]{3,2,1,0:T(8,128)(2,1)S(1)} %scale_grads.1.s_ref, bf16[512,2304]{1,0:T(8,128)(2,1)S(1)} %bitcast.47, bf16[512,2304]{1,0:T(8,128)(2,1)} %collective-permute-done.6.refs_1_, bf16[256,2304]{1,0:T(8,128)(2,1)S(1)} %collective-permute-done.15.refs_2_, ...), custom_call_target="tpu_custom_call" | custom-call | flops 1327104 | bytes 1327104 | tf_op jit(solution)/shard_map/product_own/pallas_call | solution.py:143
  154.8 3.8 %collective-permute-done.22 = bf16[144,2304]{1,0:T(8,128)(2,1)S(1)} collective-permute-done((bf16[144,2304]{1,0:T(8,128)(2,1)S(1)}, bf16[144,2304]{1,0:T(8,128)(2,1)S(1)}, u32[]{:S(2)}, u32[]{:S(2)}) %collective-permute-start.22) | collective-permute-done | bytes 663584 | tf_op jit(solution)/shard_map/ppermute | solution.py:66
  158.6 5.1 %collective-permute-done.21 = bf16[144,2304]{1,0:T(8,128)(2,1)S(1)} collective-permute-done((bf16[144,2304]{1,0:T(8,128)(2,1)S(1)}, bf16[144,2304]{1,0:T(8,128)(2,1)S(1)}, u32[]{:S(2)}, u32[]{:S(2)}) %collective-permute-start.21) | collective-permute-done | bytes 663584 | tf_op jit(solution)/shard_map/ppermute | solution.py:66
  163.6 0.1 convert_add_fusion.1
  163.8 11.4 %collective-permute-done.23 = bf16[144,2304]{1,0:T(8,128)(2,1)S(1)} collective-permute-done((bf16[144,2304]{1,0:T(8,128)(2,1)S(1)}, bf16[144,2304]{1,0:T(8,128)(2,1)S(1)}, u32[]{:S(2)}, u32[]{:S(2)}) %collective-permute-start.23) | collective-permute-done | bytes 663584 | tf_op jit(solution)/shard_map/ppermute | solution.py:66
  175.2 0.1 convert_add_fusion
  175.3 2.1 %fusion.2 = f32[288,2304]{1,0:T(8,128)} fusion(f32[288,2304]{1,0:T(8,128)S(1)} %copy-done.5, f32[288,2304]{1,0:T(8,128)S(1)} %product_own.1, f32[144,2304]{1,0:T(8,128)S(1)} %convert_add_fusion, f32[144,2304]{1,0:T(8,128)S(1)} %convert_add_fusion.1), kind=kLoop, calls=%fused_computation.3 | loop fusion | flops 3317760 | bytes 10616832 | tf_op jit(solution)/shard_map/div | solution.py:236
  (43 shorter events, 0.5 us)
Async XLA Ops:
  1.0 24.0 %collective-permute-start.1 = (bf16[288,512]{1,0:T(8,128)(2,1)S(1)}, bf16[288,512]{1,0:T(8,128)(2,1)S(1)}, u32[]{:S(2)}, u32[]{:S(2)}) collective-permute-start(bf16[288,512]{1,0:T(8,128)(2,1)S(1)} %bitcast.50), channel_id=1, source_target_pairs={{0,8},{1,26},{2,44},{3,58},{4,12},{5,30},{6,40},{7,62},{8,0},{9,18... | collective-permute-start | bytes 884744 | tf_op jit(solution)/shard_map/ppermute | solution.py:66
  3.3 21.6 %collective-permute-start = (bf16[288,512]{1,0:T(8,128)(2,1)S(1)}, bf16[288,512]{1,0:T(8,128)(2,1)}, u32[]{:S(2)}, u32[]{:S(2)}) collective-permute-start(bf16[288,512]{1,0:T(8,128)(2,1)S(1)} %bitcast.51), channel_id=1, source_target_pairs={{0,0},{1,18},{2,36},{3,50},{4,4},{5,22},{6,32},{7,54},{8,8},{9,26}... | collective-permute-start | bytes 884744 | tf_op jit(solution)/shard_map/ppermute | solution.py:66
  11.5 1.2 copy-start.7
  12.4 15.7 %copy-start = (bf16[2,256,2304]{2,1,0:T(8,128)(2,1)S(1)}, bf16[2,256,2304]{2,1,0:T(8,128)(2,1)}, u32[]{:S(2)}) copy-start(bf16[2,256,2304]{2,1,0:T(8,128)(2,1)} %param.5) | copy-start | bytes 7077892
  12.4 14.3 %collective-permute-start.2 = (bf16[2,3,2,128,128]{4,3,2,1,0:T(8,128)(2,1)}, bf16[2,3,2,128,128]{4,3,2,1,0:T(8,128)(2,1)}, u32[]{:S(2)}, u32[]{:S(2)}) collective-permute-start(bf16[2,3,2,128,128]{4,3,2,1,0:T(8,128)(2,1)} %pad_maximum_fusion.1), channel_id=1, source_target_pairs={{0,8},{1,9},{2,10},{3,11},{4,12},{5,13},{6,14},{7,15},{8,0},{9,1},... | collective-permute-start | bytes 1179656 | tf_op jit(solution)/shard_map/ppermute | solution.py:66
  12.8 12.2 %collective-permute-start.3 = (f32[2]{0:T(128)S(1)}, f32[2]{0:T(128)S(1)}, u32[]{:S(2)}, u32[]{:S(2)}) collective-permute-start(f32[2]{0:T(128)S(1)} %reduce_sum.36), channel_id=1, source_target_pairs={{0,8},{1,9},{2,10},{3,11},{4,12},{5,13},{6,14},{7,15},{8,0},{9,1},... | collective-permute-start | bytes 32 | tf_op jit(solution)/shard_map/ppermute | solution.py:66
  25.0 0.7 copy-start.6
  26.8 14.7 %copy-start.1 = (bf16[2,288,512]{2,1,0:T(8,128)(2,1)}, bf16[2,288,512]{2,1,0:T(8,128)(2,1)S(1)}, u32[]{:S(2)}) copy-start(bf16[2,288,512]{2,1,0:T(8,128)(2,1)S(1)} %pad_maximum_fusion.refs_0_) | copy-start | bytes 1769476
  28.1 36.4 %collective-permute-start.6 = (bf16[512,2304]{1,0:T(8,128)(2,1)S(1)}, bf16[512,2304]{1,0:T(8,128)(2,1)}, u32[]{:S(2)}, u32[]{:S(2)}) collective-permute-start(bf16[512,2304]{1,0:T(8,128)(2,1)S(1)} %bitcast.43), channel_id=1, source_target_pairs={{0,16},{1,17},{2,18},{3,19},{4,20},{5,21},{6,22},{7,23},{8,24},{9,... | collective-permute-start | bytes 7077896 | tf_op jit(solution)/shard_map/ppermute | solution.py:66
  29.8 26.2 %copy-start.8 = (f32[3]{0:T(128)S(1)}, f32[3]{0:T(128)}, u32[]{:S(2)}) copy-start(f32[3]{0:T(128)} %constant.20.clone) | copy-start | bytes 40
  29.8 34.8 %collective-permute-start.5 = (bf16[256,2304]{1,0:T(8,128)(2,1)}, bf16[256,2304]{1,0:T(8,128)(2,1)}, u32[]{:S(2)}, u32[]{:S(2)}) collective-permute-start(bf16[256,2304]{1,0:T(8,128)(2,1)} %get-tuple-element.63), channel_id=1, source_target_pairs={{0,40},{1,41},{2,42},{3,43},{4,44},{5,45},{6,46},{7,47},{8,0},{9,1... | collective-permute-start | bytes 3538952 | tf_op jit(solution)/shard_map/ppermute | solution.py:66
  30.9 33.6 %collective-permute-start.4 = (bf16[256,2304]{1,0:T(8,128)(2,1)}, bf16[256,2304]{1,0:T(8,128)(2,1)}, u32[]{:S(2)}, u32[]{:S(2)}) collective-permute-start(bf16[256,2304]{1,0:T(8,128)(2,1)} %get-tuple-element.64), channel_id=1, source_target_pairs={{0,8},{1,9},{2,10},{3,11},{4,12},{5,13},{6,14},{7,15},{8,32},{9,33... | collective-permute-start | bytes 3538952 | tf_op jit(solution)/shard_map/ppermute | solution.py:66
  32.6 23.3 %all-to-all-start = ((bf16[8,2,3,2,16,128]{5,4,3,2,1,0:T(8,128)(2,1)}), bf16[8,2,3,2,16,128]{5,4,3,2,1,0:T(8,128)(2,1)S(1)}, u32[]{:S(2)}, u32[]{:S(2)}) async-start(bf16[8,2,3,2,16,128]{5,4,3,2,1,0:T(8,128)(2,1)} %bitcast.42), calls=%async_computation | async-start | bytes 786432 | tf_op jit(solution)/shard_map/all_to_all | solution.py:161
  41.5 23.1 %collective-permute-start.8 = (bf16[2,288,512]{2,1,0:T(8,128)(2,1)S(1)}, bf16[2,288,512]{2,1,0:T(8,128)(2,1)}, u32[]{:S(2)}, u32[]{:S(2)}) collective-permute-start(bf16[2,288,512]{2,1,0:T(8,128)(2,1)S(1)} %pad_maximum_fusion.refs_0_), channel_id=1, source_target_pairs={{0,7},{1,0},{2,1},{3,2},{4,3},{5,4},{6,5},{7,6},{8,15},{9,8},{10,9... | collective-permute-start | bytes 1769480 | tf_op jit(solution)/shard_map/ppermute | solution.py:66
  41.5 23.0 %collective-permute-start.7 = (bf16[2,288,512]{2,1,0:T(8,128)(2,1)S(1)}, bf16[2,288,512]{2,1,0:T(8,128)(2,1)}, u32[]{:S(2)}, u32[]{:S(2)}) collective-permute-start(bf16[2,288,512]{2,1,0:T(8,128)(2,1)S(1)} %pad_maximum_fusion.refs_0_), channel_id=1, source_target_pairs={{0,1},{1,2},{2,3},{3,4},{4,5},{5,6},{6,7},{7,0},{8,9},{9,10},{10,1... | collective-permute-start | bytes 1769480 | tf_op jit(solution)/shard_map/ppermute | solution.py:66
  64.6 19.6 %collective-permute-start.9 = (bf16[2,288,512]{2,1,0:T(8,128)(2,1)}, bf16[2,288,512]{2,1,0:T(8,128)(2,1)}, u32[]{:S(2)}, u32[]{:S(2)}) collective-permute-start(bf16[2,288,512]{2,1,0:T(8,128)(2,1)} %collective-permute-done.7.refs_1_), channel_id=1, source_target_pairs={{0,1},{1,2},{2,3},{3,4},{4,5},{5,6},{6,7},{7,0},{8,9},{9,10},{10,1... | collective-permute-start | bytes 1769480 | tf_op jit(solution)/shard_map/ppermute | solution.py:66
  66.1 18.1 %collective-permute-start.10 = (bf16[2,288,512]{2,1,0:T(8,128)(2,1)}, bf16[2,288,512]{2,1,0:T(8,128)(2,1)}, u32[]{:S(2)}, u32[]{:S(2)}) collective-permute-start(bf16[2,288,512]{2,1,0:T(8,128)(2,1)} %collective-permute-done.8.refs_8_), channel_id=1, source_target_pairs={{0,7},{1,0},{2,1},{3,2},{4,3},{5,4},{6,5},{7,6},{8,15},{9,8},{10,9... | collective-permute-start | bytes 1769480 | tf_op jit(solution)/shard_map/ppermute | solution.py:66
  66.7 47.2 %collective-permute-start.15 = (bf16[256,2304]{1,0:T(8,128)(2,1)}, bf16[256,2304]{1,0:T(8,128)(2,1)S(1)}, u32[]{:S(2)}, u32[]{:S(2)}) collective-permute-start(bf16[256,2304]{1,0:T(8,128)(2,1)} %collective-permute-done.4), channel_id=1, source_target_pairs={{0,8},{1,9},{2,10},{3,11},{4,12},{5,13},{6,14},{7,15},{8,32},{9,33... | collective-permute-start | bytes 3538952 | tf_op jit(solution)/shard_map/ppermute | solution.py:66
  67.3 46.6 %collective-permute-start.16 = (bf16[256,2304]{1,0:T(8,128)(2,1)}, bf16[256,2304]{1,0:T(8,128)(2,1)}, u32[]{:S(2)}, u32[]{:S(2)}) collective-permute-start(bf16[256,2304]{1,0:T(8,128)(2,1)} %collective-permute-done.5), channel_id=1, source_target_pairs={{0,40},{1,41},{2,42},{3,43},{4,44},{5,45},{6,46},{7,47},{8,0},{9,1... | collective-permute-start | bytes 3538952 | tf_op jit(solution)/shard_map/ppermute | solution.py:66
  85.2 17.1 %collective-permute-start.14 = (bf16[288,512]{1,0:T(8,128)(2,1)S(1)}, bf16[288,512]{1,0:T(8,128)(2,1)S(1)}, u32[]{:S(2)}, u32[]{:S(2)}) collective-permute-start(bf16[288,512]{1,0:T(8,128)(2,1)S(1)} %slice_bitcast_fusion), channel_id=1, source_target_pairs={{0,6},{1,7},{2,0},{3,1},{4,2},{5,3},{6,4},{7,5},{8,14},{9,15},{10,... | collective-permute-start | bytes 884744 | tf_op jit(solution)/shard_map/ppermute | solution.py:66
  87.1 26.8 %collective-permute-start.11 = (bf16[2,288,512]{2,1,0:T(8,128)(2,1)}, bf16[2,288,512]{2,1,0:T(8,128)(2,1)}, u32[]{:S(2)}, u32[]{:S(2)}) collective-permute-start(bf16[2,288,512]{2,1,0:T(8,128)(2,1)} %collective-permute-done.9.refs_2_), channel_id=1, source_target_pairs={{0,1},{1,2},{2,3},{3,4},{4,5},{5,6},{6,7},{7,0},{8,9},{9,10},{10,1... | collective-permute-start | bytes 1769480 | tf_op jit(solution)/shard_map/ppermute | solution.py:66
  87.5 26.4 %collective-permute-start.12 = (bf16[2,288,512]{2,1,0:T(8,128)(2,1)}, bf16[2,288,512]{2,1,0:T(8,128)(2,1)}, u32[]{:S(2)}, u32[]{:S(2)}) collective-permute-start(bf16[2,288,512]{2,1,0:T(8,128)(2,1)} %collective-permute-done.10.refs_7_), channel_id=1, source_target_pairs={{0,7},{1,0},{2,1},{3,2},{4,3},{5,4},{6,5},{7,6},{8,15},{9,8},{10,9... | collective-permute-start | bytes 1769480 | tf_op jit(solution)/shard_map/ppermute | solution.py:66
  102.3 0.7 copy-start.3
  103.1 10.8 %collective-permute-start.13 = (bf16[288,512]{1,0:T(8,128)(2,1)}, bf16[288,512]{1,0:T(8,128)(2,1)}, u32[]{:S(2)}, u32[]{:S(2)}) collective-permute-start(bf16[288,512]{1,0:T(8,128)(2,1)} %slice_bitcast_fusion.1), channel_id=1, source_target_pairs={{0,2},{1,3},{2,4},{3,5},{4,6},{5,7},{6,0},{7,1},{8,10},{9,11},{10,... | collective-permute-start | bytes 884744 | tf_op jit(solution)/shard_map/ppermute | solution.py:66
  113.9 5.6 %collective-permute-start.17 = (bf16[256,2304]{1,0:T(8,128)(2,1)S(1)}, bf16[256,2304]{1,0:T(8,128)(2,1)}, u32[]{:S(2)}, u32[]{:S(2)}) collective-permute-start(bf16[256,2304]{1,0:T(8,128)(2,1)S(1)} %collective-permute-done.15.refs_2_), channel_id=1, source_target_pairs={{0,16},{1,17},{2,18},{3,19},{4,20},{5,21},{6,22},{7,23},{8,24},{9,... | collective-permute-start | bytes 3538952 | tf_op jit(solution)/shard_map/ppermute | solution.py:66
  114.0 5.5 %collective-permute-start.18 = (bf16[256,2304]{1,0:T(8,128)(2,1)}, bf16[256,2304]{1,0:T(8,128)(2,1)}, u32[]{:S(2)}, u32[]{:S(2)}) collective-permute-start(bf16[256,2304]{1,0:T(8,128)(2,1)} %collective-permute-done.16.refs_3_), channel_id=1, source_target_pairs={{0,16},{1,17},{2,18},{3,19},{4,20},{5,21},{6,22},{7,23},{8,24},{9,... | collective-permute-start | bytes 3538952 | tf_op jit(solution)/shard_map/ppermute | solution.py:66
  114.6 1.1 copy-start.2
  115.6 1.0 copy-start.4
  124.9 18.3 %collective-permute-start.19 = (bf16[144,2304]{1,0:T(8,128)(2,1)S(1)}, bf16[144,2304]{1,0:T(8,128)(2,1)S(1)}, u32[]{:S(2)}, u32[]{:S(2)}) collective-permute-start(bf16[144,2304]{1,0:T(8,128)(2,1)S(1)} %get-tuple-element.55), channel_id=1, source_target_pairs={{0,64},{1,65},{2,66},{3,67},{4,68},{5,69},{6,70},{7,71},{8,72},{9,... | collective-permute-start | bytes 1990664 | tf_op jit(solution)/shard_map/ppermute | solution.py:66
  126.5 17.8 %collective-permute-start.20 = (bf16[144,2304]{1,0:T(8,128)(2,1)S(1)}, bf16[144,2304]{1,0:T(8,128)(2,1)S(1)}, u32[]{:S(2)}, u32[]{:S(2)}) collective-permute-start(bf16[144,2304]{1,0:T(8,128)(2,1)S(1)} %get-tuple-element.57), channel_id=1, source_target_pairs={{0,192},{1,193},{2,194},{3,195},{4,196},{5,197},{6,198},{7,199},{8... | collective-permute-start | bytes 1990664 | tf_op jit(solution)/shard_map/ppermute | solution.py:66
  136.1 22.5 %collective-permute-start.22 = (bf16[144,2304]{1,0:T(8,128)(2,1)S(1)}, bf16[144,2304]{1,0:T(8,128)(2,1)S(1)}, u32[]{:S(2)}, u32[]{:S(2)}) collective-permute-start(bf16[144,2304]{1,0:T(8,128)(2,1)S(1)} %get-tuple-element.60), channel_id=1, source_target_pairs={{0,192},{1,193},{2,194},{3,195},{4,196},{5,197},{6,198},{7,199},{8... | collective-permute-start | bytes 1990664 | tf_op jit(solution)/shard_map/ppermute | solution.py:66
  144.5 19.1 %collective-permute-start.21 = (bf16[144,2304]{1,0:T(8,128)(2,1)S(1)}, bf16[144,2304]{1,0:T(8,128)(2,1)S(1)}, u32[]{:S(2)}, u32[]{:S(2)}) collective-permute-start(bf16[144,2304]{1,0:T(8,128)(2,1)S(1)} %add_convert_fusion.1), channel_id=1, source_target_pairs={{0,64},{1,65},{2,66},{3,67},{4,68},{5,69},{6,70},{7,71},{8,72},{9,... | collective-permute-start | bytes 1990664 | tf_op jit(solution)/shard_map/ppermute | solution.py:66
  146.2 29.0 %collective-permute-start.23 = (bf16[144,2304]{1,0:T(8,128)(2,1)S(1)}, bf16[144,2304]{1,0:T(8,128)(2,1)S(1)}, u32[]{:S(2)}, u32[]{:S(2)}) collective-permute-start(bf16[144,2304]{1,0:T(8,128)(2,1)S(1)} %get-tuple-element.61), channel_id=1, source_target_pairs={{0,64},{1,65},{2,66},{3,67},{4,68},{5,69},{6,70},{7,71},{8,72},{9,... | collective-permute-start | bytes 1990664 | tf_op jit(solution)/shard_map/ppermute | solution.py:66
  147.4 27.7 %collective-permute-start.24 = (bf16[144,2304]{1,0:T(8,128)(2,1)S(1)}, bf16[144,2304]{1,0:T(8,128)(2,1)S(1)}, u32[]{:S(2)}, u32[]{:S(2)}) collective-permute-start(bf16[144,2304]{1,0:T(8,128)(2,1)S(1)} %add_convert_fusion), channel_id=1, source_target_pairs={{0,192},{1,193},{2,194},{3,195},{4,196},{5,197},{6,198},{7,199},{8... | collective-permute-start | bytes 1990664 | tf_op jit(solution)/shard_map/ppermute | solution.py:66
  163.8 11.5 %copy-start.5 = (f32[288,2304]{1,0:T(8,128)S(1)}, f32[288,2304]{1,0:T(8,128)}, u32[]{:S(2)}) copy-start(f32[288,2304]{1,0:T(8,128)} %param.8) | copy-start | bytes 7962628

commit v8 on v7

--- a/solution.py
+++ b/solution.py
@@ -103,7 +103,7 @@
     return pl.pallas_call(
         scale_kernel,
         out_shape=jax.ShapeDtypeStruct((4, 4, rows, tokens), BF),
-        in_specs=[smem, smem] + [pl.BlockSpec(memory_space=pl.ANY)] * len(pieces),
+        in_specs=[smem, smem] + [pl.BlockSpec(memory_space=pltpu.HBM)] * len(pieces),
         out_specs=pl.BlockSpec(memory_space=pltpu.VMEM),
         scratch_shapes=[
             pltpu.VMEM((2 * NZ, rows, tokens), BF),
@@ -191,6 +191,7 @@
     down = send(flat[seq:], along_x(-1))
     sibling = send(flat, CORE)
     fwd, bwd = [own, send(own, along_z(1))], [own, send(own, along_z(-1))]
+    grams, sibling = stage((grams, sibling))
     shape = grams.shape
     grams = jnp.moveaxis(grams.reshape(shape[:3] + (NZ, -1, shape[4])), 3, 0)
     grams = all_to_all(grams, "tensor", z_rings).astype(F32).sum(axis=0)

time: 178 us -> 181 us (1.017)
    unnamed x18 -> x22, local copies, waits for them, and re-layouts: 3.46 us -> 4.91 us
  transfers between devices with their start and end apart: 26 -> 26, of which waited for: 10 -> 11; matrix products, arithmetic and copies ran while one was open for 8% -> 8% of each run, Pallas kernels for 9% -> 9%
where the time goes in v8:
time: 181 us; the launch traced here: 180 us
  waiting for transfers between devices  72 us (40%)
  starting transfers between devices  41.5 us (23%)
  blocking collectives  22.2 us (12%)
  Pallas kernels  20.8 us (11%)
  local copies, waits for them, and re-layouts  11.7 us (6%)
  other arithmetic  7.16 us (4%)
  matrix products  4.61 us (3%)
    ppermute x25, waiting for transfers between devices, send(): return lax.ppermute(value, AXES, perm)  59.4 us
    ppermute x25, starting transfers between devices, send(): return lax.ppermute(value, AXES, perm)  32.7 us
    all_to_all x2, blocking collectives, all_to_all(): lax.all_to_all(value, axis, 0, 0, tiled=True, axis_index_groups=groups)  22.2 us
    pallas_call x3, Pallas kernels, product(): pl.pallas_call(product_kernel, out_shape=[jax.ShapeDtypeStruct((count, wi...  17.9 us
    all_to_all x1, waiting for transfers between devices, all_to_all(): lax.all_to_all(value, axis, 0, 0, tiled=True, axis_index_groups=groups)  12.5 us
    all_to_all x1, starting transfers between devices, all_to_all(): lax.all_to_all(value, axis, 0, 0, tiled=True, axis_index_groups=groups)  8.86 us
    unnamed x22, local copies, waits for them, and re-layouts  4.91 us
    dot_general x2, matrix products, blocks(): jnp.einsum('btf,bsf->bts', x, x, preferred_element_type=F32).astype(BF)  4.61 us
  transfers between devices with their start and end apart: 26, of which 11 were waited for; matrix products, arithmetic and copies ran while one was open for 8% of the time, Pallas kernels for 9%

profile of v8, /device:TPU:32, one launch (start us, length us, event | category | flops | bytes accessed | tf_op | source)
XLA Modules:
  0.0 180.3 jit_solution(10748381892270854437)
XLA Ops:
  0.0 1.0 copy.16
  1.0 2.4 %collective-permute-start.1 = (bf16[288,512]{1,0:T(8,128)(2,1)S(1)}, bf16[288,512]{1,0:T(8,128)(2,1)S(1)}, u32[]{:S(2)}, u32[]{:S(2)}) collective-permute-start(bf16[288,512]{1,0:T(8,128)(2,1)S(1)} %bitcast.50), channel_id=1, source_target_pairs={{0,8},{1,26},{2,44},{3,58},{4,12},{5,30},{6,40},{7,62},{8,0},{9,18... | collective-permute-start | bytes 884744 | tf_op jit(solution)/shard_map/ppermute | solution.py:66
  3.3 3.6 %collective-permute-start = (bf16[288,512]{1,0:T(8,128)(2,1)S(1)}, bf16[288,512]{1,0:T(8,128)(2,1)}, u32[]{:S(2)}, u32[]{:S(2)}) collective-permute-start(bf16[288,512]{1,0:T(8,128)(2,1)S(1)} %bitcast.51), channel_id=1, source_target_pairs={{0,0},{1,18},{2,36},{3,50},{4,4},{5,22},{6,32},{7,54},{8,8},{9,26}... | collective-permute-start | bytes 884744 | tf_op jit(solution)/shard_map/ppermute | solution.py:66
  6.9 1.4 convolution_convert_fusion
  8.3 3.2 %convolution_convert_fusion.1 = bf16[2,256,256]{2,1,0:T(8,128)(2,1)S(1)} fusion(bf16[2,256,2304]{2,1,0:T(8,128)(2,1)} %param.5), kind=kOutput, calls=%fused_computation.9 | convolution fusion | flops 604110848 | bytes 2621440 | tf_op jit(solution)/shard_map/btf,bsf->bts/dot_general | solution.py:180
  11.7 0.8 pad_maximum_fusion.1
  12.5 0.2 collective-permute-start.2
  12.7 0.1 reduce_sum.36
  12.8 1.9 %collective-permute-start.3 = (f32[2]{0:T(128)S(1)}, f32[2]{0:T(128)S(1)}, u32[]{:S(2)}, u32[]{:S(2)}) collective-permute-start(f32[2]{0:T(128)S(1)} %reduce_sum.36), channel_id=1, source_target_pairs={{0,8},{1,9},{2,10},{3,11},{4,12},{5,13},{6,14},{7,15},{8,0},{9,1},... | collective-permute-start | bytes 32 | tf_op jit(solution)/shard_map/ppermute | solution.py:66
  14.7 10.3 %collective-permute-done.3 = f32[2]{0:T(128)S(1)} collective-permute-done((f32[2]{0:T(128)S(1)}, f32[2]{0:T(128)S(1)}, u32[]{:S(2)}, u32[]{:S(2)}) %collective-permute-start.3) | collective-permute-done | bytes 40 | tf_op jit(solution)/shard_map/ppermute | solution.py:66
  25.0 0.7 copy-done.8
  25.7 1.1 pad_maximum_fusion.refs_0_
  26.8 1.3 add_convert_fusion.2
  28.2 1.6 fusion.6
  29.8 1.2 collective-permute-start.5
  31.0 0.9 collective-permute-start.4
  31.9 0.9 collective-permute-done.6.refs_1_
  32.8 1.4 copy-done.1
  34.2 0.8 copy.18
  35.0 8.9 %all-to-all-start = ((bf16[8,2,3,2,16,128]{5,4,3,2,1,0:T(8,128)(2,1)}), bf16[8,2,3,2,16,128]{5,4,3,2,1,0:T(8,128)(2,1)S(1)}, u32[]{:S(2)}, u32[]{:S(2)}) async-start(bf16[8,2,3,2,16,128]{5,4,3,2,1,0:T(8,128)(2,1)} %bitcast.42), calls=%async_computation | async-start | bytes 786432 | tf_op jit(solution)/shard_map/all_to_all | solution.py:161
  43.9 2.0 %collective-permute-start.7 = (bf16[2,288,512]{2,1,0:T(8,128)(2,1)S(1)}, bf16[2,288,512]{2,1,0:T(8,128)(2,1)}, u32[]{:S(2)}, u32[]{:S(2)}) collective-permute-start(bf16[2,288,512]{2,1,0:T(8,128)(2,1)S(1)} %pad_maximum_fusion.refs_0_), channel_id=1, source_target_pairs={{0,1},{1,2},{2,3},{3,4},{4,5},{5,6},{6,7},{7,0},{8,9},{9,10},{10,1... | collective-permute-start | bytes 1769480 | tf_op jit(solution)/shard_map/ppermute | solution.py:66
  45.9 12.5 %all-to-all-done = bf16[8,2,3,2,16,128]{5,4,3,2,1,0:T(8,128)(2,1)S(1)} async-done(((bf16[8,2,3,2,16,128]{5,4,3,2,1,0:T(8,128)(2,1)}), bf16[8,2,3,2,16,128]{5,4,3,2,1,0:T(8,128)(2,1)S(1)}, u32[]{:S(2)}, u32[]{:S(2)}) %all-to-all-start) | async-done | bytes 393248 | tf_op jit(solution)/shard_map/all_to_all | solution.py:161
  58.4 0.2 fusion.5
  58.6 8.5 %collective-permute-done.8.refs_8_ = bf16[2,288,512]{2,1,0:T(8,128)(2,1)} collective-permute-done((bf16[2,288,512]{2,1,0:T(8,128)(2,1)S(1)}, bf16[2,288,512]{2,1,0:T(8,128)(2,1)}, u32[]{:S(2)}, u32[]{:S(2)}) %collective-permute-start.8) | collective-permute-done | bytes 589856 | tf_op jit(solution)/shard_map/ppermute | solution.py:66
  67.1 1.5 collective-permute-start.9
  68.6 0.6 collective-permute-start.10
  69.2 0.6 collective-permute-start.15
  69.8 2.6 %collective-permute-start.16 = (bf16[256,2304]{1,0:T(8,128)(2,1)}, bf16[256,2304]{1,0:T(8,128)(2,1)}, u32[]{:S(2)}, u32[]{:S(2)}) collective-permute-start(bf16[256,2304]{1,0:T(8,128)(2,1)} %collective-permute-done.5), channel_id=1, source_target_pairs={{0,40},{1,41},{2,42},{3,43},{4,44},{5,45},{6,46},{7,47},{8,0},{9,1... | collective-permute-start | bytes 3538952 | tf_op jit(solution)/shard_map/ppermute | solution.py:66
  72.5 14.4 %all_to_all.17 = f32[8,1,2]{2,1,0:T(1,128)S(1)} all-to-all(f32[8,1,2]{2,1,0:T(1,128)S(1)} %broadcast_in_dim.7), channel_id=1, replica_groups={{0,1,2,3,4,5,6,7},{8,9,10,11,12,13,14,15},{16,17,18,19,20,21,22,23},{24..., dimensions={0} | all-to-all | bytes 128 | tf_op jit(solution)/shard_map/all_to_all | solution.py:161
  86.9 1.0 slice_bitcast_fusion
  87.8 1.9 %collective-permute-start.14 = (bf16[288,512]{1,0:T(8,128)(2,1)S(1)}, bf16[288,512]{1,0:T(8,128)(2,1)S(1)}, u32[]{:S(2)}, u32[]{:S(2)}) collective-permute-start(bf16[288,512]{1,0:T(8,128)(2,1)S(1)} %slice_bitcast_fusion), channel_id=1, source_target_pairs={{0,6},{1,7},{2,0},{3,1},{4,2},{5,3},{6,4},{7,5},{8,14},{9,15},{10,... | collective-permute-start | bytes 884744 | tf_op jit(solution)/shard_map/ppermute | solution.py:66
  89.7 0.3 collective-permute-start.11
  90.0 1.7 collective-permute-start.12
  91.7 1.7 slice_bitcast_fusion.1
  93.4 11.5 %collective-permute-done.14.refs_5_ = bf16[288,512]{1,0:T(8,128)(2,1)S(1)} collective-permute-done((bf16[288,512]{1,0:T(8,128)(2,1)S(1)}, bf16[288,512]{1,0:T(8,128)(2,1)S(1)}, u32[]{:S(2)}, u32[]{:S(2)}) %collective-permute-start.14) | collective-permute-done | bytes 294944 | tf_op jit(solution)/shard_map/ppermute | solution.py:66
  105.0 0.7 copy-done.5
  105.7 0.6 collective-permute-start.13
  106.4 7.9 %all_to_all.18 = f32[4,1,2]{2,1,0:T(1,128)S(1)} all-to-all(f32[4,1,2]{2,1,0:T(1,128)S(1)} %broadcast_in_dim.8), channel_id=1, replica_groups={{0,16,32,48},{64,80,96,112},{128,144,160,176},{192,208,224,240},{1,17,3..., dimensions={0} | all-to-all | bytes 64 | tf_op jit(solution)/shard_map/all_to_all | solution.py:161
  114.2 0.6 broadcast.21
  114.8 0.7 reduce.4
  115.6 1.4 collective-permute-done.13.refs_4_
  117.1 0.5 collective-permute-start.18
  117.7 1.1 copy-done.4
  118.8 1.0 copy-done.6
  119.7 2.9 %scale_grads.1.s_ref = bf16[4,4,288,512]{3,2,1,0:T(8,128)(2,1)S(1)} custom-call(s32[2]{0:T(128)S(1)} %pad_add_fusion.place_ref, f32[8]{0:T(128)S(1)} %reshape.26.clip_ref, bf16[2,288,512]{2,1,0:T(8,128)(2,1)S(1)} %copy-done.4, bf16[2,288,512]{2,1,0:T(8,128)(2,1)} %collective-permute-done.7.refs_1_, bf16[2,288,512]{2,1,0:T(8,128)(2,1)} %collective-permute-done.9.refs_2_, ...), custom_call_target="tpu_custom_call" | custom-call | flops 2359296 | bytes 147456 | tf_op jit(solution)/shard_map/scale_grads/pallas_call | solution.py:103
  122.7 5.0 %product_far.1 = (bf16[144,2304]{1,0:T(8,128)(2,1)S(1)}, bf16[144,2304]{1,0:T(8,128)(2,1)S(1)}) custom-call(bf16[4,4,288,512]{3,2,1,0:T(8,128)(2,1)S(1)} %scale_grads.1.s_ref, bf16[512,2304]{1,0:T(8,128)(2,1)S(1)} %bitcast.45, bf16[512,2304]{1,0:T(8,128)(2,1)S(1)} %copy-done.2, bf16[256,2304]{1,0:T(8,128)(2,1)S(1)} %collective-permute-done.15.refs_2_, ...), custom_call_target="tpu_custom_call" | custom-call | flops 1327104 | bytes 1327104 | tf_op jit(solution)/shard_map/product_far/pallas_call | solution.py:143
  127.8 1.7 collective-permute-start.19
  129.4 1.7 collective-permute-start.20
  131.1 7.8 %product_near.1 = (bf16[144,2304]{1,0:T(8,128)(2,1)S(1)}, bf16[144,2304]{1,0:T(8,128)(2,1)S(1)}, bf16[144,2304]{1,0:T(8,128)(2,1)S(1)}, bf16[144,2304]{1,0:T(8,128)(2,1)S(1)}) custom-call(bf16[4,4,288,512]{3,2,1,0:T(8,128)(2,1)S(1)} %scale_grads.1.s_ref, bf16[512,2304]{1,0:T(8,128)(2,1)S(1)} %bitcast.46, bf16[512,2304]{1,0:T(8,128)(2,1)S(1)} %copy-done.2, ...), custom_call_target="tpu_custom_call" | custom-call | flops 2654208 | bytes 1327104 | tf_op jit(solution)/shard_map/product_near/pallas_call | solution.py:143
  138.9 1.9 %collective-permute-start.22 = (bf16[144,2304]{1,0:T(8,128)(2,1)S(1)}, bf16[144,2304]{1,0:T(8,128)(2,1)S(1)}, u32[]{:S(2)}, u32[]{:S(2)}) collective-permute-start(bf16[144,2304]{1,0:T(8,128)(2,1)S(1)} %get-tuple-element.64), channel_id=1, source_target_pairs={{0,192},{1,193},{2,194},{3,195},{4,196},{5,197},{6,198},{7,199},{8... | collective-permute-start | bytes 1990664 | tf_op jit(solution)/shard_map/ppermute | solution.py:66
  140.7 5.3 %collective-permute-done.19 = bf16[144,2304]{1,0:T(8,128)(2,1)S(1)} collective-permute-done((bf16[144,2304]{1,0:T(8,128)(2,1)S(1)}, bf16[144,2304]{1,0:T(8,128)(2,1)S(1)}, u32[]{:S(2)}, u32[]{:S(2)}) %collective-permute-start.19) | collective-permute-done | bytes 663584 | tf_op jit(solution)/shard_map/ppermute | solution.py:66
  146.0 0.2 add_convert_fusion.1
  146.2 1.0 collective-permute-done.20
  147.2 0.2 add_convert_fusion
  147.4 1.6 collective-permute-start.21
  149.0 1.3 collective-permute-start.23
  150.3 2.0 %collective-permute-start.24 = (bf16[144,2304]{1,0:T(8,128)(2,1)S(1)}, bf16[144,2304]{1,0:T(8,128)(2,1)S(1)}, u32[]{:S(2)}, u32[]{:S(2)}) collective-permute-start(bf16[144,2304]{1,0:T(8,128)(2,1)S(1)} %add_convert_fusion), channel_id=1, source_target_pairs={{0,192},{1,193},{2,194},{3,195},{4,196},{5,197},{6,198},{7,199},{8... | collective-permute-start | bytes 1990664 | tf_op jit(solution)/shard_map/ppermute | solution.py:66
  152.2 5.0 %product_own.1 = f32[288,2304]{1,0:T(8,128)S(1)} custom-call(bf16[4,4,288,512]{3,2,1,0:T(8,128)(2,1)S(1)} %scale_grads.1.s_ref, bf16[512,2304]{1,0:T(8,128)(2,1)S(1)} %bitcast.47, bf16[512,2304]{1,0:T(8,128)(2,1)S(1)} %copy-done.2, bf16[256,2304]{1,0:T(8,128)(2,1)S(1)} %collective-permute-done.15.refs_2_, bf16[256,2304]{1,0:T(8,128)(2,1)} %collective-permute-done.16.refs_3_, ...), custom_call_target="tpu_custom_call" | custom-call | flops 1327104 | bytes 1327104 | tf_op jit(solution)/shard_map/product_own/pallas_call | solution.py:143
  157.3 4.1 %collective-permute-done.22 = bf16[144,2304]{1,0:T(8,128)(2,1)S(1)} collective-permute-done((bf16[144,2304]{1,0:T(8,128)(2,1)S(1)}, bf16[144,2304]{1,0:T(8,128)(2,1)S(1)}, u32[]{:S(2)}, u32[]{:S(2)}) %collective-permute-start.22) | collective-permute-done | bytes 663584 | tf_op jit(solution)/shard_map/ppermute | solution.py:66
  161.4 5.1 %collective-permute-done.21 = bf16[144,2304]{1,0:T(8,128)(2,1)S(1)} collective-permute-done((bf16[144,2304]{1,0:T(8,128)(2,1)S(1)}, bf16[144,2304]{1,0:T(8,128)(2,1)S(1)}, u32[]{:S(2)}, u32[]{:S(2)}) %collective-permute-start.21) | collective-permute-done | bytes 663584 | tf_op jit(solution)/shard_map/ppermute | solution.py:66
  166.5 0.1 convert_add_fusion.1
  166.7 11.3 %collective-permute-done.23 = bf16[144,2304]{1,0:T(8,128)(2,1)S(1)} collective-permute-done((bf16[144,2304]{1,0:T(8,128)(2,1)S(1)}, bf16[144,2304]{1,0:T(8,128)(2,1)S(1)}, u32[]{:S(2)}, u32[]{:S(2)}) %collective-permute-start.23) | collective-permute-done | bytes 663584 | tf_op jit(solution)/shard_map/ppermute | solution.py:66
  178.0 0.1 convert_add_fusion
  178.1 2.2 %fusion.2 = f32[288,2304]{1,0:T(8,128)} fusion(f32[288,2304]{1,0:T(8,128)S(1)} %copy-done.7, f32[288,2304]{1,0:T(8,128)S(1)} %product_own.1, f32[144,2304]{1,0:T(8,128)S(1)} %convert_add_fusion, f32[144,2304]{1,0:T(8,128)S(1)} %convert_add_fusion.1), kind=kLoop, calls=%fused_computation.3 | loop fusion | flops 3317760 | bytes 10616832 | tf_op jit(solution)/shard_map/div | solution.py:237
  (47 shorter events, 0.7 us)
Async XLA Ops:
  1.0 24.0 %collective-permute-start.1 = (bf16[288,512]{1,0:T(8,128)(2,1)S(1)}, bf16[288,512]{1,0:T(8,128)(2,1)S(1)}, u32[]{:S(2)}, u32[]{:S(2)}) collective-permute-start(bf16[288,512]{1,0:T(8,128)(2,1)S(1)} %bitcast.50), channel_id=1, source_target_pairs={{0,8},{1,26},{2,44},{3,58},{4,12},{5,30},{6,40},{7,62},{8,0},{9,18... | collective-permute-start | bytes 884744 | tf_op jit(solution)/shard_map/ppermute | solution.py:66
  3.3 21.6 %collective-permute-start = (bf16[288,512]{1,0:T(8,128)(2,1)S(1)}, bf16[288,512]{1,0:T(8,128)(2,1)}, u32[]{:S(2)}, u32[]{:S(2)}) collective-permute-start(bf16[288,512]{1,0:T(8,128)(2,1)S(1)} %bitcast.51), channel_id=1, source_target_pairs={{0,0},{1,18},{2,36},{3,50},{4,4},{5,22},{6,32},{7,54},{8,8},{9,26}... | collective-permute-start | bytes 884744 | tf_op jit(solution)/shard_map/ppermute | solution.py:66
  11.5 1.2 copy-start.9
  12.5 15.7 %copy-start = (bf16[2,256,2304]{2,1,0:T(8,128)(2,1)S(1)}, bf16[2,256,2304]{2,1,0:T(8,128)(2,1)}, u32[]{:S(2)}) copy-start(bf16[2,256,2304]{2,1,0:T(8,128)(2,1)} %param.5) | copy-start | bytes 7077892
  12.5 14.3 %collective-permute-start.2 = (bf16[2,3,2,128,128]{4,3,2,1,0:T(8,128)(2,1)}, bf16[2,3,2,128,128]{4,3,2,1,0:T(8,128)(2,1)}, u32[]{:S(2)}, u32[]{:S(2)}) collective-permute-start(bf16[2,3,2,128,128]{4,3,2,1,0:T(8,128)(2,1)} %pad_maximum_fusion.1), channel_id=1, source_target_pairs={{0,8},{1,9},{2,10},{3,11},{4,12},{5,13},{6,14},{7,15},{8,0},{9,1},... | collective-permute-start | bytes 1179656 | tf_op jit(solution)/shard_map/ppermute | solution.py:66
  12.8 12.1 %collective-permute-start.3 = (f32[2]{0:T(128)S(1)}, f32[2]{0:T(128)S(1)}, u32[]{:S(2)}, u32[]{:S(2)}) collective-permute-start(f32[2]{0:T(128)S(1)} %reduce_sum.36), channel_id=1, source_target_pairs={{0,8},{1,9},{2,10},{3,11},{4,12},{5,13},{6,14},{7,15},{8,0},{9,1},... | collective-permute-start | bytes 32 | tf_op jit(solution)/shard_map/ppermute | solution.py:66
  25.0 0.7 copy-start.8
  26.8 17.1 %copy-start.3 = (bf16[2,288,512]{2,1,0:T(8,128)(2,1)}, bf16[2,288,512]{2,1,0:T(8,128)(2,1)S(1)}, u32[]{:S(2)}) copy-start(bf16[2,288,512]{2,1,0:T(8,128)(2,1)S(1)} %pad_maximum_fusion.refs_0_) | copy-start | bytes 1769476
  28.1 4.6 %collective-permute-start.6 = (bf16[512,2304]{1,0:T(8,128)(2,1)S(1)}, bf16[512,2304]{1,0:T(8,128)(2,1)S(1)}, u32[]{:S(2)}, u32[]{:S(2)}) collective-permute-start(bf16[512,2304]{1,0:T(8,128)(2,1)S(1)} %bitcast.43), channel_id=1, source_target_pairs={{0,16},{1,17},{2,18},{3,19},{4,20},{5,21},{6,22},{7,23},{8,24},{9,... | collective-permute-start | bytes 7077896 | tf_op jit(solution)/shard_map/ppermute | solution.py:66
  29.8 28.6 %copy-start.10 = (f32[3]{0:T(128)S(1)}, f32[3]{0:T(128)}, u32[]{:S(2)}) copy-start(f32[3]{0:T(128)} %constant.20.clone) | copy-start | bytes 40
  29.8 37.3 %collective-permute-start.5 = (bf16[256,2304]{1,0:T(8,128)(2,1)}, bf16[256,2304]{1,0:T(8,128)(2,1)}, u32[]{:S(2)}, u32[]{:S(2)}) collective-permute-start(bf16[256,2304]{1,0:T(8,128)(2,1)} %get-tuple-element.67), channel_id=1, source_target_pairs={{0,40},{1,41},{2,42},{3,43},{4,44},{5,45},{6,46},{7,47},{8,0},{9,1... | collective-permute-start | bytes 3538952 | tf_op jit(solution)/shard_map/ppermute | solution.py:66
  31.0 36.1 %collective-permute-start.4 = (bf16[256,2304]{1,0:T(8,128)(2,1)}, bf16[256,2304]{1,0:T(8,128)(2,1)}, u32[]{:S(2)}, u32[]{:S(2)}) collective-permute-start(bf16[256,2304]{1,0:T(8,128)(2,1)} %get-tuple-element.68), channel_id=1, source_target_pairs={{0,8},{1,9},{2,10},{3,11},{4,12},{5,13},{6,14},{7,15},{8,32},{9,33... | collective-permute-start | bytes 3538952 | tf_op jit(solution)/shard_map/ppermute | solution.py:66
  32.8 1.4 copy-start.1
  35.0 23.4 %all-to-all-start = ((bf16[8,2,3,2,16,128]{5,4,3,2,1,0:T(8,128)(2,1)}), bf16[8,2,3,2,16,128]{5,4,3,2,1,0:T(8,128)(2,1)S(1)}, u32[]{:S(2)}, u32[]{:S(2)}) async-start(bf16[8,2,3,2,16,128]{5,4,3,2,1,0:T(8,128)(2,1)} %bitcast.42), calls=%async_computation | async-start | bytes 786432 | tf_op jit(solution)/shard_map/all_to_all | solution.py:161
  43.8 23.3 %collective-permute-start.8 = (bf16[2,288,512]{2,1,0:T(8,128)(2,1)S(1)}, bf16[2,288,512]{2,1,0:T(8,128)(2,1)}, u32[]{:S(2)}, u32[]{:S(2)}) collective-permute-start(bf16[2,288,512]{2,1,0:T(8,128)(2,1)S(1)} %pad_maximum_fusion.refs_0_), channel_id=1, source_target_pairs={{0,7},{1,0},{2,1},{3,2},{4,3},{5,4},{6,5},{7,6},{8,15},{9,8},{10,9... | collective-permute-start | bytes 1769480 | tf_op jit(solution)/shard_map/ppermute | solution.py:66
  43.9 23.2 %collective-permute-start.7 = (bf16[2,288,512]{2,1,0:T(8,128)(2,1)S(1)}, bf16[2,288,512]{2,1,0:T(8,128)(2,1)}, u32[]{:S(2)}, u32[]{:S(2)}) collective-permute-start(bf16[2,288,512]{2,1,0:T(8,128)(2,1)S(1)} %pad_maximum_fusion.refs_0_), channel_id=1, source_target_pairs={{0,1},{1,2},{2,3},{3,4},{4,5},{5,6},{6,7},{7,0},{8,9},{9,10},{10,1... | collective-permute-start | bytes 1769480 | tf_op jit(solution)/shard_map/ppermute | solution.py:66
  67.1 19.7 %collective-permute-start.9 = (bf16[2,288,512]{2,1,0:T(8,128)(2,1)}, bf16[2,288,512]{2,1,0:T(8,128)(2,1)}, u32[]{:S(2)}, u32[]{:S(2)}) collective-permute-start(bf16[2,288,512]{2,1,0:T(8,128)(2,1)} %collective-permute-done.7.refs_1_), channel_id=1, source_target_pairs={{0,1},{1,2},{2,3},{3,4},{4,5},{5,6},{6,7},{7,0},{8,9},{9,10},{10,1... | collective-permute-start | bytes 1769480 | tf_op jit(solution)/shard_map/ppermute | solution.py:66
  68.6 18.2 %collective-permute-start.10 = (bf16[2,288,512]{2,1,0:T(8,128)(2,1)}, bf16[2,288,512]{2,1,0:T(8,128)(2,1)}, u32[]{:S(2)}, u32[]{:S(2)}) collective-permute-start(bf16[2,288,512]{2,1,0:T(8,128)(2,1)} %collective-permute-done.8.refs_8_), channel_id=1, source_target_pairs={{0,7},{1,0},{2,1},{3,2},{4,3},{5,4},{6,5},{7,6},{8,15},{9,8},{10,9... | collective-permute-start | bytes 1769480 | tf_op jit(solution)/shard_map/ppermute | solution.py:66
  69.2 47.8 %collective-permute-start.15 = (bf16[256,2304]{1,0:T(8,128)(2,1)}, bf16[256,2304]{1,0:T(8,128)(2,1)S(1)}, u32[]{:S(2)}, u32[]{:S(2)}) collective-permute-start(bf16[256,2304]{1,0:T(8,128)(2,1)} %collective-permute-done.4), channel_id=1, source_target_pairs={{0,8},{1,9},{2,10},{3,11},{4,12},{5,13},{6,14},{7,15},{8,32},{9,33... | collective-permute-start | bytes 3538952 | tf_op jit(solution)/shard_map/ppermute | solution.py:66
  69.8 47.2 %collective-permute-start.16 = (bf16[256,2304]{1,0:T(8,128)(2,1)}, bf16[256,2304]{1,0:T(8,128)(2,1)}, u32[]{:S(2)}, u32[]{:S(2)}) collective-permute-start(bf16[256,2304]{1,0:T(8,128)(2,1)} %collective-permute-done.5), channel_id=1, source_target_pairs={{0,40},{1,41},{2,42},{3,43},{4,44},{5,45},{6,46},{7,47},{8,0},{9,1... | collective-permute-start | bytes 3538952 | tf_op jit(solution)/shard_map/ppermute | solution.py:66
  87.8 17.1 %collective-permute-start.14 = (bf16[288,512]{1,0:T(8,128)(2,1)S(1)}, bf16[288,512]{1,0:T(8,128)(2,1)S(1)}, u32[]{:S(2)}, u32[]{:S(2)}) collective-permute-start(bf16[288,512]{1,0:T(8,128)(2,1)S(1)} %slice_bitcast_fusion), channel_id=1, source_target_pairs={{0,6},{1,7},{2,0},{3,1},{4,2},{5,3},{6,4},{7,5},{8,14},{9,15},{10,... | collective-permute-start | bytes 884744 | tf_op jit(solution)/shard_map/ppermute | solution.py:66
  89.7 27.3 %collective-permute-start.11 = (bf16[2,288,512]{2,1,0:T(8,128)(2,1)}, bf16[2,288,512]{2,1,0:T(8,128)(2,1)}, u32[]{:S(2)}, u32[]{:S(2)}) collective-permute-start(bf16[2,288,512]{2,1,0:T(8,128)(2,1)} %collective-permute-done.9.refs_2_), channel_id=1, source_target_pairs={{0,1},{1,2},{2,3},{3,4},{4,5},{5,6},{6,7},{7,0},{8,9},{9,10},{10,1... | collective-permute-start | bytes 1769480 | tf_op jit(solution)/shard_map/ppermute | solution.py:66
  90.0 27.0 %collective-permute-start.12 = (bf16[2,288,512]{2,1,0:T(8,128)(2,1)}, bf16[2,288,512]{2,1,0:T(8,128)(2,1)}, u32[]{:S(2)}, u32[]{:S(2)}) collective-permute-start(bf16[2,288,512]{2,1,0:T(8,128)(2,1)} %collective-permute-done.10.refs_7_), channel_id=1, source_target_pairs={{0,7},{1,0},{2,1},{3,2},{4,3},{5,4},{6,5},{7,6},{8,15},{9,8},{10,9... | collective-permute-start | bytes 1769480 | tf_op jit(solution)/shard_map/ppermute | solution.py:66
  105.0 0.7 copy-start.5
  105.7 11.3 %collective-permute-start.13 = (bf16[288,512]{1,0:T(8,128)(2,1)}, bf16[288,512]{1,0:T(8,128)(2,1)}, u32[]{:S(2)}, u32[]{:S(2)}) collective-permute-start(bf16[288,512]{1,0:T(8,128)(2,1)} %slice_bitcast_fusion.1), channel_id=1, source_target_pairs={{0,2},{1,3},{2,4},{3,5},{4,6},{5,7},{6,0},{7,1},{8,10},{9,11},{10,... | collective-permute-start | bytes 884744 | tf_op jit(solution)/shard_map/ppermute | solution.py:66
  117.0 5.7 %collective-permute-start.17 = (bf16[256,2304]{1,0:T(8,128)(2,1)S(1)}, bf16[256,2304]{1,0:T(8,128)(2,1)}, u32[]{:S(2)}, u32[]{:S(2)}) collective-permute-start(bf16[256,2304]{1,0:T(8,128)(2,1)S(1)} %collective-permute-done.15.refs_2_), channel_id=1, source_target_pairs={{0,16},{1,17},{2,18},{3,19},{4,20},{5,21},{6,22},{7,23},{8,24},{9,... | collective-permute-start | bytes 3538952 | tf_op jit(solution)/shard_map/ppermute | solution.py:66
  117.1 5.6 %collective-permute-start.18 = (bf16[256,2304]{1,0:T(8,128)(2,1)}, bf16[256,2304]{1,0:T(8,128)(2,1)}, u32[]{:S(2)}, u32[]{:S(2)}) collective-permute-start(bf16[256,2304]{1,0:T(8,128)(2,1)} %collective-permute-done.16.refs_3_), channel_id=1, source_target_pairs={{0,16},{1,17},{2,18},{3,19},{4,20},{5,21},{6,22},{7,23},{8,24},{9,... | collective-permute-start | bytes 3538952 | tf_op jit(solution)/shard_map/ppermute | solution.py:66
  117.7 1.1 copy-start.4
  118.8 1.0 copy-start.6
  119.7 3.0 %copy-start.2 = (bf16[512,2304]{1,0:T(8,128)(2,1)S(1)}, bf16[512,2304]{1,0:T(8,128)(2,1)}, u32[]{:S(2)}) copy-start(bf16[512,2304]{1,0:T(8,128)(2,1)} %copy-done.1) | copy-start | bytes 7077892
  127.8 18.2 %collective-permute-start.19 = (bf16[144,2304]{1,0:T(8,128)(2,1)S(1)}, bf16[144,2304]{1,0:T(8,128)(2,1)S(1)}, u32[]{:S(2)}, u32[]{:S(2)}) collective-permute-start(bf16[144,2304]{1,0:T(8,128)(2,1)S(1)} %get-tuple-element.59), channel_id=1, source_target_pairs={{0,64},{1,65},{2,66},{3,67},{4,68},{5,69},{6,70},{7,71},{8,72},{9,... | collective-permute-start | bytes 1990664 | tf_op jit(solution)/shard_map/ppermute | solution.py:66
  129.4 17.8 %collective-permute-start.20 = (bf16[144,2304]{1,0:T(8,128)(2,1)S(1)}, bf16[144,2304]{1,0:T(8,128)(2,1)S(1)}, u32[]{:S(2)}, u32[]{:S(2)}) collective-permute-start(bf16[144,2304]{1,0:T(8,128)(2,1)S(1)} %get-tuple-element.61), channel_id=1, source_target_pairs={{0,192},{1,193},{2,194},{3,195},{4,196},{5,197},{6,198},{7,199},{8... | collective-permute-start | bytes 1990664 | tf_op jit(solution)/shard_map/ppermute | solution.py:66
  138.9 22.6 %collective-permute-start.22 = (bf16[144,2304]{1,0:T(8,128)(2,1)S(1)}, bf16[144,2304]{1,0:T(8,128)(2,1)S(1)}, u32[]{:S(2)}, u32[]{:S(2)}) collective-permute-start(bf16[144,2304]{1,0:T(8,128)(2,1)S(1)} %get-tuple-element.64), channel_id=1, source_target_pairs={{0,192},{1,193},{2,194},{3,195},{4,196},{5,197},{6,198},{7,199},{8... | collective-permute-start | bytes 1990664 | tf_op jit(solution)/shard_map/ppermute | solution.py:66
  147.4 19.1 %collective-permute-start.21 = (bf16[144,2304]{1,0:T(8,128)(2,1)S(1)}, bf16[144,2304]{1,0:T(8,128)(2,1)S(1)}, u32[]{:S(2)}, u32[]{:S(2)}) collective-permute-start(bf16[144,2304]{1,0:T(8,128)(2,1)S(1)} %add_convert_fusion.1), channel_id=1, source_target_pairs={{0,64},{1,65},{2,66},{3,67},{4,68},{5,69},{6,70},{7,71},{8,72},{9,... | collective-permute-start | bytes 1990664 | tf_op jit(solution)/shard_map/ppermute | solution.py:66
  149.0 29.0 %collective-permute-start.23 = (bf16[144,2304]{1,0:T(8,128)(2,1)S(1)}, bf16[144,2304]{1,0:T(8,128)(2,1)S(1)}, u32[]{:S(2)}, u32[]{:S(2)}) collective-permute-start(bf16[144,2304]{1,0:T(8,128)(2,1)S(1)} %get-tuple-element.65), channel_id=1, source_target_pairs={{0,64},{1,65},{2,66},{3,67},{4,68},{5,69},{6,70},{7,71},{8,72},{9,... | collective-permute-start | bytes 1990664 | tf_op jit(solution)/shard_map/ppermute | solution.py:66
  150.3 27.7 %collective-permute-start.24 = (bf16[144,2304]{1,0:T(8,128)(2,1)S(1)}, bf16[144,2304]{1,0:T(8,128)(2,1)S(1)}, u32[]{:S(2)}, u32[]{:S(2)}) collective-permute-start(bf16[144,2304]{1,0:T(8,128)(2,1)S(1)} %add_convert_fusion), channel_id=1, source_target_pairs={{0,192},{1,193},{2,194},{3,195},{4,196},{5,197},{6,198},{7,199},{8... | collective-permute-start | bytes 1990664 | tf_op jit(solution)/shard_map/ppermute | solution.py:66
  166.6 11.5 %copy-start.7 = (f32[288,2304]{1,0:T(8,128)S(1)}, f32[288,2304]{1,0:T(8,128)}, u32[]{:S(2)}) copy-start(f32[288,2304]{1,0:T(8,128)} %param.8) | copy-start | bytes 7962628

commit v9 on v5

--- a/solution.py
+++ b/solution.py
@@ -66,55 +66,87 @@
     return lax.ppermute(value, AXES, perm)
 
 
+def position(place_ref, r, f):
+    dp, te = place_ref[0], place_ref[1]
+    y, xh, c, xl, z = dp // 4, (dp // 2) % 2, dp % 2, te // NZ, te % NZ
+    q = (z - r - 2 * xh - c + 2 * NZ) % NZ
+    m = q % 4
+    k = ((q + 1) // 4) % 2
+    step = (2 * ((f + xl) % 2) + k - y + 4) % 4
+    slot = jnp.where(step == 0, 3, jnp.where(step == 1, 0, jnp.where(step == 2, 2, 1)))
+    return slot, m, 2 * (xh ^ (m // 2)) + (c ^ (m % 2))
+
+
 def scale_kernel(place_ref, clip_ref, *refs):
     pieces, out_ref, held_ref, arrived = refs[:-3], refs[-3], refs[-2], refs[-1]
-    dp, te = place_ref[0], place_ref[1]
-    y, xh, c, xl, z = dp // 4, (dp // 2) % 2, dp % 2, te // NZ, te % NZ
     half = out_ref.shape[3] // 2
-    copies = []
-    for i, piece in enumerate(pieces):
-        if i in (4, 5):
-            place = held_ref.at[4 + i]
-        else:
-            place = held_ref.at[pl.ds(2 * (i - (i > 5)), 2)]
-        copies.append(pltpu.make_async_copy(piece, place, arrived.at[i]))
+    copies = [
+        pltpu.make_async_copy(piece, held_ref.at[pl.ds(2 * i, 2)], arrived.at[i])
+        for i, piece in enumerate(pieces)
+    ]
     for copy in copies:
         copy.start()
-    for r in range(NZ):
-        q = (z - r - 2 * xh - c + 2 * NZ) % NZ
-        m = q % 4
-        k = ((q + 1) // 4) % 2
-        member = 2 * (xh ^ (m // 2)) + (c ^ (m % 2))
-        for copy in copies[4:6] if r == 4 else [copies[r + (r > 4)]]:
-            copy.wait()
+    for i, copy in enumerate(copies):
+        copy.wait()
         for f in range(2):
-            step = (2 * ((f + xl) % 2) + k - y + 4) % 4
-            slot = jnp.where(step == 0, 3, jnp.where(step == 1, 0, jnp.where(step == 2, 2, 1)))
+            slot, m, member = position(place_ref, i + (i > 3), f)
             for e in range(2):
                 cols = slice(e * half, (e + 1) * half)
                 out_ref[slot, m, :, cols] = (
-                    clip_ref[2 * member + e] * held_ref[2 * r + f, :, cols].astype(F32)
+                    clip_ref[2 * member + e] * held_ref[2 * i + f, :, cols].astype(F32)
                 ).astype(BF)
 
 
-def scale_grads(places, clips, pieces):
+def last_kernel(place_ref, clip_ref, first_ref, second_ref, _, out_ref, held_ref, done):
+    half = held_ref.shape[2] // 2
+    copies = []
+    for f, ref in enumerate((first_ref, second_ref)):
+        slot, m, member = position(place_ref, 4, f)
+        for e in range(2):
+            cols = slice(e * half, (e + 1) * half)
+            held_ref[f, :, cols] = (
+                clip_ref[2 * member + e] * ref[:, cols].astype(F32)
+            ).astype(BF)
+        copies.append(pltpu.make_async_copy(held_ref.at[f], out_ref.at[slot, m], done.at[f]))
+        copies[-1].start()
+    for copy in copies:
+        copy.wait()
+
+
+def scale_grads(places, clips, pieces, far):
     _, rows, tokens = pieces[0].shape
     smem = pl.BlockSpec(memory_space=pltpu.SMEM)
-    return pl.pallas_call(
+    vmem = pl.BlockSpec(memory_space=pltpu.VMEM)
+    anywhere = pl.BlockSpec(memory_space=pl.ANY)
+    shape = jax.ShapeDtypeStruct((4, 4, rows, tokens), BF)
+    cost = pl.CostEstimate(
+        flops=16 * rows * tokens, bytes_accessed=rows * tokens, transcendentals=0
+    )
+    params = pltpu.CompilerParams(vmem_limit_bytes=24 * 1024 * 1024)
+    most = pl.pallas_call(
         scale_kernel,
-        out_shape=jax.ShapeDtypeStruct((4, 4, rows, tokens), BF),
-        in_specs=[smem, smem] + [pl.BlockSpec(memory_space=pl.ANY)] * len(pieces),
-        out_specs=pl.BlockSpec(memory_space=pltpu.VMEM),
+        out_shape=shape,
+        in_specs=[smem, smem] + [anywhere] * len(pieces),
+        out_specs=vmem,
         scratch_shapes=[
-            pltpu.VMEM((2 * NZ, rows, tokens), BF),
+            pltpu.VMEM((2 * len(pieces), rows, tokens), BF),
             pltpu.SemaphoreType.DMA((len(pieces),)),
         ],
-        cost_estimate=pl.CostEstimate(
-            flops=16 * rows * tokens, bytes_accessed=rows * tokens, transcendentals=0
-        ),
-        compiler_params=pltpu.CompilerParams(vmem_limit_bytes=24 * 1024 * 1024),
+        cost_estimate=cost,
+        compiler_params=params,
         name="scale_grads",
     )(places, clips, *pieces)
+    return pl.pallas_call(
+        last_kernel,
+        out_shape=shape,
+        in_specs=[smem, smem, vmem, vmem, anywhere],
+        out_specs=anywhere,
+        scratch_shapes=[pltpu.VMEM((2, rows, tokens), BF), pltpu.SemaphoreType.DMA((2,))],
+        input_output_aliases={4: 0},
+        cost_estimate=cost,
+        compiler_params=params,
+        name="scale_last",
+    )(places, clips, *far, most)
 
 
 def product_kernel(s_ref, *refs):
@@ -213,9 +245,9 @@
 
     far = [send(fwd[3][0], along_z(1)), send(bwd[3][1], along_z(-1))]
     up_sibling, down_sibling = send(up, CORE), send(down, CORE)
-    pieces = [own, fwd[1], fwd[2], fwd[3], far[0], far[1], bwd[3], bwd[2], bwd[1]]
+    pieces = [own, fwd[1], fwd[2], fwd[3], bwd[3], bwd[2], bwd[1]]
     places = jnp.stack([dp, te]).astype(jnp.int32)
-    scaled = scale_grads(places, clips, pieces)
+    scaled = scale_grads(places, clips, pieces, far)
 
     held = [flat, sibling, up, down, up_sibling, down_sibling]
     tile = columns // 3

time: 176 us -> 174 us (0.989)
  waiting for transfers between devices: 69.6 us -> 65.8 us
    ppermute x25, waiting for transfers between devices: 58.3 us -> 54.4 us  [send(): return lax.ppermute(value, AXES, perm)]
    pallas_call x1 -> x2, Pallas kernels: 2.99 us -> 4.22 us  [the longest x1 2.82 us: scale_grads(): pl.pallas_call(scale_kernel, out_shape=shape, in_specs=[smem, smem] + [an...]
  transfers between devices with their start and end apart: 26 -> 26, of which waited for: 12 -> 12; matrix products, arithmetic and copies ran while one was open for 5% -> 5% of each run, Pallas kernels for 9% -> 10%
where the time goes in v9:
time: 174 us; the launch traced here: 171 us
  waiting for transfers between devices  65.8 us (38%)
  starting transfers between devices  39.9 us (23%)
  blocking collectives  24.9 us (14%)
  Pallas kernels  22.8 us (13%)
  local copies, waits for them, and re-layouts  8.28 us (5%)
  other arithmetic  5.19 us (3%)
  matrix products  3.57 us (2%)
    ppermute x25, waiting for transfers between devices, send(): return lax.ppermute(value, AXES, perm)  54.4 us
    ppermute x25, starting transfers between devices, send(): return lax.ppermute(value, AXES, perm)  31.6 us
    all_to_all x2, blocking collectives, all_to_all(): lax.all_to_all(value, axis, 0, 0, tiled=True, axis_index_groups=groups)  24.9 us
    pallas_call x3, Pallas kernels, product(): pl.pallas_call(product_kernel, out_shape=[jax.ShapeDtypeStruct((count, wi...  18.6 us
    all_to_all x1, waiting for transfers between devices, all_to_all(): lax.all_to_all(value, axis, 0, 0, tiled=True, axis_index_groups=groups)  11.4 us
    all_to_all x1, starting transfers between devices, all_to_all(): lax.all_to_all(value, axis, 0, 0, tiled=True, axis_index_groups=groups)  8.26 us
    dot_general x2, matrix products, blocks(): jnp.einsum('btf,bsf->bts', x, x, preferred_element_type=F32).astype(BF)  3.57 us
  transfers between devices with their start and end apart: 26, of which 12 were waited for; matrix products, arithmetic and copies ran while one was open for 5% of the time, Pallas kernels for 10%

profile of v9, /device:TPU:32, one launch (start us, length us, event | category | flops | bytes accessed | tf_op | source)
XLA Modules:
  0.0 170.6 jit_solution(3127606435178120038)
XLA Ops:
  0.0 3.2 %convolution_convert_fusion.1 = bf16[2,256,256]{2,1,0:T(8,128)(2,1)S(1)} fusion(bf16[2,256,2304]{2,1,0:T(8,128)(2,1)} %param.5), kind=kOutput, calls=%fused_computation.9 | convolution fusion | flops 604110848 | bytes 2621440 | tf_op jit(solution)/shard_map/btf,bsf->bts/dot_general | solution.py:212
  3.3 0.4 convolution_convert_fusion
  3.8 1.6 collective-permute-start.2
  5.4 0.7 copy.17
  6.1 1.1 collective-permute-start.1
  7.2 4.1 %collective-permute-start = (bf16[288,512]{1,0:T(8,128)(2,1)}, bf16[288,512]{1,0:T(8,128)(2,1)}, u32[]{:S(2)}, u32[]{:S(2)}) collective-permute-start(bf16[288,512]{1,0:T(8,128)(2,1)} %bitcast.2), channel_id=1, source_target_pairs={{0,0},{1,18},{2,36},{3,50},{4,4},{5,22},{6,32},{7,54},{8,8},{9,26}... | collective-permute-start | bytes 884744 | tf_op jit(solution)/shard_map/ppermute | solution.py:66
  11.3 0.1 reduce_sum.36
  11.4 0.7 collective-permute-start.3
  12.1 13.3 %collective-permute-done.3 = f32[2]{0:T(128)S(1)} collective-permute-done((f32[2]{0:T(128)S(1)}, f32[2]{0:T(128)S(1)}, u32[]{:S(2)}, u32[]{:S(2)}) %collective-permute-start.3) | collective-permute-done | bytes 40 | tf_op jit(solution)/shard_map/ppermute | solution.py:66
  25.5 0.1 add_convert_fusion.2
  25.6 1.6 fusion.6
  27.2 2.0 %collective-permute-start.4 = (bf16[256,2304]{1,0:T(8,128)(2,1)}, bf16[256,2304]{1,0:T(8,128)(2,1)}, u32[]{:S(2)}, u32[]{:S(2)}) collective-permute-start(bf16[256,2304]{1,0:T(8,128)(2,1)} %get-tuple-element.60), channel_id=1, source_target_pairs={{0,8},{1,9},{2,10},{3,11},{4,12},{5,13},{6,14},{7,15},{8,32},{9,33... | collective-permute-start | bytes 3538952 | tf_op jit(solution)/shard_map/ppermute | solution.py:66
  29.2 0.8 copy.19
  30.0 8.3 %all-to-all-start = ((bf16[8,2,3,2,16,128]{5,4,3,2,1,0:T(8,128)(2,1)}), bf16[8,2,3,2,16,128]{5,4,3,2,1,0:T(8,128)(2,1)S(1)}, u32[]{:S(2)}, u32[]{:S(2)}) async-start(bf16[8,2,3,2,16,128]{5,4,3,2,1,0:T(8,128)(2,1)} %bitcast.42), calls=%async_computation | async-start | bytes 786432 | tf_op jit(solution)/shard_map/all_to_all | solution.py:193
  38.3 1.1 pad_maximum_fusion.refs_0_
  39.4 0.1 collective-permute-start.7
  39.5 2.0 %collective-permute-start.6 = (bf16[2,288,512]{2,1,0:T(8,128)(2,1)S(1)}, bf16[2,288,512]{2,1,0:T(8,128)(2,1)}, u32[]{:S(2)}, u32[]{:S(2)}) collective-permute-start(bf16[2,288,512]{2,1,0:T(8,128)(2,1)S(1)} %pad_maximum_fusion.refs_0_), channel_id=1, source_target_pairs={{0,1},{1,2},{2,3},{3,4},{4,5},{5,6},{6,7},{7,0},{8,9},{9,10},{10,1... | collective-permute-start | bytes 1769480 | tf_op jit(solution)/shard_map/ppermute | solution.py:66
  41.5 11.4 %all-to-all-done = bf16[8,2,3,2,16,128]{5,4,3,2,1,0:T(8,128)(2,1)S(1)} async-done(((bf16[8,2,3,2,16,128]{5,4,3,2,1,0:T(8,128)(2,1)}), bf16[8,2,3,2,16,128]{5,4,3,2,1,0:T(8,128)(2,1)S(1)}, u32[]{:S(2)}, u32[]{:S(2)}) %all-to-all-start) | async-done | bytes 393248 | tf_op jit(solution)/shard_map/all_to_all | solution.py:193
  52.9 0.1 convert_reduce_fusion
  52.9 0.2 fusion.5
  53.1 9.4 %collective-permute-done.7.refs_6_ = bf16[2,288,512]{2,1,0:T(8,128)(2,1)} collective-permute-done((bf16[2,288,512]{2,1,0:T(8,128)(2,1)S(1)}, bf16[2,288,512]{2,1,0:T(8,128)(2,1)}, u32[]{:S(2)}, u32[]{:S(2)}) %collective-permute-start.7) | collective-permute-done | bytes 589856 | tf_op jit(solution)/shard_map/ppermute | solution.py:66
  62.5 1.5 collective-permute-start.8
  64.0 0.6 collective-permute-start.9
  64.6 1.6 collective-permute-start.12
  66.2 1.6 collective-permute-start.13
  67.8 14.8 %all_to_all.17 = f32[8,1,2]{2,1,0:T(1,128)S(1)} all-to-all(f32[8,1,2]{2,1,0:T(1,128)S(1)} %broadcast_in_dim.7), channel_id=1, replica_groups={{0,1,2,3,4,5,6,7},{8,9,10,11,12,13,14,15},{16,17,18,19,20,21,22,23},{24..., dimensions={0} | all-to-all | bytes 128 | tf_op jit(solution)/shard_map/all_to_all | solution.py:193
  82.7 0.6 collective-permute-start.10
  83.4 1.5 collective-permute-start.11
  84.9 10.0 %all_to_all.18 = f32[4,1,2]{2,1,0:T(1,128)S(1)} all-to-all(f32[4,1,2]{2,1,0:T(1,128)S(1)} %broadcast_in_dim.8), channel_id=1, replica_groups={{0,16,32,48},{64,80,96,112},{128,144,160,176},{192,208,224,240},{1,17,3..., dimensions={0} | all-to-all | bytes 64 | tf_op jit(solution)/shard_map/all_to_all | solution.py:193
  94.9 0.5 broadcast.21
  95.4 0.7 reduce.4
  96.1 0.1 reshape.26.clip_ref
  96.1 0.9 collective-permute-done.10.refs_3_
  97.0 0.3 collective-permute-done.11.refs_4_
  97.3 0.5 collective-permute-start.18
  97.8 1.7 slice_bitcast_fusion.1
  99.5 1.7 %slice_bitcast_fusion = bf16[288,512]{1,0:T(8,128)(2,1)} fusion(bf16[2,288,512]{2,1,0:T(8,128)(2,1)} %collective-permute-done.11.refs_4_), kind=kLoop, calls=%fused_computation.15 | loop fusion | bytes 589824 | tf_op jit(solution)/shard_map/squeeze | solution.py:246
  101.2 1.8 %collective-permute-start.15 = (bf16[288,512]{1,0:T(8,128)(2,1)}, bf16[288,512]{1,0:T(8,128)(2,1)}, u32[]{:S(2)}, u32[]{:S(2)}) collective-permute-start(bf16[288,512]{1,0:T(8,128)(2,1)} %slice_bitcast_fusion), channel_id=1, source_target_pairs={{0,7},{1,0},{2,1},{3,2},{4,3},{5,4},{6,5},{7,6},{8,15},{9,8},{10,9... | collective-permute-start | bytes 884744 | tf_op jit(solution)/shard_map/ppermute | solution.py:66
  103.0 0.2 collective-permute-start.14
  103.3 0.1 pad_add_fusion.place_ref
  103.3 1.1 copy-done.2
  104.4 2.8 %scale_grads.1._ = bf16[4,4,288,512]{3,2,1,0:T(8,128)(2,1)S(1)} custom-call(s32[2]{0:T(128)S(1)} %pad_add_fusion.place_ref, f32[8]{0:T(128)S(1)} %reshape.26.clip_ref, bf16[2,288,512]{2,1,0:T(8,128)(2,1)S(1)} %copy-done.2, bf16[2,288,512]{2,1,0:T(8,128)(2,1)} %collective-permute-done.6.refs_1_, bf16[2,288,512]{2,1,0:T(8,128)(2,1)} %collective-permute-done.8.refs_2_, ...), custom_call_target="tpu_custom_call" | custom-call | flops 2359296 | bytes 147456 | tf_op jit(solution)/shard_map/scale_grads/pallas_call | solution.py:126
  107.2 3.3 %collective-permute-done.15.second_ref = bf16[288,512]{1,0:T(8,128)(2,1)} collective-permute-done((bf16[288,512]{1,0:T(8,128)(2,1)}, bf16[288,512]{1,0:T(8,128)(2,1)}, u32[]{:S(2)}, u32[]{:S(2)}) %collective-permute-start.15) | collective-permute-done | bytes 294944 | tf_op jit(solution)/shard_map/ppermute | solution.py:66
  110.6 2.5 %collective-permute-done.14.first_ref = bf16[288,512]{1,0:T(8,128)(2,1)} collective-permute-done((bf16[288,512]{1,0:T(8,128)(2,1)}, bf16[288,512]{1,0:T(8,128)(2,1)}, u32[]{:S(2)}, u32[]{:S(2)}) %collective-permute-start.14) | collective-permute-done | bytes 294944 | tf_op jit(solution)/shard_map/ppermute | solution.py:66
  113.0 1.4 scale_last.1.s_ref
  114.5 5.3 %product_far.1 = (bf16[144,2304]{1,0:T(8,128)(2,1)S(1)}, bf16[144,2304]{1,0:T(8,128)(2,1)S(1)}) custom-call(bf16[4,4,288,512]{3,2,1,0:T(8,128)(2,1)S(1)} %scale_last.1.s_ref, bf16[512,2304]{1,0:T(8,128)(2,1)S(1)} %bitcast.45, bf16[512,2304]{1,0:T(8,128)(2,1)} %collective-permute-done.16.refs_1_, bf16[256,2304]{1,0:T(8,128)(2,1)S(1)} %collective-permute-done.12.refs_2_, ...), custom_call_target="tpu_custom_call" | custom-call | flops 1327104 | bytes 1327104 | tf_op jit(solution)/shard_map/product_far/pallas_call | solution.py:175
  119.8 1.7 collective-permute-start.19
  121.5 1.7 collective-permute-start.20
  123.1 7.9 %product_near.1 = (bf16[144,2304]{1,0:T(8,128)(2,1)S(1)}, bf16[144,2304]{1,0:T(8,128)(2,1)S(1)}, bf16[144,2304]{1,0:T(8,128)(2,1)S(1)}, bf16[144,2304]{1,0:T(8,128)(2,1)S(1)}) custom-call(bf16[4,4,288,512]{3,2,1,0:T(8,128)(2,1)S(1)} %scale_last.1.s_ref, bf16[512,2304]{1,0:T(8,128)(2,1)S(1)} %bitcast.46, bf16[512,2304]{1,0:T(8,128)(2,1)} %collective-permute-done.16.refs_1_, ...), custom_call_target="tpu_custom_call" | custom-call | flops 2654208 | bytes 1327104 | tf_op jit(solution)/shard_map/product_near/pallas_call | solution.py:175
  131.0 1.9 %collective-permute-start.22 = (bf16[144,2304]{1,0:T(8,128)(2,1)S(1)}, bf16[144,2304]{1,0:T(8,128)(2,1)S(1)}, u32[]{:S(2)}, u32[]{:S(2)}) collective-permute-start(bf16[144,2304]{1,0:T(8,128)(2,1)S(1)} %get-tuple-element.56), channel_id=1, source_target_pairs={{0,192},{1,193},{2,194},{3,195},{4,196},{5,197},{6,198},{7,199},{8... | collective-permute-start | bytes 1990664 | tf_op jit(solution)/shard_map/ppermute | solution.py:66
  132.9 4.3 %collective-permute-done.19 = bf16[144,2304]{1,0:T(8,128)(2,1)S(1)} collective-permute-done((bf16[144,2304]{1,0:T(8,128)(2,1)S(1)}, bf16[144,2304]{1,0:T(8,128)(2,1)S(1)}, u32[]{:S(2)}, u32[]{:S(2)}) %collective-permute-start.19) | collective-permute-done | bytes 663584 | tf_op jit(solution)/shard_map/ppermute | solution.py:66
  137.2 0.2 add_convert_fusion.1
  137.4 1.9 %collective-permute-done.20 = bf16[144,2304]{1,0:T(8,128)(2,1)S(1)} collective-permute-done((bf16[144,2304]{1,0:T(8,128)(2,1)S(1)}, bf16[144,2304]{1,0:T(8,128)(2,1)S(1)}, u32[]{:S(2)}, u32[]{:S(2)}) %collective-permute-start.20) | collective-permute-done | bytes 663584 | tf_op jit(solution)/shard_map/ppermute | solution.py:66
  139.3 0.2 add_convert_fusion
  139.5 1.7 collective-permute-start.21
  141.1 1.3 collective-permute-start.23
  142.4 2.0 %collective-permute-start.24 = (bf16[144,2304]{1,0:T(8,128)(2,1)S(1)}, bf16[144,2304]{1,0:T(8,128)(2,1)S(1)}, u32[]{:S(2)}, u32[]{:S(2)}) collective-permute-start(bf16[144,2304]{1,0:T(8,128)(2,1)S(1)} %add_convert_fusion), channel_id=1, source_target_pairs={{0,192},{1,193},{2,194},{3,195},{4,196},{5,197},{6,198},{7,199},{8... | collective-permute-start | bytes 1990664 | tf_op jit(solution)/shard_map/ppermute | solution.py:66
  144.4 5.4 %product_own.1 = f32[288,2304]{1,0:T(8,128)S(1)} custom-call(bf16[4,4,288,512]{3,2,1,0:T(8,128)(2,1)S(1)} %scale_last.1.s_ref, bf16[512,2304]{1,0:T(8,128)(2,1)S(1)} %bitcast.47, bf16[512,2304]{1,0:T(8,128)(2,1)} %collective-permute-done.16.refs_1_, bf16[256,2304]{1,0:T(8,128)(2,1)S(1)} %collective-permute-done.12.refs_2_, ...), custom_call_target="tpu_custom_call" | custom-call | flops 1327104 | bytes 1327104 | tf_op jit(solution)/shard_map/product_own/pallas_call | solution.py:175
  149.7 3.8 %collective-permute-done.22 = bf16[144,2304]{1,0:T(8,128)(2,1)S(1)} collective-permute-done((bf16[144,2304]{1,0:T(8,128)(2,1)S(1)}, bf16[144,2304]{1,0:T(8,128)(2,1)S(1)}, u32[]{:S(2)}, u32[]{:S(2)}) %collective-permute-start.22) | collective-permute-done | bytes 663584 | tf_op jit(solution)/shard_map/ppermute | solution.py:66
  153.5 5.1 %collective-permute-done.21 = bf16[144,2304]{1,0:T(8,128)(2,1)S(1)} collective-permute-done((bf16[144,2304]{1,0:T(8,128)(2,1)S(1)}, bf16[144,2304]{1,0:T(8,128)(2,1)S(1)}, u32[]{:S(2)}, u32[]{:S(2)}) %collective-permute-start.21) | collective-permute-done | bytes 663584 | tf_op jit(solution)/shard_map/ppermute | solution.py:66
  158.6 0.1 convert_add_fusion.1
  158.8 9.5 %collective-permute-done.23 = bf16[144,2304]{1,0:T(8,128)(2,1)S(1)} collective-permute-done((bf16[144,2304]{1,0:T(8,128)(2,1)S(1)}, bf16[144,2304]{1,0:T(8,128)(2,1)S(1)}, u32[]{:S(2)}, u32[]{:S(2)}) %collective-permute-start.23) | collective-permute-done | bytes 663584 | tf_op jit(solution)/shard_map/ppermute | solution.py:66
  168.3 0.1 convert_add_fusion
  168.4 2.2 %fusion.2 = f32[288,2304]{1,0:T(8,128)} fusion(f32[288,2304]{1,0:T(8,128)S(1)} %copy-done.4, f32[288,2304]{1,0:T(8,128)S(1)} %product_own.1, f32[144,2304]{1,0:T(8,128)S(1)} %convert_add_fusion, f32[144,2304]{1,0:T(8,128)S(1)} %convert_add_fusion.1), kind=kLoop, calls=%fused_computation.3 | loop fusion | flops 3317760 | bytes 10616832 | tf_op jit(solution)/shard_map/div | solution.py:270
  (40 shorter events, 0.3 us)
Async XLA Ops:
  0.0 3.3 %copy-start.3 = (bf16[2,256,288]{1,2,0:T(8,128)(2,1)S(1)}, bf16[2,256,288]{1,2,0:T(8,128)(2,1)}, u32[]{:S(2)}) copy-start(bf16[2,256,288]{1,2,0:T(8,128)(2,1)} %param.6) | copy-start | bytes 884740
  3.6 7.7 %copy-start.5 = (f32[2,8]{1,0:T(2,128)S(1)}, f32[2,8]{1,0:T(2,128)}, u32[]{:S(2)}) copy-start(f32[2,8]{1,0:T(2,128)} %param.7) | copy-start | bytes 196
  3.8 21.8 %copy-start = (bf16[2,256,2304]{2,1,0:T(8,128)(2,1)S(1)}, bf16[2,256,2304]{2,1,0:T(8,128)(2,1)}, u32[]{:S(2)}) copy-start(bf16[2,256,2304]{2,1,0:T(8,128)(2,1)} %param.5) | copy-start | bytes 7077892
  3.8 21.6 %collective-permute-start.2 = (bf16[2,3,2,128,128]{4,3,2,1,0:T(8,128)(2,1)S(1)}, bf16[2,3,2,128,128]{4,3,2,1,0:T(8,128)(2,1)S(1)}, u32[]{:S(2)}, u32[]{:S(2)}) collective-permute-start(bf16[2,3,2,128,128]{4,3,2,1,0:T(8,128)(2,1)S(1)} %pad_maximum_fusion.1), channel_id=1, source_target_pairs={{0,8},{1,9},{2,10},{3,11},{4,12},{5,13},{6,14},{7,15},{8,0},{9,1},... | collective-permute-start | bytes 1179656 | tf_op jit(solution)/shard_map/ppermute | solution.py:66
  6.1 19.4 %collective-permute-start.1 = (bf16[288,512]{1,0:T(8,128)(2,1)}, bf16[288,512]{1,0:T(8,128)(2,1)}, u32[]{:S(2)}, u32[]{:S(2)}) collective-permute-start(bf16[288,512]{1,0:T(8,128)(2,1)} %bitcast.2), channel_id=1, source_target_pairs={{0,8},{1,26},{2,44},{3,58},{4,12},{5,30},{6,40},{7,62},{8,0},{9,18... | collective-permute-start | bytes 884744 | tf_op jit(solution)/shard_map/ppermute | solution.py:66
  7.2 18.4 %collective-permute-start = (bf16[288,512]{1,0:T(8,128)(2,1)}, bf16[288,512]{1,0:T(8,128)(2,1)}, u32[]{:S(2)}, u32[]{:S(2)}) collective-permute-start(bf16[288,512]{1,0:T(8,128)(2,1)} %bitcast.2), channel_id=1, source_target_pairs={{0,0},{1,18},{2,36},{3,50},{4,4},{5,22},{6,32},{7,54},{8,8},{9,26}... | collective-permute-start | bytes 884744 | tf_op jit(solution)/shard_map/ppermute | solution.py:66
  11.4 14.0 %collective-permute-start.3 = (f32[2]{0:T(128)S(1)}, f32[2]{0:T(128)S(1)}, u32[]{:S(2)}, u32[]{:S(2)}) collective-permute-start(f32[2]{0:T(128)S(1)} %reduce_sum.36), channel_id=1, source_target_pairs={{0,8},{1,9},{2,10},{3,11},{4,12},{5,13},{6,14},{7,15},{8,0},{9,1},... | collective-permute-start | bytes 32 | tf_op jit(solution)/shard_map/ppermute | solution.py:66
  27.2 35.3 %collective-permute-start.5 = (bf16[256,2304]{1,0:T(8,128)(2,1)}, bf16[256,2304]{1,0:T(8,128)(2,1)}, u32[]{:S(2)}, u32[]{:S(2)}) collective-permute-start(bf16[256,2304]{1,0:T(8,128)(2,1)} %get-tuple-element.59), channel_id=1, source_target_pairs={{0,40},{1,41},{2,42},{3,43},{4,44},{5,45},{6,46},{7,47},{8,0},{9,1... | collective-permute-start | bytes 3538952 | tf_op jit(solution)/shard_map/ppermute | solution.py:66
  27.2 35.3 %collective-permute-start.4 = (bf16[256,2304]{1,0:T(8,128)(2,1)}, bf16[256,2304]{1,0:T(8,128)(2,1)}, u32[]{:S(2)}, u32[]{:S(2)}) collective-permute-start(bf16[256,2304]{1,0:T(8,128)(2,1)} %get-tuple-element.60), channel_id=1, source_target_pairs={{0,8},{1,9},{2,10},{3,11},{4,12},{5,13},{6,14},{7,15},{8,32},{9,33... | collective-permute-start | bytes 3538952 | tf_op jit(solution)/shard_map/ppermute | solution.py:66
  30.0 22.9 %copy-start.6 = (f32[3]{0:T(128)S(1)}, f32[3]{0:T(128)}, u32[]{:S(2)}) copy-start(f32[3]{0:T(128)} %constant.20.clone) | copy-start | bytes 40
  30.0 22.9 %all-to-all-start = ((bf16[8,2,3,2,16,128]{5,4,3,2,1,0:T(8,128)(2,1)}), bf16[8,2,3,2,16,128]{5,4,3,2,1,0:T(8,128)(2,1)S(1)}, u32[]{:S(2)}, u32[]{:S(2)}) async-start(bf16[8,2,3,2,16,128]{5,4,3,2,1,0:T(8,128)(2,1)} %bitcast.42), calls=%async_computation | async-start | bytes 786432 | tf_op jit(solution)/shard_map/all_to_all | solution.py:193
  39.4 24.7 %copy-start.1 = (bf16[2,288,512]{2,1,0:T(8,128)(2,1)}, bf16[2,288,512]{2,1,0:T(8,128)(2,1)S(1)}, u32[]{:S(2)}) copy-start(bf16[2,288,512]{2,1,0:T(8,128)(2,1)S(1)} %pad_maximum_fusion.refs_0_) | copy-start | bytes 1769476
  39.4 23.1 %collective-permute-start.7 = (bf16[2,288,512]{2,1,0:T(8,128)(2,1)S(1)}, bf16[2,288,512]{2,1,0:T(8,128)(2,1)}, u32[]{:S(2)}, u32[]{:S(2)}) collective-permute-start(bf16[2,288,512]{2,1,0:T(8,128)(2,1)S(1)} %pad_maximum_fusion.refs_0_), channel_id=1, source_target_pairs={{0,7},{1,0},{2,1},{3,2},{4,3},{5,4},{6,5},{7,6},{8,15},{9,8},{10,9... | collective-permute-start | bytes 1769480 | tf_op jit(solution)/shard_map/ppermute | solution.py:66
  39.5 23.0 %collective-permute-start.6 = (bf16[2,288,512]{2,1,0:T(8,128)(2,1)S(1)}, bf16[2,288,512]{2,1,0:T(8,128)(2,1)}, u32[]{:S(2)}, u32[]{:S(2)}) collective-permute-start(bf16[2,288,512]{2,1,0:T(8,128)(2,1)S(1)} %pad_maximum_fusion.refs_0_), channel_id=1, source_target_pairs={{0,1},{1,2},{2,3},{3,4},{4,5},{5,6},{6,7},{7,0},{8,9},{9,10},{10,1... | collective-permute-start | bytes 1769480 | tf_op jit(solution)/shard_map/ppermute | solution.py:66
  62.5 20.2 %collective-permute-start.8 = (bf16[2,288,512]{2,1,0:T(8,128)(2,1)}, bf16[2,288,512]{2,1,0:T(8,128)(2,1)}, u32[]{:S(2)}, u32[]{:S(2)}) collective-permute-start(bf16[2,288,512]{2,1,0:T(8,128)(2,1)} %collective-permute-done.6.refs_1_), channel_id=1, source_target_pairs={{0,1},{1,2},{2,3},{3,4},{4,5},{5,6},{6,7},{7,0},{8,9},{9,10},{10,1... | collective-permute-start | bytes 1769480 | tf_op jit(solution)/shard_map/ppermute | solution.py:66
  64.0 18.7 %collective-permute-start.9 = (bf16[2,288,512]{2,1,0:T(8,128)(2,1)}, bf16[2,288,512]{2,1,0:T(8,128)(2,1)}, u32[]{:S(2)}, u32[]{:S(2)}) collective-permute-start(bf16[2,288,512]{2,1,0:T(8,128)(2,1)} %collective-permute-done.7.refs_6_), channel_id=1, source_target_pairs={{0,7},{1,0},{2,1},{3,2},{4,3},{5,4},{6,5},{7,6},{8,15},{9,8},{10,9... | collective-permute-start | bytes 1769480 | tf_op jit(solution)/shard_map/ppermute | solution.py:66
  64.6 32.7 %collective-permute-start.12 = (bf16[256,2304]{1,0:T(8,128)(2,1)}, bf16[256,2304]{1,0:T(8,128)(2,1)S(1)}, u32[]{:S(2)}, u32[]{:S(2)}) collective-permute-start(bf16[256,2304]{1,0:T(8,128)(2,1)} %collective-permute-done.4), channel_id=1, source_target_pairs={{0,8},{1,9},{2,10},{3,11},{4,12},{5,13},{6,14},{7,15},{8,32},{9,33... | collective-permute-start | bytes 3538952 | tf_op jit(solution)/shard_map/ppermute | solution.py:66
  66.2 31.1 %collective-permute-start.13 = (bf16[256,2304]{1,0:T(8,128)(2,1)}, bf16[256,2304]{1,0:T(8,128)(2,1)}, u32[]{:S(2)}, u32[]{:S(2)}) collective-permute-start(bf16[256,2304]{1,0:T(8,128)(2,1)} %collective-permute-done.5), channel_id=1, source_target_pairs={{0,40},{1,41},{2,42},{3,43},{4,44},{5,45},{6,46},{7,47},{8,0},{9,1... | collective-permute-start | bytes 3538952 | tf_op jit(solution)/shard_map/ppermute | solution.py:66
  67.8 46.6 %collective-permute-start.16 = (bf16[512,2304]{1,0:T(8,128)(2,1)S(1)}, bf16[512,2304]{1,0:T(8,128)(2,1)}, u32[]{:S(2)}, u32[]{:S(2)}) collective-permute-start(bf16[512,2304]{1,0:T(8,128)(2,1)S(1)} %bitcast.44), channel_id=1, source_target_pairs={{0,16},{1,17},{2,18},{3,19},{4,20},{5,21},{6,22},{7,23},{8,24},{9,... | collective-permute-start | bytes 7077896 | tf_op jit(solution)/shard_map/ppermute | solution.py:66
  82.7 14.3 %collective-permute-start.10 = (bf16[2,288,512]{2,1,0:T(8,128)(2,1)}, bf16[2,288,512]{2,1,0:T(8,128)(2,1)}, u32[]{:S(2)}, u32[]{:S(2)}) collective-permute-start(bf16[2,288,512]{2,1,0:T(8,128)(2,1)} %collective-permute-done.8.refs_2_), channel_id=1, source_target_pairs={{0,1},{1,2},{2,3},{3,4},{4,5},{5,6},{6,7},{7,0},{8,9},{9,10},{10,1... | collective-permute-start | bytes 1769480 | tf_op jit(solution)/shard_map/ppermute | solution.py:66
  83.4 13.9 %collective-permute-start.11 = (bf16[2,288,512]{2,1,0:T(8,128)(2,1)}, bf16[2,288,512]{2,1,0:T(8,128)(2,1)}, u32[]{:S(2)}, u32[]{:S(2)}) collective-permute-start(bf16[2,288,512]{2,1,0:T(8,128)(2,1)} %collective-permute-done.9.refs_5_), channel_id=1, source_target_pairs={{0,7},{1,0},{2,1},{3,2},{4,3},{5,4},{6,5},{7,6},{8,15},{9,8},{10,9... | collective-permute-start | bytes 1769480 | tf_op jit(solution)/shard_map/ppermute | solution.py:66
  97.3 17.1 %collective-permute-start.17 = (bf16[256,2304]{1,0:T(8,128)(2,1)S(1)}, bf16[256,2304]{1,0:T(8,128)(2,1)}, u32[]{:S(2)}, u32[]{:S(2)}) collective-permute-start(bf16[256,2304]{1,0:T(8,128)(2,1)S(1)} %collective-permute-done.12.refs_2_), channel_id=1, source_target_pairs={{0,16},{1,17},{2,18},{3,19},{4,20},{5,21},{6,22},{7,23},{8,24},{9,... | collective-permute-start | bytes 3538952 | tf_op jit(solution)/shard_map/ppermute | solution.py:66
  97.3 17.1 %collective-permute-start.18 = (bf16[256,2304]{1,0:T(8,128)(2,1)}, bf16[256,2304]{1,0:T(8,128)(2,1)}, u32[]{:S(2)}, u32[]{:S(2)}) collective-permute-start(bf16[256,2304]{1,0:T(8,128)(2,1)} %collective-permute-done.13.refs_3_), channel_id=1, source_target_pairs={{0,16},{1,17},{2,18},{3,19},{4,20},{5,21},{6,22},{7,23},{8,24},{9,... | collective-permute-start | bytes 3538952 | tf_op jit(solution)/shard_map/ppermute | solution.py:66
  101.2 9.3 %collective-permute-start.15 = (bf16[288,512]{1,0:T(8,128)(2,1)}, bf16[288,512]{1,0:T(8,128)(2,1)}, u32[]{:S(2)}, u32[]{:S(2)}) collective-permute-start(bf16[288,512]{1,0:T(8,128)(2,1)} %slice_bitcast_fusion), channel_id=1, source_target_pairs={{0,7},{1,0},{2,1},{3,2},{4,3},{5,4},{6,5},{7,6},{8,15},{9,8},{10,9... | collective-permute-start | bytes 884744 | tf_op jit(solution)/shard_map/ppermute | solution.py:66
  103.0 10.0 %collective-permute-start.14 = (bf16[288,512]{1,0:T(8,128)(2,1)}, bf16[288,512]{1,0:T(8,128)(2,1)}, u32[]{:S(2)}, u32[]{:S(2)}) collective-permute-start(bf16[288,512]{1,0:T(8,128)(2,1)} %slice_bitcast_fusion.1), channel_id=1, source_target_pairs={{0,1},{1,2},{2,3},{3,4},{4,5},{5,6},{6,7},{7,0},{8,9},{9,10},{10,1... | collective-permute-start | bytes 884744 | tf_op jit(solution)/shard_map/ppermute | solution.py:66
  103.3 1.1 copy-start.2
  119.8 17.4 %collective-permute-start.19 = (bf16[144,2304]{1,0:T(8,128)(2,1)S(1)}, bf16[144,2304]{1,0:T(8,128)(2,1)S(1)}, u32[]{:S(2)}, u32[]{:S(2)}) collective-permute-start(bf16[144,2304]{1,0:T(8,128)(2,1)S(1)} %get-tuple-element.51), channel_id=1, source_target_pairs={{0,64},{1,65},{2,66},{3,67},{4,68},{5,69},{6,70},{7,71},{8,72},{9,... | collective-permute-start | bytes 1990664 | tf_op jit(solution)/shard_map/ppermute | solution.py:66
  121.5 17.8 %collective-permute-start.20 = (bf16[144,2304]{1,0:T(8,128)(2,1)S(1)}, bf16[144,2304]{1,0:T(8,128)(2,1)S(1)}, u32[]{:S(2)}, u32[]{:S(2)}) collective-permute-start(bf16[144,2304]{1,0:T(8,128)(2,1)S(1)} %get-tuple-element.53), channel_id=1, source_target_pairs={{0,192},{1,193},{2,194},{3,195},{4,196},{5,197},{6,198},{7,199},{8... | collective-permute-start | bytes 1990664 | tf_op jit(solution)/shard_map/ppermute | solution.py:66
  131.0 22.5 %collective-permute-start.22 = (bf16[144,2304]{1,0:T(8,128)(2,1)S(1)}, bf16[144,2304]{1,0:T(8,128)(2,1)S(1)}, u32[]{:S(2)}, u32[]{:S(2)}) collective-permute-start(bf16[144,2304]{1,0:T(8,128)(2,1)S(1)} %get-tuple-element.56), channel_id=1, source_target_pairs={{0,192},{1,193},{2,194},{3,195},{4,196},{5,197},{6,198},{7,199},{8... | collective-permute-start | bytes 1990664 | tf_op jit(solution)/shard_map/ppermute | solution.py:66
  139.5 19.1 %collective-permute-start.21 = (bf16[144,2304]{1,0:T(8,128)(2,1)S(1)}, bf16[144,2304]{1,0:T(8,128)(2,1)S(1)}, u32[]{:S(2)}, u32[]{:S(2)}) collective-permute-start(bf16[144,2304]{1,0:T(8,128)(2,1)S(1)} %add_convert_fusion.1), channel_id=1, source_target_pairs={{0,64},{1,65},{2,66},{3,67},{4,68},{5,69},{6,70},{7,71},{8,72},{9,... | collective-permute-start | bytes 1990664 | tf_op jit(solution)/shard_map/ppermute | solution.py:66
  141.1 27.2 %collective-permute-start.23 = (bf16[144,2304]{1,0:T(8,128)(2,1)S(1)}, bf16[144,2304]{1,0:T(8,128)(2,1)S(1)}, u32[]{:S(2)}, u32[]{:S(2)}) collective-permute-start(bf16[144,2304]{1,0:T(8,128)(2,1)S(1)} %get-tuple-element.57), channel_id=1, source_target_pairs={{0,64},{1,65},{2,66},{3,67},{4,68},{5,69},{6,70},{7,71},{8,72},{9,... | collective-permute-start | bytes 1990664 | tf_op jit(solution)/shard_map/ppermute | solution.py:66
  142.4 25.9 %collective-permute-start.24 = (bf16[144,2304]{1,0:T(8,128)(2,1)S(1)}, bf16[144,2304]{1,0:T(8,128)(2,1)S(1)}, u32[]{:S(2)}, u32[]{:S(2)}) collective-permute-start(bf16[144,2304]{1,0:T(8,128)(2,1)S(1)} %add_convert_fusion), channel_id=1, source_target_pairs={{0,192},{1,193},{2,194},{3,195},{4,196},{5,197},{6,198},{7,199},{8... | collective-permute-start | bytes 1990664 | tf_op jit(solution)/shard_map/ppermute | solution.py:66
  158.7 9.7 %copy-start.4 = (f32[288,2304]{1,0:T(8,128)S(1)}, f32[288,2304]{1,0:T(8,128)}, u32[]{:S(2)}) copy-start(f32[288,2304]{1,0:T(8,128)} %param.8) | copy-start | bytes 7962628

commit v10 on v9

--- a/solution.py
+++ b/solution.py
@@ -1,3 +1,4 @@
+import functools
 import math
 
 import jax
@@ -77,23 +78,29 @@
     return slot, m, 2 * (xh ^ (m // 2)) + (c ^ (m % 2))
 
 
+NEAR = (3, 4)
+
+
 def scale_kernel(place_ref, clip_ref, *refs):
     pieces, out_ref, held_ref, arrived = refs[:-3], refs[-3], refs[-2], refs[-1]
     half = out_ref.shape[3] // 2
-    copies = [
-        pltpu.make_async_copy(piece, held_ref.at[pl.ds(2 * i, 2)], arrived.at[i])
-        for i, piece in enumerate(pieces)
-    ]
-    for copy in copies:
-        copy.start()
-    for i, copy in enumerate(copies):
-        copy.wait()
+    copies = {}
+    for i, piece in enumerate(pieces):
+        if i not in NEAR:
+            place = held_ref.at[pl.ds(2 * len(copies), 2)]
+            copies[i] = (pltpu.make_async_copy(piece, place, arrived.at[i]), place)
+            copies[i][0].start()
+    for i, piece in enumerate(pieces):
+        blocks = piece
+        if i in copies:
+            copies[i][0].wait()
+            blocks = copies[i][1]
         for f in range(2):
             slot, m, member = position(place_ref, i + (i > 3), f)
             for e in range(2):
                 cols = slice(e * half, (e + 1) * half)
                 out_ref[slot, m, :, cols] = (
-                    clip_ref[2 * member + e] * held_ref[2 * i + f, :, cols].astype(F32)
+                    clip_ref[member, e] * blocks[f, :, cols].astype(F32)
                 ).astype(BF)
 
 
@@ -105,7 +112,7 @@
         for e in range(2):
             cols = slice(e * half, (e + 1) * half)
             held_ref[f, :, cols] = (
-                clip_ref[2 * member + e] * ref[:, cols].astype(F32)
+                clip_ref[member, e] * ref[:, cols].astype(F32)
             ).astype(BF)
         copies.append(pltpu.make_async_copy(held_ref.at[f], out_ref.at[slot, m], done.at[f]))
         copies[-1].start()
@@ -126,10 +133,11 @@
     most = pl.pallas_call(
         scale_kernel,
         out_shape=shape,
-        in_specs=[smem, smem] + [anywhere] * len(pieces),
+        in_specs=[smem, smem]
+        + [vmem if i in NEAR else anywhere for i in range(len(pieces))],
         out_specs=vmem,
         scratch_shapes=[
-            pltpu.VMEM((2 * len(pieces), rows, tokens), BF),
+            pltpu.VMEM((2 * (len(pieces) - len(NEAR)), rows, tokens), BF),
             pltpu.SemaphoreType.DMA((len(pieces),)),
         ],
         cost_estimate=cost,
@@ -149,7 +157,7 @@
     )(places, clips, *far, most)
 
 
-def product_kernel(s_ref, *refs):
+def product_kernel(scale, s_ref, *refs):
     acts, outs = refs[:6], refs[6:]
     slots, _, rows, tokens = s_ref.shape
     total = None
@@ -161,6 +169,9 @@
         part = jnp.dot(left, a_ref[...], preferred_element_type=F32)
         total = part if total is None else total + part
         first += count
+    if scale is not None:
+        noise_ref, outs = outs[0], outs[1:]
+        total = (scale[0] * total + noise_ref[...]) / scale[1]
     first = 0
     for out_ref in outs:
         count = out_ref.shape[0]
@@ -168,25 +179,25 @@
         first += count
 
 
-def product(name, scaled, first, slots, acts, tile, parts, dtype):
+def product(name, scaled, first, slots, acts, tile, parts, dtype, noise=(), scale=None):
     _, quarters, rows, tokens = scaled.shape
     width = acts[0].shape[1]
     count = slots * rows // parts
     return pl.pallas_call(
-        product_kernel,
+        functools.partial(product_kernel, scale),
         out_shape=[jax.ShapeDtypeStruct((count, width), dtype)] * parts,
         grid=(width // tile,),
         in_specs=[
             pl.BlockSpec((slots, quarters, rows, tokens), lambda j: (first // slots, 0, 0, 0))
         ]
-        + [pl.BlockSpec((a.shape[0], tile), lambda j: (0, j)) for a in acts],
+        + [pl.BlockSpec((a.shape[0], tile), lambda j: (0, j)) for a in [*acts, *noise]],
         out_specs=[pl.BlockSpec((count, tile), lambda j: (0, j))] * parts,
         cost_estimate=pl.CostEstimate(
             flops=2 * slots * rows * width, bytes_accessed=2 * rows * width, transcendentals=0
         ),
         compiler_params=pltpu.CompilerParams(vmem_limit_bytes=24 * 1024 * 1024),
         name=name,
-    )(scaled, *acts)
+    )(scaled, *acts, *noise)
 
 
 def all_to_all(value, axis, groups):
@@ -240,7 +251,7 @@
     fwd.append(send(fwd[2], along_z(1)))
     bwd.append(send(bwd[2], along_z(-1)))
     clip = jnp.minimum(1.0, clip_norm / jnp.sqrt(total))
-    clips = all_to_all(jnp.broadcast_to(clip, (4, examples)), "dp", chip_pairs).reshape(-1)
+    clips = all_to_all(jnp.broadcast_to(clip, (4, examples)), "dp", chip_pairs)
     fwd[3], bwd[3], clips, up, down = stage((fwd[3], bwd[3], clips, up, down))
 
     far = [send(fwd[3][0], along_z(1)), send(bwd[3][1], along_z(-1))]
@@ -259,15 +270,16 @@
     prev_b = (prev_b.astype(F32) + from_up.astype(F32)).astype(BF)
     next_a, prev_b, scaled = stage((next_a, prev_b, scaled))
     next_a, prev_b = send(next_a, along_y(1)), send(prev_b, along_y(-1))
-    (mine,) = product("product_own", scaled, 3, 1, held, tile, 1, F32)
-
     width = features * 2 * NZ
     factor = math.sqrt(columns * 2 * NZ * width) / clip_norm
     root = math.sqrt(examples * 4 * NY)
+    (mine,) = product(
+        "product_own", scaled, 3, 1, held, tile, 1, F32, [noise], (factor, root)
+    )
     summed = jnp.concatenate(
         [next_a.astype(F32) + prev_a.astype(F32), next_b.astype(F32) + prev_b.astype(F32)]
     )
-    return (factor * (mine + summed) + noise) / root
+    return mine + (factor / root) * summed
 
 
 def solution(mesh):

time: 174 us -> 173 us (level)
    div x1 -> x0, other arithmetic: 2.18 us -> none  [shards(): return (factor * (mine + summed) + noise) / root]
    add x0 -> x1, other arithmetic: none -> 1.81 us  [shards(): return mine + factor / root * summed]
  transfers between devices with their start and end apart: 26 -> 26, of which waited for: 12 -> 12; matrix products, arithmetic and copies ran while one was open for 5% -> 4% of each run, Pallas kernels for 10% -> 11%
where the time goes in v10:
time: 173 us; the launch traced here: 170 us
  waiting for transfers between devices  66.3 us (38%)
  starting transfers between devices  39.9 us (23%)
  blocking collectives  24.9 us (14%)
  Pallas kernels  23.4 us (14%)
  local copies, waits for them, and re-layouts  7.85 us (5%)
  other arithmetic  4.15 us (2%)
  matrix products  3.57 us (2%)
    ppermute x25, waiting for transfers between devices, send(): return lax.ppermute(value, AXES, perm)  54.9 us
    ppermute x25, starting transfers between devices, send(): return lax.ppermute(value, AXES, perm)  31.6 us
    all_to_all x2, blocking collectives, all_to_all(): lax.all_to_all(value, axis, 0, 0, tiled=True, axis_index_groups=groups)  24.9 us
    pallas_call x3, Pallas kernels, product(): pl.pallas_call(functools.partial(product_kernel, scale), out_shape=[jax.S...  18.6 us
    all_to_all x1, waiting for transfers between devices, all_to_all(): lax.all_to_all(value, axis, 0, 0, tiled=True, axis_index_groups=groups)  11.4 us
    all_to_all x1, starting transfers between devices, all_to_all(): lax.all_to_all(value, axis, 0, 0, tiled=True, axis_index_groups=groups)  8.26 us
    dot_general x2, matrix products, blocks(): jnp.einsum('btf,bsf->bts', x, x, preferred_element_type=F32).astype(BF)  3.57 us
  transfers between devices with their start and end apart: 26, of which 12 were waited for; matrix products, arithmetic and copies ran while one was open for 4% of the time, Pallas kernels for 11%

profile of v10, /device:TPU:32, one launch (start us, length us, event | category | flops | bytes accessed | tf_op | source)
XLA Modules:
  0.0 170.2 jit_solution(2904604021879990941)
XLA Ops:
  0.0 3.2 %convolution_convert_fusion.1 = bf16[2,256,256]{2,1,0:T(8,128)(2,1)S(1)} fusion(bf16[2,256,2304]{2,1,0:T(8,128)(2,1)} %param.5), kind=kOutput, calls=%fused_computation.7 | convolution fusion | flops 604110848 | bytes 2621440 | tf_op jit(solution)/shard_map/btf,bsf->bts/dot_general | solution.py:223
  3.3 0.4 convolution_convert_fusion
  3.8 0.0 copy-start
  3.8 1.6 collective-permute-start.2
  5.4 0.7 copy.27
  6.1 1.1 collective-permute-start.1
  7.2 4.1 %collective-permute-start = (bf16[288,512]{1,0:T(8,128)(2,1)}, bf16[288,512]{1,0:T(8,128)(2,1)}, u32[]{:S(2)}, u32[]{:S(2)}) collective-permute-start(bf16[288,512]{1,0:T(8,128)(2,1)} %bitcast.2), channel_id=1, source_target_pairs={{0,0},{1,18},{2,36},{3,50},{4,4},{5,22},{6,32},{7,54},{8,8},{9,26}... | collective-permute-start | bytes 884744 | tf_op jit(solution)/shard_map/ppermute | solution.py:67
  11.3 0.1 reduce_sum.36
  11.4 0.7 collective-permute-start.3
  12.1 13.3 %collective-permute-done.3 = f32[2]{0:T(128)S(1)} collective-permute-done((f32[2]{0:T(128)S(1)}, f32[2]{0:T(128)S(1)}, u32[]{:S(2)}, u32[]{:S(2)}) %collective-permute-start.3) | collective-permute-done | bytes 40 | tf_op jit(solution)/shard_map/ppermute | solution.py:67
  25.5 0.1 add_convert_fusion.2
  25.6 1.6 fusion.4
  27.2 2.0 %collective-permute-start.4 = (bf16[256,2304]{1,0:T(8,128)(2,1)}, bf16[256,2304]{1,0:T(8,128)(2,1)}, u32[]{:S(2)}, u32[]{:S(2)}) collective-permute-start(bf16[256,2304]{1,0:T(8,128)(2,1)} %get-tuple-element.60), channel_id=1, source_target_pairs={{0,8},{1,9},{2,10},{3,11},{4,12},{5,13},{6,14},{7,15},{8,32},{9,33... | collective-permute-start | bytes 3538952 | tf_op jit(solution)/shard_map/ppermute | solution.py:67
  29.2 0.8 copy.29
  30.0 8.3 %all-to-all-start = ((bf16[8,2,3,2,16,128]{5,4,3,2,1,0:T(8,128)(2,1)}), bf16[8,2,3,2,16,128]{5,4,3,2,1,0:T(8,128)(2,1)S(1)}, u32[]{:S(2)}, u32[]{:S(2)}) async-start(bf16[8,2,3,2,16,128]{5,4,3,2,1,0:T(8,128)(2,1)} %bitcast.43), calls=%async_computation | async-start | bytes 786432 | tf_op jit(solution)/shard_map/all_to_all | solution.py:204
  38.3 1.1 pad_maximum_fusion.refs_0_
  39.4 0.1 collective-permute-start.7
  39.5 2.0 %collective-permute-start.6 = (bf16[2,288,512]{2,1,0:T(8,128)(2,1)S(1)}, bf16[2,288,512]{2,1,0:T(8,128)(2,1)}, u32[]{:S(2)}, u32[]{:S(2)}) collective-permute-start(bf16[2,288,512]{2,1,0:T(8,128)(2,1)S(1)} %pad_maximum_fusion.refs_0_), channel_id=1, source_target_pairs={{0,1},{1,2},{2,3},{3,4},{4,5},{5,6},{6,7},{7,0},{8,9},{9,10},{10,1... | collective-permute-start | bytes 1769480 | tf_op jit(solution)/shard_map/ppermute | solution.py:67
  41.5 11.4 %all-to-all-done = bf16[8,2,3,2,16,128]{5,4,3,2,1,0:T(8,128)(2,1)S(1)} async-done(((bf16[8,2,3,2,16,128]{5,4,3,2,1,0:T(8,128)(2,1)}), bf16[8,2,3,2,16,128]{5,4,3,2,1,0:T(8,128)(2,1)S(1)}, u32[]{:S(2)}, u32[]{:S(2)}) %all-to-all-start) | async-done | bytes 393248 | tf_op jit(solution)/shard_map/all_to_all | solution.py:204
  52.9 0.1 convert_reduce_fusion
  52.9 0.2 fusion.3
  53.1 9.4 %collective-permute-done.7.refs_6_ = bf16[2,288,512]{2,1,0:T(8,128)(2,1)} collective-permute-done((bf16[2,288,512]{2,1,0:T(8,128)(2,1)S(1)}, bf16[2,288,512]{2,1,0:T(8,128)(2,1)}, u32[]{:S(2)}, u32[]{:S(2)}) %collective-permute-start.7) | collective-permute-done | bytes 589856 | tf_op jit(solution)/shard_map/ppermute | solution.py:67
  62.5 1.5 collective-permute-start.8
  64.1 0.6 collective-permute-start.9
  64.6 1.6 collective-permute-start.12
  66.2 1.6 collective-permute-start.13
  67.9 14.8 %all_to_all.20 = f32[8,1,2]{2,1,0:T(1,128)S(1)} all-to-all(f32[8,1,2]{2,1,0:T(1,128)S(1)} %broadcast_in_dim.7), channel_id=1, replica_groups={{0,1,2,3,4,5,6,7},{8,9,10,11,12,13,14,15},{16,17,18,19,20,21,22,23},{24..., dimensions={0} | all-to-all | bytes 128 | tf_op jit(solution)/shard_map/all_to_all | solution.py:204
  82.7 0.6 collective-permute-start.10
  83.4 1.5 collective-permute-start.11
  84.9 10.0 %all_to_all.21 = f32[4,1,2]{2,1,0:T(1,128)S(1)} all-to-all(f32[4,1,2]{2,1,0:T(1,128)S(1)} %broadcast_in_dim.8), channel_id=1, replica_groups={{0,16,32,48},{64,80,96,112},{128,144,160,176},{192,208,224,240},{1,17,3..., dimensions={0} | all-to-all | bytes 64 | tf_op jit(solution)/shard_map/all_to_all | solution.py:204
  94.9 0.1 copy.23
  95.0 2.1 %collective-permute-done.10.refs_3_ = bf16[2,288,512]{2,1,0:T(8,128)(2,1)} collective-permute-done((bf16[2,288,512]{2,1,0:T(8,128)(2,1)}, bf16[2,288,512]{2,1,0:T(8,128)(2,1)}, u32[]{:S(2)}, u32[]{:S(2)}) %collective-permute-start.10) | collective-permute-done | bytes 589856 | tf_op jit(solution)/shard_map/ppermute | solution.py:67
  97.0 0.3 collective-permute-done.11.refs_4_
  97.3 0.5 collective-permute-start.18
  97.8 1.7 slice_bitcast_fusion.1
  99.5 1.7 slice_bitcast_fusion
  101.2 1.6 collective-permute-start.15
  102.8 0.4 collective-permute-start.14
  103.2 0.1 pad_add_fusion.place_ref
  103.3 0.1 copy.25.clip_ref
  103.4 1.1 copy-done.3
  104.5 3.3 %scale_grads.1._ = bf16[4,4,288,512]{3,2,1,0:T(8,128)(2,1)S(1)} custom-call(s32[2]{0:T(128)S(1)} %pad_add_fusion.place_ref, f32[4,2]{1,0:T(4,128)S(1)} %copy.25.clip_ref, bf16[2,288,512]{2,1,0:T(8,128)(2,1)S(1)} %copy-done.3, bf16[2,288,512]{2,1,0:T(8,128)(2,1)} %collective-permute-done.6.refs_1_, bf16[2,288,512]{2,1,0:T(8,128)(2,1)} %collective-permute-done.8.refs_2_, ...), custom_call_target="tpu_custom_call" | custom-call | flops 2359296 | bytes 147456 | tf_op jit(solution)/shard_map/scale_grads/pallas_call | solution.py:133
  107.8 2.7 %collective-permute-done.15.second_ref = bf16[288,512]{1,0:T(8,128)(2,1)} collective-permute-done((bf16[288,512]{1,0:T(8,128)(2,1)}, bf16[288,512]{1,0:T(8,128)(2,1)}, u32[]{:S(2)}, u32[]{:S(2)}) %collective-permute-start.15) | collective-permute-done | bytes 294944 | tf_op jit(solution)/shard_map/ppermute | solution.py:67
  110.5 2.5 %collective-permute-done.14.first_ref = bf16[288,512]{1,0:T(8,128)(2,1)} collective-permute-done((bf16[288,512]{1,0:T(8,128)(2,1)}, bf16[288,512]{1,0:T(8,128)(2,1)}, u32[]{:S(2)}, u32[]{:S(2)}) %collective-permute-start.14) | collective-permute-done | bytes 294944 | tf_op jit(solution)/shard_map/ppermute | solution.py:67
  113.0 1.4 scale_last.1.s_ref
  114.4 5.3 %product_far.1 = (bf16[144,2304]{1,0:T(8,128)(2,1)S(1)}, bf16[144,2304]{1,0:T(8,128)(2,1)S(1)}) custom-call(bf16[4,4,288,512]{3,2,1,0:T(8,128)(2,1)S(1)} %scale_last.1.s_ref, bf16[512,2304]{1,0:T(8,128)(2,1)S(1)} %bitcast.46, bf16[512,2304]{1,0:T(8,128)(2,1)} %collective-permute-done.16.refs_1_, bf16[256,2304]{1,0:T(8,128)(2,1)S(1)} %collective-permute-done.12.refs_2_, ...), custom_call_target="tpu_custom_call" | custom-call | flops 1327104 | bytes 1327104 | tf_op jit(solution)/shard_map/product_far/pallas_call | solution.py:186
  119.8 1.7 collective-permute-start.19
  121.4 1.7 collective-permute-start.20
  123.1 7.9 %product_near.1 = (bf16[144,2304]{1,0:T(8,128)(2,1)S(1)}, bf16[144,2304]{1,0:T(8,128)(2,1)S(1)}, bf16[144,2304]{1,0:T(8,128)(2,1)S(1)}, bf16[144,2304]{1,0:T(8,128)(2,1)S(1)}) custom-call(bf16[4,4,288,512]{3,2,1,0:T(8,128)(2,1)S(1)} %scale_last.1.s_ref, bf16[512,2304]{1,0:T(8,128)(2,1)S(1)} %bitcast.47, bf16[512,2304]{1,0:T(8,128)(2,1)} %collective-permute-done.16.refs_1_, ...), custom_call_target="tpu_custom_call" | custom-call | flops 2654208 | bytes 1327104 | tf_op jit(solution)/shard_map/product_near/pallas_call | solution.py:186
  131.0 1.9 %collective-permute-start.22 = (bf16[144,2304]{1,0:T(8,128)(2,1)S(1)}, bf16[144,2304]{1,0:T(8,128)(2,1)S(1)}, u32[]{:S(2)}, u32[]{:S(2)}) collective-permute-start(bf16[144,2304]{1,0:T(8,128)(2,1)S(1)} %get-tuple-element.56), channel_id=1, source_target_pairs={{0,192},{1,193},{2,194},{3,195},{4,196},{5,197},{6,198},{7,199},{8... | collective-permute-start | bytes 1990664 | tf_op jit(solution)/shard_map/ppermute | solution.py:67
  132.9 4.3 %collective-permute-done.19 = bf16[144,2304]{1,0:T(8,128)(2,1)S(1)} collective-permute-done((bf16[144,2304]{1,0:T(8,128)(2,1)S(1)}, bf16[144,2304]{1,0:T(8,128)(2,1)S(1)}, u32[]{:S(2)}, u32[]{:S(2)}) %collective-permute-start.19) | collective-permute-done | bytes 663584 | tf_op jit(solution)/shard_map/ppermute | solution.py:67
  137.2 0.2 add_convert_fusion.1
  137.4 1.9 %collective-permute-done.20 = bf16[144,2304]{1,0:T(8,128)(2,1)S(1)} collective-permute-done((bf16[144,2304]{1,0:T(8,128)(2,1)S(1)}, bf16[144,2304]{1,0:T(8,128)(2,1)S(1)}, u32[]{:S(2)}, u32[]{:S(2)}) %collective-permute-start.20) | collective-permute-done | bytes 663584 | tf_op jit(solution)/shard_map/ppermute | solution.py:67
  139.3 0.2 add_convert_fusion
  139.4 1.7 collective-permute-start.21
  141.1 1.3 collective-permute-start.23
  142.4 2.0 %collective-permute-start.24 = (bf16[144,2304]{1,0:T(8,128)(2,1)S(1)}, bf16[144,2304]{1,0:T(8,128)(2,1)S(1)}, u32[]{:S(2)}, u32[]{:S(2)}) collective-permute-start(bf16[144,2304]{1,0:T(8,128)(2,1)S(1)} %add_convert_fusion), channel_id=1, source_target_pairs={{0,192},{1,193},{2,194},{3,195},{4,196},{5,197},{6,198},{7,199},{8... | collective-permute-start | bytes 1990664 | tf_op jit(solution)/shard_map/ppermute | solution.py:67
  144.3 5.4 %product_own.1 = f32[288,2304]{1,0:T(8,128)S(1)} custom-call(bf16[4,4,288,512]{3,2,1,0:T(8,128)(2,1)S(1)} %scale_last.1.s_ref, bf16[512,2304]{1,0:T(8,128)(2,1)S(1)} %bitcast.48, bf16[512,2304]{1,0:T(8,128)(2,1)} %collective-permute-done.16.refs_1_, bf16[256,2304]{1,0:T(8,128)(2,1)S(1)} %collective-permute-done.12.refs_2_, ...), custom_call_target="tpu_custom_call" | custom-call | flops 1327104 | bytes 1327104 | tf_op jit(solution)/shard_map/product_own/pallas_call | solution.py:186
  149.8 3.8 %collective-permute-done.22 = bf16[144,2304]{1,0:T(8,128)(2,1)S(1)} collective-permute-done((bf16[144,2304]{1,0:T(8,128)(2,1)S(1)}, bf16[144,2304]{1,0:T(8,128)(2,1)S(1)}, u32[]{:S(2)}, u32[]{:S(2)}) %collective-permute-start.22) | collective-permute-done | bytes 663584 | tf_op jit(solution)/shard_map/ppermute | solution.py:67
  153.5 5.1 %collective-permute-done.21 = bf16[144,2304]{1,0:T(8,128)(2,1)S(1)} collective-permute-done((bf16[144,2304]{1,0:T(8,128)(2,1)S(1)}, bf16[144,2304]{1,0:T(8,128)(2,1)S(1)}, u32[]{:S(2)}, u32[]{:S(2)}) %collective-permute-start.21) | collective-permute-done | bytes 663584 | tf_op jit(solution)/shard_map/ppermute | solution.py:67
  158.6 0.1 convert_add_fusion.1
  158.7 9.6 %collective-permute-done.23 = bf16[144,2304]{1,0:T(8,128)(2,1)S(1)} collective-permute-done((bf16[144,2304]{1,0:T(8,128)(2,1)S(1)}, bf16[144,2304]{1,0:T(8,128)(2,1)S(1)}, u32[]{:S(2)}, u32[]{:S(2)}) %collective-permute-start.23) | collective-permute-done | bytes 663584 | tf_op jit(solution)/shard_map/ppermute | solution.py:67
  168.3 0.1 convert_add_fusion
  168.4 1.8 %fusion = f32[288,2304]{1,0:T(8,128)} fusion(f32[288,2304]{1,0:T(8,128)S(1)} %product_own.1, f32[144,2304]{1,0:T(8,128)S(1)} %convert_add_fusion, f32[144,2304]{1,0:T(8,128)S(1)} %convert_add_fusion.1), kind=kLoop, calls=%fused_computation.1 | loop fusion | flops 1990656 | bytes 7962624 | tf_op jit(solution)/shard_map/add | solution.py:282
  (39 shorter events, 0.3 us)
Async XLA Ops:
  0.0 3.3 %copy-start.4 = (bf16[2,256,288]{1,2,0:T(8,128)(2,1)S(1)}, bf16[2,256,288]{1,2,0:T(8,128)(2,1)}, u32[]{:S(2)}) copy-start(bf16[2,256,288]{1,2,0:T(8,128)(2,1)} %param.6) | copy-start | bytes 884740
  3.6 7.7 %copy-start.5 = (f32[2,8]{1,0:T(2,128)S(1)}, f32[2,8]{1,0:T(2,128)}, u32[]{:S(2)}) copy-start(f32[2,8]{1,0:T(2,128)} %param.7) | copy-start | bytes 196
  3.8 21.8 %copy-start = (bf16[2,256,2304]{2,1,0:T(8,128)(2,1)S(1)}, bf16[2,256,2304]{2,1,0:T(8,128)(2,1)}, u32[]{:S(2)}) copy-start(bf16[2,256,2304]{2,1,0:T(8,128)(2,1)} %param.5) | copy-start | bytes 7077892
  3.8 21.6 %collective-permute-start.2 = (bf16[2,3,2,128,128]{4,3,2,1,0:T(8,128)(2,1)S(1)}, bf16[2,3,2,128,128]{4,3,2,1,0:T(8,128)(2,1)S(1)}, u32[]{:S(2)}, u32[]{:S(2)}) collective-permute-start(bf16[2,3,2,128,128]{4,3,2,1,0:T(8,128)(2,1)S(1)} %pad_maximum_fusion.1), channel_id=1, source_target_pairs={{0,8},{1,9},{2,10},{3,11},{4,12},{5,13},{6,14},{7,15},{8,0},{9,1},... | collective-permute-start | bytes 1179656 | tf_op jit(solution)/shard_map/ppermute | solution.py:67
  6.1 19.4 %collective-permute-start.1 = (bf16[288,512]{1,0:T(8,128)(2,1)}, bf16[288,512]{1,0:T(8,128)(2,1)}, u32[]{:S(2)}, u32[]{:S(2)}) collective-permute-start(bf16[288,512]{1,0:T(8,128)(2,1)} %bitcast.2), channel_id=1, source_target_pairs={{0,8},{1,26},{2,44},{3,58},{4,12},{5,30},{6,40},{7,62},{8,0},{9,18... | collective-permute-start | bytes 884744 | tf_op jit(solution)/shard_map/ppermute | solution.py:67
  7.2 18.4 %collective-permute-start = (bf16[288,512]{1,0:T(8,128)(2,1)}, bf16[288,512]{1,0:T(8,128)(2,1)}, u32[]{:S(2)}, u32[]{:S(2)}) collective-permute-start(bf16[288,512]{1,0:T(8,128)(2,1)} %bitcast.2), channel_id=1, source_target_pairs={{0,0},{1,18},{2,36},{3,50},{4,4},{5,22},{6,32},{7,54},{8,8},{9,26}... | collective-permute-start | bytes 884744 | tf_op jit(solution)/shard_map/ppermute | solution.py:67
  11.4 14.0 %collective-permute-start.3 = (f32[2]{0:T(128)S(1)}, f32[2]{0:T(128)S(1)}, u32[]{:S(2)}, u32[]{:S(2)}) collective-permute-start(f32[2]{0:T(128)S(1)} %reduce_sum.36), channel_id=1, source_target_pairs={{0,8},{1,9},{2,10},{3,11},{4,12},{5,13},{6,14},{7,15},{8,0},{9,1},... | collective-permute-start | bytes 32 | tf_op jit(solution)/shard_map/ppermute | solution.py:67
  27.2 35.3 %collective-permute-start.5 = (bf16[256,2304]{1,0:T(8,128)(2,1)}, bf16[256,2304]{1,0:T(8,128)(2,1)}, u32[]{:S(2)}, u32[]{:S(2)}) collective-permute-start(bf16[256,2304]{1,0:T(8,128)(2,1)} %get-tuple-element.59), channel_id=1, source_target_pairs={{0,40},{1,41},{2,42},{3,43},{4,44},{5,45},{6,46},{7,47},{8,0},{9,1... | collective-permute-start | bytes 3538952 | tf_op jit(solution)/shard_map/ppermute | solution.py:67
  27.2 35.3 %collective-permute-start.4 = (bf16[256,2304]{1,0:T(8,128)(2,1)}, bf16[256,2304]{1,0:T(8,128)(2,1)}, u32[]{:S(2)}, u32[]{:S(2)}) collective-permute-start(bf16[256,2304]{1,0:T(8,128)(2,1)} %get-tuple-element.60), channel_id=1, source_target_pairs={{0,8},{1,9},{2,10},{3,11},{4,12},{5,13},{6,14},{7,15},{8,32},{9,33... | collective-permute-start | bytes 3538952 | tf_op jit(solution)/shard_map/ppermute | solution.py:67
  30.0 22.9 %copy-start.6 = (f32[3]{0:T(128)S(1)}, f32[3]{0:T(128)}, u32[]{:S(2)}) copy-start(f32[3]{0:T(128)} %constant.17.clone) | copy-start | bytes 40
  30.0 22.9 %all-to-all-start = ((bf16[8,2,3,2,16,128]{5,4,3,2,1,0:T(8,128)(2,1)}), bf16[8,2,3,2,16,128]{5,4,3,2,1,0:T(8,128)(2,1)S(1)}, u32[]{:S(2)}, u32[]{:S(2)}) async-start(bf16[8,2,3,2,16,128]{5,4,3,2,1,0:T(8,128)(2,1)} %bitcast.43), calls=%async_computation | async-start | bytes 786432 | tf_op jit(solution)/shard_map/all_to_all | solution.py:204
  39.4 24.7 %copy-start.2 = (bf16[2,288,512]{2,1,0:T(8,128)(2,1)}, bf16[2,288,512]{2,1,0:T(8,128)(2,1)S(1)}, u32[]{:S(2)}) copy-start(bf16[2,288,512]{2,1,0:T(8,128)(2,1)S(1)} %pad_maximum_fusion.refs_0_) | copy-start | bytes 1769476
  39.4 23.1 %collective-permute-start.7 = (bf16[2,288,512]{2,1,0:T(8,128)(2,1)S(1)}, bf16[2,288,512]{2,1,0:T(8,128)(2,1)}, u32[]{:S(2)}, u32[]{:S(2)}) collective-permute-start(bf16[2,288,512]{2,1,0:T(8,128)(2,1)S(1)} %pad_maximum_fusion.refs_0_), channel_id=1, source_target_pairs={{0,7},{1,0},{2,1},{3,2},{4,3},{5,4},{6,5},{7,6},{8,15},{9,8},{10,9... | collective-permute-start | bytes 1769480 | tf_op jit(solution)/shard_map/ppermute | solution.py:67
  39.5 23.0 %collective-permute-start.6 = (bf16[2,288,512]{2,1,0:T(8,128)(2,1)S(1)}, bf16[2,288,512]{2,1,0:T(8,128)(2,1)}, u32[]{:S(2)}, u32[]{:S(2)}) collective-permute-start(bf16[2,288,512]{2,1,0:T(8,128)(2,1)S(1)} %pad_maximum_fusion.refs_0_), channel_id=1, source_target_pairs={{0,1},{1,2},{2,3},{3,4},{4,5},{5,6},{6,7},{7,0},{8,9},{9,10},{10,1... | collective-permute-start | bytes 1769480 | tf_op jit(solution)/shard_map/ppermute | solution.py:67
  62.5 20.2 %collective-permute-start.8 = (bf16[2,288,512]{2,1,0:T(8,128)(2,1)}, bf16[2,288,512]{2,1,0:T(8,128)(2,1)}, u32[]{:S(2)}, u32[]{:S(2)}) collective-permute-start(bf16[2,288,512]{2,1,0:T(8,128)(2,1)} %collective-permute-done.6.refs_1_), channel_id=1, source_target_pairs={{0,1},{1,2},{2,3},{3,4},{4,5},{5,6},{6,7},{7,0},{8,9},{9,10},{10,1... | collective-permute-start | bytes 1769480 | tf_op jit(solution)/shard_map/ppermute | solution.py:67
  64.1 18.7 %collective-permute-start.9 = (bf16[2,288,512]{2,1,0:T(8,128)(2,1)}, bf16[2,288,512]{2,1,0:T(8,128)(2,1)}, u32[]{:S(2)}, u32[]{:S(2)}) collective-permute-start(bf16[2,288,512]{2,1,0:T(8,128)(2,1)} %collective-permute-done.7.refs_6_), channel_id=1, source_target_pairs={{0,7},{1,0},{2,1},{3,2},{4,3},{5,4},{6,5},{7,6},{8,15},{9,8},{10,9... | collective-permute-start | bytes 1769480 | tf_op jit(solution)/shard_map/ppermute | solution.py:67
  64.6 32.7 %collective-permute-start.12 = (bf16[256,2304]{1,0:T(8,128)(2,1)}, bf16[256,2304]{1,0:T(8,128)(2,1)S(1)}, u32[]{:S(2)}, u32[]{:S(2)}) collective-permute-start(bf16[256,2304]{1,0:T(8,128)(2,1)} %collective-permute-done.4), channel_id=1, source_target_pairs={{0,8},{1,9},{2,10},{3,11},{4,12},{5,13},{6,14},{7,15},{8,32},{9,33... | collective-permute-start | bytes 3538952 | tf_op jit(solution)/shard_map/ppermute | solution.py:67
  66.2 31.1 %collective-permute-start.13 = (bf16[256,2304]{1,0:T(8,128)(2,1)}, bf16[256,2304]{1,0:T(8,128)(2,1)}, u32[]{:S(2)}, u32[]{:S(2)}) collective-permute-start(bf16[256,2304]{1,0:T(8,128)(2,1)} %collective-permute-done.5), channel_id=1, source_target_pairs={{0,40},{1,41},{2,42},{3,43},{4,44},{5,45},{6,46},{7,47},{8,0},{9,1... | collective-permute-start | bytes 3538952 | tf_op jit(solution)/shard_map/ppermute | solution.py:67
  67.9 46.6 %collective-permute-start.16 = (bf16[512,2304]{1,0:T(8,128)(2,1)S(1)}, bf16[512,2304]{1,0:T(8,128)(2,1)}, u32[]{:S(2)}, u32[]{:S(2)}) collective-permute-start(bf16[512,2304]{1,0:T(8,128)(2,1)S(1)} %bitcast.45), channel_id=1, source_target_pairs={{0,16},{1,17},{2,18},{3,19},{4,20},{5,21},{6,22},{7,23},{8,24},{9,... | collective-permute-start | bytes 7077896 | tf_op jit(solution)/shard_map/ppermute | solution.py:67
  82.7 14.3 %collective-permute-start.10 = (bf16[2,288,512]{2,1,0:T(8,128)(2,1)}, bf16[2,288,512]{2,1,0:T(8,128)(2,1)}, u32[]{:S(2)}, u32[]{:S(2)}) collective-permute-start(bf16[2,288,512]{2,1,0:T(8,128)(2,1)} %collective-permute-done.8.refs_2_), channel_id=1, source_target_pairs={{0,1},{1,2},{2,3},{3,4},{4,5},{5,6},{6,7},{7,0},{8,9},{9,10},{10,1... | collective-permute-start | bytes 1769480 | tf_op jit(solution)/shard_map/ppermute | solution.py:67
  83.4 13.9 %collective-permute-start.11 = (bf16[2,288,512]{2,1,0:T(8,128)(2,1)}, bf16[2,288,512]{2,1,0:T(8,128)(2,1)}, u32[]{:S(2)}, u32[]{:S(2)}) collective-permute-start(bf16[2,288,512]{2,1,0:T(8,128)(2,1)} %collective-permute-done.9.refs_5_), channel_id=1, source_target_pairs={{0,7},{1,0},{2,1},{3,2},{4,3},{5,4},{6,5},{7,6},{8,15},{9,8},{10,9... | collective-permute-start | bytes 1769480 | tf_op jit(solution)/shard_map/ppermute | solution.py:67
  97.3 17.1 %collective-permute-start.17 = (bf16[256,2304]{1,0:T(8,128)(2,1)S(1)}, bf16[256,2304]{1,0:T(8,128)(2,1)}, u32[]{:S(2)}, u32[]{:S(2)}) collective-permute-start(bf16[256,2304]{1,0:T(8,128)(2,1)S(1)} %collective-permute-done.12.refs_2_), channel_id=1, source_target_pairs={{0,16},{1,17},{2,18},{3,19},{4,20},{5,21},{6,22},{7,23},{8,24},{9,... | collective-permute-start | bytes 3538952 | tf_op jit(solution)/shard_map/ppermute | solution.py:67
  97.3 17.1 %collective-permute-start.18 = (bf16[256,2304]{1,0:T(8,128)(2,1)}, bf16[256,2304]{1,0:T(8,128)(2,1)}, u32[]{:S(2)}, u32[]{:S(2)}) collective-permute-start(bf16[256,2304]{1,0:T(8,128)(2,1)} %collective-permute-done.13.refs_3_), channel_id=1, source_target_pairs={{0,16},{1,17},{2,18},{3,19},{4,20},{5,21},{6,22},{7,23},{8,24},{9,... | collective-permute-start | bytes 3538952 | tf_op jit(solution)/shard_map/ppermute | solution.py:67
  101.2 9.3 %collective-permute-start.15 = (bf16[288,512]{1,0:T(8,128)(2,1)}, bf16[288,512]{1,0:T(8,128)(2,1)}, u32[]{:S(2)}, u32[]{:S(2)}) collective-permute-start(bf16[288,512]{1,0:T(8,128)(2,1)} %slice_bitcast_fusion), channel_id=1, source_target_pairs={{0,7},{1,0},{2,1},{3,2},{4,3},{5,4},{6,5},{7,6},{8,15},{9,8},{10,9... | collective-permute-start | bytes 884744 | tf_op jit(solution)/shard_map/ppermute | solution.py:67
  102.8 10.2 %collective-permute-start.14 = (bf16[288,512]{1,0:T(8,128)(2,1)}, bf16[288,512]{1,0:T(8,128)(2,1)}, u32[]{:S(2)}, u32[]{:S(2)}) collective-permute-start(bf16[288,512]{1,0:T(8,128)(2,1)} %slice_bitcast_fusion.1), channel_id=1, source_target_pairs={{0,1},{1,2},{2,3},{3,4},{4,5},{5,6},{6,7},{7,0},{8,9},{9,10},{10,1... | collective-permute-start | bytes 884744 | tf_op jit(solution)/shard_map/ppermute | solution.py:67
  103.4 1.1 copy-start.3
  119.8 17.4 %collective-permute-start.19 = (bf16[144,2304]{1,0:T(8,128)(2,1)S(1)}, bf16[144,2304]{1,0:T(8,128)(2,1)S(1)}, u32[]{:S(2)}, u32[]{:S(2)}) collective-permute-start(bf16[144,2304]{1,0:T(8,128)(2,1)S(1)} %get-tuple-element.51), channel_id=1, source_target_pairs={{0,64},{1,65},{2,66},{3,67},{4,68},{5,69},{6,70},{7,71},{8,72},{9,... | collective-permute-start | bytes 1990664 | tf_op jit(solution)/shard_map/ppermute | solution.py:67
  121.4 17.8 %collective-permute-start.20 = (bf16[144,2304]{1,0:T(8,128)(2,1)S(1)}, bf16[144,2304]{1,0:T(8,128)(2,1)S(1)}, u32[]{:S(2)}, u32[]{:S(2)}) collective-permute-start(bf16[144,2304]{1,0:T(8,128)(2,1)S(1)} %get-tuple-element.53), channel_id=1, source_target_pairs={{0,192},{1,193},{2,194},{3,195},{4,196},{5,197},{6,198},{7,199},{8... | collective-permute-start | bytes 1990664 | tf_op jit(solution)/shard_map/ppermute | solution.py:67
  131.0 22.5 %collective-permute-start.22 = (bf16[144,2304]{1,0:T(8,128)(2,1)S(1)}, bf16[144,2304]{1,0:T(8,128)(2,1)S(1)}, u32[]{:S(2)}, u32[]{:S(2)}) collective-permute-start(bf16[144,2304]{1,0:T(8,128)(2,1)S(1)} %get-tuple-element.56), channel_id=1, source_target_pairs={{0,192},{1,193},{2,194},{3,195},{4,196},{5,197},{6,198},{7,199},{8... | collective-permute-start | bytes 1990664 | tf_op jit(solution)/shard_map/ppermute | solution.py:67
  137.2 7.1 %copy-start.1 = (f32[288,2304]{1,0:T(8,128)S(1)}, f32[288,2304]{1,0:T(8,128)}, u32[]{:S(2)}) copy-start(f32[288,2304]{1,0:T(8,128)} %refs_6_.1) | copy-start | bytes 7962628
  139.4 19.1 %collective-permute-start.21 = (bf16[144,2304]{1,0:T(8,128)(2,1)S(1)}, bf16[144,2304]{1,0:T(8,128)(2,1)S(1)}, u32[]{:S(2)}, u32[]{:S(2)}) collective-permute-start(bf16[144,2304]{1,0:T(8,128)(2,1)S(1)} %add_convert_fusion.1), channel_id=1, source_target_pairs={{0,64},{1,65},{2,66},{3,67},{4,68},{5,69},{6,70},{7,71},{8,72},{9,... | collective-permute-start | bytes 1990664 | tf_op jit(solution)/shard_map/ppermute | solution.py:67
  141.1 27.2 %collective-permute-start.23 = (bf16[144,2304]{1,0:T(8,128)(2,1)S(1)}, bf16[144,2304]{1,0:T(8,128)(2,1)S(1)}, u32[]{:S(2)}, u32[]{:S(2)}) collective-permute-start(bf16[144,2304]{1,0:T(8,128)(2,1)S(1)} %get-tuple-element.57), channel_id=1, source_target_pairs={{0,64},{1,65},{2,66},{3,67},{4,68},{5,69},{6,70},{7,71},{8,72},{9,... | collective-permute-start | bytes 1990664 | tf_op jit(solution)/shard_map/ppermute | solution.py:67
  142.4 25.9 %collective-permute-start.24 = (bf16[144,2304]{1,0:T(8,128)(2,1)S(1)}, bf16[144,2304]{1,0:T(8,128)(2,1)S(1)}, u32[]{:S(2)}, u32[]{:S(2)}) collective-permute-start(bf16[144,2304]{1,0:T(8,128)(2,1)S(1)} %add_convert_fusion), channel_id=1, source_target_pairs={{0,192},{1,193},{2,194},{3,195},{4,196},{5,197},{6,198},{7,199},{8... | collective-permute-start | bytes 1990664 | tf_op jit(solution)/shard_map/ppermute | solution.py:67

commit v11 on v10

--- a/solution.py
+++ b/solution.py
@@ -58,6 +58,7 @@
     return perm_of(move)
 
 
+APART = perm_of(lambda y, xh, c, xl, z: (y, xh, c, xl, z + 1 - 2 * c))
 CORE = perm_of(lambda y, xh, c, xl, z: (y, xh, 1 - c, xl, z))
 XHI = perm_of(lambda y, xh, c, xl, z: (y, 1 - xh, c, xl, z))
 XLO = perm_of(lambda y, xh, c, xl, z: (y, xh, c, 1 - xl, z))
@@ -104,15 +105,15 @@
                 ).astype(BF)
 
 
-def last_kernel(place_ref, clip_ref, first_ref, second_ref, _, out_ref, held_ref, done):
+def last_kernel(place_ref, clip_ref, far_ref, _, out_ref, held_ref, done):
     half = held_ref.shape[2] // 2
     copies = []
-    for f, ref in enumerate((first_ref, second_ref)):
+    for f in range(2):
         slot, m, member = position(place_ref, 4, f)
         for e in range(2):
             cols = slice(e * half, (e + 1) * half)
             held_ref[f, :, cols] = (
-                clip_ref[member, e] * ref[:, cols].astype(F32)
+                clip_ref[member, e] * far_ref[f, :, cols].astype(F32)
             ).astype(BF)
         copies.append(pltpu.make_async_copy(held_ref.at[f], out_ref.at[slot, m], done.at[f]))
         copies[-1].start()
@@ -147,14 +148,14 @@
     return pl.pallas_call(
         last_kernel,
         out_shape=shape,
-        in_specs=[smem, smem, vmem, vmem, anywhere],
+        in_specs=[smem, smem, vmem, anywhere],
         out_specs=anywhere,
         scratch_shapes=[pltpu.VMEM((2, rows, tokens), BF), pltpu.SemaphoreType.DMA((2,))],
-        input_output_aliases={4: 0},
+        input_output_aliases={3: 0},
         cost_estimate=cost,
         compiler_params=params,
         name="scale_last",
-    )(places, clips, *far, most)
+    )(places, clips, far, most)
 
 
 def product_kernel(scale, s_ref, *refs):
@@ -254,7 +255,7 @@
     clips = all_to_all(jnp.broadcast_to(clip, (4, examples)), "dp", chip_pairs)
     fwd[3], bwd[3], clips, up, down = stage((fwd[3], bwd[3], clips, up, down))
 
-    far = [send(fwd[3][0], along_z(1)), send(bwd[3][1], along_z(-1))]
+    far = send(jnp.where(c == 0, fwd[3], bwd[3]), APART)
     up_sibling, down_sibling = send(up, CORE), send(down, CORE)
     pieces = [own, fwd[1], fwd[2], fwd[3], bwd[3], bwd[2], bwd[1]]
     places = jnp.stack([dp, te]).astype(jnp.int32)

time: 173 us -> 170 us (0.983)
  local copies, waits for them, and re-layouts: 7.85 us -> 4.47 us
  other arithmetic: 4.15 us -> 6.09 us
    squeeze x2 -> x0, local copies, waits for them, and re-layouts: 3.39 us -> none  [shards(): far = [send(fwd[3][0], along_z(1)), send(bwd[3][1], along_z(-1))]]
    select_n x0 -> x1, other arithmetic: none -> 1.94 us  [shards(): far = send(jnp.where(c == 0, fwd[3], bwd[3]), APART)]
    ppermute x25 -> x24, starting transfers between devices: 31.6 us -> 30.5 us  [send(): return lax.ppermute(value, AXES, perm)]
    ppermute x25 -> x24, waiting for transfers between devices: 54.9 us -> 54.3 us  [send(): return lax.ppermute(value, AXES, perm)]
  transfers between devices with their start and end apart: 26 -> 25, of which waited for: 12 -> 11; matrix products, arithmetic and copies ran while one was open for 4% -> 3% of each run, Pallas kernels for 11% -> 11%
where the time goes in v11:
time: 170 us; the launch traced here: 167 us
  waiting for transfers between devices  65.7 us (39%)
  starting transfers between devices  38.8 us (23%)
  blocking collectives  24.9 us (15%)
  Pallas kernels  23.4 us (14%)
  other arithmetic  6.09 us (4%)
  local copies, waits for them, and re-layouts  4.47 us (3%)
  matrix products  3.57 us (2%)
    ppermute x24, waiting for transfers between devices, send(): return lax.ppermute(value, AXES, perm)  54.3 us
    ppermute x24, starting transfers between devices, send(): return lax.ppermute(value, AXES, perm)  30.5 us
    all_to_all x2, blocking collectives, all_to_all(): lax.all_to_all(value, axis, 0, 0, tiled=True, axis_index_groups=groups)  24.9 us
    pallas_call x3, Pallas kernels, product(): pl.pallas_call(functools.partial(product_kernel, scale), out_shape=[jax.S...  18.6 us
    all_to_all x1, waiting for transfers between devices, all_to_all(): lax.all_to_all(value, axis, 0, 0, tiled=True, axis_index_groups=groups)  11.4 us
    all_to_all x1, starting transfers between devices, all_to_all(): lax.all_to_all(value, axis, 0, 0, tiled=True, axis_index_groups=groups)  8.26 us
    dot_general x2, matrix products, blocks(): jnp.einsum('btf,bsf->bts', x, x, preferred_element_type=F32).astype(BF)  3.57 us
  transfers between devices with their start and end apart: 25, of which 11 were waited for; matrix products, arithmetic and copies ran while one was open for 3% of the time, Pallas kernels for 11%

profile of v11, /device:TPU:32, one launch (start us, length us, event | category | flops | bytes accessed | tf_op | source)
XLA Modules:
  0.0 167.1 jit_solution(14757801955676136081)
XLA Ops:
  0.0 3.2 %convolution_convert_fusion.1 = bf16[2,256,256]{2,1,0:T(8,128)(2,1)S(1)} fusion(bf16[2,256,2304]{2,1,0:T(8,128)(2,1)} %param.5), kind=kOutput, calls=%fused_computation.7 | convolution fusion | flops 604110848 | bytes 2621440 | tf_op jit(solution)/shard_map/btf,bsf->bts/dot_general | solution.py:224
  3.3 0.4 convolution_convert_fusion
  3.6 0.0 copy-start.5
  3.8 0.0 copy-start
  3.8 1.6 collective-permute-start.2
  5.4 0.7 copy.27
  6.1 1.1 collective-permute-start.1
  7.2 4.1 %collective-permute-start = (bf16[288,512]{1,0:T(8,128)(2,1)}, bf16[288,512]{1,0:T(8,128)(2,1)}, u32[]{:S(2)}, u32[]{:S(2)}) collective-permute-start(bf16[288,512]{1,0:T(8,128)(2,1)} %bitcast.2), channel_id=1, source_target_pairs={{0,0},{1,18},{2,36},{3,50},{4,4},{5,22},{6,32},{7,54},{8,8},{9,26}... | collective-permute-start | bytes 884744 | tf_op jit(solution)/shard_map/ppermute | solution.py:68
  11.3 0.1 reduce_sum.36
  11.4 0.7 collective-permute-start.3
  12.1 13.3 %collective-permute-done.3 = f32[2]{0:T(128)S(1)} collective-permute-done((f32[2]{0:T(128)S(1)}, f32[2]{0:T(128)S(1)}, u32[]{:S(2)}, u32[]{:S(2)}) %collective-permute-start.3) | collective-permute-done | bytes 40 | tf_op jit(solution)/shard_map/ppermute | solution.py:68
  25.5 0.0 collective-permute-done.2
  25.5 0.1 add_convert_fusion.2
  25.6 0.0 collective-permute-done.1
  25.6 1.6 fusion.4
  27.2 2.0 %collective-permute-start.4 = (bf16[256,2304]{1,0:T(8,128)(2,1)}, bf16[256,2304]{1,0:T(8,128)(2,1)}, u32[]{:S(2)}, u32[]{:S(2)}) collective-permute-start(bf16[256,2304]{1,0:T(8,128)(2,1)} %get-tuple-element.60), channel_id=1, source_target_pairs={{0,8},{1,9},{2,10},{3,11},{4,12},{5,13},{6,14},{7,15},{8,32},{9,33... | collective-permute-start | bytes 3538952 | tf_op jit(solution)/shard_map/ppermute | solution.py:68
  29.2 0.8 copy.29
  30.0 8.3 %all-to-all-start = ((bf16[8,2,3,2,16,128]{5,4,3,2,1,0:T(8,128)(2,1)}), bf16[8,2,3,2,16,128]{5,4,3,2,1,0:T(8,128)(2,1)S(1)}, u32[]{:S(2)}, u32[]{:S(2)}) async-start(bf16[8,2,3,2,16,128]{5,4,3,2,1,0:T(8,128)(2,1)} %bitcast.39), calls=%async_computation | async-start | bytes 786432 | tf_op jit(solution)/shard_map/all_to_all | solution.py:205
  38.3 1.1 pad_maximum_fusion.refs_0_
  39.4 0.1 collective-permute-start.7
  39.5 2.0 %collective-permute-start.6 = (bf16[2,288,512]{2,1,0:T(8,128)(2,1)S(1)}, bf16[2,288,512]{2,1,0:T(8,128)(2,1)}, u32[]{:S(2)}, u32[]{:S(2)}) collective-permute-start(bf16[2,288,512]{2,1,0:T(8,128)(2,1)S(1)} %pad_maximum_fusion.refs_0_), channel_id=1, source_target_pairs={{0,1},{1,2},{2,3},{3,4},{4,5},{5,6},{6,7},{7,0},{8,9},{9,10},{10,1... | collective-permute-start | bytes 1769480 | tf_op jit(solution)/shard_map/ppermute | solution.py:68
  41.5 11.4 %all-to-all-done = bf16[8,2,3,2,16,128]{5,4,3,2,1,0:T(8,128)(2,1)S(1)} async-done(((bf16[8,2,3,2,16,128]{5,4,3,2,1,0:T(8,128)(2,1)}), bf16[8,2,3,2,16,128]{5,4,3,2,1,0:T(8,128)(2,1)S(1)}, u32[]{:S(2)}, u32[]{:S(2)}) %all-to-all-start) | async-done | bytes 393248 | tf_op jit(solution)/shard_map/all_to_all | solution.py:205
  52.9 0.1 convert_reduce_fusion
  52.9 0.2 fusion.3
  53.1 9.4 %collective-permute-done.7.refs_6_ = bf16[2,288,512]{2,1,0:T(8,128)(2,1)} collective-permute-done((bf16[2,288,512]{2,1,0:T(8,128)(2,1)S(1)}, bf16[2,288,512]{2,1,0:T(8,128)(2,1)}, u32[]{:S(2)}, u32[]{:S(2)}) %collective-permute-start.7) | collective-permute-done | bytes 589856 | tf_op jit(solution)/shard_map/ppermute | solution.py:68
  62.5 1.5 collective-permute-start.8
  64.1 0.6 collective-permute-start.9
  64.6 1.6 collective-permute-start.12
  66.2 1.6 collective-permute-start.13
  67.9 14.8 %all_to_all.20 = f32[8,1,2]{2,1,0:T(1,128)S(1)} all-to-all(f32[8,1,2]{2,1,0:T(1,128)S(1)} %broadcast_in_dim.7), channel_id=1, replica_groups={{0,1,2,3,4,5,6,7},{8,9,10,11,12,13,14,15},{16,17,18,19,20,21,22,23},{24..., dimensions={0} | all-to-all | bytes 128 | tf_op jit(solution)/shard_map/all_to_all | solution.py:205
  82.7 0.6 collective-permute-start.10
  83.4 1.5 collective-permute-start.11
  84.9 10.0 %all_to_all.21 = f32[4,1,2]{2,1,0:T(1,128)S(1)} all-to-all(f32[4,1,2]{2,1,0:T(1,128)S(1)} %broadcast_in_dim.8), channel_id=1, replica_groups={{0,16,32,48},{64,80,96,112},{128,144,160,176},{192,208,224,240},{1,17,3..., dimensions={0} | all-to-all | bytes 64 | tf_op jit(solution)/shard_map/all_to_all | solution.py:205
  94.9 0.1 copy.23
  95.0 2.1 %collective-permute-done.10.refs_3_ = bf16[2,288,512]{2,1,0:T(8,128)(2,1)} collective-permute-done((bf16[2,288,512]{2,1,0:T(8,128)(2,1)}, bf16[2,288,512]{2,1,0:T(8,128)(2,1)}, u32[]{:S(2)}, u32[]{:S(2)}) %collective-permute-start.10) | collective-permute-done | bytes 589856 | tf_op jit(solution)/shard_map/ppermute | solution.py:68
  97.0 0.3 collective-permute-done.11.refs_4_
  97.3 0.5 collective-permute-start.17
  97.8 1.9 %broadcast_select_fusion = bf16[2,288,512]{2,1,0:T(8,128)(2,1)} fusion(bf16[2,288,512]{2,1,0:T(8,128)(2,1)} %collective-permute-done.10.refs_3_, bf16[2,288,512]{2,1,0:T(8,128)(2,1)} %collective-permute-done.11.refs_4_, pred[]{:T(512)S(6)} %eq.5), kind=kLoop, calls=%fused_computation.11 | loop fusion | flops 294912 | bytes 1769473 | tf_op jit(solution)/shard_map/jit(_where)/select_n | solution.py:258
  99.8 1.0 collective-permute-start.14
  100.7 0.1 pad_add_fusion.place_ref
  100.8 0.1 copy.25.clip_ref
  100.9 1.1 copy-done.3
  102.0 3.3 %scale_grads.1._ = bf16[4,4,288,512]{3,2,1,0:T(8,128)(2,1)S(1)} custom-call(s32[2]{0:T(128)S(1)} %pad_add_fusion.place_ref, f32[4,2]{1,0:T(4,128)S(1)} %copy.25.clip_ref, bf16[2,288,512]{2,1,0:T(8,128)(2,1)S(1)} %copy-done.3, bf16[2,288,512]{2,1,0:T(8,128)(2,1)} %collective-permute-done.6.refs_1_, bf16[2,288,512]{2,1,0:T(8,128)(2,1)} %collective-permute-done.8.refs_2_, ...), custom_call_target="tpu_custom_call" | custom-call | flops 2359296 | bytes 147456 | tf_op jit(solution)/shard_map/scale_grads/pallas_call | solution.py:134
  105.3 4.6 %collective-permute-done.14.far_ref = bf16[2,288,512]{2,1,0:T(8,128)(2,1)} collective-permute-done((bf16[2,288,512]{2,1,0:T(8,128)(2,1)}, bf16[2,288,512]{2,1,0:T(8,128)(2,1)}, u32[]{:S(2)}, u32[]{:S(2)}) %collective-permute-start.14) | collective-permute-done | bytes 589856 | tf_op jit(solution)/shard_map/ppermute | solution.py:68
  110.0 1.4 scale_last.1.s_ref
  111.4 5.3 %product_far.1 = (bf16[144,2304]{1,0:T(8,128)(2,1)S(1)}, bf16[144,2304]{1,0:T(8,128)(2,1)S(1)}) custom-call(bf16[4,4,288,512]{3,2,1,0:T(8,128)(2,1)S(1)} %scale_last.1.s_ref, bf16[512,2304]{1,0:T(8,128)(2,1)S(1)} %bitcast.42, bf16[512,2304]{1,0:T(8,128)(2,1)} %collective-permute-done.15.refs_1_, bf16[256,2304]{1,0:T(8,128)(2,1)S(1)} %collective-permute-done.12.refs_2_, ...), custom_call_target="tpu_custom_call" | custom-call | flops 1327104 | bytes 1327104 | tf_op jit(solution)/shard_map/product_far/pallas_call | solution.py:187
  116.8 1.7 collective-permute-start.18
  118.4 1.7 collective-permute-start.19
  120.1 7.9 %product_near.1 = (bf16[144,2304]{1,0:T(8,128)(2,1)S(1)}, bf16[144,2304]{1,0:T(8,128)(2,1)S(1)}, bf16[144,2304]{1,0:T(8,128)(2,1)S(1)}, bf16[144,2304]{1,0:T(8,128)(2,1)S(1)}) custom-call(bf16[4,4,288,512]{3,2,1,0:T(8,128)(2,1)S(1)} %scale_last.1.s_ref, bf16[512,2304]{1,0:T(8,128)(2,1)S(1)} %bitcast.43, bf16[512,2304]{1,0:T(8,128)(2,1)} %collective-permute-done.15.refs_1_, ...), custom_call_target="tpu_custom_call" | custom-call | flops 2654208 | bytes 1327104 | tf_op jit(solution)/shard_map/product_near/pallas_call | solution.py:187
  128.0 1.9 %collective-permute-start.21 = (bf16[144,2304]{1,0:T(8,128)(2,1)S(1)}, bf16[144,2304]{1,0:T(8,128)(2,1)S(1)}, u32[]{:S(2)}, u32[]{:S(2)}) collective-permute-start(bf16[144,2304]{1,0:T(8,128)(2,1)S(1)} %get-tuple-element.56), channel_id=1, source_target_pairs={{0,192},{1,193},{2,194},{3,195},{4,196},{5,197},{6,198},{7,199},{8... | collective-permute-start | bytes 1990664 | tf_op jit(solution)/shard_map/ppermute | solution.py:68
  129.9 4.3 %collective-permute-done.18 = bf16[144,2304]{1,0:T(8,128)(2,1)S(1)} collective-permute-done((bf16[144,2304]{1,0:T(8,128)(2,1)S(1)}, bf16[144,2304]{1,0:T(8,128)(2,1)S(1)}, u32[]{:S(2)}, u32[]{:S(2)}) %collective-permute-start.18) | collective-permute-done | bytes 663584 | tf_op jit(solution)/shard_map/ppermute | solution.py:68
  134.2 0.2 add_convert_fusion.1
  134.3 1.9 %collective-permute-done.19 = bf16[144,2304]{1,0:T(8,128)(2,1)S(1)} collective-permute-done((bf16[144,2304]{1,0:T(8,128)(2,1)S(1)}, bf16[144,2304]{1,0:T(8,128)(2,1)S(1)}, u32[]{:S(2)}, u32[]{:S(2)}) %collective-permute-start.19) | collective-permute-done | bytes 663584 | tf_op jit(solution)/shard_map/ppermute | solution.py:68
  136.3 0.2 add_convert_fusion
  136.4 1.7 collective-permute-start.20
  138.1 1.3 collective-permute-start.22
  139.4 2.0 %collective-permute-start.23 = (bf16[144,2304]{1,0:T(8,128)(2,1)S(1)}, bf16[144,2304]{1,0:T(8,128)(2,1)S(1)}, u32[]{:S(2)}, u32[]{:S(2)}) collective-permute-start(bf16[144,2304]{1,0:T(8,128)(2,1)S(1)} %add_convert_fusion), channel_id=1, source_target_pairs={{0,192},{1,193},{2,194},{3,195},{4,196},{5,197},{6,198},{7,199},{8... | collective-permute-start | bytes 1990664 | tf_op jit(solution)/shard_map/ppermute | solution.py:68
  141.3 5.4 %product_own.1 = f32[288,2304]{1,0:T(8,128)S(1)} custom-call(bf16[4,4,288,512]{3,2,1,0:T(8,128)(2,1)S(1)} %scale_last.1.s_ref, bf16[512,2304]{1,0:T(8,128)(2,1)S(1)} %bitcast.44, bf16[512,2304]{1,0:T(8,128)(2,1)} %collective-permute-done.15.refs_1_, bf16[256,2304]{1,0:T(8,128)(2,1)S(1)} %collective-permute-done.12.refs_2_, ...), custom_call_target="tpu_custom_call" | custom-call | flops 1327104 | bytes 1327104 | tf_op jit(solution)/shard_map/product_own/pallas_call | solution.py:187
  146.7 3.8 %collective-permute-done.21 = bf16[144,2304]{1,0:T(8,128)(2,1)S(1)} collective-permute-done((bf16[144,2304]{1,0:T(8,128)(2,1)S(1)}, bf16[144,2304]{1,0:T(8,128)(2,1)S(1)}, u32[]{:S(2)}, u32[]{:S(2)}) %collective-permute-start.21) | collective-permute-done | bytes 663584 | tf_op jit(solution)/shard_map/ppermute | solution.py:68
  150.5 5.1 %collective-permute-done.20 = bf16[144,2304]{1,0:T(8,128)(2,1)S(1)} collective-permute-done((bf16[144,2304]{1,0:T(8,128)(2,1)S(1)}, bf16[144,2304]{1,0:T(8,128)(2,1)S(1)}, u32[]{:S(2)}, u32[]{:S(2)}) %collective-permute-start.20) | collective-permute-done | bytes 663584 | tf_op jit(solution)/shard_map/ppermute | solution.py:68
  155.6 0.1 convert_add_fusion.1
  155.7 9.5 %collective-permute-done.22 = bf16[144,2304]{1,0:T(8,128)(2,1)S(1)} collective-permute-done((bf16[144,2304]{1,0:T(8,128)(2,1)S(1)}, bf16[144,2304]{1,0:T(8,128)(2,1)S(1)}, u32[]{:S(2)}, u32[]{:S(2)}) %collective-permute-start.22) | collective-permute-done | bytes 663584 | tf_op jit(solution)/shard_map/ppermute | solution.py:68
  165.2 0.1 convert_add_fusion
  165.3 1.8 %fusion = f32[288,2304]{1,0:T(8,128)} fusion(f32[288,2304]{1,0:T(8,128)S(1)} %product_own.1, f32[144,2304]{1,0:T(8,128)S(1)} %convert_add_fusion, f32[144,2304]{1,0:T(8,128)S(1)} %convert_add_fusion.1), kind=kLoop, calls=%fused_computation.1 | loop fusion | flops 1990656 | bytes 7962624 | tf_op jit(solution)/shard_map/add | solution.py:283
  (36 shorter events, 0.3 us)
Async XLA Ops:
  0.0 3.3 %copy-start.4 = (bf16[2,256,288]{1,2,0:T(8,128)(2,1)S(1)}, bf16[2,256,288]{1,2,0:T(8,128)(2,1)}, u32[]{:S(2)}) copy-start(bf16[2,256,288]{1,2,0:T(8,128)(2,1)} %param.6) | copy-start | bytes 884740
  3.6 7.7 %copy-start.5 = (f32[2,8]{1,0:T(2,128)S(1)}, f32[2,8]{1,0:T(2,128)}, u32[]{:S(2)}) copy-start(f32[2,8]{1,0:T(2,128)} %param.7) | copy-start | bytes 196
  3.8 21.8 %copy-start = (bf16[2,256,2304]{2,1,0:T(8,128)(2,1)S(1)}, bf16[2,256,2304]{2,1,0:T(8,128)(2,1)}, u32[]{:S(2)}) copy-start(bf16[2,256,2304]{2,1,0:T(8,128)(2,1)} %param.5) | copy-start | bytes 7077892
  3.8 21.6 %collective-permute-start.2 = (bf16[2,3,2,128,128]{4,3,2,1,0:T(8,128)(2,1)S(1)}, bf16[2,3,2,128,128]{4,3,2,1,0:T(8,128)(2,1)S(1)}, u32[]{:S(2)}, u32[]{:S(2)}) collective-permute-start(bf16[2,3,2,128,128]{4,3,2,1,0:T(8,128)(2,1)S(1)} %pad_maximum_fusion.1), channel_id=1, source_target_pairs={{0,8},{1,9},{2,10},{3,11},{4,12},{5,13},{6,14},{7,15},{8,0},{9,1},... | collective-permute-start | bytes 1179656 | tf_op jit(solution)/shard_map/ppermute | solution.py:68
  6.1 19.4 %collective-permute-start.1 = (bf16[288,512]{1,0:T(8,128)(2,1)}, bf16[288,512]{1,0:T(8,128)(2,1)}, u32[]{:S(2)}, u32[]{:S(2)}) collective-permute-start(bf16[288,512]{1,0:T(8,128)(2,1)} %bitcast.2), channel_id=1, source_target_pairs={{0,8},{1,26},{2,44},{3,58},{4,12},{5,30},{6,40},{7,62},{8,0},{9,18... | collective-permute-start | bytes 884744 | tf_op jit(solution)/shard_map/ppermute | solution.py:68
  7.2 18.4 %collective-permute-start = (bf16[288,512]{1,0:T(8,128)(2,1)}, bf16[288,512]{1,0:T(8,128)(2,1)}, u32[]{:S(2)}, u32[]{:S(2)}) collective-permute-start(bf16[288,512]{1,0:T(8,128)(2,1)} %bitcast.2), channel_id=1, source_target_pairs={{0,0},{1,18},{2,36},{3,50},{4,4},{5,22},{6,32},{7,54},{8,8},{9,26}... | collective-permute-start | bytes 884744 | tf_op jit(solution)/shard_map/ppermute | solution.py:68
  11.4 14.0 %collective-permute-start.3 = (f32[2]{0:T(128)S(1)}, f32[2]{0:T(128)S(1)}, u32[]{:S(2)}, u32[]{:S(2)}) collective-permute-start(f32[2]{0:T(128)S(1)} %reduce_sum.36), channel_id=1, source_target_pairs={{0,8},{1,9},{2,10},{3,11},{4,12},{5,13},{6,14},{7,15},{8,0},{9,1},... | collective-permute-start | bytes 32 | tf_op jit(solution)/shard_map/ppermute | solution.py:68
  27.2 35.3 %collective-permute-start.5 = (bf16[256,2304]{1,0:T(8,128)(2,1)}, bf16[256,2304]{1,0:T(8,128)(2,1)}, u32[]{:S(2)}, u32[]{:S(2)}) collective-permute-start(bf16[256,2304]{1,0:T(8,128)(2,1)} %get-tuple-element.59), channel_id=1, source_target_pairs={{0,40},{1,41},{2,42},{3,43},{4,44},{5,45},{6,46},{7,47},{8,0},{9,1... | collective-permute-start | bytes 3538952 | tf_op jit(solution)/shard_map/ppermute | solution.py:68
  27.2 35.3 %collective-permute-start.4 = (bf16[256,2304]{1,0:T(8,128)(2,1)}, bf16[256,2304]{1,0:T(8,128)(2,1)}, u32[]{:S(2)}, u32[]{:S(2)}) collective-permute-start(bf16[256,2304]{1,0:T(8,128)(2,1)} %get-tuple-element.60), channel_id=1, source_target_pairs={{0,8},{1,9},{2,10},{3,11},{4,12},{5,13},{6,14},{7,15},{8,32},{9,33... | collective-permute-start | bytes 3538952 | tf_op jit(solution)/shard_map/ppermute | solution.py:68
  30.0 22.9 %copy-start.6 = (f32[3]{0:T(128)S(1)}, f32[3]{0:T(128)}, u32[]{:S(2)}) copy-start(f32[3]{0:T(128)} %constant.31.clone) | copy-start | bytes 40
  30.0 22.9 %all-to-all-start = ((bf16[8,2,3,2,16,128]{5,4,3,2,1,0:T(8,128)(2,1)}), bf16[8,2,3,2,16,128]{5,4,3,2,1,0:T(8,128)(2,1)S(1)}, u32[]{:S(2)}, u32[]{:S(2)}) async-start(bf16[8,2,3,2,16,128]{5,4,3,2,1,0:T(8,128)(2,1)} %bitcast.39), calls=%async_computation | async-start | bytes 786432 | tf_op jit(solution)/shard_map/all_to_all | solution.py:205
  39.4 24.7 %copy-start.2 = (bf16[2,288,512]{2,1,0:T(8,128)(2,1)}, bf16[2,288,512]{2,1,0:T(8,128)(2,1)S(1)}, u32[]{:S(2)}) copy-start(bf16[2,288,512]{2,1,0:T(8,128)(2,1)S(1)} %pad_maximum_fusion.refs_0_) | copy-start | bytes 1769476
  39.4 23.1 %collective-permute-start.7 = (bf16[2,288,512]{2,1,0:T(8,128)(2,1)S(1)}, bf16[2,288,512]{2,1,0:T(8,128)(2,1)}, u32[]{:S(2)}, u32[]{:S(2)}) collective-permute-start(bf16[2,288,512]{2,1,0:T(8,128)(2,1)S(1)} %pad_maximum_fusion.refs_0_), channel_id=1, source_target_pairs={{0,7},{1,0},{2,1},{3,2},{4,3},{5,4},{6,5},{7,6},{8,15},{9,8},{10,9... | collective-permute-start | bytes 1769480 | tf_op jit(solution)/shard_map/ppermute | solution.py:68
  39.5 23.0 %collective-permute-start.6 = (bf16[2,288,512]{2,1,0:T(8,128)(2,1)S(1)}, bf16[2,288,512]{2,1,0:T(8,128)(2,1)}, u32[]{:S(2)}, u32[]{:S(2)}) collective-permute-start(bf16[2,288,512]{2,1,0:T(8,128)(2,1)S(1)} %pad_maximum_fusion.refs_0_), channel_id=1, source_target_pairs={{0,1},{1,2},{2,3},{3,4},{4,5},{5,6},{6,7},{7,0},{8,9},{9,10},{10,1... | collective-permute-start | bytes 1769480 | tf_op jit(solution)/shard_map/ppermute | solution.py:68
  62.5 20.2 %collective-permute-start.8 = (bf16[2,288,512]{2,1,0:T(8,128)(2,1)}, bf16[2,288,512]{2,1,0:T(8,128)(2,1)}, u32[]{:S(2)}, u32[]{:S(2)}) collective-permute-start(bf16[2,288,512]{2,1,0:T(8,128)(2,1)} %collective-permute-done.6.refs_1_), channel_id=1, source_target_pairs={{0,1},{1,2},{2,3},{3,4},{4,5},{5,6},{6,7},{7,0},{8,9},{9,10},{10,1... | collective-permute-start | bytes 1769480 | tf_op jit(solution)/shard_map/ppermute | solution.py:68
  64.1 18.7 %collective-permute-start.9 = (bf16[2,288,512]{2,1,0:T(8,128)(2,1)}, bf16[2,288,512]{2,1,0:T(8,128)(2,1)}, u32[]{:S(2)}, u32[]{:S(2)}) collective-permute-start(bf16[2,288,512]{2,1,0:T(8,128)(2,1)} %collective-permute-done.7.refs_6_), channel_id=1, source_target_pairs={{0,7},{1,0},{2,1},{3,2},{4,3},{5,4},{6,5},{7,6},{8,15},{9,8},{10,9... | collective-permute-start | bytes 1769480 | tf_op jit(solution)/shard_map/ppermute | solution.py:68
  64.6 32.7 %collective-permute-start.12 = (bf16[256,2304]{1,0:T(8,128)(2,1)}, bf16[256,2304]{1,0:T(8,128)(2,1)S(1)}, u32[]{:S(2)}, u32[]{:S(2)}) collective-permute-start(bf16[256,2304]{1,0:T(8,128)(2,1)} %collective-permute-done.4), channel_id=1, source_target_pairs={{0,8},{1,9},{2,10},{3,11},{4,12},{5,13},{6,14},{7,15},{8,32},{9,33... | collective-permute-start | bytes 3538952 | tf_op jit(solution)/shard_map/ppermute | solution.py:68
  66.2 31.1 %collective-permute-start.13 = (bf16[256,2304]{1,0:T(8,128)(2,1)}, bf16[256,2304]{1,0:T(8,128)(2,1)}, u32[]{:S(2)}, u32[]{:S(2)}) collective-permute-start(bf16[256,2304]{1,0:T(8,128)(2,1)} %collective-permute-done.5), channel_id=1, source_target_pairs={{0,40},{1,41},{2,42},{3,43},{4,44},{5,45},{6,46},{7,47},{8,0},{9,1... | collective-permute-start | bytes 3538952 | tf_op jit(solution)/shard_map/ppermute | solution.py:68
  67.9 43.5 %collective-permute-start.15 = (bf16[512,2304]{1,0:T(8,128)(2,1)S(1)}, bf16[512,2304]{1,0:T(8,128)(2,1)}, u32[]{:S(2)}, u32[]{:S(2)}) collective-permute-start(bf16[512,2304]{1,0:T(8,128)(2,1)S(1)} %bitcast.41), channel_id=1, source_target_pairs={{0,16},{1,17},{2,18},{3,19},{4,20},{5,21},{6,22},{7,23},{8,24},{9,... | collective-permute-start | bytes 7077896 | tf_op jit(solution)/shard_map/ppermute | solution.py:68
  82.7 14.3 %collective-permute-start.10 = (bf16[2,288,512]{2,1,0:T(8,128)(2,1)}, bf16[2,288,512]{2,1,0:T(8,128)(2,1)}, u32[]{:S(2)}, u32[]{:S(2)}) collective-permute-start(bf16[2,288,512]{2,1,0:T(8,128)(2,1)} %collective-permute-done.8.refs_2_), channel_id=1, source_target_pairs={{0,1},{1,2},{2,3},{3,4},{4,5},{5,6},{6,7},{7,0},{8,9},{9,10},{10,1... | collective-permute-start | bytes 1769480 | tf_op jit(solution)/shard_map/ppermute | solution.py:68
  83.4 13.9 %collective-permute-start.11 = (bf16[2,288,512]{2,1,0:T(8,128)(2,1)}, bf16[2,288,512]{2,1,0:T(8,128)(2,1)}, u32[]{:S(2)}, u32[]{:S(2)}) collective-permute-start(bf16[2,288,512]{2,1,0:T(8,128)(2,1)} %collective-permute-done.9.refs_5_), channel_id=1, source_target_pairs={{0,7},{1,0},{2,1},{3,2},{4,3},{5,4},{6,5},{7,6},{8,15},{9,8},{10,9... | collective-permute-start | bytes 1769480 | tf_op jit(solution)/shard_map/ppermute | solution.py:68
  97.3 14.1 %collective-permute-start.16 = (bf16[256,2304]{1,0:T(8,128)(2,1)S(1)}, bf16[256,2304]{1,0:T(8,128)(2,1)}, u32[]{:S(2)}, u32[]{:S(2)}) collective-permute-start(bf16[256,2304]{1,0:T(8,128)(2,1)S(1)} %collective-permute-done.12.refs_2_), channel_id=1, source_target_pairs={{0,16},{1,17},{2,18},{3,19},{4,20},{5,21},{6,22},{7,23},{8,24},{9,... | collective-permute-start | bytes 3538952 | tf_op jit(solution)/shard_map/ppermute | solution.py:68
  97.3 14.1 %collective-permute-start.17 = (bf16[256,2304]{1,0:T(8,128)(2,1)}, bf16[256,2304]{1,0:T(8,128)(2,1)}, u32[]{:S(2)}, u32[]{:S(2)}) collective-permute-start(bf16[256,2304]{1,0:T(8,128)(2,1)} %collective-permute-done.13.refs_3_), channel_id=1, source_target_pairs={{0,16},{1,17},{2,18},{3,19},{4,20},{5,21},{6,22},{7,23},{8,24},{9,... | collective-permute-start | bytes 3538952 | tf_op jit(solution)/shard_map/ppermute | solution.py:68
  99.8 10.2 %collective-permute-start.14 = (bf16[2,288,512]{2,1,0:T(8,128)(2,1)}, bf16[2,288,512]{2,1,0:T(8,128)(2,1)}, u32[]{:S(2)}, u32[]{:S(2)}) collective-permute-start(bf16[2,288,512]{2,1,0:T(8,128)(2,1)} %broadcast_select_fusion), channel_id=1, source_target_pairs={{0,1},{1,2},{2,3},{3,4},{4,5},{5,6},{6,7},{7,0},{8,9},{9,10},{10,1... | collective-permute-start | bytes 1769480 | tf_op jit(solution)/shard_map/ppermute | solution.py:68
  100.9 1.1 copy-start.3
  116.8 17.4 %collective-permute-start.18 = (bf16[144,2304]{1,0:T(8,128)(2,1)S(1)}, bf16[144,2304]{1,0:T(8,128)(2,1)S(1)}, u32[]{:S(2)}, u32[]{:S(2)}) collective-permute-start(bf16[144,2304]{1,0:T(8,128)(2,1)S(1)} %get-tuple-element.51), channel_id=1, source_target_pairs={{0,64},{1,65},{2,66},{3,67},{4,68},{5,69},{6,70},{7,71},{8,72},{9,... | collective-permute-start | bytes 1990664 | tf_op jit(solution)/shard_map/ppermute | solution.py:68
  118.4 17.8 %collective-permute-start.19 = (bf16[144,2304]{1,0:T(8,128)(2,1)S(1)}, bf16[144,2304]{1,0:T(8,128)(2,1)S(1)}, u32[]{:S(2)}, u32[]{:S(2)}) collective-permute-start(bf16[144,2304]{1,0:T(8,128)(2,1)S(1)} %get-tuple-element.53), channel_id=1, source_target_pairs={{0,192},{1,193},{2,194},{3,195},{4,196},{5,197},{6,198},{7,199},{8... | collective-permute-start | bytes 1990664 | tf_op jit(solution)/shard_map/ppermute | solution.py:68
  128.0 22.5 %collective-permute-start.21 = (bf16[144,2304]{1,0:T(8,128)(2,1)S(1)}, bf16[144,2304]{1,0:T(8,128)(2,1)S(1)}, u32[]{:S(2)}, u32[]{:S(2)}) collective-permute-start(bf16[144,2304]{1,0:T(8,128)(2,1)S(1)} %get-tuple-element.56), channel_id=1, source_target_pairs={{0,192},{1,193},{2,194},{3,195},{4,196},{5,197},{6,198},{7,199},{8... | collective-permute-start | bytes 1990664 | tf_op jit(solution)/shard_map/ppermute | solution.py:68
  134.2 7.1 %copy-start.1 = (f32[288,2304]{1,0:T(8,128)S(1)}, f32[288,2304]{1,0:T(8,128)}, u32[]{:S(2)}) copy-start(f32[288,2304]{1,0:T(8,128)} %refs_6_.1) | copy-start | bytes 7962628
  136.4 19.1 %collective-permute-start.20 = (bf16[144,2304]{1,0:T(8,128)(2,1)S(1)}, bf16[144,2304]{1,0:T(8,128)(2,1)S(1)}, u32[]{:S(2)}, u32[]{:S(2)}) collective-permute-start(bf16[144,2304]{1,0:T(8,128)(2,1)S(1)} %add_convert_fusion.1), channel_id=1, source_target_pairs={{0,64},{1,65},{2,66},{3,67},{4,68},{5,69},{6,70},{7,71},{8,72},{9,... | collective-permute-start | bytes 1990664 | tf_op jit(solution)/shard_map/ppermute | solution.py:68
  138.1 27.1 %collective-permute-start.22 = (bf16[144,2304]{1,0:T(8,128)(2,1)S(1)}, bf16[144,2304]{1,0:T(8,128)(2,1)S(1)}, u32[]{:S(2)}, u32[]{:S(2)}) collective-permute-start(bf16[144,2304]{1,0:T(8,128)(2,1)S(1)} %get-tuple-element.57), channel_id=1, source_target_pairs={{0,64},{1,65},{2,66},{3,67},{4,68},{5,69},{6,70},{7,71},{8,72},{9,... | collective-permute-start | bytes 1990664 | tf_op jit(solution)/shard_map/ppermute | solution.py:68
  139.4 25.8 %collective-permute-start.23 = (bf16[144,2304]{1,0:T(8,128)(2,1)S(1)}, bf16[144,2304]{1,0:T(8,128)(2,1)S(1)}, u32[]{:S(2)}, u32[]{:S(2)}) collective-permute-start(bf16[144,2304]{1,0:T(8,128)(2,1)S(1)} %add_convert_fusion), channel_id=1, source_target_pairs={{0,192},{1,193},{2,194},{3,195},{4,196},{5,197},{6,198},{7,199},{8... | collective-permute-start | bytes 1990664 | tf_op jit(solution)/shard_map/ppermute | solution.py:68
